TPU v7x, 32 devices: a whole 2x2x4 slice. The times are simulated.
32 devices in a mesh: seq: 8 (over z, y), ctx: 4 (over x, core).
Axes of the slice: x: 2, y: 2, z: 4, core: 2. Of those that a mesh axis runs over, the one named last changes fastest.
Arguments:
- tokens: bfloat16 [64, 512, 1024], P('seq', 'ctx'), may hold values from -6 to 6
- segment_ids: int32 [64, 512], P('seq'), may hold values from 0 to 2, as said below
- project_weight: bfloat16 [1024, 3072], P(('seq', 'ctx')), may hold values from -0.25 to 0.25
- query_bias: bfloat16 [1024], P(('seq', 'ctx')), may hold values from -3 to 3
- value_bias: bfloat16 [1024], P(('seq', 'ctx')), may hold values from -3 to 3
- output_weight: bfloat16 [1024, 1024], P(('seq', 'ctx')), may hold values from -0.5 to 0.5
- output_bias: bfloat16 [1024], P(('seq', 'ctx')), may hold values from -2 to 2
- first_gain: bfloat16 [1024], P(('seq', 'ctx')), may hold values from 0.5 to 1.5
- first_shift: bfloat16 [1024], P(('seq', 'ctx')), may hold values from -2 to 2
- expand_weight: bfloat16 [1024, 4096], P(('seq', 'ctx')), may hold values from -0.1875 to 0.1875
- expand_bias: bfloat16 [4096], P(('seq', 'ctx')), may hold values from -3 to 3
- reduce_weight: bfloat16 [4096, 1024], P(('seq', 'ctx')), may hold values from -0.09375 to 0.09375
- reduce_bias: bfloat16 [1024], P(('seq', 'ctx')), may hold values from -2 to 2
- second_gain: bfloat16 [1024], P(('seq', 'ctx')), may hold values from 0.5 to 1.5
- second_shift: bfloat16 [1024], P(('seq', 'ctx')), may hold values from -2 to 2
- grad_out: bfloat16 [64, 512, 1024], P('seq', 'ctx'), may hold values from -6 to 6
Outputs:
- layer_out: bfloat16 [64, 512, 1024], P('seq', 'ctx')
- grad_tokens: float32 [64, 512, 1024], P('seq', 'ctx')
- project_grad: float32 [1024, 3072], P(('seq', 'ctx'))
- query_bias_grad: float32 [1024], P(('seq', 'ctx'))
- value_bias_grad: float32 [1024], P(('seq', 'ctx'))
- output_grad: float32 [1024, 1024], P(('seq', 'ctx'))
- output_bias_grad: float32 [1024], P(('seq', 'ctx'))
- first_gain_grad: float32 [1024], P(('seq', 'ctx'))
- first_shift_grad: float32 [1024], P(('seq', 'ctx'))
- expand_grad: float32 [1024, 4096], P(('seq', 'ctx'))
- expand_bias_grad: float32 [4096], P(('seq', 'ctx'))
- reduce_grad: float32 [4096, 1024], P(('seq', 'ctx'))
- reduce_bias_grad: float32 [1024], P(('seq', 'ctx'))
- second_gain_grad: float32 [1024], P(('seq', 'ctx'))
- second_shift_grad: float32 [1024], P(('seq', 'ctx'))
Inputs may be any that keep to these rules, and one draw needn't show every extreme that they name: `segment_ids`: within each sequence the ids start at 0 and never fall; equal ids mark one document's piece, and every piece has 64 tokens or more. In each aligned block of 8 sequences one holds a single document; the others hold three.
All inputs are finite; a program needn't handle non-finite values.
Results may differ from a plain program's by a relative error of at most 0.014.
The roundings to bfloat16 on the way count: a program that leaves them out, or rounds other values in their place, can miss the bound.
Values may be sent and summed in bfloat16 or wider, within the bound.
No kernel may reach another device: no remote copies, remote signals or barrier semaphores. Data moves between devices by JAX's collectives and lax.ppermute only.
A program may use at most 320 MiB of HBM per device.

v0:
```python
import math

import jax
import jax.numpy as jnp
from jax import lax
from jax.sharding import PartitionSpec as P

HEADS = 16
HEAD_DIM = 64


def times_right(left, right):
    return lax.dot_general(
        left, right, (((1,), (1,)), ((), ())), preferred_element_type=jnp.float32
    )


def times_left(left, right):
    return lax.dot_general(
        left, right, (((0,), (0,)), ((), ())), preferred_element_type=jnp.float32
    )


def normalize(values, gain, shift):
    center = values - jnp.mean(values, axis=-1, keepdims=True)
    inverse = lax.rsqrt(jnp.mean(center * center, axis=-1, keepdims=True) + 1e-05)
    scaled = center * inverse
    return (scaled * gain + shift, scaled, inverse)


def normalize_back(incoming, scaled, inverse, gain):
    grad_scaled = incoming * gain
    mean_one = jnp.mean(grad_scaled, axis=-1, keepdims=True)
    mean_two = jnp.mean(grad_scaled * scaled, axis=-1, keepdims=True)
    outgoing = inverse * (grad_scaled - mean_one - scaled * mean_two)
    return (outgoing, jnp.sum(incoming * scaled, axis=0), jnp.sum(incoming, axis=0))


def attend(queries, keyvals, seg_query, seg_key):
    factor = queries.shape[-1] ** (-0.5)
    scores = (
        jnp.einsum("bqhd,bkhd->bhqk", queries, keyvals[:, :, 0], preferred_element_type=jnp.float32)
        * factor
    )
    allowed = seg_query[:, None, :, None] == seg_key[:, None, None, :]
    scores = jnp.where(allowed, scores, -1e30)
    top = jnp.max(scores, axis=-1, keepdims=True)
    expo = jnp.exp(scores - top)
    total = jnp.sum(expo, axis=-1, keepdims=True)
    weights = (expo / total).astype(jnp.bfloat16)
    mixed = jnp.einsum(
        "bhqk,bkhd->bqhd", weights, keyvals[:, :, 1], preferred_element_type=jnp.float32
    )
    return (mixed, top, total)


def attend_back(queries, keyvals, seg_query, seg_key, top, total, grad_mixed):
    factor = queries.shape[-1] ** (-0.5)
    keys_part = keyvals[:, :, 0]
    values_part = keyvals[:, :, 1]
    scores = (
        jnp.einsum("bqhd,bkhd->bhqk", queries, keys_part, preferred_element_type=jnp.float32)
        * factor
    )
    allowed = seg_query[:, None, :, None] == seg_key[:, None, None, :]
    scores = jnp.where(allowed, scores, -1e30)
    chances = jnp.exp(scores - top) / total
    weights = chances.astype(jnp.bfloat16)
    grad_weights = jnp.einsum(
        "bqhd,bkhd->bhqk", grad_mixed, values_part, preferred_element_type=jnp.float32
    )
    inner = jnp.sum(chances * grad_weights, axis=-1, keepdims=True)
    grad_scores = (chances * (grad_weights - inner)).astype(jnp.bfloat16)
    grad_queries = (
        jnp.einsum("bhqk,bkhd->bqhd", grad_scores, keys_part, preferred_element_type=jnp.float32)
        * factor
    )
    grad_keys = (
        jnp.einsum("bhqk,bqhd->bkhd", grad_scores, queries, preferred_element_type=jnp.float32)
        * factor
    )
    grad_values = jnp.einsum(
        "bhqk,bqhd->bkhd", weights, grad_mixed, preferred_element_type=jnp.float32
    )
    return (grad_queries, jnp.stack([grad_keys, grad_values], axis=2))


def on_device(
    tokens,
    segment_ids,
    project_weight,
    query_bias,
    value_bias,
    output_weight,
    output_bias,
    first_gain,
    first_shift,
    expand_weight,
    expand_bias,
    reduce_weight,
    reduce_bias,
    second_gain,
    second_shift,
    grad_out,
):
    gathered = (
        lax.all_gather(project_weight, ("seq", "ctx"), axis=0, tiled=True),
        lax.all_gather(query_bias, ("seq", "ctx"), axis=0, tiled=True),
        lax.all_gather(value_bias, ("seq", "ctx"), axis=0, tiled=True),
        lax.all_gather(output_weight, ("seq", "ctx"), axis=0, tiled=True),
        lax.all_gather(output_bias, ("seq", "ctx"), axis=0, tiled=True),
        lax.all_gather(first_gain, ("seq", "ctx"), axis=0, tiled=True),
        lax.all_gather(first_shift, ("seq", "ctx"), axis=0, tiled=True),
        lax.all_gather(expand_weight, ("seq", "ctx"), axis=0, tiled=True),
        lax.all_gather(expand_bias, ("seq", "ctx"), axis=0, tiled=True),
        lax.all_gather(reduce_weight, ("seq", "ctx"), axis=0, tiled=True),
        lax.all_gather(reduce_bias, ("seq", "ctx"), axis=0, tiled=True),
        lax.all_gather(second_gain, ("seq", "ctx"), axis=0, tiled=True),
        lax.all_gather(second_shift, ("seq", "ctx"), axis=0, tiled=True),
    )
    (
        full_project,
        full_query,
        full_value,
        full_output,
        full_outbias,
        full_gain_one,
        full_shift_one,
        full_expand,
        full_expbias,
        full_reduce,
        full_redbias,
        full_gain_two,
        full_shift_two,
    ) = gathered
    position = lax.axis_index("ctx")
    seq_count = tokens.shape[0]
    seg_query = lax.dynamic_slice_in_dim(
        segment_ids, position * tokens.shape[1], tokens.shape[1], 1
    )
    local_len = tokens.shape[1]
    width = tokens.shape[2]
    full_len = segment_ids.shape[1]
    rows_count = seq_count * local_len
    rows = tokens.reshape(rows_count, width)
    bias_all = jnp.concatenate(
        [
            full_query.astype(jnp.float32),
            jnp.zeros((width,), jnp.float32),
            full_value.astype(jnp.float32),
        ]
    )
    project = (jnp.dot(rows, full_project, preferred_element_type=jnp.float32) + bias_all).astype(
        jnp.bfloat16
    )
    queries = project[:, :width].reshape(seq_count, local_len, HEADS, HEAD_DIM)
    keyval_local = project[:, width:].reshape(seq_count, local_len, 2 * width)
    keyval_whole = lax.all_gather(keyval_local, "ctx", axis=1, tiled=True)
    keyvals = keyval_whole.reshape(seq_count, full_len, 2, HEADS, HEAD_DIM)
    per_block = math.gcd(seq_count, max(1, 512 // local_len))
    blocks = seq_count // per_block

    def split_blocks(array):
        return array.reshape((blocks, per_block) + array.shape[1:])

    def join_blocks(array):
        return array.reshape((seq_count,) + array.shape[2:])

    mixed, top, total = lax.map(
        lambda parts: attend(*parts),
        (
            split_blocks(queries),
            split_blocks(keyvals),
            split_blocks(seg_query),
            split_blocks(segment_ids),
        ),
    )
    mixed_low = join_blocks(mixed).reshape(rows_count, width).astype(jnp.bfloat16)
    attended = jnp.dot(
        mixed_low, full_output, preferred_element_type=jnp.float32
    ) + full_outbias.astype(jnp.float32)
    first, first_scaled, first_inverse = normalize(
        rows.astype(jnp.float32) + attended,
        full_gain_one.astype(jnp.float32),
        full_shift_one.astype(jnp.float32),
    )
    first_low = first.astype(jnp.bfloat16)
    expanded = jnp.dot(
        first_low, full_expand, preferred_element_type=jnp.float32
    ) + full_expbias.astype(jnp.float32)
    activated = jax.nn.gelu(expanded, approximate=True).astype(jnp.bfloat16)
    reduced = jnp.dot(
        activated, full_reduce, preferred_element_type=jnp.float32
    ) + full_redbias.astype(jnp.float32)
    second, second_scaled, second_inverse = normalize(
        first + reduced, full_gain_two.astype(jnp.float32), full_shift_two.astype(jnp.float32)
    )
    layer_work = second.astype(jnp.bfloat16).reshape(seq_count, local_len, width)
    back_set = (
        lax.all_gather(project_weight, ("seq", "ctx"), axis=0, tiled=True),
        lax.all_gather(query_bias, ("seq", "ctx"), axis=0, tiled=True),
        lax.all_gather(value_bias, ("seq", "ctx"), axis=0, tiled=True),
        lax.all_gather(output_weight, ("seq", "ctx"), axis=0, tiled=True),
        lax.all_gather(output_bias, ("seq", "ctx"), axis=0, tiled=True),
        lax.all_gather(first_gain, ("seq", "ctx"), axis=0, tiled=True),
        lax.all_gather(first_shift, ("seq", "ctx"), axis=0, tiled=True),
        lax.all_gather(expand_weight, ("seq", "ctx"), axis=0, tiled=True),
        lax.all_gather(expand_bias, ("seq", "ctx"), axis=0, tiled=True),
        lax.all_gather(reduce_weight, ("seq", "ctx"), axis=0, tiled=True),
        lax.all_gather(reduce_bias, ("seq", "ctx"), axis=0, tiled=True),
        lax.all_gather(second_gain, ("seq", "ctx"), axis=0, tiled=True),
        lax.all_gather(second_shift, ("seq", "ctx"), axis=0, tiled=True),
    )
    back_project = back_set[0]
    back_output = back_set[3]
    back_gain_one = back_set[5].astype(jnp.float32)
    back_expand = back_set[7]
    back_reduce = back_set[9]
    back_gain_two = back_set[11].astype(jnp.float32)
    grad_rows = grad_out.reshape(rows_count, width).astype(jnp.float32)
    grad_second, grad_gain_two, grad_shift_two = normalize_back(
        grad_rows, second_scaled, second_inverse, back_gain_two
    )
    grad_reduced = grad_second.astype(jnp.bfloat16)
    reduce_bias_grad = jnp.sum(grad_reduced.astype(jnp.float32), axis=0)
    reduce_grad = times_left(activated, grad_reduced)
    grad_activated = times_right(grad_reduced, back_reduce)
    gelu_pull = jax.vjp(lambda inside: jax.nn.gelu(inside, approximate=True), expanded)[1]
    grad_expanded = gelu_pull(grad_activated)[0].astype(jnp.bfloat16)
    expand_bias_grad = jnp.sum(grad_expanded.astype(jnp.float32), axis=0)
    expand_grad = times_left(first_low, grad_expanded)
    grad_first = grad_second + times_right(grad_expanded, back_expand)
    grad_hidden, grad_gain_one, grad_shift_one = normalize_back(
        grad_first, first_scaled, first_inverse, back_gain_one
    )
    grad_attended = grad_hidden.astype(jnp.bfloat16)
    output_bias_grad = jnp.sum(grad_attended.astype(jnp.float32), axis=0)
    output_grad = times_left(mixed_low, grad_attended)
    grad_mixed = times_right(grad_attended, back_output).astype(jnp.bfloat16)
    grad_mixed = grad_mixed.reshape(seq_count, local_len, HEADS, HEAD_DIM)
    grad_queries, grad_keyvals = lax.map(
        lambda parts: attend_back(*parts),
        (
            split_blocks(queries),
            split_blocks(keyvals),
            split_blocks(seg_query),
            split_blocks(segment_ids),
            top,
            total,
            split_blocks(grad_mixed),
        ),
    )
    grad_keyvals = join_blocks(grad_keyvals).reshape(seq_count, full_len, 2 * width)
    owned_keyvals = lax.psum_scatter(
        grad_keyvals.astype(jnp.bfloat16), "ctx", scatter_dimension=1, tiled=True
    ).astype(jnp.float32)
    grad_project = jnp.concatenate(
        [
            join_blocks(grad_queries).reshape(rows_count, width).astype(jnp.bfloat16),
            owned_keyvals.reshape(rows_count, 2 * width).astype(jnp.bfloat16),
        ],
        axis=1,
    )
    query_bias_grad = jnp.sum(grad_project[:, :width].astype(jnp.float32), axis=0)
    value_bias_grad = jnp.sum(grad_project[:, 2 * width :].astype(jnp.float32), axis=0)
    project_grad = times_left(rows, grad_project)
    grad_work = (grad_hidden + times_right(grad_project, back_project)).reshape(
        seq_count, local_len, width
    )
    owned = (
        lax.psum_scatter(project_grad, ("seq", "ctx"), scatter_dimension=0, tiled=True),
        lax.psum_scatter(query_bias_grad, ("seq", "ctx"), scatter_dimension=0, tiled=True),
        lax.psum_scatter(value_bias_grad, ("seq", "ctx"), scatter_dimension=0, tiled=True),
        lax.psum_scatter(output_grad, ("seq", "ctx"), scatter_dimension=0, tiled=True),
        lax.psum_scatter(output_bias_grad, ("seq", "ctx"), scatter_dimension=0, tiled=True),
        lax.psum_scatter(grad_gain_one, ("seq", "ctx"), scatter_dimension=0, tiled=True),
        lax.psum_scatter(grad_shift_one, ("seq", "ctx"), scatter_dimension=0, tiled=True),
        lax.psum_scatter(expand_grad, ("seq", "ctx"), scatter_dimension=0, tiled=True),
        lax.psum_scatter(expand_bias_grad, ("seq", "ctx"), scatter_dimension=0, tiled=True),
        lax.psum_scatter(reduce_grad, ("seq", "ctx"), scatter_dimension=0, tiled=True),
        lax.psum_scatter(reduce_bias_grad, ("seq", "ctx"), scatter_dimension=0, tiled=True),
        lax.psum_scatter(grad_gain_two, ("seq", "ctx"), scatter_dimension=0, tiled=True),
        lax.psum_scatter(grad_shift_two, ("seq", "ctx"), scatter_dimension=0, tiled=True),
    )
    return (
        layer_work,
        grad_work,
        owned[0],
        owned[1],
        owned[2],
        owned[3],
        owned[4],
        owned[5],
        owned[6],
        owned[7],
        owned[8],
        owned[9],
        owned[10],
        owned[11],
        owned[12],
    )


def solution(mesh):
    placed = (
        P("seq", "ctx", None),
        P("seq", None),
        P(("seq", "ctx"), None),
        P(("seq", "ctx")),
        P(("seq", "ctx")),
        P(("seq", "ctx"), None),
        P(("seq", "ctx")),
        P(("seq", "ctx")),
        P(("seq", "ctx")),
        P(("seq", "ctx"), None),
        P(("seq", "ctx")),
        P(("seq", "ctx"), None),
        P(("seq", "ctx")),
        P(("seq", "ctx")),
        P(("seq", "ctx")),
        P("seq", "ctx", None),
    )
    return jax.shard_map(
        on_device,
        mesh=mesh,
        in_specs=placed,
        out_specs=(
            P("seq", "ctx", None),
            P("seq", "ctx", None),
            P(("seq", "ctx"), None),
            P(("seq", "ctx")),
            P(("seq", "ctx")),
            P(("seq", "ctx"), None),
            P(("seq", "ctx")),
            P(("seq", "ctx")),
            P(("seq", "ctx")),
            P(("seq", "ctx"), None),
            P(("seq", "ctx")),
            P(("seq", "ctx"), None),
            P(("seq", "ctx")),
            P(("seq", "ctx")),
            P(("seq", "ctx")),
        ),
        check_vma=False,
    )
```

profile of v0, /device:TPU:0, one launch (start us, length us, event | category | flops | bytes accessed | tf_op | source)
XLA Modules:
  0.0 1498.3 jit_solution(17959895961105573700)
XLA Ops:
  14.7 42.6 %all-reduce.18 = (bf16[1024]{0:T(1024)(128)(2,1)S(1)}, bf16[1024]{0:T(1024)(128)(2,1)S(1)}, bf16[1024]{0:T(1024)(128)(2,1)S(1)}, bf16[1024]{0:T(1024)(128)(2,1)S...) all-reduce(bf16[1024]{0:T(1024)(128)(2,1)S(1)} %dynamic-update-slic, ...), channel_id=1, replica_groups=mesh['seq'=8,'ctx'=4] {'seq','ctx'}, use_global_device_ids=true, to_apply=%add.2 | all-reduce | flops 8192 | bytes 32768
  57.2 26.0 %all-gather.7.cloned.1.call-done = bf16[1024,3072]{1,0:T(8,128)(2,1)} async-done(((bf16[32,3072]{1,0:T(8,128)(2,1)}), bf16[1024,3072]{1,0:T(8,128)(2,1)}) %all-gather.7.cloned.1.call-update) | async-done | bytes 6291472 | tf_op jit(solution)/shard_map/all_gather | solution.py:107
  108.0 39.4 %all-gather = bf16[32,1,128]{2,1,0:T(2,128)(2,1)S(1)} all-gather(bf16[1,1,128]{2,1,0:T(2,128)(2,1)S(1)} %bitcast.201), channel_id=1, replica_groups=mesh['seq'=8,'ctx'=4] {'seq','ctx'}, dimensions={0}, use_global_device_ids=true | all-gather | bytes 8448 | tf_op jit(solution)/shard_map/all_gather | solution.py:115
  160.8 49.3 %all-gather.9.cloned.1.call-done = bf16[8,512,2048]{1,2,0:T(8,128)(2,1)} async-done(((bf16[8,128,2048]{1,2,0:T(8,128)(2,1)}), bf16[8,512,2048]{1,2,0:T(8,128)(2,1)}) %all-gather.9.cloned.1.call-update) | async-done | bytes 16777232 | tf_op jit(solution)/shard_map/all_gather | solution.py:158
  225.9 54.9 %while.26 = (s32[]{:T(128)}, bf16[2,4,128,16,64]{2,4,3,1,0:T(8,128)(2,1)}, f32[2,4,16,128,1]{3,2,1,4,0:T(8,128)S(1)}, f32[2,4,16,128,1]{3,2,1,4,0:T(8,128)S(1)},...) while((s32[]{:T(128)}, ...), condition=%wide.region_3.4_spmd, body=%wide.region_0.3_spmd.sunk | while | flops 1124319232 | bytes 80017536 | solution.py:169
  295.4 53.0 %all-gather.13.cloned.1.call-done = bf16[1024,4096]{1,0:T(8,128)(2,1)} async-done(((bf16[32,4096]{1,0:T(8,128)(2,1)}), bf16[1024,4096]{1,0:T(8,128)(2,1)}) %all-gather.13.cloned.1.call-update) | async-done | bytes 8388624 | tf_op jit(solution)/shard_map/all_gather | solution.py:114
  348.4 16.6 %fusion.59 = f32[1024,4096]{1,0:T(8,128)} fusion(bf16[1024,4096]{1,0:T(8,128)(2,1)} %all-gather.13.cloned.1.call-done, f32[1024,1024]{1,0:T(8,128)} %copy-done.4, f32[1024]{0:T(1024)S(1)} %copy-done.31, f32[1024]{0:T(1024)S(1)} %copy-done.21, f32[1024]{0:T(1024)S(1)} %add_rsqrt_fusion.1, f32[1024]{0:T(1024)S(1)} %broadcast_multiply_fusion.4), kind=kOutput, calls=%fused_computation.120 | convolution fusion | flops 8595177472 | bytes 29376512 | tf_op jit(solution)/shard_map/dot_general | solution.py:188
  365.0 62.2 %all-gather.15.cloned.1.call-done = bf16[4096,1024]{1,0:T(8,128)(2,1)} async-done(((bf16[128,1024]{1,0:T(8,128)(2,1)}), bf16[4096,1024]{1,0:T(8,128)(2,1)}) %all-gather.15.cloned.1.call-update) | async-done | bytes 8388624 | tf_op jit(solution)/shard_map/all_gather | solution.py:116
  427.2 18.0 %fusion.63 = (f32[1024]{0:T(1024)S(1)}, f32[1024,1024]{1,0:T(8,128)S(1)}) fusion(f32[1024]{0:T(1024)S(1)} %copy-done.33, bf16[4096,1024]{1,0:T(8,128)(2,1)} %all-gather.15.cloned.1.call-done, f32[1024,4096]{1,0:T(8,128)} %fusion.59, f32[4096]{0:T(1024)S(1)} %bitcast.198, f32[1024]{0:T(1024)S(1)} %copy-done.31, f32[1024]{0:T(1024)S(1)} %copy-done.21, ...), kind=kOutput, calls=%fused_computation.122 | convolution fusion | flops 8639216640 | bytes 33595392 | tf_op jit(solution)/shard_map/dot_general | solution.py:192
  453.6 27.0 %convert_reduce_fusion = (f32[4096]{0:T(1024)}, bf16[1024,4096]{1,0:T(8,128)(2,1)}) fusion(f32[1024,4096]{1,0:T(8,128)} %fusion.59, f32[4096]{0:T(1024)S(1)} %bitcast.199, bf16[4096,1024]{1,0:T(8,128)(2,1)} %all-gather.15.cloned.1.call-done, f32[1024,1024]{1,0:T(8,128)} %get-tuple-element.311), kind=kOutput, calls=%fused_computation.63 | convolution fusion | flops 8687448064 | bytes 37781504 | tf_op jit(solution)/shard_map/dot_general | solution.py:13
  480.6 17.9 %multiply_reduce_fusion.1 = (f32[1024]{0:T(1024)}, f32[1024]{0:T(1024)S(1)}, f32[1024]{0:T(1024)S(1)}, f32[1024]{0:T(1024)}, f32[1024,1024]{1,0:T(8,128)S(1)}) fusion(f32[1024,1024]{1,0:T(8,128)} %copy-done.4, f32[1024]{0:T(1024)S(1)} %add_rsqrt_fusion.1, f32[1024]{0:T(1024)S(1)} %broadcast_multiply_fusion.4, f32[1024]{0:T(1024)S(1)} %copy-done.21, ...), kind=kOutput, calls=%fused_computation.80 | convolution fusion | flops 8600416256 | bytes 29388800 | tf_op jit(solution)/shard_map/dot_general | solution.py:13
  515.7 129.4 %while.27 = (s32[]{:T(128)}, bf16[2,4,128,16,64]{2,4,3,1,0:T(8,128)(2,1)}, bf16[2,4,512,2,16,64]{2,5,4,3,1,0:T(8,128)(2,1)}, bf16[2,4,512,2,16,64]{2,5,4,1,3,0:T...) while((s32[]{:T(128)}, ...), condition=%wide.region_14.15_spmd, body=%wide.region_12.14_spmd.sunk | while | flops 2735464448 | bytes 195852464 | solution.py:241
  534.4 15.3 %multiply_reduce_fusion.7 = (f32[4,16,128]{2,1,0:T(8,128)S(1)}, f32[4,16,128,512]{3,2,1,0:T(8,128)}) fusion(f32[4,16,128,512]{3,2,1,0:T(8,128)} %fusion.99, f32[4,16,128]{2,1,0:T(8,128)S(1)} %get-tuple-element.454, f32[4,16,128]{2,1,0:T(8,128)S(1)} %get-tuple-element.455, bf16[4,512,2,16,64]{1,4,3,0,2:T(8,128)(2,1)} %dynamic-slice_bitcast_fusion.16, ...), kind=kOutput, calls=%fused_computation.24.clone.1 | convolution fusion | flops 562028544 | bytes 39157764 | tf_op jit(solution)/shard_map/while/body/eval_jaxpr/bqhd,bkhd->bhqk/dot_general | solution.py:62
  599.0 15.3 %multiply_reduce_fusion.7 = (f32[4,16,128]{2,1,0:T(8,128)S(1)}, f32[4,16,128,512]{3,2,1,0:T(8,128)}) fusion(f32[4,16,128,512]{3,2,1,0:T(8,128)} %fusion.99, f32[4,16,128]{2,1,0:T(8,128)S(1)} %get-tuple-element.454, f32[4,16,128]{2,1,0:T(8,128)S(1)} %get-tuple-element.455, bf16[4,512,2,16,64]{1,4,3,0,2:T(8,128)(2,1)} %dynamic-slice_bitcast_fusion.16, ...), kind=kOutput, calls=%fused_computation.24.clone.1 | convolution fusion | flops 562028544 | bytes 39157764 | tf_op jit(solution)/shard_map/while/body/eval_jaxpr/bqhd,bkhd->bhqk/dot_general | solution.py:62
  645.1 24.6 %copy.79 = bf16[8,512,2048]{2,0,1:T(8,128)(2,1)} copy(bf16[8,512,2048]{1,2,0:T(8,128)(2,1)} %bitcast.188) | data formatting | bytes 33554432
  669.8 18.6 %copy.106 = bf16[64,8,8,2048]{3,1,2,0:T(8,128)(2,1)} copy(bf16[64,8,8,2048]{3,2,1,0:T(8,128)(2,1)} %bitcast.187) | data formatting | bytes 33554432
  697.7 23.7 %fusion.51 = f32[4096,1024]{1,0:T(8,128)} fusion(f32[1024,1024]{1,0:T(8,128)} %get-tuple-element.311, f32[1024,4096]{1,0:T(8,128)} %fusion.59, f32[4096]{0:T(1024)S(1)} %bitcast.200), kind=kOutput, calls=%fused_computation.115 | convolution fusion | flops 8632926208 | bytes 37765120 | tf_op jit(solution)/shard_map/dot_general | solution.py:19
  722.2 16.7 %fusion.57 = f32[1024,4096]{1,0:T(8,128)} fusion(bf16[1024,4096]{1,0:T(8,128)(2,1)} %get-tuple-element.329, f32[1024,1024]{1,0:T(8,128)} %copy-done.4, f32[1024]{0:T(1024)S(1)} %copy-done.32, f32[1024]{0:T(1024)S(1)} %copy-done.22, f32[1024]{0:T(1024)S(1)} %copy-done.24, f32[1024]{0:T(1024)S(1)} %copy-done.14), kind=kOutput, calls=%fused_computation.119 | convolution fusion | flops 8595177472 | bytes 29376512 | tf_op jit(solution)/shard_map/dot_general | solution.py:19
  751.2 62.0 %reduce-scatter.16.cloned.1.call-done = bf16[128,16384]{1,0:T(8,128)(2,1)} async-done(((bf16[512,16384]{1,0:T(8,128)(2,1)}), bf16[128,16384]{1,0:T(8,128)(2,1)}) %reduce-scatter.16.cloned.1.call-update) | async-done | bytes 4194320
  847.5 40.6 %all-reduce.17 = (f32[1024]{0:T(1024)S(1)}, f32[1024]{0:T(1024)S(1)}, f32[1024]{0:T(1024)S(1)}, f32[1024]{0:T(1024)S(1)}, f32[1024]{0:T(1024)S(1)}, /*index=5*/f...) all-reduce(f32[1024]{0:T(1024)S(1)} %reduce_sum.182, ...), channel_id=4, replica_groups=mesh['seq'=8,'ctx'=4] {'seq','ctx'}, use_global_device_ids=true, to_apply=%region_18.19.clone | all-reduce | flops 12288 | bytes 98304
  905.9 51.3 %reduce-scatter.10.cloned.1.call-done = f32[32,1024]{1,0:T(8,128)} async-done(((f32[1024,1024]{1,0:T(8,128)}), f32[32,1024]{1,0:T(8,128)}) %reduce-scatter.10.cloned.1.call-update) | async-done | bytes 131088 | tf_op jit(solution)/shard_map/reduce_scatter | solution.py:274
  957.2 182.4 %reduce-scatter.14.cloned.1.call-done = f32[128,1024]{1,0:T(8,128)} async-done(((f32[4096,1024]{1,0:T(8,128)}), f32[128,1024]{1,0:T(8,128)}) %reduce-scatter.14.cloned.1.call-update) | async-done | bytes 524304 | tf_op jit(solution)/shard_map/reduce_scatter | solution.py:280
  1139.6 186.7 %reduce-scatter.12.cloned.1.call-done = f32[32,4096]{1,0:T(8,128)} async-done(((f32[1024,4096]{1,0:T(8,128)}), f32[32,4096]{1,0:T(8,128)}) %reduce-scatter.12.cloned.1.call-update) | async-done | bytes 524304 | tf_op jit(solution)/shard_map/reduce_scatter | solution.py:278
  1326.3 165.0 %reduce-scatter.18.cloned.1.call-done = f32[32,3072]{1,0:T(8,128)} async-done(((f32[1024,3072]{1,0:T(8,128)}), f32[32,3072]{1,0:T(8,128)}) %reduce-scatter.18.cloned.1.call-update) | async-done | bytes 393232
  (218 shorter events, 329.0 us)
Async XLA Ops:
  7.2 76.1 %all-gather.7.cloned.1.call-start = ((), (), s32[]{:S(2)}) async-start(), calls=%async_computation.5 | async-start | bytes 6488064 | tf_op jit(solution)/shard_map/all_gather | solution.py:107
  7.9 202.1 %all-gather.9.cloned.1.call-start = ((), (), s32[]{:S(2)}) async-start(), calls=%async_computation.6 | async-start | bytes 20971520 | tf_op jit(solution)/shard_map/all_gather | solution.py:158
  103.0 5.0 copy-start.15
  103.0 5.0 copy-start.35
  103.0 45.0 %copy-start.2 = (bf16[8,128,1024]{2,1,0:T(8,128)(2,1)S(1)}, bf16[8,128,1024]{2,1,0:T(8,128)(2,1)}, u32[]{:S(2)}) copy-start(bf16[8,128,1024]{2,1,0:T(8,128)(2,1)} %param.35) | copy-start | bytes 6291460
  103.1 183.9 %all-gather.11.cloned.1.call-start = ((), (), s32[]{:S(2)}) async-start(), calls=%async_computation.7 | async-start | bytes 2162688 | tf_op jit(solution)/shard_map/all_gather | solution.py:110
  103.8 244.6 %all-gather.13.cloned.1.call-start = ((), (), s32[]{:S(2)}) async-start(), calls=%async_computation.8 | async-start | bytes 8650752 | tf_op jit(solution)/shard_map/all_gather | solution.py:114
  104.4 322.8 %all-gather.15.cloned.1.call-start = ((), (), s32[]{:S(2)}) async-start(), calls=%async_computation.9 | async-start | bytes 8650752 | tf_op jit(solution)/shard_map/all_gather | solution.py:116
  105.0 708.3 %reduce-scatter.16.cloned.1.call-start = ((), (), s32[]{:S(2)}) async-start(), calls=%async_computation.13 | async-start | bytes 20971520
  106.8 48.1 %copy-start.11 = (f32[1024]{0:T(1024)}, f32[1024]{0:T(1024)S(1)}, u32[]{:S(2)}) copy-start(f32[1024]{0:T(1024)S(1)} %convert_element_type.128) | copy-start | bytes 12292
  280.8 6.3 copy-start.34
  292.8 55.6 %copy-start.21 = (f32[1024]{0:T(1024)S(1)}, f32[1024]{0:T(1024)}, u32[]{:S(2)}) copy-start(f32[1024]{0:T(1024)} %convert_element_type.122) | copy-start | bytes 12292
  292.8 55.6 %copy-start.31 = (f32[1024]{0:T(1024)S(1)}, f32[1024]{0:T(1024)}, u32[]{:S(2)}) copy-start(f32[1024]{0:T(1024)} %convert_element_type.123) | copy-start | bytes 12292
  292.8 205.7 %copy-start.13 = (f32[1024]{0:T(1024)}, f32[1024]{0:T(1024)S(1)}, u32[]{:S(2)}) copy-start(f32[1024]{0:T(1024)S(1)} %broadcast_multiply_fusion.4) | copy-start | bytes 12292
  295.3 203.1 %copy-start.23 = (f32[1024]{0:T(1024)}, f32[1024]{0:T(1024)S(1)}, u32[]{:S(2)}) copy-start(f32[1024]{0:T(1024)S(1)} %add_rsqrt_fusion.1) | copy-start | bytes 12292
  295.4 131.8 %copy-start.26 = (f32[32,1,128]{2,1,0:T(1,128)S(1)}, f32[32,1,128]{2,1,0:T(1,128)}, u32[]{:S(2)}) copy-start(f32[32,1,128]{2,1,0:T(1,128)} %convert_element_type.149) | copy-start | bytes 49156
  295.4 131.8 %copy-start.33 = (f32[1024]{0:T(1024)S(1)}, f32[1024]{0:T(1024)}, u32[]{:S(2)}) copy-start(f32[1024]{0:T(1024)} %convert_element_type.127) | copy-start | bytes 12292
  480.6 17.9 %copy-start.5 = (f32[1024,1024]{1,0:T(8,128)S(1)}, f32[1024,1024]{1,0:T(8,128)}, u32[]{:S(2)}) copy-start(f32[1024,1024]{1,0:T(8,128)} %copy-done.4) | copy-start | bytes 12582916
  523.9 10.4 copy-start
  588.6 10.4 copy-start
  688.4 268.8 %reduce-scatter.10.cloned.1.call-start = ((), (), s32[]{:S(2)}) async-start(), calls=%async_computation.10 | async-start | bytes 4325376 | tf_op jit(solution)/shard_map/reduce_scatter | solution.py:274
  697.0 442.6 %reduce-scatter.14.cloned.1.call-start = ((), (), s32[]{:S(2)}) async-start(), calls=%async_computation.12 | async-start | bytes 17301504 | tf_op jit(solution)/shard_map/reduce_scatter | solution.py:280
  721.5 604.8 %reduce-scatter.12.cloned.1.call-start = ((), (), s32[]{:S(2)}) async-start(), calls=%async_computation.11 | async-start | bytes 17301504 | tf_op jit(solution)/shard_map/reduce_scatter | solution.py:278
  738.9 752.3 %reduce-scatter.18.cloned.1.call-start = ((), (), s32[]{:S(2)}) async-start(), calls=%async_computation.14 | async-start | bytes 12976128
  (26 other events, 58.3 us)
Sparse Core Ops, SparseCore 0:
  10.9 72.3 all-gather.6
  103.2 106.7 all-gather.8
  212.9 56.3 all-gather.10
  272.0 76.2 all-gather.12
  351.1 76.0 all-gather.14
  688.5 124.6 reduce-scatter.15
  816.2 140.9 reduce-scatter.9
  960.2 179.3 reduce-scatter.13
  1142.6 183.6 reduce-scatter.11
  1333.8 157.4 reduce-scatter.17
where the time goes:
time: 1510 us; the launch traced here: 1500 us
  waiting for transfers between devices  840 us (56%)
  matrix products  280 us (19%)
  local copies, waits for them, and re-layouts  182 us (12%)
  blocking collectives  123 us (8%)
  other arithmetic  57.4 us (4%)
    unnamed x12, waiting for transfers between devices  229 us
    reduce_scatter x1, waiting for transfers between devices, on_device(): lax.psum_scatter(expand_grad, ('seq', 'ctx'), scatter_dimension=0, tiled=...  187 us
    reduce_scatter x1, waiting for transfers between devices, on_device(): lax.psum_scatter(reduce_grad, ('seq', 'ctx'), scatter_dimension=0, tiled=...  182 us
    unnamed x103, local copies, waits for them, and re-layouts  84.9 us
    unnamed x2, blocking collectives  83.2 us
    all_gather x1, waiting for transfers between devices, on_device(): lax.all_gather(reduce_weight, ('seq', 'ctx'), axis=0, tiled=True)  62.2 us
    dot_general x4, matrix products, times_right(): lax.dot_general(left, right, (((1,), (1,)), ((), ())), preferred_element_...  59.9 us
    dot_general x4, matrix products, times_left(): lax.dot_general(left, right, (((0,), (0,)), ((), ())), preferred_element_...  57.3 us
  transfers between devices with their start and end apart: 10, of which 9 were waited for; matrix products, arithmetic and copies ran while one was open for 15% of the time, Pallas kernels for 0%

commit v1 on v0

v1 whole, which is shorter than its diff:
```python
import functools

import jax
import jax.numpy as jnp
from jax import lax
from jax.experimental import pallas as pl
from jax.experimental.pallas import tpu as pltpu
from jax.sharding import Mesh
from jax.sharding import PartitionSpec as P

HEADS = 16
HEAD_DIM = 64
CHUNKS = 4
MIB = 1 << 20
CHIPS = ("z", "y", "x")
SEQ = ("z", "y")
CTX = ("x", "c")
ALL = ("z", "y", "x", "c")
F32 = jnp.float32
BF16 = jnp.bfloat16


def dot(left, right, contract=(1, 0)):
    return lax.dot_general(
        left, right, (((contract[0],), (contract[1],)), ((), ())), preferred_element_type=F32
    )


def resident(shape):
    return pl.BlockSpec(shape, lambda i: (0,) * len(shape), pipeline_mode=pl.Buffered(1))


def by_row(shape):
    return pl.BlockSpec(shape, lambda i: (i,) + (0,) * (len(shape) - 1))


def softmax_down(scores, allowed):
    scores = jnp.where(allowed, scores, -1e30)
    top = jnp.max(scores, axis=0, keepdims=True)
    expo = jnp.exp(scores - top)
    total = jnp.sum(expo, axis=0, keepdims=True)
    return expo * (1.0 / total)


def head_lanes(width, head):
    lane = lax.broadcasted_iota(jnp.int32, (1, width), 1)
    return (lane // HEAD_DIM == head).astype(F32)


def attend_kernel(t0, t1, t2, t3, weight, bias, seg_key, seg_query, m0, m1, m2, m3, kept, saved):
    part = t0.shape[1]
    rows = jnp.concatenate([t[0] for t in (t0, t1, t2, t3)], axis=0)
    kept[0] = rows
    project = dot(rows, weight[...]) + bias[...]
    saved[0] = project.astype(BF16)
    width = project.shape[1] // 3
    queries = (project[:, :width].astype(BF16).astype(F32) * HEAD_DIM**-0.5).astype(BF16)
    keys = project[:, width : 2 * width].astype(BF16).astype(F32)
    values_t = jnp.transpose(project[:, 2 * width :]).astype(BF16)
    allowed = seg_key[0] == seg_query[0]
    mixed = []
    for head in range(width // HEAD_DIM):
        own_keys = (keys * head_lanes(width, head)).astype(BF16)
        chances = softmax_down(dot(own_keys, queries, (1, 1)), allowed)
        own_values = values_t[head * HEAD_DIM : (head + 1) * HEAD_DIM]
        mixed.append(dot(own_values, chances.astype(BF16)))
    mixed = jnp.transpose(jnp.concatenate(mixed, axis=0)).astype(BF16)
    for index, out in enumerate((m0, m1, m2, m3)):
        out[0] = mixed[index * part : (index + 1) * part]


def attend(tokens, weight, bias, seg_key, seg_query):
    count, part, depth = tokens[0].shape
    wide = weight.shape[1]
    length = 4 * part
    return pl.pallas_call(
        attend_kernel,
        grid=(count,),
        in_specs=[by_row((1, part, depth))] * 4
        + [
            resident((depth, wide)),
            resident((1, wide)),
            by_row((1, length, 1)),
            by_row((1, 1, length)),
        ],
        out_specs=[by_row((1, part, wide // 3))] * 4
        + [by_row((1, length, depth)), by_row((1, length, wide))],
        out_shape=[jax.ShapeDtypeStruct((count, part, wide // 3), BF16)] * 4
        + [
            jax.ShapeDtypeStruct((count, length, depth), BF16),
            jax.ShapeDtypeStruct((count, length, wide), BF16),
        ],
        compiler_params=pltpu.CompilerParams(vmem_limit_bytes=40 * MIB),
        cost_estimate=pl.CostEstimate(
            flops=count * length * wide * (2 * depth + 16 * length // 3),
            bytes_accessed=count * length * (depth + 2 * wide) * 2,
            transcendentals=count * length * length * wide // (3 * HEAD_DIM),
        ),
        name="attend_forward",
    )(*tokens, weight, bias, seg_key, seg_query)


def attend_back_kernel(
    saved, g0, g1, g2, g3, weight, seg_key, seg_query, grad_project, r0, r1, r2, r3, sums
):
    part = g0.shape[1]
    width = saved.shape[2] // 3
    factor = HEAD_DIM**-0.5
    queries = (saved[0, :, :width].astype(F32) * factor).astype(BF16)
    keys = saved[0, :, width : 2 * width].astype(F32)
    values = saved[0, :, 2 * width :].astype(F32)
    keys_t = jnp.transpose(keys * factor).astype(BF16)
    grad_mixed = jnp.concatenate([g[0] for g in (g0, g1, g2, g3)], axis=0)
    allowed = seg_key[0] == seg_query[0]
    grad_queries = []
    grad_keys = None
    grad_values = None
    for head in range(width // HEAD_DIM):
        lanes = head_lanes(width, head)
        chances = softmax_down(
            dot((keys * lanes).astype(BF16), queries, (1, 1)), allowed
        )
        grad_weights = dot((values * lanes).astype(BF16), grad_mixed, (1, 1))
        inner = jnp.sum(chances * grad_weights, axis=0, keepdims=True)
        grad_scores = (chances * (grad_weights - inner)).astype(BF16)
        grad_queries.append(dot(keys_t[head * HEAD_DIM : (head + 1) * HEAD_DIM], grad_scores))
        keys_term = dot(grad_scores, queries)
        values_term = dot(chances.astype(BF16), grad_mixed)
        if head == 0:
            grad_keys, grad_values = keys_term, values_term
        else:
            here = lanes > 0.5
            grad_keys = jnp.where(here, keys_term, grad_keys)
            grad_values = jnp.where(here, values_term, grad_values)
    grad_queries = jnp.transpose(jnp.concatenate(grad_queries, axis=0))
    whole = jnp.concatenate(
        [grad_queries.astype(BF16), grad_keys.astype(BF16), grad_values.astype(BF16)], axis=1
    )
    grad_project[0] = whole
    sums[0] = jnp.sum(whole.astype(F32), axis=0, keepdims=True)
    for index, out in enumerate((r0, r1, r2, r3)):
        out[0] = dot(whole[index * part : (index + 1) * part], weight[...], (1, 1)).astype(
            out.dtype
        )


def attend_back(saved, grads, weight, seg_key, seg_query):
    count, part, width = grads[0].shape
    depth, wide = weight.shape
    length = 4 * part
    return pl.pallas_call(
        attend_back_kernel,
        grid=(count,),
        in_specs=[by_row((1, length, wide))]
        + [by_row((1, part, width))] * 4
        + [
            resident((depth, wide)),
            by_row((1, length, 1)),
            by_row((1, 1, length)),
        ],
        out_specs=[by_row((1, length, wide))]
        + [by_row((1, part, depth))] * 4
        + [by_row((1, 1, wide))],
        out_shape=[jax.ShapeDtypeStruct((count, length, wide), BF16)]
        + [jax.ShapeDtypeStruct((count, part, depth), t) for t in (F32, BF16, F32, BF16)]
        + [jax.ShapeDtypeStruct((count, 1, wide), F32)],
        compiler_params=pltpu.CompilerParams(vmem_limit_bytes=48 * MIB),
        cost_estimate=pl.CostEstimate(
            flops=count * length * wide * (2 * depth + 40 * length // 3),
            bytes_accessed=count * length * (3 * depth + 3 * wide) * 2,
            transcendentals=count * length * length * wide // (3 * HEAD_DIM),
        ),
        name="attend_backward",
    )(saved, *grads, weight, seg_key, seg_query)


def pick(first_half, own, other):
    return jnp.where(first_half, own, other)


def feed_kernel(steps, own, other, expand, bias, reduce, act, slope, own_out, other_out):
    step = pl.program_id(0)
    rows = pick(step < steps, own[...], other[...])
    hidden = expand.shape[1]
    piece = hidden // 4
    for index in range(4):
        at = slice(index * piece, (index + 1) * piece)
        inside = dot(rows, expand[:, at]) + bias[:, at]
        square = inside * inside
        curve = jnp.tanh(0.7978845608028654 * inside * (1.0 + 0.044715 * square))
        half = 0.5 * (1.0 + curve)
        act[:, at] = (inside * half).astype(BF16)
        slope[:, at] = (
            half
            + 0.5
            * inside
            * (1.0 - curve * curve)
            * (0.7978845608028654 * (1.0 + 3 * 0.044715 * square))
        ).astype(BF16)
    total = dot(act[...], reduce[...])

    @pl.when(step < steps)
    def _():
        own_out[...] = total

    @pl.when(step >= steps)
    def _():
        other_out[...] = total.astype(BF16)


def halves(steps, shape):
    return [
        pl.BlockSpec(shape, lambda i: (jnp.minimum(i, steps - 1), 0)),
        pl.BlockSpec(shape, lambda i: (jnp.maximum(i - steps, 0), 0)),
    ]


def feed(own, other, expand, bias, reduce):
    rows, depth = own.shape
    hidden = expand.shape[1]
    block = 256
    steps = rows // block
    return pl.pallas_call(
        functools.partial(feed_kernel, steps),
        grid=(2 * steps,),
        in_specs=halves(steps, (block, depth))
        + [resident((depth, hidden)), resident((1, hidden)), resident((hidden, depth))],
        out_specs=[by_row((block, hidden))] * 2 + halves(steps, (block, depth)),
        out_shape=[jax.ShapeDtypeStruct((2 * rows, hidden), BF16)] * 2
        + [
            jax.ShapeDtypeStruct((rows, depth), F32),
            jax.ShapeDtypeStruct((rows, depth), BF16),
        ],
        compiler_params=pltpu.CompilerParams(vmem_limit_bytes=48 * MIB),
        cost_estimate=pl.CostEstimate(
            flops=8 * rows * depth * hidden,
            bytes_accessed=4 * rows * (2 * hidden + 3 * depth),
            transcendentals=2 * rows * hidden,
        ),
        name="feed_forward",
    )(own, other, expand, bias, reduce)


def feed_back_kernel(
    steps,
    own_grad,
    other_grad,
    own_rows,
    other_rows,
    act,
    slope,
    expand,
    reduce,
    expand_grad,
    reduce_grad,
    bias_grad,
    own_out,
    other_out,
    expand_sum,
    reduce_sum,
):
    step = pl.program_id(0)
    grad = pick(step < steps, own_grad[...], other_grad[...])
    rows = pick(step < steps, own_rows[...], other_rows[...])
    grad_act = dot(grad, reduce[...], (1, 1))
    grad_inside = (grad_act * slope[...].astype(F32)).astype(BF16)
    bias_part = jnp.sum(grad_inside.astype(F32), axis=0, keepdims=True)
    expand_part = dot(rows, grad_inside, (0, 0))
    reduce_part = dot(act[...], grad, (0, 0))

    @pl.when(step == 0)
    def _():
        bias_grad[...] = bias_part
        expand_sum[...] = expand_part
        reduce_sum[...] = reduce_part

    @pl.when(step > 0)
    def _():
        bias_grad[...] += bias_part
        expand_sum[...] += expand_part
        reduce_sum[...] += reduce_part

    total = dot(grad_inside, expand[...], (1, 1))

    @pl.when(step < steps)
    def _():
        own_out[...] = total

    @pl.when(step >= steps)
    def _():
        other_out[...] = total.astype(BF16)

    @pl.when(step == 2 * steps - 1)
    def _():
        expand_grad[...] = expand_sum[...].astype(BF16)
        reduce_grad[...] = reduce_sum[...].astype(BF16)


def feed_back(own_grad, other_grad, own_rows, other_rows, act, slope, expand, reduce):
    rows, depth = own_grad.shape
    hidden = expand.shape[1]
    block = 256
    steps = rows // block
    return pl.pallas_call(
        functools.partial(feed_back_kernel, steps),
        grid=(2 * steps,),
        in_specs=halves(steps, (block, depth))
        + halves(steps, (block, depth))
        + [by_row((block, hidden))] * 2
        + [resident((depth, hidden)), resident((hidden, depth))],
        out_specs=[
            resident((depth, hidden)),
            resident((hidden, depth)),
            resident((1, hidden)),
        ]
        + halves(steps, (block, depth)),
        out_shape=[
            jax.ShapeDtypeStruct((depth, hidden), BF16),
            jax.ShapeDtypeStruct((hidden, depth), BF16),
            jax.ShapeDtypeStruct((1, hidden), F32),
            jax.ShapeDtypeStruct((rows, depth), F32),
            jax.ShapeDtypeStruct((rows, depth), BF16),
        ],
        scratch_shapes=[
            pltpu.VMEM((depth, hidden), F32),
            pltpu.VMEM((hidden, depth), F32),
        ],
        compiler_params=pltpu.CompilerParams(vmem_limit_bytes=60 * MIB),
        cost_estimate=pl.CostEstimate(
            flops=16 * rows * depth * hidden,
            bytes_accessed=4 * rows * (2 * hidden + 5 * depth) + 8 * depth * hidden,
            transcendentals=0,
        ),
        name="feed_backward",
    )(own_grad, other_grad, own_rows, other_rows, act, slope, expand, reduce)


def normalize(values):
    center = values - jnp.mean(values, axis=-1, keepdims=True)
    inverse = lax.rsqrt(jnp.mean(center * center, axis=-1, keepdims=True) + 1e-05)
    return (center * inverse, inverse)


def normalize_back(incoming, scaled, inverse, gain):
    grad_scaled = incoming * gain
    mean_one = jnp.mean(grad_scaled, axis=-1, keepdims=True)
    mean_two = jnp.mean(grad_scaled * scaled, axis=-1, keepdims=True)
    outgoing = inverse * (grad_scaled - mean_one - scaled * mean_two)
    return (outgoing, jnp.sum(incoming * scaled, axis=0), jnp.sum(incoming, axis=0))


def on_device(
    sizes,
    tokens,
    segment_ids,
    project_weight,
    query_bias,
    value_bias,
    output_weight,
    output_bias,
    first_gain,
    first_shift,
    expand_weight,
    expand_bias,
    reduce_weight,
    reduce_bias,
    second_gain,
    second_shift,
    grad_out,
):
    chips = sizes["z"] * sizes["y"] * sizes["x"]
    ctx_size = sizes["x"] * sizes["c"]
    everyone = chips * sizes["c"]
    seq_count, part, width = tokens.shape
    rows_count = seq_count * part
    hidden = expand_weight.shape[1]
    share = width // everyone
    own_hidden = hidden // 2
    lanes = width // ctx_size
    place = lax.axis_index(CTX)
    core = lax.axis_index("c")
    low_core = core == 0

    def hop(array, step):
        return lax.ppermute(array, CTX, [(i, i ^ step) for i in range(ctx_size)])

    def swap(array):
        return lax.ppermute(array, "c", [(0, 1), (1, 0)])

    def chosen(array, index, axis):
        return lax.dynamic_index_in_dim(array, index, axis, keepdims=False)

    def by_core(own, other, axis):
        return jnp.where(
            low_core, jnp.stack([own, other], axis=axis), jnp.stack([other, own], axis=axis)
        )

    pieces = [tokens[i * seq_count // CHUNKS : (i + 1) * seq_count // CHUNKS] for i in range(CHUNKS)]
    gathered = []
    for piece in pieces:
        across = hop(piece, 2)
        gathered.append((piece, swap(piece), across, swap(across)))
    seg_parts = segment_ids.reshape(seq_count, ctx_size, part)
    seg = jnp.concatenate([chosen(seg_parts, place ^ r, 1) for r in range(ctx_size)], axis=1)
    seg_key = seg[:, :, None]
    seg_query = seg[:, None, :]

    mine = lax.all_to_all(
        project_weight.reshape(share, 3, ctx_size, lanes), CTX, 2, 0, tiled=False
    ).reshape(ctx_size * share, 3 * lanes)
    full_project = lax.all_gather(mine, SEQ, axis=0, tiled=True)

    vectors = (
        query_bias,
        value_bias,
        output_bias,
        first_gain,
        first_shift,
        reduce_bias,
        second_gain,
        second_shift,
    )
    packed = lax.all_gather(
        jnp.concatenate(vectors + (expand_bias,))[None], ALL, axis=0, tiled=True
    ).astype(F32)
    full_query, full_value, out_bias, gain_one, shift_one, red_bias, gain_two, shift_two = [
        packed[:, i * share : (i + 1) * share].reshape(width) for i in range(8)
    ]
    exp_bias = chosen(packed[:, 8 * share :].reshape(chips, 2, -1), core, 1).reshape(1, own_hidden)
    bias_all = jnp.concatenate(
        [
            lax.dynamic_slice_in_dim(full_query, place * lanes, lanes),
            jnp.zeros((lanes,), F32),
            lax.dynamic_slice_in_dim(full_value, place * lanes, lanes),
        ]
    )[None]

    out_half = lax.all_gather(output_weight, CHIPS, axis=0, tiled=True).reshape(
        chips, share, width
    )
    full_output = by_core(out_half, swap(out_half), 1).reshape(ctx_size, lanes, width)
    full_output = jnp.concatenate(
        [chosen(full_output, place ^ r, 0) for r in range(ctx_size)], axis=0
    )

    columns = expand_weight.reshape(share, chips, 2, own_hidden // chips)
    own_columns = chosen(columns, core, 2).reshape(share, own_hidden)
    far_columns = chosen(columns, 1 - core, 2).reshape(share, own_hidden)
    both = by_core(own_columns, swap(far_columns), 0).reshape(2 * share, own_hidden)
    full_expand = lax.all_gather(both, CHIPS, axis=0, tiled=True)
    full_reduce = lax.all_gather(reduce_weight, CHIPS, axis=0, tiled=True)

    saved = []
    kept_rows = []
    mixed_parts = []
    for index in range(CHUNKS):
        at = slice(index * seq_count // CHUNKS, (index + 1) * seq_count // CHUNKS)
        *mixed, all_rows, kept = attend(
            gathered[index], full_project, bias_all, seg_key[at], seg_query[at]
        )
        kept_rows.append(all_rows.reshape(-1, width))
        saved.append(kept)
        mixed_parts.append(
            jnp.concatenate([mixed[0]] + [hop(mixed[r], r) for r in (1, 2, 3)], axis=2)
        )
    mixed_low = jnp.concatenate(mixed_parts, axis=0).reshape(rows_count, width)

    rows = tokens.reshape(rows_count, width)
    attended = dot(mixed_low, full_output) + out_bias
    scaled_one, inverse_one = normalize(rows.astype(F32) + attended)
    first = scaled_one * gain_one + shift_one
    first_low = first.astype(BF16)
    first_far = swap(first_low)
    act, slope, own_sum, far_sum = feed(first_low, first_far, full_expand, exp_bias, full_reduce)
    reduced = own_sum + swap(far_sum).astype(F32) + red_bias
    scaled_two, inverse_two = normalize(first + reduced)
    layer_work = (scaled_two * gain_two + shift_two).astype(BF16).reshape(tokens.shape)

    grad_rows = grad_out.reshape(rows_count, width).astype(F32)
    grad_second, grad_gain_two, grad_shift_two = normalize_back(
        grad_rows, scaled_two, inverse_two, gain_two
    )
    grad_reduced = grad_second.astype(BF16)
    reduce_bias_grad = jnp.sum(grad_reduced.astype(F32), axis=0)
    expand_grad, reduce_grad, expand_bias_grad, own_back, far_back = feed_back(
        grad_reduced,
        swap(grad_reduced),
        first_low,
        first_far,
        act,
        slope,
        full_expand,
        full_reduce,
    )
    reduce_owned = lax.psum_scatter(reduce_grad, CHIPS, scatter_dimension=0, tiled=True)
    expand_owned = lax.psum_scatter(expand_grad, CHIPS, scatter_dimension=0, tiled=True)
    grad_first = grad_second + own_back + swap(far_back).astype(F32)
    grad_hidden, grad_gain_one, grad_shift_one = normalize_back(
        grad_first, scaled_one, inverse_one, gain_one
    )
    grad_attended = grad_hidden.astype(BF16)
    output_bias_grad = jnp.sum(grad_attended.astype(F32), axis=0)
    grad_mixed = dot(grad_attended, full_output, (1, 1)).astype(BF16)
    grad_mixed = grad_mixed.reshape(seq_count, part, ctx_size, lanes)

    output_grad = dot(mixed_low, grad_attended, (0, 0)).astype(BF16)
    output_grad = output_grad.reshape(ctx_size, lanes, width)
    output_grad = jnp.concatenate(
        [chosen(output_grad, place ^ r, 0) for r in range(ctx_size)], axis=0
    ).reshape(chips, 2, share, width)
    output_grad = chosen(output_grad, core, 1).astype(F32) + swap(
        chosen(output_grad, 1 - core, 1)
    ).astype(F32)
    output_owned = lax.psum_scatter(
        output_grad.astype(BF16).reshape(chips * share, width),
        CHIPS,
        scatter_dimension=0,
        tiled=True,
    )

    project_parts = []
    work_parts = []
    sum_parts = []
    for index in range(CHUNKS):
        at = slice(index * seq_count // CHUNKS, (index + 1) * seq_count // CHUNKS)
        grads = [grad_mixed[at, :, 0]] + [hop(grad_mixed[at, :, r], r) for r in (1, 2, 3)]
        grad_part, r0, r1, r2, r3, sums = attend_back(
            saved[index], grads, full_project, seg_key[at], seg_query[at]
        )
        across = r2 + swap(r3).astype(F32)
        work_parts.append(r0 + swap(r1).astype(F32) + hop(across.astype(BF16), 2).astype(F32))
        project_parts.append(grad_part)
        sum_parts.append(sums)
    project_grad = sum(
        dot(all_rows, grad_part.reshape(-1, 3 * lanes), (0, 0))
        for all_rows, grad_part in zip(kept_rows, project_parts)
    )
    grad_work = grad_hidden.reshape(tokens.shape) + jnp.concatenate(work_parts, axis=0)
    project_owned = lax.psum_scatter(
        project_grad.astype(BF16), SEQ, scatter_dimension=0, tiled=True
    )
    project_owned = lax.all_to_all(
        project_owned.reshape(ctx_size, share, 3, lanes), CTX, 0, 2, tiled=False
    ).reshape(share, 3 * width)

    far_rows = expand_owned.reshape(2, share, own_hidden)
    expand_owned = by_core(
        chosen(far_rows, core, 0).reshape(share, chips, -1),
        swap(chosen(far_rows, 1 - core, 0)).reshape(share, chips, -1),
        2,
    ).reshape(share, hidden)

    column_sums = jnp.sum(jnp.concatenate(sum_parts, axis=0), axis=(0, 1))
    zeros = jnp.zeros((width,), F32)
    grad_vectors = (
        lax.dynamic_update_slice_in_dim(zeros, column_sums[:lanes], place * lanes, 0),
        lax.dynamic_update_slice_in_dim(zeros, column_sums[2 * lanes :], place * lanes, 0),
        output_bias_grad,
        grad_gain_one,
        grad_shift_one,
        reduce_bias_grad,
        grad_gain_two,
        grad_shift_two,
    )
    hidden_sums = expand_bias_grad.reshape(chips, 1, own_hidden // chips)
    hidden_sums = jnp.where(
        low_core,
        jnp.concatenate([hidden_sums, jnp.zeros_like(hidden_sums)], axis=1),
        jnp.concatenate([jnp.zeros_like(hidden_sums), hidden_sums], axis=1),
    )
    packed_grads = jnp.concatenate(
        [vector.reshape(everyone, share) for vector in grad_vectors]
        + [hidden_sums.reshape(everyone, -1)],
        axis=1,
    )
    owned = lax.psum_scatter(packed_grads, ALL, scatter_dimension=0, tiled=True)[0]
    small = [owned[i * share : (i + 1) * share] for i in range(8)]
    return (
        layer_work,
        grad_work,
        project_owned.astype(F32),
        small[0],
        small[1],
        output_owned.astype(F32),
        small[2],
        small[3],
        small[4],
        expand_owned.astype(F32),
        owned[8 * share :],
        reduce_owned.astype(F32),
        small[5],
        small[6],
        small[7],
    )


def solution(mesh):
    seq_size, ctx_size = mesh.shape["seq"], mesh.shape["ctx"]
    sizes = {"z": seq_size // 2, "y": 2, "x": ctx_size // 2, "c": 2}
    fine = Mesh(mesh.devices.reshape(tuple(sizes.values())), tuple(sizes))
    rows = P(SEQ, CTX, None)
    matrix = P(ALL, None)
    vector = P(ALL)
    return jax.shard_map(
        functools.partial(on_device, sizes),
        mesh=fine,
        in_specs=(
            rows,
            P(SEQ, None),
            matrix,
            vector,
            vector,
            matrix,
            vector,
            vector,
            vector,
            matrix,
            vector,
            matrix,
            vector,
            vector,
            vector,
            rows,
        ),
        out_specs=(
            rows,
            rows,
            matrix,
            vector,
            vector,
            matrix,
            vector,
            vector,
            vector,
            matrix,
            vector,
            matrix,
            vector,
            vector,
            vector,
        ),
        check_vma=False,
    )
```

time: 1510 us -> 869 us (0.58)
  waiting for transfers between devices: 840 us -> 388 us
  matrix products: 280 us -> 26.4 us
  Pallas kernels: 0 us -> 189 us
  local copies, waits for them, and re-layouts: 182 us -> 50.8 us
  starting transfers between devices: 1.02 us -> 32.6 us
    dot_general x26 -> x7, matrix products: 280 us -> 26.4 us  [dot(): lax.dot_general(left, right, (((contract[0],), (contract[1],)), ((), ()))...]
    unnamed x12 -> x8, waiting for transfers between devices: 229 us -> 2.82 us
    reduce_scatter x3 -> x4, waiting for transfers between devices: 420 us -> 194 us  [the longest x1 94.7 us: on_device(): lax.psum_scatter(reduce_grad, CHIPS, scatter_dimension=0, tiled=True)]
    pallas_call x0 -> x10, Pallas kernels: none -> 189 us  [the longest x1 61.4 us: feed_back(): pl.pallas_call(functools.partial(feed_back_kernel, steps), grid=(2 * step...]
    ppermute x0 -> x56, waiting for transfers between devices: none -> 88.5 us  [the longest x32 70.6 us: hop(): return lax.ppermute(array, CTX, [(i, i ^ step) for i in range(ctx_size)])]
    all_gather x5 -> x4, waiting for transfers between devices: 190 us -> 103 us  [the longest x1 77.9 us: on_device(): full_expand = lax.all_gather(both, CHIPS, axis=0, tiled=True)]
    unnamed x103 -> x174, local copies, waits for them, and re-layouts: 84.9 us -> 28.1 us
    unnamed x2 -> x1, blocking collectives: 83.2 us -> 39.9 us
  transfers between devices with their start and end apart: 10 -> 65, of which waited for: 9 -> 23; matrix products, arithmetic and copies ran while one was open for 15% -> 7% of each run, Pallas kernels for 0% -> 9%
where the time goes in v1:
time: 869 us; the launch traced here: 865 us
  waiting for transfers between devices  388 us (45%)
  Pallas kernels  189 us (22%)
  blocking collectives  116 us (13%)
  local copies, waits for them, and re-layouts  50.8 us (6%)
  other arithmetic  46 us (5%)
  starting transfers between devices  32.6 us (4%)
  matrix products  26.4 us (3%)
  between operations  15.8 us (2%)
    reduce_scatter x1, waiting for transfers between devices, on_device(): lax.psum_scatter(reduce_grad, CHIPS, scatter_dimension=0, tiled=True)  94.7 us
    reduce_scatter x1, waiting for transfers between devices, on_device(): lax.psum_scatter(expand_grad, CHIPS, scatter_dimension=0, tiled=True)  93.6 us
    all_gather x1, waiting for transfers between devices, on_device(): full_expand = lax.all_gather(both, CHIPS, axis=0, tiled=True)  77.9 us
    ppermute x32, waiting for transfers between devices, hop(): return lax.ppermute(array, CTX, [(i, i ^ step) for i in range(ctx_size)])  70.6 us
    all_gather x1, blocking collectives, on_device(): lax.all_gather(jnp.concatenate(vectors + (expand_bias,))[None], ALL, axis...  66.7 us
    pallas_call x1, Pallas kernels, feed_back(): pl.pallas_call(functools.partial(feed_back_kernel, steps), grid=(2 * step...  61.4 us
    pallas_call x4, Pallas kernels, attend_back(): pl.pallas_call(attend_back_kernel, grid=(count,), in_specs=[by_row((1, le...  60.4 us
    unnamed x1, blocking collectives  39.9 us
  transfers between devices with their start and end apart: 65, of which 23 were waited for; matrix products, arithmetic and copies ran while one was open for 7% of the time, Pallas kernels for 9%

profile of v1, /device:TPU:0, one launch (start us, length us, event | category | flops | bytes accessed | tf_op | source)
XLA Modules:
  0.0 864.8 jit_solution(17907065955735656705)
XLA Ops:
  8.3 9.3 %all_to_all.24 = bf16[1,32,3,4,256]{4,1,2,0,3:T(8,128)(2,1)S(1)} all-to-all(bf16[1,32,3,4,256]{4,1,2,0,3:T(8,128)(2,1)S(1)} %copy.175), channel_id=1, replica_groups=mesh['z'=4,'y'=2,'x'=2,'c'=2] {'x','c'}, dimensions={3} | all-to-all | bytes 393216 | tf_op jit(solution)/shard_map/all_to_all | solution.py:408
  30.5 66.7 %all-gather.1 = bf16[32,1,384]{2,1,0:T(2,128)(2,1)S(1)} all-gather(bf16[1,1,384]{2,1,0:T(2,128)(2,1)S(1)} %reshape.259), channel_id=2, replica_groups=mesh['z'=4,'y'=2,'x'=2,'c'=2] {'z','y','x','c'}, dimensions={0}, use_global_device_ids=true | all-gather | bytes 25344 | tf_op jit(solution)/shard_map/all_gather | solution.py:423
  103.6 7.9 attend_forward.5
  115.8 5.9 all-gather.9.cloned.1.call-done
  123.1 8.1 attend_forward.4
  135.6 8.0 attend_forward.6
  146.8 8.1 attend_forward.7
  182.7 18.9 %all-gather.13.cloned.1.call-done.reduce = bf16[2048,1024]{1,0:T(8,128)(2,1)} async-done(((bf16[128,1024]{1,0:T(8,128)(2,1)}), bf16[2048,1024]{1,0:T(8,128)(2,1)}) %all-gather.13.cloned.1.call-update) | async-done | bytes 4194320 | tf_op jit(solution)/shard_map/all_gather | solution.py:451
  201.6 77.9 %all-gather.11.cloned.1.call-done.expand = bf16[1024,2048]{1,0:T(8,128)(2,1)} async-done(((bf16[64,2048]{1,0:T(8,128)(2,1)}), bf16[1024,2048]{1,0:T(8,128)(2,1)}) %all-gather.11.cloned.1.call-update) | async-done | bytes 4194320 | tf_op jit(solution)/shard_map/all_gather | solution.py:450
  279.5 35.3 %feed_forward.1 = (bf16[2048,2048]{1,0:T(8,128)(2,1)}, bf16[2048,2048]{1,0:T(8,128)(2,1)}, f32[1024,1024]{1,0:T(8,128)}, bf16[1024,1024]{1,0:T(8,128)(2,1)}) custom-call(bf16[1024,1024]{1,0:T(8,128)(2,1)S(1)} %fusion.7.own.own_rows, bf16[1024,1024]{1,0:T(8,128)(2,1)} %collective-permute-done.25.other.other_rows, ...), custom_call_target="tpu_custom_call" | custom-call | flops 17179869184 | bytes 29360128 | tf_op jit(solution)/shard_map/feed_forward/pallas_call | solution.py:223
  337.2 61.4 %feed_backward.1 = (bf16[1024,2048]{1,0:T(8,128)(2,1)}, bf16[2048,1024]{1,0:T(8,128)(2,1)}, f32[1,2048]{1,0:T(1,128)}, f32[1024,1024]{1,0:T(8,128)}, bf16[1024,1024]{1,0:T(8,128)(2,1)}) custom-call(bf16[1024,1024]{1,0:T(8,128)(2,1)} %copy-done.52, bf16[1024,1024]{1,0:T(8,128)(2,1)} %copy-done.75, bf16[1024,1024]{1,0:T(8,128)(2,1)} %copy-done, ...), custom_call_target="tpu_custom_call" | custom-call | flops 34359738368 | bytes 54525952 | tf_op jit(solution)/shard_map/feed_backward/pallas_call | solution.py:304
  403.2 9.1 %multiply_reduce_fusion = (f32[1024]{0:T(1024)S(1)}, f32[1024]{0:T(1024)S(1)}, f32[1024]{0:T(1024)S(1)}, f32[1024]{0:T(1024)S(1)}, f32[1024,1024]{1,0:T(8,128)S(1)}, /*index=5*/bf16[1024,1024]{1,0:T(8,128)(2,1)}) fusion(f32[1024,1024]{1,0:T(8,128)} %copy-done.44, f32[1024]{0:T(1024)S(1)} %add_rsqrt_fusion.1, f32[1024]{0:T(1024)S(1)} %broadcast_multiply_fusion.4, ...), kind=kLoop, calls=%fused_computation.14 | loop fusion | flops 24113152 | bytes 23121920 | tf_op jit(solution)/shard_map/reduce_sum | solution.py:349
  436.5 15.0 %attend_backward.4 = (bf16[2,512,768]{2,1,0:T(8,128)(2,1)S(1)}, f32[2,128,1024]{2,1,0:T(8,128)S(1)}, bf16[2,128,1024]{2,1,0:T(8,128)(2,1)S(1)}, f32[2,128,1024]{...) custom-call(bf16[2,512,768]{2,1,0:T(8,128)(2,1)} %copy-done.43, ...), custom_call_target="tpu_custom_call" | custom-call | flops 6978797568 | bytes 11010048 | tf_op jit(solution)/shard_map/attend_backward/pallas_call | solution.py:151
  455.8 15.0 %attend_backward.5 = (bf16[2,512,768]{2,1,0:T(8,128)(2,1)S(1)}, f32[2,128,1024]{2,1,0:T(8,128)S(1)}, bf16[2,128,1024]{2,1,0:T(8,128)(2,1)S(1)}, f32[2,128,1024]{...) custom-call(bf16[2,512,768]{2,1,0:T(8,128)(2,1)} %copy-done.40, ...), custom_call_target="tpu_custom_call" | custom-call | flops 6978797568 | bytes 11010048 | tf_op jit(solution)/shard_map/attend_backward/pallas_call | solution.py:151
  474.8 15.1 %attend_backward.6 = (bf16[2,512,768]{2,1,0:T(8,128)(2,1)S(1)}, f32[2,128,1024]{2,1,0:T(8,128)S(1)}, bf16[2,128,1024]{2,1,0:T(8,128)(2,1)S(1)}, f32[2,128,1024]{...) custom-call(bf16[2,512,768]{2,1,0:T(8,128)(2,1)} %copy-done.42, ...), custom_call_target="tpu_custom_call" | custom-call | flops 6978797568 | bytes 11010048 | tf_op jit(solution)/shard_map/attend_backward/pallas_call | solution.py:151
  494.3 15.3 %attend_backward.7 = (bf16[2,512,768]{2,1,0:T(8,128)(2,1)S(1)}, f32[2,128,1024]{2,1,0:T(8,128)S(1)}, bf16[2,128,1024]{2,1,0:T(8,128)(2,1)S(1)}, f32[2,128,1024]{...) custom-call(bf16[2,512,768]{2,1,0:T(8,128)(2,1)} %copy-done.41, ...), custom_call_target="tpu_custom_call" | custom-call | flops 6978797568 | bytes 11010048 | tf_op jit(solution)/shard_map/attend_backward/pallas_call | solution.py:151
  513.2 6.1 fusion.8
  533.0 39.9 %all-reduce.2 = f32[32,384]{1,0:T(8,128)S(1)} all-reduce(f32[32,384]{1,0:T(8,128)S(1)} %concatenate.55), channel_id=4, replica_groups=mesh['z'=4,'y'=2,'x'=2,'c'=2] {'z','y','x','c'}, use_global_device_ids=true, to_apply=%region_19.20.clone | all-reduce | flops 12288 | bytes 98304
  581.8 12.2 %collective-permute-done.35 = bf16[2,128,1024]{2,1,0:T(8,128)(2,1)S(1)} collective-permute-done((bf16[2,128,1024]{2,1,0:T(8,128)(2,1)S(1)}, bf16[2,128,1024]{2,1,0:T(8,128)(2,1)S(1)}, u32[]{:S(2)}, u32[]{:S(2)}) %collective-permute-start.35) | collective-permute-done | bytes 524320 | tf_op jit(solution)/shard_map/ppermute | solution.py:385
  598.8 12.2 %collective-permute-done.41 = bf16[2,128,1024]{2,1,0:T(8,128)(2,1)S(1)} collective-permute-done((bf16[2,128,1024]{2,1,0:T(8,128)(2,1)S(1)}, bf16[2,128,1024]{2,1,0:T(8,128)(2,1)S(1)}, u32[]{:S(2)}, u32[]{:S(2)}) %collective-permute-start.41) | collective-permute-done | bytes 524320 | tf_op jit(solution)/shard_map/ppermute | solution.py:385
  613.2 15.1 %collective-permute-done.47 = bf16[2,128,1024]{2,1,0:T(8,128)(2,1)S(1)} collective-permute-done((bf16[2,128,1024]{2,1,0:T(8,128)(2,1)S(1)}, bf16[2,128,1024]{2,1,0:T(8,128)(2,1)S(1)}, u32[]{:S(2)}, u32[]{:S(2)}) %collective-permute-start.47) | collective-permute-done | bytes 524320 | tf_op jit(solution)/shard_map/ppermute | solution.py:385
  629.5 14.8 %collective-permute-done.53 = bf16[2,128,1024]{2,1,0:T(8,128)(2,1)S(1)} collective-permute-done((bf16[2,128,1024]{2,1,0:T(8,128)(2,1)S(1)}, bf16[2,128,1024]{2,1,0:T(8,128)(2,1)S(1)}, u32[]{:S(2)}, u32[]{:S(2)}) %collective-permute-start.53) | collective-permute-done | bytes 524320 | tf_op jit(solution)/shard_map/ppermute | solution.py:385
  663.6 93.6 %reduce-scatter.9.cloned.1.call-done = bf16[64,2048]{1,0:T(8,128)(2,1)} async-done(((bf16[1024,2048]{1,0:T(8,128)(2,1)}), bf16[64,2048]{1,0:T(8,128)(2,1)}) %reduce-scatter.9.cloned.1.call-update) | async-done | bytes 262160 | tf_op jit(solution)/shard_map/reduce_scatter | solution.py:496
  759.6 94.7 %reduce-scatter.11.cloned.1.call-done = bf16[128,1024]{1,0:T(8,128)(2,1)} async-done(((bf16[2048,1024]{1,0:T(8,128)(2,1)}), bf16[128,1024]{1,0:T(8,128)(2,1)}) %reduce-scatter.11.cloned.1.call-update) | async-done | bytes 262160 | tf_op jit(solution)/shard_map/reduce_scatter | solution.py:495
  (411 shorter events, 183.3 us)
Async XLA Ops:
  7.2 93.0 %all-gather.7.cloned.1.call-start = ((), (), s32[]{:S(2)}) async-start(), calls=%async_computation.6 | async-start | bytes 1769472 | tf_op jit(solution)/shard_map/all_gather | solution.py:411
  18.7 103.0 %all-gather.9.cloned.1.call-start = ((), (), s32[]{:S(2)}) async-start(), calls=%async_computation.7 | async-start | bytes 1114112 | tf_op jit(solution)/shard_map/all_gather | solution.py:438
  19.4 182.2 %all-gather.13.cloned.1.call-start = ((), (), s32[]{:S(2)}) async-start(), calls=%async_computation.9 | async-start | bytes 4456448 | tf_op jit(solution)/shard_map/all_gather | solution.py:451
  20.1 259.4 %all-gather.11.cloned.1.call-start = ((), (), s32[]{:S(2)}) async-start(), calls=%async_computation.8 | async-start | bytes 4456448 | tf_op jit(solution)/shard_map/all_gather | solution.py:450
  25.1 620.5 %reduce-scatter.5.cloned.1.call-start = ((), (), s32[]{:S(2)}) async-start(), calls=%async_computation.10 | async-start | bytes 1769472 | tf_op jit(solution)/shard_map/reduce_scatter | solution.py:539
  27.7 69.5 %collective-permute-start.7 = (bf16[2,128,1024]{2,1,0:T(8,128)(2,1)S(1)}, bf16[2,128,1024]{2,1,0:T(8,128)(2,1)}, u32[]{:S(2)}, u32[]{:S(2)}) collective-permute-start(bf16[2,128,1024]{2,1,0:T(8,128)(2,1)S(1)} %get-tuple-element.172.t0), channel_id=1, source_target_pairs={{0,2},{1,3},{2,0},{3,1},{4,6},{5,7},{6,4},{7,5},{8,10},{9,11},{10,... | collective-permute-start | bytes 1572872 | tf_op jit(solution)/shard_map/ppermute | solution.py:385
  28.0 69.7 %collective-permute-start.6 = (bf16[2,128,1024]{2,1,0:T(8,128)(2,1)S(1)}, bf16[2,128,1024]{2,1,0:T(8,128)(2,1)S(1)}, u32[]{:S(2)}, u32[]{:S(2)}) collective-permute-start(bf16[2,128,1024]{2,1,0:T(8,128)(2,1)S(1)} %get-tuple-element.172.t0), channel_id=1, source_target_pairs={{0,1},{1,0},{2,3},{3,2},{4,5},{5,4},{6,7},{7,6},{8,9},{9,8},{10,11... | collective-permute-start | bytes 1572872 | tf_op jit(solution)/shard_map/ppermute | solution.py:388
  28.0 69.8 %collective-permute-start.1 = (bf16[2,128,1024]{2,1,0:T(8,128)(2,1)}, bf16[2,128,1024]{2,1,0:T(8,128)(2,1)}, u32[]{:S(2)}, u32[]{:S(2)}) collective-permute-start(bf16[2,128,1024]{2,1,0:T(8,128)(2,1)} %get-tuple-element.171.t0), channel_id=1, source_target_pairs={{0,2},{1,3},{2,0},{3,1},{4,6},{5,7},{6,4},{7,5},{8,10},{9,11},{10,... | collective-permute-start | bytes 1572872 | tf_op jit(solution)/shard_map/ppermute | solution.py:385
  29.7 85.6 %collective-permute-start = (bf16[2,128,1024]{2,1,0:T(8,128)(2,1)}, bf16[2,128,1024]{2,1,0:T(8,128)(2,1)}, u32[]{:S(2)}, u32[]{:S(2)}) collective-permute-start(bf16[2,128,1024]{2,1,0:T(8,128)(2,1)} %get-tuple-element.171.t0), channel_id=1, source_target_pairs={{0,1},{1,0},{2,3},{3,2},{4,5},{5,4},{6,7},{7,6},{8,9},{9,8},{10,11... | collective-permute-start | bytes 1572872 | tf_op jit(solution)/shard_map/ppermute | solution.py:388
  30.0 69.7 %collective-permute-start.13 = (bf16[2,128,1024]{2,1,0:T(8,128)(2,1)S(1)}, bf16[2,128,1024]{2,1,0:T(8,128)(2,1)}, u32[]{:S(2)}, u32[]{:S(2)}) collective-permute-start(bf16[2,128,1024]{2,1,0:T(8,128)(2,1)S(1)} %get-tuple-element.174.t0), channel_id=1, source_target_pairs={{0,2},{1,3},{2,0},{3,1},{4,6},{5,7},{6,4},{7,5},{8,10},{9,11},{10,... | collective-permute-start | bytes 1572872 | tf_op jit(solution)/shard_map/ppermute | solution.py:385
  433.3 41.1 %collective-permute-start.42 = (bf16[2,128,256]{2,1,0:T(8,128)(2,1)S(1)}, bf16[2,128,256]{2,1,0:T(8,128)(2,1)S(1)}, u32[]{:S(2)}, u32[]{:S(2)}) collective-permute-start(bf16[2,128,256]{2,1,0:T(8,128)(2,1)S(1)} %bitcast.240), channel_id=1, source_target_pairs={{0,1},{1,0},{2,3},{3,2},{4,5},{5,4},{6,7},{7,6},{8,9},{9,8},{10,11... | collective-permute-start | bytes 393224 | tf_op jit(solution)/shard_map/ppermute | solution.py:385
  454.3 40.0 %collective-permute-start.48 = (bf16[2,128,256]{2,1,0:T(8,128)(2,1)S(1)}, bf16[2,128,256]{2,1,0:T(8,128)(2,1)S(1)}, u32[]{:S(2)}, u32[]{:S(2)}) collective-permute-start(bf16[2,128,256]{2,1,0:T(8,128)(2,1)S(1)} %bitcast.237), channel_id=1, source_target_pairs={{0,1},{1,0},{2,3},{3,2},{4,5},{5,4},{6,7},{7,6},{8,9},{9,8},{10,11... | collective-permute-start | bytes 393224 | tf_op jit(solution)/shard_map/ppermute | solution.py:385
  519.3 142.8 %reduce-scatter.7.cloned.1.call-start = ((), (), s32[]{:S(2)}) async-start(), calls=%async_computation.11 | async-start | bytes 1114112 | tf_op jit(solution)/shard_map/reduce_scatter | solution.py:514
  529.2 228.1 %reduce-scatter.9.cloned.1.call-start = ((), (), s32[]{:S(2)}) async-start(), calls=%async_computation.12 | async-start | bytes 4456448 | tf_op jit(solution)/shard_map/reduce_scatter | solution.py:496
  529.9 324.3 %reduce-scatter.11.cloned.1.call-start = ((), (), s32[]{:S(2)}) async-start(), calls=%async_computation.13 | async-start | bytes 4456448 | tf_op jit(solution)/shard_map/reduce_scatter | solution.py:495
  531.1 43.1 %collective-permute-start.34 = (bf16[2,128,1024]{2,1,0:T(8,128)(2,1)}, bf16[2,128,1024]{2,1,0:T(8,128)(2,1)}, u32[]{:S(2)}, u32[]{:S(2)}) collective-permute-start(bf16[2,128,1024]{2,1,0:T(8,128)(2,1)} %copy-done.20), channel_id=1, source_target_pairs={{0,1},{1,0},{2,3},{3,2},{4,5},{5,4},{6,7},{7,6},{8,9},{9,8},{10,11... | collective-permute-start | bytes 1572872 | tf_op jit(solution)/shard_map/ppermute | solution.py:388
  531.5 44.4 %collective-permute-start.40 = (bf16[2,128,1024]{2,1,0:T(8,128)(2,1)}, bf16[2,128,1024]{2,1,0:T(8,128)(2,1)}, u32[]{:S(2)}, u32[]{:S(2)}) collective-permute-start(bf16[2,128,1024]{2,1,0:T(8,128)(2,1)} %copy-done.23), channel_id=1, source_target_pairs={{0,1},{1,0},{2,3},{3,2},{4,5},{5,4},{6,7},{7,6},{8,9},{9,8},{10,11... | collective-permute-start | bytes 1572872 | tf_op jit(solution)/shard_map/ppermute | solution.py:388
  532.1 49.6 %collective-permute-start.33 = (bf16[2,128,1024]{2,1,0:T(8,128)(2,1)}, bf16[2,128,1024]{2,1,0:T(8,128)(2,1)}, u32[]{:S(2)}, u32[]{:S(2)}) collective-permute-start(bf16[2,128,1024]{2,1,0:T(8,128)(2,1)} %copy-done.17), channel_id=1, source_target_pairs={{0,1},{1,0},{2,3},{3,2},{4,5},{5,4},{6,7},{7,6},{8,9},{9,8},{10,11... | collective-permute-start | bytes 1572872 | tf_op jit(solution)/shard_map/ppermute | solution.py:388
  532.4 66.4 %collective-permute-start.39 = (bf16[2,128,1024]{2,1,0:T(8,128)(2,1)}, bf16[2,128,1024]{2,1,0:T(8,128)(2,1)}, u32[]{:S(2)}, u32[]{:S(2)}) collective-permute-start(bf16[2,128,1024]{2,1,0:T(8,128)(2,1)} %copy-done.18), channel_id=1, source_target_pairs={{0,1},{1,0},{2,3},{3,2},{4,5},{5,4},{6,7},{7,6},{8,9},{9,8},{10,11... | collective-permute-start | bytes 1572872 | tf_op jit(solution)/shard_map/ppermute | solution.py:388
  532.6 45.3 %collective-permute-start.46 = (bf16[2,128,1024]{2,1,0:T(8,128)(2,1)}, bf16[2,128,1024]{2,1,0:T(8,128)(2,1)}, u32[]{:S(2)}, u32[]{:S(2)}) collective-permute-start(bf16[2,128,1024]{2,1,0:T(8,128)(2,1)} %copy-done.24), channel_id=1, source_target_pairs={{0,1},{1,0},{2,3},{3,2},{4,5},{5,4},{6,7},{7,6},{8,9},{9,8},{10,11... | collective-permute-start | bytes 1572872 | tf_op jit(solution)/shard_map/ppermute | solution.py:388
  581.7 47.8 %collective-permute-start.51 = (bf16[2,128,1024]{2,1,0:T(8,128)(2,1)S(1)}, bf16[2,128,1024]{2,1,0:T(8,128)(2,1)S(1)}, u32[]{:S(2)}, u32[]{:S(2)}) collective-permute-start(bf16[2,128,1024]{2,1,0:T(8,128)(2,1)S(1)} %copy-done.22), channel_id=1, source_target_pairs={{0,1},{1,0},{2,3},{3,2},{4,5},{5,4},{6,7},{7,6},{8,9},{9,8},{10,11... | collective-permute-start | bytes 1572872 | tf_op jit(solution)/shard_map/ppermute | solution.py:388
  598.8 45.5 %collective-permute-start.53 = (bf16[2,128,1024]{2,1,0:T(8,128)(2,1)S(1)}, bf16[2,128,1024]{2,1,0:T(8,128)(2,1)S(1)}, u32[]{:S(2)}, u32[]{:S(2)}) collective-permute-start(bf16[2,128,1024]{2,1,0:T(8,128)(2,1)S(1)} %add_convert_fusion.1), channel_id=1, source_target_pairs={{0,2},{1,3},{2,0},{3,1},{4,6},{5,7},{6,4},{7,5},{8,10},{9,11},{10,... | collective-permute-start | bytes 1572872 | tf_op jit(solution)/shard_map/ppermute | solution.py:385
  647.3 111.0 %all-to-all-start.1 = ((bf16[4,32,3,1,256]{4,1,3,2,0:T(8,128)(2,1)}), bf16[4,32,3,1,256]{4,1,3,2,0:T(8,128)(2,1)S(1)}, u32[]{:S(2)}, u32[]{:S(2)}) async-start(bf16[4,32,3,1,256]{4,1,3,2,0:T(8,128)(2,1)} %copy.215), calls=%async_computation.2 | async-start | bytes 393216 | tf_op jit(solution)/shard_map/all_to_all | solution.py:542
  758.2 97.8 %collective-permute-start.55 = (bf16[32,2048]{1,0:T(8,128)(2,1)S(1)}, bf16[32,2048]{1,0:T(8,128)(2,1)S(1)}, u32[]{:S(2)}, u32[]{:S(2)}) collective-permute-start(bf16[32,2048]{1,0:T(8,128)(2,1)S(1)} %get-tuple-element.176), channel_id=1, source_target_pairs={{0,1},{1,0},{2,3},{3,2},{4,5},{5,4},{6,7},{7,6},{8,9},{9,8},{10,11... | collective-permute-start | bytes 393224 | tf_op jit(solution)/shard_map/ppermute | solution.py:388
  (117 other events, 1624.4 us)
Sparse Core Ops, SparseCore 0:
  18.8 44.5 all-gather.6
  66.1 55.5 all-gather.8
  124.5 77.0 all-gather.12
  204.8 74.6 all-gather.10
  519.4 63.4 reduce-scatter.4
  585.1 76.9 reduce-scatter.6
  664.4 92.7 reduce-scatter.8
  759.5 94.6 reduce-scatter.10

commit v2 on v1

--- a/solution.py
+++ b/solution.py
@@ -18,6 +18,7 @@
 ALL = ("z", "y", "x", "c")
 F32 = jnp.float32
 BF16 = jnp.bfloat16
+ELSEWHERE = pl.BlockSpec(memory_space=pl.ANY)
 
 
 def dot(left, right, contract=(1, 0)):
@@ -47,7 +48,8 @@
     return (lane // HEAD_DIM == head).astype(F32)
 
 
-def attend_kernel(t0, t1, t2, t3, weight, bias, seg_key, seg_query, m0, m1, m2, m3, kept, saved):
+def attend_kernel(late, t0, t1, t2, t3, weight, bias, seg_key, seg_query, *refs):
+    m0, m1, m2, m3, kept, saved = refs[late:]
     part = t0.shape[1]
     rows = jnp.concatenate([t[0] for t in (t0, t1, t2, t3)], axis=0)
     kept[0] = rows
@@ -69,12 +71,12 @@
         out[0] = mixed[index * part : (index + 1) * part]
 
 
-def attend(tokens, weight, bias, seg_key, seg_query):
+def attend(tokens, weight, bias, seg_key, seg_query, after):
     count, part, depth = tokens[0].shape
     wide = weight.shape[1]
     length = 4 * part
     return pl.pallas_call(
-        attend_kernel,
+        functools.partial(attend_kernel, len(after)),
         grid=(count,),
         in_specs=[by_row((1, part, depth))] * 4
         + [
@@ -82,7 +84,8 @@
             resident((1, wide)),
             by_row((1, length, 1)),
             by_row((1, 1, length)),
-        ],
+        ]
+        + [ELSEWHERE] * len(after),
         out_specs=[by_row((1, part, wide // 3))] * 4
         + [by_row((1, length, depth)), by_row((1, length, wide))],
         out_shape=[jax.ShapeDtypeStruct((count, part, wide // 3), BF16)] * 4
@@ -97,12 +100,11 @@
             transcendentals=count * length * length * wide // (3 * HEAD_DIM),
         ),
         name="attend_forward",
-    )(*tokens, weight, bias, seg_key, seg_query)
-
-
-def attend_back_kernel(
-    saved, g0, g1, g2, g3, weight, seg_key, seg_query, grad_project, r0, r1, r2, r3, sums
-):
+    )(*tokens, weight, bias, seg_key, seg_query, *after)
+
+
+def attend_back_kernel(late, saved, g0, g1, g2, g3, weight, seg_key, seg_query, *refs):
+    grad_project, r0, r1, r2, r3, sums = refs[late:]
     part = g0.shape[1]
     width = saved.shape[2] // 3
     factor = HEAD_DIM**-0.5
@@ -144,12 +146,12 @@
         )
 
 
-def attend_back(saved, grads, weight, seg_key, seg_query):
+def attend_back(saved, grads, weight, seg_key, seg_query, after):
     count, part, width = grads[0].shape
     depth, wide = weight.shape
     length = 4 * part
     return pl.pallas_call(
-        attend_back_kernel,
+        functools.partial(attend_back_kernel, len(after)),
         grid=(count,),
         in_specs=[by_row((1, length, wide))]
         + [by_row((1, part, width))] * 4
@@ -157,7 +159,8 @@
             resident((depth, wide)),
             by_row((1, length, 1)),
             by_row((1, 1, length)),
-        ],
+        ]
+        + [ELSEWHERE] * len(after),
         out_specs=[by_row((1, length, wide))]
         + [by_row((1, part, depth))] * 4
         + [by_row((1, 1, wide))],
@@ -171,67 +174,63 @@
             transcendentals=count * length * length * wide // (3 * HEAD_DIM),
         ),
         name="attend_backward",
-    )(saved, *grads, weight, seg_key, seg_query)
-
-
-def pick(first_half, own, other):
-    return jnp.where(first_half, own, other)
-
-
-def feed_kernel(steps, own, other, expand, bias, reduce, act, slope, own_out, other_out):
+    )(saved, *grads, weight, seg_key, seg_query, *after)
+
+
+def column(shape):
+    return pl.BlockSpec(shape, lambda i: (0, i))
+
+
+def feed_kernel(block, own, other, expand, bias, reduce, act, slope, own_out, other_out, far_sum):
     step = pl.program_id(0)
-    rows = pick(step < steps, own[...], other[...])
-    hidden = expand.shape[1]
-    piece = hidden // 4
-    for index in range(4):
-        at = slice(index * piece, (index + 1) * piece)
-        inside = dot(rows, expand[:, at]) + bias[:, at]
-        square = inside * inside
-        curve = jnp.tanh(0.7978845608028654 * inside * (1.0 + 0.044715 * square))
-        half = 0.5 * (1.0 + curve)
-        act[:, at] = (inside * half).astype(BF16)
-        slope[:, at] = (
-            half
-            + 0.5
-            * inside
-            * (1.0 - curve * curve)
-            * (0.7978845608028654 * (1.0 + 3 * 0.044715 * square))
-        ).astype(BF16)
-    total = dot(act[...], reduce[...])
-
-    @pl.when(step < steps)
+    rows = own.shape[0]
+
+    @pl.when(step == 0)
     def _():
-        own_out[...] = total
-
-    @pl.when(step >= steps)
+        own_out[...] = jnp.zeros_like(own_out)
+        far_sum[...] = jnp.zeros_like(far_sum)
+
+    for source, total, start in ((own, own_out, 0), (other, far_sum, rows)):
+        for index in range(rows // block):
+            at = slice(index * block, (index + 1) * block)
+            to = slice(start + index * block, start + (index + 1) * block)
+            inside = dot(source[at], expand[...]) + bias[...]
+            square = inside * inside
+            curve = jnp.tanh(0.7978845608028654 * inside * (1.0 + 0.044715 * square))
+            half = 0.5 * (1.0 + curve)
+            active = (inside * half).astype(BF16)
+            act[to] = active
+            slope[to] = (
+                half
+                + 0.5
+                * inside
+                * (1.0 - curve * curve)
+                * (0.7978845608028654 * (1.0 + 3 * 0.044715 * square))
+            ).astype(BF16)
+            total[at] += dot(active, reduce[...])
+
+    @pl.when(step == pl.num_programs(0) - 1)
     def _():
-        other_out[...] = total.astype(BF16)
-
-
-def halves(steps, shape):
-    return [
-        pl.BlockSpec(shape, lambda i: (jnp.minimum(i, steps - 1), 0)),
-        pl.BlockSpec(shape, lambda i: (jnp.maximum(i - steps, 0), 0)),
-    ]
+        other_out[...] = far_sum[...].astype(BF16)
 
 
 def feed(own, other, expand, bias, reduce):
     rows, depth = own.shape
     hidden = expand.shape[1]
-    block = 256
-    steps = rows // block
+    piece = 512
     return pl.pallas_call(
-        functools.partial(feed_kernel, steps),
-        grid=(2 * steps,),
-        in_specs=halves(steps, (block, depth))
-        + [resident((depth, hidden)), resident((1, hidden)), resident((hidden, depth))],
-        out_specs=[by_row((block, hidden))] * 2 + halves(steps, (block, depth)),
+        functools.partial(feed_kernel, 512),
+        grid=(hidden // piece,),
+        in_specs=[resident((rows, depth))] * 2
+        + [column((depth, piece)), column((1, piece)), by_row((piece, depth))],
+        out_specs=[column((2 * rows, piece))] * 2 + [resident((rows, depth))] * 2,
         out_shape=[jax.ShapeDtypeStruct((2 * rows, hidden), BF16)] * 2
         + [
             jax.ShapeDtypeStruct((rows, depth), F32),
             jax.ShapeDtypeStruct((rows, depth), BF16),
         ],
-        compiler_params=pltpu.CompilerParams(vmem_limit_bytes=48 * MIB),
+        scratch_shapes=[pltpu.VMEM((rows, depth), F32)],
+        compiler_params=pltpu.CompilerParams(vmem_limit_bytes=56 * MIB),
         cost_estimate=pl.CostEstimate(
             flops=8 * rows * depth * hidden,
             bytes_accessed=4 * rows * (2 * hidden + 3 * depth),
@@ -242,7 +241,7 @@
 
 
 def feed_back_kernel(
-    steps,
+    block,
     own_grad,
     other_grad,
     own_rows,
@@ -256,64 +255,57 @@
     bias_grad,
     own_out,
     other_out,
-    expand_sum,
-    reduce_sum,
+    far_sum,
+    inside,
 ):
     step = pl.program_id(0)
-    grad = pick(step < steps, own_grad[...], other_grad[...])
-    rows = pick(step < steps, own_rows[...], other_rows[...])
-    grad_act = dot(grad, reduce[...], (1, 1))
-    grad_inside = (grad_act * slope[...].astype(F32)).astype(BF16)
-    bias_part = jnp.sum(grad_inside.astype(F32), axis=0, keepdims=True)
-    expand_part = dot(rows, grad_inside, (0, 0))
-    reduce_part = dot(act[...], grad, (0, 0))
+    rows = own_grad.shape[0]
 
     @pl.when(step == 0)
     def _():
-        bias_grad[...] = bias_part
-        expand_sum[...] = expand_part
-        reduce_sum[...] = reduce_part
-
-    @pl.when(step > 0)
+        own_out[...] = jnp.zeros_like(own_out)
+        far_sum[...] = jnp.zeros_like(far_sum)
+
+    bias_sum = jnp.zeros(bias_grad.shape, F32)
+    for source, total, start in ((own_grad, own_out, 0), (other_grad, far_sum, rows)):
+        for index in range(rows // block):
+            at = slice(index * block, (index + 1) * block)
+            to = slice(start + index * block, start + (index + 1) * block)
+            grad_act = dot(source[at], reduce[...], (1, 1))
+            part = (grad_act * slope[to].astype(F32)).astype(BF16)
+            inside[to] = part
+            bias_sum += jnp.sum(part.astype(F32), axis=0, keepdims=True)
+            total[at] += dot(part, expand[...], (1, 1))
+    bias_grad[...] = bias_sum
+    reduce_grad[...] = (
+        dot(act[:rows], own_grad[...], (0, 0)) + dot(act[rows:], other_grad[...], (0, 0))
+    ).astype(BF16)
+    flipped = dot(inside[:rows], own_rows[...], (0, 0)) + dot(
+        inside[rows:], other_rows[...], (0, 0)
+    )
+    expand_grad[...] = jnp.transpose(flipped).astype(BF16)
+
+    @pl.when(step == pl.num_programs(0) - 1)
     def _():
-        bias_grad[...] += bias_part
-        expand_sum[...] += expand_part
-        reduce_sum[...] += reduce_part
-
-    total = dot(grad_inside, expand[...], (1, 1))
-
-    @pl.when(step < steps)
-    def _():
-        own_out[...] = total
-
-    @pl.when(step >= steps)
-    def _():
-        other_out[...] = total.astype(BF16)
-
-    @pl.when(step == 2 * steps - 1)
-    def _():
-        expand_grad[...] = expand_sum[...].astype(BF16)
-        reduce_grad[...] = reduce_sum[...].astype(BF16)
+        other_out[...] = far_sum[...].astype(BF16)
 
 
 def feed_back(own_grad, other_grad, own_rows, other_rows, act, slope, expand, reduce):
     rows, depth = own_grad.shape
     hidden = expand.shape[1]
-    block = 256
-    steps = rows // block
+    piece = 256
     return pl.pallas_call(
-        functools.partial(feed_back_kernel, steps),
-        grid=(2 * steps,),
-        in_specs=halves(steps, (block, depth))
-        + halves(steps, (block, depth))
-        + [by_row((block, hidden))] * 2
-        + [resident((depth, hidden)), resident((hidden, depth))],
+        functools.partial(feed_back_kernel, 512),
+        grid=(hidden // piece,),
+        in_specs=[resident((rows, depth))] * 4
+        + [column((2 * rows, piece))] * 2
+        + [column((depth, piece)), by_row((piece, depth))],
         out_specs=[
-            resident((depth, hidden)),
-            resident((hidden, depth)),
-            resident((1, hidden)),
+            column((depth, piece)),
+            by_row((piece, depth)),
+            column((1, piece)),
         ]
-        + halves(steps, (block, depth)),
+        + [resident((rows, depth))] * 2,
         out_shape=[
             jax.ShapeDtypeStruct((depth, hidden), BF16),
             jax.ShapeDtypeStruct((hidden, depth), BF16),
@@ -322,10 +314,10 @@
             jax.ShapeDtypeStruct((rows, depth), BF16),
         ],
         scratch_shapes=[
-            pltpu.VMEM((depth, hidden), F32),
-            pltpu.VMEM((hidden, depth), F32),
+            pltpu.VMEM((rows, depth), F32),
+            pltpu.VMEM((2 * rows, piece), BF16),
         ],
-        compiler_params=pltpu.CompilerParams(vmem_limit_bytes=60 * MIB),
+        compiler_params=pltpu.CompilerParams(vmem_limit_bytes=56 * MIB),
         cost_estimate=pl.CostEstimate(
             flops=16 * rows * depth * hidden,
             bytes_accessed=4 * rows * (2 * hidden + 5 * depth) + 8 * depth * hidden,
@@ -390,10 +382,59 @@
     def chosen(array, index, axis):
         return lax.dynamic_index_in_dim(array, index, axis, keepdims=False)
 
+    def trade(array, name):
+        return lax.ppermute(array, name, [(0, 1), (1, 0)])
+
+    def pair(own, other, axis, name):
+        return jnp.where(
+            lax.axis_index(name) == 0,
+            jnp.stack([own, other], axis=axis),
+            jnp.stack([other, own], axis=axis),
+        )
+
     def by_core(own, other, axis):
-        return jnp.where(
-            low_core, jnp.stack([own, other], axis=axis), jnp.stack([other, own], axis=axis)
-        )
+        return pair(own, other, axis, "c")
+
+    def halve(array, axis, name):
+        me = lax.axis_index(name)
+        return chosen(array, me, axis).astype(F32) + trade(
+            chosen(array, 1 - me, axis), name
+        ).astype(F32)
+
+    last = sizes["z"] - 1
+    up = [(i, i + 1) for i in range(last)]
+    down = [(i + 1, i) for i in range(last)]
+    height = lax.axis_index("z")
+
+    def chain_gather(block):
+        if last > 3:
+            return lax.all_gather(block, "z"), [[block]] * 3
+        below, above, steps = [], [], []
+        low_block, high_block = block, block
+        for _ in range(last):
+            low_block = lax.ppermute(low_block, "z", up)
+            high_block = lax.ppermute(high_block, "z", down)
+            below.append(low_block)
+            above.append(high_block)
+            steps.append([low_block, high_block])
+        line = jnp.stack(below[::-1] + [block] + above)
+        return lax.dynamic_slice_in_dim(line, last - height, last + 1, 0), steps
+
+    def chain_scatter(blocks, kind=BF16):
+        if last > 3:
+            return lax.psum_scatter(blocks, "z").astype(F32), [[blocks]] * 3
+        low_sum, high_sum, steps = None, None, []
+        for step in range(last):
+            low_send = chosen(blocks, jnp.minimum(last - step + height, last), 0)
+            high_send = chosen(blocks, jnp.maximum(height - last + step, 0), 0)
+            if step:
+                low_send = (low_send.astype(F32) + low_sum.astype(F32)).astype(kind)
+                high_send = (high_send.astype(F32) + high_sum.astype(F32)).astype(kind)
+            low_sum = lax.ppermute(low_send, "z", up)
+            high_sum = lax.ppermute(high_send, "z", down)
+            steps.append([low_sum, high_sum])
+        own = chosen(blocks, height, 0).astype(F32)
+        return own + low_sum.astype(F32) + high_sum.astype(F32), steps
 
     pieces = [tokens[i * seq_count // CHUNKS : (i + 1) * seq_count // CHUNKS] for i in range(CHUNKS)]
     gathered = []
@@ -405,11 +446,6 @@
     seg_key = seg[:, :, None]
     seg_query = seg[:, None, :]
 
-    mine = lax.all_to_all(
-        project_weight.reshape(share, 3, ctx_size, lanes), CTX, 2, 0, tiled=False
-    ).reshape(ctx_size * share, 3 * lanes)
-    full_project = lax.all_gather(mine, SEQ, axis=0, tiled=True)
-
     vectors = (
         query_bias,
         value_bias,
@@ -419,10 +455,31 @@
         reduce_bias,
         second_gain,
         second_shift,
-    )
-    packed = lax.all_gather(
-        jnp.concatenate(vectors + (expand_bias,))[None], ALL, axis=0, tiled=True
-    ).astype(F32)
+        expand_bias,
+    )
+    vector_count = 8 * share + expand_bias.shape[0]
+    blocks = project_weight.reshape(share, 3, ctx_size, lanes)
+    own_vectors = jnp.concatenate(vectors)
+    columns_of = [chosen(blocks, place ^ r, 2) for r in range(ctx_size)]
+    weights_from = [columns_of[0]] + [hop(columns_of[r], r) for r in (1, 2, 3)]
+    vectors_from = [own_vectors] + [hop(own_vectors, r) for r in (1, 2, 3)]
+    weights_from = jnp.stack(weights_from).reshape(ctx_size, share, 3 * lanes)
+    mine = jnp.concatenate([chosen(weights_from, place ^ r, 0) for r in range(ctx_size)], axis=0)
+    vectors_from = jnp.stack(vectors_from)
+    vectors_from = jnp.stack([chosen(vectors_from, place ^ r, 0) for r in range(ctx_size)])
+    below = 16 * -(-ctx_size * vector_count // (48 * lanes))
+    vector_rows = jnp.pad(
+        vectors_from.reshape(-1), (0, below * 3 * lanes - ctx_size * vector_count)
+    ).reshape(below, 3 * lanes)
+    whole_project = lax.all_gather(jnp.concatenate([mine, vector_rows]), SEQ, axis=0)
+    whole_project = whole_project.reshape(-1, ctx_size * share + below, 3 * lanes)
+    full_project = whole_project[:, : ctx_size * share].reshape(width, 3 * lanes)
+    packed = (
+        whole_project[:, ctx_size * share :]
+        .reshape(-1, below * 3 * lanes)[:, : ctx_size * vector_count]
+        .reshape(everyone, vector_count)
+        .astype(F32)
+    )
     full_query, full_value, out_bias, gain_one, shift_one, red_bias, gain_two, shift_two = [
         packed[:, i * share : (i + 1) * share].reshape(width) for i in range(8)
     ]
@@ -435,20 +492,23 @@
         ]
     )[None]
 
-    out_half = lax.all_gather(output_weight, CHIPS, axis=0, tiled=True).reshape(
-        chips, share, width
-    )
-    full_output = by_core(out_half, swap(out_half), 1).reshape(ctx_size, lanes, width)
-    full_output = jnp.concatenate(
-        [chosen(full_output, place ^ r, 0) for r in range(ctx_size)], axis=0
-    )
-
+    full_reduce = lax.all_gather(reduce_weight, CHIPS, axis=0, tiled=True)
     columns = expand_weight.reshape(share, chips, 2, own_hidden // chips)
     own_columns = chosen(columns, core, 2).reshape(share, own_hidden)
     far_columns = chosen(columns, 1 - core, 2).reshape(share, own_hidden)
     both = by_core(own_columns, swap(far_columns), 0).reshape(2 * share, own_hidden)
-    full_expand = lax.all_gather(both, CHIPS, axis=0, tiled=True)
-    full_reduce = lax.all_gather(reduce_weight, CHIPS, axis=0, tiled=True)
+    both = pair(both, trade(both, "x"), 0, "x")
+    both = pair(both, trade(both, "y"), 0, "y")
+    full_expand, expand_steps = chain_gather(both)
+    full_expand = full_expand.reshape(width, own_hidden)
+
+    quarter = pair(output_weight, trade(output_weight, "x"), 0, "x")
+    quarter, output_steps = chain_gather(quarter)
+    out_half = pair(quarter, trade(quarter, "y"), 1, "y").reshape(chips, share, width)
+    full_output = by_core(out_half, swap(out_half), 1).reshape(ctx_size, lanes, width)
+    full_output = jnp.concatenate(
+        [chosen(full_output, place ^ r, 0) for r in range(ctx_size)], axis=0
+    )
 
     saved = []
     kept_rows = []
@@ -456,7 +516,12 @@
     for index in range(CHUNKS):
         at = slice(index * seq_count // CHUNKS, (index + 1) * seq_count // CHUNKS)
         *mixed, all_rows, kept = attend(
-            gathered[index], full_project, bias_all, seg_key[at], seg_query[at]
+            gathered[index],
+            full_project,
+            bias_all,
+            seg_key[at],
+            seg_query[at],
+            (expand_steps[0], expand_steps[1], [out_half], expand_steps[2])[index],
         )
         kept_rows.append(all_rows.reshape(-1, width))
         saved.append(kept)
@@ -493,7 +558,9 @@
         full_reduce,
     )
     reduce_owned = lax.psum_scatter(reduce_grad, CHIPS, scatter_dimension=0, tiled=True)
-    expand_owned = lax.psum_scatter(expand_grad, CHIPS, scatter_dimension=0, tiled=True)
+    expand_grad = expand_grad.reshape(sizes["z"], 2, sizes["x"], 2 * share, own_hidden)
+    expand_half = halve(expand_grad, 1, "y").astype(BF16)
+    expand_line, expand_steps = chain_scatter(expand_half)
     grad_first = grad_second + own_back + swap(far_back).astype(F32)
     grad_hidden, grad_gain_one, grad_shift_one = normalize_back(
         grad_first, scaled_one, inverse_one, gain_one
@@ -507,16 +574,10 @@
     output_grad = output_grad.reshape(ctx_size, lanes, width)
     output_grad = jnp.concatenate(
         [chosen(output_grad, place ^ r, 0) for r in range(ctx_size)], axis=0
-    ).reshape(chips, 2, share, width)
-    output_grad = chosen(output_grad, core, 1).astype(F32) + swap(
-        chosen(output_grad, 1 - core, 1)
-    ).astype(F32)
-    output_owned = lax.psum_scatter(
-        output_grad.astype(BF16).reshape(chips * share, width),
-        CHIPS,
-        scatter_dimension=0,
-        tiled=True,
-    )
+    ).reshape(sizes["z"], 2, sizes["x"], 2, share, width)
+    output_half = halve(output_grad, 3, "c").astype(BF16)
+    output_half = halve(output_half, 1, "y").astype(BF16)
+    output_line, output_steps = chain_scatter(output_half)
 
     project_parts = []
     work_parts = []
@@ -525,23 +586,43 @@
         at = slice(index * seq_count // CHUNKS, (index + 1) * seq_count // CHUNKS)
         grads = [grad_mixed[at, :, 0]] + [hop(grad_mixed[at, :, r], r) for r in (1, 2, 3)]
         grad_part, r0, r1, r2, r3, sums = attend_back(
-            saved[index], grads, full_project, seg_key[at], seg_query[at]
+            saved[index],
+            grads,
+            full_project,
+            seg_key[at],
+            seg_query[at],
+            (
+                [],
+                [expand_half],
+                expand_steps[0] + output_steps[0] + work_parts[:1],
+                expand_steps[2] + output_steps[2] + work_parts[1:2] + [reduce_owned],
+            )[index],
         )
         across = r2 + swap(r3).astype(F32)
-        work_parts.append(r0 + swap(r1).astype(F32) + hop(across.astype(BF16), 2).astype(F32))
+        work_parts.append(
+            grad_hidden[index * rows_count // CHUNKS : (index + 1) * rows_count // CHUNKS]
+            .reshape(r0.shape)
+            + r0
+            + swap(r1).astype(F32)
+            + hop(across.astype(BF16), 2).astype(F32)
+        )
         project_parts.append(grad_part)
         sum_parts.append(sums)
     project_grad = sum(
         dot(all_rows, grad_part.reshape(-1, 3 * lanes), (0, 0))
         for all_rows, grad_part in zip(kept_rows, project_parts)
     )
-    grad_work = grad_hidden.reshape(tokens.shape) + jnp.concatenate(work_parts, axis=0)
-    project_owned = lax.psum_scatter(
-        project_grad.astype(BF16), SEQ, scatter_dimension=0, tiled=True
+    grad_work = jnp.concatenate(work_parts, axis=0)
+    project_owned, _ = chain_scatter(
+        halve(
+            project_grad.astype(BF16).reshape(sizes["z"], 2, ctx_size * share, 3 * lanes), 1, "y"
+        ).astype(BF16)
     )
     project_owned = lax.all_to_all(
         project_owned.reshape(ctx_size, share, 3, lanes), CTX, 0, 2, tiled=False
     ).reshape(share, 3 * width)
+    expand_owned = halve(expand_line.astype(BF16), 0, "x")
+    output_owned = halve(output_line.astype(BF16), 0, "x")
 
     far_rows = expand_owned.reshape(2, share, own_hidden)
     expand_owned = by_core(
@@ -573,7 +654,10 @@
         + [hidden_sums.reshape(everyone, -1)],
         axis=1,
     )
-    owned = lax.psum_scatter(packed_grads, ALL, scatter_dimension=0, tiled=True)[0]
+    packed_grads = packed_grads.reshape(sizes["z"], 2, sizes["x"], 2, vector_count)
+    for axis, name in ((3, "c"), (2, "x"), (1, "y")):
+        packed_grads = halve(packed_grads, axis, name)
+    owned, _ = chain_scatter(packed_grads, F32)
     small = [owned[i * share : (i + 1) * share] for i in range(8)]
     return (
         layer_work,

time: 869 us -> 769 us (0.88)
  waiting for transfers between devices: 388 us -> 220 us
  starting transfers between devices: 32.6 us -> 149 us
  blocking collectives: 116 us -> 0 us
  local copies, waits for them, and re-layouts: 50.8 us -> 104 us
  other arithmetic: 46 us -> 63.8 us
  Pallas kernels: 189 us -> 178 us
    ppermute x0 -> x49, waiting for transfers between devices: none -> 178 us  [the longest x13 116 us: trade(): return lax.ppermute(array, name, [(0, 1), (1, 0)])]
    ppermute x0 -> x49, starting transfers between devices: none -> 113 us  [the longest x12 46.3 us: chain_scatter(): low_sum = lax.ppermute(low_send, 'z', up)]
    reduce_scatter x3 -> x0, waiting for transfers between devices: 99.3 us -> none  [the longest x1 93.6 us: on_device(): lax.psum_scatter(expand_grad, CHIPS, scatter_dimension=0, tiled=True)]
    reduce_scatter x1, waiting for transfers between devices: 94.7 us -> 0.01 us  [on_device(): lax.psum_scatter(reduce_grad, CHIPS, scatter_dimension=0, tiled=True)]
    all_gather x3 -> x1, waiting for transfers between devices: 83.8 us -> 0.01 us  [on_device(): lax.all_gather(jnp.concatenate([mine, vector_rows]), SEQ, axis=0)]
    all_gather x1 -> x0, blocking collectives: 66.7 us -> none  [on_device(): lax.all_gather(jnp.concatenate(vectors + (expand_bias,))[None], ALL, axis...]
    unnamed x1 -> x0, blocking collectives: 39.9 us -> none
    ppermute x32 -> x38, waiting for transfers between devices: 70.6 us -> 31 us  [hop(): return lax.ppermute(array, CTX, [(i, i ^ step) for i in range(ctx_size)])]
  transfers between devices with their start and end apart: 65 -> 114, of which waited for: 23 -> 41; matrix products, arithmetic and copies ran while one was open for 7% -> 20% of each run, Pallas kernels for 9% -> 12%
where the time goes in v2:
time: 769 us; the launch traced here: 759 us
  waiting for transfers between devices  220 us (29%)
  Pallas kernels  178 us (23%)
  starting transfers between devices  149 us (19%)
  local copies, waits for them, and re-layouts  104 us (14%)
  other arithmetic  63.8 us (8%)
  matrix products  27.7 us (4%)
  between operations  16.4 us (2%)
    ppermute x13, waiting for transfers between devices, trade(): return lax.ppermute(array, name, [(0, 1), (1, 0)])  116 us
    pallas_call x4, Pallas kernels, attend_back(): pl.pallas_call(functools.partial(attend_back_kernel, len(after)), grid=(c...  60.9 us
    pallas_call x1, Pallas kernels, feed_back(): pl.pallas_call(functools.partial(feed_back_kernel, 512), grid=(hidden //...  50.5 us
    ppermute x12, starting transfers between devices, chain_scatter(): low_sum = lax.ppermute(low_send, 'z', up)  46.3 us
    unnamed x266, local copies, waits for them, and re-layouts  41.1 us
    pallas_call x1, Pallas kernels, feed(): pl.pallas_call(functools.partial(feed_kernel, 512), grid=(hidden // piece...  34.1 us
    pallas_call x4, Pallas kernels, attend(): pl.pallas_call(functools.partial(attend_kernel, len(after)), grid=(count,...  32.8 us
    ppermute x38, waiting for transfers between devices, hop(): return lax.ppermute(array, CTX, [(i, i ^ step) for i in range(ctx_size)])  31 us
  transfers between devices with their start and end apart: 114, of which 41 were waited for; matrix products, arithmetic and copies ran while one was open for 20% of the time, Pallas kernels for 12%

profile of v2, /device:TPU:0, one launch (start us, length us, event | category | flops | bytes accessed | tf_op | source)
XLA Modules:
  0.0 758.7 jit_solution(11594720809368269630)
XLA Ops:
  7.2 6.1 concatenate.126
  49.1 5.8 collective-permute-done.34
  58.8 13.8 %collective-permute-done.35 = bf16[4,2,32,1024]{3,2,1,0:T(8,128)(2,1)} collective-permute-done((bf16[4,2,32,1024]{3,2,1,0:T(8,128)(2,1)}, bf16[4,2,32,1024]{3,2,1,0:T(8,128)(2,1)}, u32[]{:S(2)}, u32[]{:S(2)}) %collective-permute-start.35) | collective-permute-done | bytes 524320 | tf_op jit(solution)/shard_map/ppermute | solution.py:386
  74.2 12.7 %collective-permute-done.11 = bf16[2,64,2048]{2,1,0:T(8,128)(2,1)S(1)} collective-permute-done((bf16[2,64,2048]{2,1,0:T(8,128)(2,1)}, bf16[2,64,2048]{2,1,0:T(8,128)(2,1)S(1)}, u32[]{:S(2)}, u32[]{:S(2)}) %collective-permute-start.11) | collective-permute-done | bytes 524320 | tf_op jit(solution)/shard_map/ppermute | solution.py:386
  106.1 11.8 %collective-permute-done.12.refs_0_ = bf16[2,2,64,2048]{3,2,1,0:T(8,128)(2,1)} collective-permute-done((bf16[2,2,64,2048]{3,2,1,0:T(8,128)(2,1)}, bf16[2,2,64,2048]{3,2,1,0:T(8,128)(2,1)}, u32[]{:S(2)}, u32[]{:S(2)}) %collective-permute-start.12) | collective-permute-done | bytes 1048608 | tf_op jit(solution)/shard_map/ppermute | solution.py:415
  131.3 10.9 %collective-permute-done.26.t2 = bf16[2,128,1024]{2,1,0:T(8,128)(2,1)} collective-permute-done((bf16[2,128,1024]{2,1,0:T(8,128)(2,1)S(1)}, bf16[2,128,1024]{2,1,0:T(8,128)(2,1)}, u32[]{:S(2)}, u32[]{:S(2)}) %collective-permute-start.26) | collective-permute-done | bytes 524320 | tf_op jit(solution)/shard_map/ppermute | solution.py:377
  149.6 5.8 collective-permute-start.42
  157.5 8.8 %attend_forward.4 = (bf16[2,128,256]{2,1,0:T(8,128)(2,1)S(1)}, bf16[2,128,256]{2,1,0:T(8,128)(2,1)}, bf16[2,128,256]{2,1,0:T(8,128)(2,1)S(1)}, bf16[2,128,256]{2...) custom-call(bf16[2,128,1024]{2,1,0:T(8,128)(2,1)S(1)} %copy-done.22, ...), custom_call_target="tpu_custom_call" | custom-call | flops 3757572096 | bytes 5242880 | tf_op jit(solution)/shard_map/attend_forward/pallas_call | solution.py:78
  170.0 8.0 %attend_forward.5 = (bf16[2,128,256]{2,1,0:T(8,128)(2,1)S(1)}, bf16[2,128,256]{2,1,0:T(8,128)(2,1)S(1)}, bf16[2,128,256]{2,1,0:T(8,128)(2,1)S(1)}, bf16[2,128,25...) custom-call(bf16[2,128,1024]{2,1,0:T(8,128)(2,1)S(1)} %copy-done.20, ...), custom_call_target="tpu_custom_call" | custom-call | flops 3757572096 | bytes 5242880 | tf_op jit(solution)/shard_map/attend_forward/pallas_call | solution.py:78
  184.2 7.8 %attend_forward.6 = (bf16[2,128,256]{2,1,0:T(8,128)(2,1)S(1)}, bf16[2,128,256]{2,1,0:T(8,128)(2,1)S(1)}, bf16[2,128,256]{2,1,0:T(8,128)(2,1)S(1)}, bf16[2,128,25...) custom-call(bf16[2,128,1024]{2,1,0:T(8,128)(2,1)S(1)} %copy-done.18, ...), custom_call_target="tpu_custom_call" | custom-call | flops 3757572096 | bytes 5242880 | tf_op jit(solution)/shard_map/attend_forward/pallas_call | solution.py:78
  206.0 6.6 collective-permute-done.43.refs_1_
  212.6 8.2 %attend_forward.7 = (bf16[2,128,256]{2,1,0:T(8,128)(2,1)S(1)}, bf16[2,128,256]{2,1,0:T(8,128)(2,1)S(1)}, bf16[2,128,256]{2,1,0:T(8,128)(2,1)S(1)}, bf16[2,128,25...) custom-call(bf16[2,128,1024]{2,1,0:T(8,128)(2,1)} %get-tuple-element.190.t0, ...), custom_call_target="tpu_custom_call" | custom-call | flops 3757572096 | bytes 5242880 | tf_op jit(solution)/shard_map/attend_forward/pallas_call | solution.py:78
  249.7 34.1 %feed_forward.1 = (bf16[2048,2048]{1,0:T(8,128)(2,1)}, bf16[2048,2048]{1,0:T(8,128)(2,1)}, f32[1024,1024]{1,0:T(8,128)}, bf16[1024,1024]{1,0:T(8,128)(2,1)}) custom-call(bf16[1024,1024]{1,0:T(8,128)(2,1)} %copy-done.79, bf16[1024,1024]{1,0:T(8,128)(2,1)} %collective-permute-done.48.other.other_rows, bf16[1024,2048]{1,0:T(8,128)(2,1)} %bitcast.359, ...), custom_call_target="tpu_custom_call" | custom-call | flops 17179869184 | bytes 29360128 | tf_op jit(solution)/shard_map/feed_forward/pallas_call | solution.py:221
  303.1 50.5 %feed_backward.1 = (bf16[1024,2048]{1,0:T(8,128)(2,1)}, bf16[2048,1024]{1,0:T(8,128)(2,1)}, f32[1,2048]{1,0:T(1,128)}, f32[1024,1024]{1,0:T(8,128)}, bf16[1024,1024]{1,0:T(8,128)(2,1)}) custom-call(bf16[1024,1024]{1,0:T(8,128)(2,1)} %copy-done.80, bf16[1024,1024]{1,0:T(8,128)(2,1)} %copy-done.113, bf16[1024,1024]{1,0:T(8,128)(2,1)} %copy-done.79, ...), custom_call_target="tpu_custom_call" | custom-call | flops 34359738368 | bytes 54525952 | tf_op jit(solution)/shard_map/feed_backward/pallas_call | solution.py:297
  362.0 9.4 %multiply_reduce_fusion = (f32[1024]{0:T(1024)}, f32[1024]{0:T(1024)S(1)}, f32[1024]{0:T(1024)S(1)}, f32[1024]{0:T(1024)S(1)}, f32[1024,1024]{1,0:T(8,128)S(1)}, /*index=5*/bf16[1024,1024]{1,0:T(8,128)(2,1)}) fusion(f32[1024,1024]{1,0:T(8,128)} %copy-done.64, f32[1024]{0:T(1024)S(1)} %add_rsqrt_fusion.1, f32[1024]{0:T(1024)S(1)} %broadcast_multiply_fusion.4, ...), kind=kLoop, calls=%fused_computation.16 | loop fusion | flops 24113152 | bytes 23121920 | tf_op jit(solution)/shard_map/reduce_sum | solution.py:341
  381.3 67.2 %collective-permute-done.61 = bf16[4,2,64,2048]{3,2,1,0:T(8,128)(2,1)} collective-permute-done((bf16[4,2,64,2048]{3,2,1,0:T(8,128)(2,1)}, bf16[4,2,64,2048]{3,2,1,0:T(8,128)(2,1)}, u32[]{:S(2)}, u32[]{:S(2)}) %collective-permute-start.61) | collective-permute-done | bytes 2097184 | tf_op jit(solution)/shard_map/ppermute | solution.py:386
  482.5 15.4 %attend_backward.4 = (bf16[2,512,768]{2,1,0:T(8,128)(2,1)S(1)}, f32[2,128,1024]{2,1,0:T(8,128)S(1)}, bf16[2,128,1024]{2,1,0:T(8,128)(2,1)S(1)}, f32[2,128,1024]{...) custom-call(bf16[2,512,768]{2,1,0:T(8,128)(2,1)} %copy-done.62, ...), custom_call_target="tpu_custom_call" | custom-call | flops 6978797568 | bytes 11010048 | tf_op jit(solution)/shard_map/attend_backward/pallas_call | solution.py:153
  498.7 15.1 %attend_backward.5 = (bf16[2,512,768]{2,1,0:T(8,128)(2,1)S(1)}, f32[2,128,1024]{2,1,0:T(8,128)S(1)}, bf16[2,128,1024]{2,1,0:T(8,128)(2,1)S(1)}, f32[2,128,1024]{...) custom-call(bf16[2,512,768]{2,1,0:T(8,128)(2,1)} %copy-done.61, ...), custom_call_target="tpu_custom_call" | custom-call | flops 6978797568 | bytes 11010048 | tf_op jit(solution)/shard_map/attend_backward/pallas_call | solution.py:153
  531.2 10.4 %collective-permute-done.82 = bf16[2,64,2048]{2,1,0:T(8,128)(2,1)S(1)} collective-permute-done((bf16[2,64,2048]{2,1,0:T(8,128)(2,1)S(1)}, bf16[2,64,2048]{2,1,0:T(8,128)(2,1)S(1)}, u32[]{:S(2)}, u32[]{:S(2)}) %collective-permute-start.82) | collective-permute-done | bytes 524320 | tf_op jit(solution)/shard_map/ppermute | solution.py:434
  548.7 6.8 collective-permute-done.71
  588.9 15.6 %attend_backward.6 = (bf16[2,512,768]{2,1,0:T(8,128)(2,1)}, f32[2,128,1024]{2,1,0:T(8,128)S(1)}, bf16[2,128,1024]{2,1,0:T(8,128)(2,1)}, f32[2,128,1024]{2,1,0:T(...) custom-call(bf16[2,512,768]{2,1,0:T(8,128)(2,1)} %copy-done.63, bf16[2,128,256]{2,1,0:T(8,128)(2,1)S(1)} %bitcast.352, ...), custom_call_target="tpu_custom_call" | custom-call | flops 6978797568 | bytes 11010048 | tf_op jit(solution)/shard_map/attend_backward/pallas_call | solution.py:153
  634.4 14.7 %attend_backward.7 = (bf16[2,512,768]{2,1,0:T(8,128)(2,1)}, f32[2,128,1024]{2,1,0:T(8,128)S(1)}, bf16[2,128,1024]{2,1,0:T(8,128)(2,1)}, f32[2,128,1024]{2,1,0:T(...) custom-call(bf16[2,512,768]{2,1,0:T(8,128)(2,1)} %copy-done.60, ...), custom_call_target="tpu_custom_call" | custom-call | flops 6978797568 | bytes 11010048 | tf_op jit(solution)/shard_map/attend_backward/pallas_call | solution.py:153
  652.9 6.8 fusion.9
  669.8 11.6 %collective-permute-done.100 = f32[4,384]{1,0:T(4,128)S(1)} collective-permute-done((f32[4,384]{1,0:T(4,128)S(1)}, f32[4,384]{1,0:T(4,128)S(1)}, u32[]{:S(2)}, u32[]{:S(2)}) %collective-permute-start.100) | collective-permute-done | bytes 6176 | tf_op jit(solution)/shard_map/ppermute | solution.py:386
  (678 shorter events, 378.1 us)
Async XLA Ops:
  7.2 118.0 %all-gather.6.cloned.1.call-start = ((), (), s32[]{:S(2)}) async-start(), calls=%async_computation.4 | async-start | bytes 1990656 | tf_op jit(solution)/shard_map/all_gather | solution.py:474
  40.4 209.3 %all-gather.4.cloned.1.call-start = ((), (), s32[]{:S(2)}) async-start(), calls=%async_computation.2 | async-start | bytes 4456448 | tf_op jit(solution)/shard_map/all_gather | solution.py:495
  94.7 532.9 %reduce-scatter.2.cloned.1.call-start = ((), (), s32[]{:S(2)}) async-start(), calls=%async_computation.3 | async-start | bytes 4456448 | tf_op jit(solution)/shard_map/reduce_scatter | solution.py:560
  94.8 35.2 %collective-permute-start.13 = (bf16[2,2,64,2048]{3,2,1,0:T(8,128)(2,1)}, bf16[2,2,64,2048]{3,2,1,0:T(8,128)(2,1)}, u32[]{:S(2)}, u32[]{:S(2)}) collective-permute-start(bf16[2,2,64,2048]{3,2,1,0:T(8,128)(2,1)} %maximum_select_fusion.1), channel_id=1, source_target_pairs={{8,0},{16,8},{24,16},{9,1},{17,9},{25,17},{10,2},{18,10},{26,18},{... | collective-permute-start | bytes 3145736 | tf_op jit(solution)/shard_map/ppermute | solution.py:416
  117.9 31.6 %collective-permute-start.20 = (bf16[2,2,64,2048]{3,2,1,0:T(8,128)(2,1)}, bf16[2,2,64,2048]{3,2,1,0:T(8,128)(2,1)}, u32[]{:S(2)}, u32[]{:S(2)}) collective-permute-start(bf16[2,2,64,2048]{3,2,1,0:T(8,128)(2,1)} %collective-permute-done.12.refs_0_), channel_id=1, source_target_pairs={{0,8},{8,16},{16,24},{1,9},{9,17},{17,25},{2,10},{10,18},{18,26},{... | collective-permute-start | bytes 3145736 | tf_op jit(solution)/shard_map/ppermute | solution.py:415
  130.0 39.5 %collective-permute-start.21 = (bf16[2,2,64,2048]{3,2,1,0:T(8,128)(2,1)}, bf16[2,2,64,2048]{3,2,1,0:T(8,128)(2,1)}, u32[]{:S(2)}, u32[]{:S(2)}) collective-permute-start(bf16[2,2,64,2048]{3,2,1,0:T(8,128)(2,1)} %collective-permute-done.13.refs_1_), channel_id=1, source_target_pairs={{8,0},{16,8},{24,16},{9,1},{17,9},{25,17},{10,2},{18,10},{26,18},{... | collective-permute-start | bytes 3145736 | tf_op jit(solution)/shard_map/ppermute | solution.py:416
  147.9 34.6 %collective-permute-start.25 = (bf16[2,128,1024]{2,1,0:T(8,128)(2,1)}, bf16[2,128,1024]{2,1,0:T(8,128)(2,1)S(1)}, u32[]{:S(2)}, u32[]{:S(2)}) collective-permute-start(bf16[2,128,1024]{2,1,0:T(8,128)(2,1)} %copy-done.17), channel_id=1, source_target_pairs={{0,1},{1,0},{2,3},{3,2},{4,5},{5,4},{6,7},{7,6},{8,9},{9,8},{10,11... | collective-permute-start | bytes 1572872 | tf_op jit(solution)/shard_map/ppermute | solution.py:380
  147.9 36.1 %collective-permute-start.27 = (bf16[2,128,1024]{2,1,0:T(8,128)(2,1)}, bf16[2,128,1024]{2,1,0:T(8,128)(2,1)S(1)}, u32[]{:S(2)}, u32[]{:S(2)}) collective-permute-start(bf16[2,128,1024]{2,1,0:T(8,128)(2,1)} %collective-permute-done.26.t2), channel_id=1, source_target_pairs={{0,1},{1,0},{2,3},{3,2},{4,5},{5,4},{6,7},{7,6},{8,9},{9,8},{10,11... | collective-permute-start | bytes 1572872 | tf_op jit(solution)/shard_map/ppermute | solution.py:380
  149.6 49.9 %collective-permute-start.42 = (bf16[2,2,64,2048]{3,2,1,0:T(8,128)(2,1)}, bf16[2,2,64,2048]{3,2,1,0:T(8,128)(2,1)}, u32[]{:S(2)}, u32[]{:S(2)}) collective-permute-start(bf16[2,2,64,2048]{3,2,1,0:T(8,128)(2,1)} %collective-permute-done.20.refs_0_), channel_id=1, source_target_pairs={{0,8},{8,16},{16,24},{1,9},{9,17},{17,25},{2,10},{10,18},{18,26},{... | collective-permute-start | bytes 3145736 | tf_op jit(solution)/shard_map/ppermute | solution.py:415
  169.5 31.8 %collective-permute-start.39 = (bf16[2,128,1024]{2,1,0:T(8,128)(2,1)}, bf16[2,128,1024]{2,1,0:T(8,128)(2,1)}, u32[]{:S(2)}, u32[]{:S(2)}) collective-permute-start(bf16[2,128,1024]{2,1,0:T(8,128)(2,1)} %get-tuple-element.190.t0), channel_id=1, source_target_pairs={{0,1},{1,0},{2,3},{3,2},{4,5},{5,4},{6,7},{7,6},{8,9},{9,8},{10,11... | collective-permute-start | bytes 1572872 | tf_op jit(solution)/shard_map/ppermute | solution.py:380
  169.6 33.0 %collective-permute-start.41 = (bf16[2,128,1024]{2,1,0:T(8,128)(2,1)}, bf16[2,128,1024]{2,1,0:T(8,128)(2,1)}, u32[]{:S(2)}, u32[]{:S(2)}) collective-permute-start(bf16[2,128,1024]{2,1,0:T(8,128)(2,1)} %collective-permute-done.40.t2), channel_id=1, source_target_pairs={{0,1},{1,0},{2,3},{3,2},{4,5},{5,4},{6,7},{7,6},{8,9},{9,8},{10,11... | collective-permute-start | bytes 1572872 | tf_op jit(solution)/shard_map/ppermute | solution.py:380
  359.4 89.1 %collective-permute-start.61 = (bf16[4,2,64,2048]{3,2,1,0:T(8,128)(2,1)}, bf16[4,2,64,2048]{3,2,1,0:T(8,128)(2,1)}, u32[]{:S(2)}, u32[]{:S(2)}) collective-permute-start(bf16[4,2,64,2048]{3,2,1,0:T(8,128)(2,1)} %dynamic-slice_bitcast_fusion), channel_id=1, source_target_pairs={{0,4},{4,0},{1,5},{5,1},{2,6},{6,2},{3,7},{7,3},{8,12},{12,8},{9,1... | collective-permute-start | bytes 6291464 | tf_op jit(solution)/shard_map/ppermute | solution.py:386
  452.1 70.3 %collective-permute-start.69 = (bf16[2,64,2048]{2,1,0:T(8,128)(2,1)}, bf16[2,64,2048]{2,1,0:T(8,128)(2,1)}, u32[]{:S(2)}, u32[]{:S(2)}) collective-permute-start(bf16[2,64,2048]{2,1,0:T(8,128)(2,1)} %get-tuple-element.182), channel_id=1, source_target_pairs={{8,0},{16,8},{24,16},{9,1},{17,9},{25,17},{10,2},{18,10},{26,18},{... | collective-permute-start | bytes 1572872 | tf_op jit(solution)/shard_map/ppermute | solution.py:434
  453.3 77.4 %collective-permute-start.68 = (bf16[2,64,2048]{2,1,0:T(8,128)(2,1)}, bf16[2,64,2048]{2,1,0:T(8,128)(2,1)}, u32[]{:S(2)}, u32[]{:S(2)}) collective-permute-start(bf16[2,64,2048]{2,1,0:T(8,128)(2,1)} %get-tuple-element.183), channel_id=1, source_target_pairs={{0,8},{8,16},{16,24},{1,9},{9,17},{17,25},{2,10},{10,18},{18,26},{... | collective-permute-start | bytes 1572872 | tf_op jit(solution)/shard_map/ppermute | solution.py:433
  498.2 81.2 %collective-permute-start.65 = (bf16[2,128,256]{2,1,0:T(8,128)(2,1)}, bf16[2,128,256]{2,1,0:T(8,128)(2,1)}, u32[]{:S(2)}, u32[]{:S(2)}) collective-permute-start(bf16[2,128,256]{2,1,0:T(8,128)(2,1)} %bitcast.325), channel_id=1, source_target_pairs={{0,1},{1,0},{2,3},{3,2},{4,5},{5,4},{6,7},{7,6},{8,9},{9,8},{10,11... | collective-permute-start | bytes 393224 | tf_op jit(solution)/shard_map/ppermute | solution.py:377
  530.8 49.9 %collective-permute-start.66 = (bf16[2,128,256]{2,1,0:T(8,128)(2,1)S(1)}, bf16[2,128,256]{2,1,0:T(8,128)(2,1)S(1)}, u32[]{:S(2)}, u32[]{:S(2)}) collective-permute-start(bf16[2,128,256]{2,1,0:T(8,128)(2,1)S(1)} %bitcast.393), channel_id=1, source_target_pairs={{0,2},{1,3},{2,0},{3,1},{4,6},{5,7},{6,4},{7,5},{8,10},{9,11},{10,... | collective-permute-start | bytes 393224 | tf_op jit(solution)/shard_map/ppermute | solution.py:377
  572.8 52.9 %collective-permute-start.77 = (bf16[2,128,256]{2,1,0:T(8,128)(2,1)}, bf16[2,128,256]{2,1,0:T(8,128)(2,1)S(1)}, u32[]{:S(2)}, u32[]{:S(2)}) collective-permute-start(bf16[2,128,256]{2,1,0:T(8,128)(2,1)} %bitcast.321), channel_id=1, source_target_pairs={{0,1},{1,0},{2,3},{3,2},{4,5},{5,4},{6,7},{7,6},{8,9},{9,8},{10,11... | collective-permute-start | bytes 393224 | tf_op jit(solution)/shard_map/ppermute | solution.py:377
  578.2 48.0 %collective-permute-start.78 = (bf16[2,128,256]{2,1,0:T(8,128)(2,1)}, bf16[2,128,256]{2,1,0:T(8,128)(2,1)S(1)}, u32[]{:S(2)}, u32[]{:S(2)}) collective-permute-start(bf16[2,128,256]{2,1,0:T(8,128)(2,1)} %bitcast.320), channel_id=1, source_target_pairs={{0,2},{1,3},{2,0},{3,1},{4,6},{5,7},{6,4},{7,5},{8,10},{9,11},{10,... | collective-permute-start | bytes 393224 | tf_op jit(solution)/shard_map/ppermute | solution.py:377
  622.6 42.2 %collective-permute-start.75 = (bf16[2,128,1024]{2,1,0:T(8,128)(2,1)}, bf16[2,128,1024]{2,1,0:T(8,128)(2,1)}, u32[]{:S(2)}, u32[]{:S(2)}) collective-permute-start(bf16[2,128,1024]{2,1,0:T(8,128)(2,1)} %get-tuple-element.109), channel_id=1, source_target_pairs={{0,1},{1,0},{2,3},{3,2},{4,5},{5,4},{6,7},{7,6},{8,9},{9,8},{10,11... | collective-permute-start | bytes 1572872 | tf_op jit(solution)/shard_map/ppermute | solution.py:380
  623.3 79.5 %collective-permute-start.74 = (bf16[2,128,1024]{2,1,0:T(8,128)(2,1)}, bf16[2,128,1024]{2,1,0:T(8,128)(2,1)}, u32[]{:S(2)}, u32[]{:S(2)}) collective-permute-start(bf16[2,128,1024]{2,1,0:T(8,128)(2,1)} %get-tuple-element.107), channel_id=1, source_target_pairs={{0,1},{1,0},{2,3},{3,2},{4,5},{5,4},{6,7},{7,6},{8,9},{9,8},{10,11... | collective-permute-start | bytes 1572872 | tf_op jit(solution)/shard_map/ppermute | solution.py:380
  626.3 42.3 %collective-permute-start.109 = (f32[32,2048]{1,0:T(8,128)}, f32[32,2048]{1,0:T(8,128)}, u32[]{:S(2)}, u32[]{:S(2)}) collective-permute-start(f32[32,2048]{1,0:T(8,128)} %get-tuple-element.197), channel_id=1, source_target_pairs={{0,1},{1,0},{2,3},{3,2},{4,5},{5,4},{6,7},{7,6},{8,9},{9,8},{10,11... | collective-permute-start | bytes 786440 | tf_op jit(solution)/shard_map/ppermute | solution.py:380
  661.8 34.8 %collective-permute-start.91 = (bf16[4,128,768]{2,1,0:T(8,128)(2,1)}, bf16[4,128,768]{2,1,0:T(8,128)(2,1)}, u32[]{:S(2)}, u32[]{:S(2)}) collective-permute-start(bf16[4,128,768]{2,1,0:T(8,128)(2,1)} %dynamic-slice_bitcast_fusion.1), channel_id=1, source_target_pairs={{0,4},{4,0},{1,5},{5,1},{2,6},{6,2},{3,7},{7,3},{8,12},{12,8},{9,1... | collective-permute-start | bytes 2359304 | tf_op jit(solution)/shard_map/ppermute | solution.py:386
  666.8 36.0 %collective-permute-start.76 = (bf16[2,128,1024]{2,1,0:T(8,128)(2,1)}, bf16[2,128,1024]{2,1,0:T(8,128)(2,1)}, u32[]{:S(2)}, u32[]{:S(2)}) collective-permute-start(bf16[2,128,1024]{2,1,0:T(8,128)(2,1)} %add_convert_fusion.2), channel_id=1, source_target_pairs={{0,2},{1,3},{2,0},{3,1},{4,6},{5,7},{6,4},{7,5},{8,10},{9,11},{10,... | collective-permute-start | bytes 1572872 | tf_op jit(solution)/shard_map/ppermute | solution.py:377
  705.6 37.8 %collective-permute-start.88 = (bf16[2,128,1024]{2,1,0:T(8,128)(2,1)}, bf16[2,128,1024]{2,1,0:T(8,128)(2,1)}, u32[]{:S(2)}, u32[]{:S(2)}) collective-permute-start(bf16[2,128,1024]{2,1,0:T(8,128)(2,1)} %get-tuple-element.113), channel_id=1, source_target_pairs={{0,1},{1,0},{2,3},{3,2},{4,5},{5,4},{6,7},{7,6},{8,9},{9,8},{10,11... | collective-permute-start | bytes 1572872 | tf_op jit(solution)/shard_map/ppermute | solution.py:380
  (205 other events, 3087.6 us)
Sparse Core Ops, SparseCore 0:
  40.5 53.3 all-gather.5
  96.7 101.5 all-gather.3
  361.5 92.1 reduce-scatter.1

commit v3 on v2

--- a/solution.py
+++ b/solution.py
@@ -10,7 +10,8 @@
 
 HEADS = 16
 HEAD_DIM = 64
-CHUNKS = 4
+CHUNKS = 2
+PIECE = 256
 MIB = 1 << 20
 CHIPS = ("z", "y", "x")
 SEQ = ("z", "y")
@@ -71,14 +72,15 @@
         out[0] = mixed[index * part : (index + 1) * part]
 
 
-def attend(tokens, weight, bias, seg_key, seg_query, after):
+def attend(tokens, weight, bias, seg_key, seg_query, first, after):
     count, part, depth = tokens[0].shape
+    count = count // CHUNKS
     wide = weight.shape[1]
     length = 4 * part
     return pl.pallas_call(
         functools.partial(attend_kernel, len(after)),
         grid=(count,),
-        in_specs=[by_row((1, part, depth))] * 4
+        in_specs=[pl.BlockSpec((1, part, depth), lambda i: (i + first, 0, 0))] * 4
         + [
             resident((depth, wide)),
             resident((1, wide)),
@@ -181,6 +183,26 @@
     return pl.BlockSpec(shape, lambda i: (0, i))
 
 
+def flat(block):
+    wide = block.shape[-1]
+    if block.shape[-2] % 16:
+        return block.astype(F32).reshape(-1, wide).astype(BF16)
+    return block.reshape(-1, wide)
+
+
+def expand_piece(ref):
+    return jnp.concatenate([flat(ref[:, i]) for i in range(ref.shape[1])], axis=1)
+
+
+def reduce_piece(ref):
+    columns = ref.shape[1] // 2
+    halves = [
+        jnp.concatenate([ref[:, half * columns + i] for i in range(columns)], axis=2)
+        for half in range(2)
+    ]
+    return flat(jnp.concatenate(halves, axis=1))
+
+
 def feed_kernel(block, own, other, expand, bias, reduce, act, slope, own_out, other_out, far_sum):
     step = pl.program_id(0)
     rows = own.shape[0]
@@ -190,40 +212,54 @@
         own_out[...] = jnp.zeros_like(own_out)
         far_sum[...] = jnp.zeros_like(far_sum)
 
-    for source, total, start in ((own, own_out, 0), (other, far_sum, rows)):
-        for index in range(rows // block):
-            at = slice(index * block, (index + 1) * block)
-            to = slice(start + index * block, start + (index + 1) * block)
-            inside = dot(source[at], expand[...]) + bias[...]
-            square = inside * inside
-            curve = jnp.tanh(0.7978845608028654 * inside * (1.0 + 0.044715 * square))
-            half = 0.5 * (1.0 + curve)
-            active = (inside * half).astype(BF16)
-            act[to] = active
-            slope[to] = (
-                half
-                + 0.5
-                * inside
-                * (1.0 - curve * curve)
-                * (0.7978845608028654 * (1.0 + 3 * 0.044715 * square))
-            ).astype(BF16)
-            total[at] += dot(active, reduce[...])
+    into = expand_piece(expand)
+    back = reduce_piece(reduce)
+    work = [
+        (source, total, slice(i * block, (i + 1) * block), slice(start + i * block, start + (i + 1) * block))
+        for source, total, start in ((own, own_out, 0), (other, far_sum, rows))
+        for i in range(rows // block)
+    ]
+    ahead = dot(work[0][0][work[0][2]], into) + bias[...]
+    for index, (_, total, at, to) in enumerate(work):
+        inside = ahead
+        if index + 1 < len(work):
+            ahead = dot(work[index + 1][0][work[index + 1][2]], into) + bias[...]
+        square = inside * inside
+        curve = jnp.tanh(inside * (0.7978845608028654 + 0.7978845608028654 * 0.044715 * square))
+        half = 0.5 * curve + 0.5
+        active = (inside * half).astype(BF16)
+        act[to] = active
+        tilt = 0.7978845608028654 * 0.5 + 0.7978845608028654 * 1.5 * 0.044715 * square
+        slope[to] = (half + inside * (1.0 - curve * curve) * tilt).astype(BF16)
+        total[at] += dot(active, back)
 
     @pl.when(step == pl.num_programs(0) - 1)
     def _():
         other_out[...] = far_sum[...].astype(BF16)
 
 
-def feed(own, other, expand, bias, reduce):
+def feed_weights(weights, pieces, columns):
+    chips, _, rows, _ = weights.shape
+    return [
+        pl.BlockSpec((chips, pieces, rows, PIECE), lambda i: (0, i, 0, 0)),
+        pl.BlockSpec(
+            (pieces * PIECE // (2 * rows), 2 * columns, rows, PIECE), lambda i: (i, 1, 0, 0)
+        ),
+    ]
+
+
+def feed(own, other, weights, bias):
     rows, depth = own.shape
-    hidden = expand.shape[1]
-    piece = 512
+    hidden = bias.shape[1]
+    pieces = 2
+    wide = pieces * PIECE
+    expand_spec, reduce_spec = feed_weights(weights, pieces, depth // PIECE)
     return pl.pallas_call(
         functools.partial(feed_kernel, 512),
-        grid=(hidden // piece,),
+        grid=(hidden // wide,),
         in_specs=[resident((rows, depth))] * 2
-        + [column((depth, piece)), column((1, piece)), by_row((piece, depth))],
-        out_specs=[column((2 * rows, piece))] * 2 + [resident((rows, depth))] * 2,
+        + [expand_spec, column((1, wide)), reduce_spec],
+        out_specs=[column((2 * rows, wide))] * 2 + [resident((rows, depth))] * 2,
         out_shape=[jax.ShapeDtypeStruct((2 * rows, hidden), BF16)] * 2
         + [
             jax.ShapeDtypeStruct((rows, depth), F32),
@@ -237,7 +273,7 @@
             transcendentals=2 * rows * hidden,
         ),
         name="feed_forward",
-    )(own, other, expand, bias, reduce)
+    )(own, other, weights, bias, weights)
 
 
 def feed_back_kernel(
@@ -250,8 +286,7 @@
     slope,
     expand,
     reduce,
-    expand_grad,
-    reduce_grad,
+    weight_grad,
     bias_grad,
     own_out,
     other_out,
@@ -266,56 +301,67 @@
         own_out[...] = jnp.zeros_like(own_out)
         far_sum[...] = jnp.zeros_like(far_sum)
 
+    into = expand_piece(expand)
+    back = reduce_piece(reduce)
     bias_sum = jnp.zeros(bias_grad.shape, F32)
     for source, total, start in ((own_grad, own_out, 0), (other_grad, far_sum, rows)):
         for index in range(rows // block):
             at = slice(index * block, (index + 1) * block)
             to = slice(start + index * block, start + (index + 1) * block)
-            grad_act = dot(source[at], reduce[...], (1, 1))
+            grad_act = dot(source[at], back, (1, 1))
             part = (grad_act * slope[to].astype(F32)).astype(BF16)
             inside[to] = part
             bias_sum += jnp.sum(part.astype(F32), axis=0, keepdims=True)
-            total[at] += dot(part, expand[...], (1, 1))
+            total[at] += dot(part, into, (1, 1))
     bias_grad[...] = bias_sum
-    reduce_grad[...] = (
-        dot(act[:rows], own_grad[...], (0, 0)) + dot(act[rows:], other_grad[...], (0, 0))
-    ).astype(BF16)
+    chips, pieces, height, _ = weight_grad.shape
+    columns = pieces // 4
+    reduce_grad = dot(act[:rows], own_grad[...], (0, 0)) + dot(act[rows:], other_grad[...], (0, 0))
+    count = PIECE // (2 * height)
+    reduce_grad = reduce_grad.reshape(count, 2 * height, reduce_grad.shape[1]).astype(BF16)
+    mine = pl.ds(step * count, count)
+    for half in range(2):
+        for i in range(columns):
+            weight_grad[mine, (2 + half) * columns + i] = reduce_grad[
+                :, half * height : (half + 1) * height, i * PIECE : (i + 1) * PIECE
+            ]
     flipped = dot(inside[:rows], own_rows[...], (0, 0)) + dot(
         inside[rows:], other_rows[...], (0, 0)
     )
-    expand_grad[...] = jnp.transpose(flipped).astype(BF16)
+    expand_grad = jnp.transpose(flipped).reshape(chips, height, PIECE).astype(BF16)
+    weight_grad[:, step] = expand_grad
 
     @pl.when(step == pl.num_programs(0) - 1)
     def _():
         other_out[...] = far_sum[...].astype(BF16)
 
 
-def feed_back(own_grad, other_grad, own_rows, other_rows, act, slope, expand, reduce):
+def feed_back(own_grad, other_grad, own_rows, other_rows, act, slope, weights):
     rows, depth = own_grad.shape
-    hidden = expand.shape[1]
-    piece = 256
+    hidden = act.shape[1]
+    chips, _, height, _ = weights.shape
+    pieces = 2 * hidden // PIECE
+    expand_spec, reduce_spec = feed_weights(weights, 1, depth // PIECE)
     return pl.pallas_call(
         functools.partial(feed_back_kernel, 512),
-        grid=(hidden // piece,),
+        grid=(hidden // PIECE,),
         in_specs=[resident((rows, depth))] * 4
-        + [column((2 * rows, piece))] * 2
-        + [column((depth, piece)), by_row((piece, depth))],
+        + [column((2 * rows, PIECE))] * 2
+        + [expand_spec, reduce_spec],
         out_specs=[
-            column((depth, piece)),
-            by_row((piece, depth)),
-            column((1, piece)),
+            resident((chips, pieces, height, PIECE)),
+            column((1, PIECE)),
         ]
         + [resident((rows, depth))] * 2,
         out_shape=[
-            jax.ShapeDtypeStruct((depth, hidden), BF16),
-            jax.ShapeDtypeStruct((hidden, depth), BF16),
+            jax.ShapeDtypeStruct((chips, pieces, height, PIECE), BF16),
             jax.ShapeDtypeStruct((1, hidden), F32),
             jax.ShapeDtypeStruct((rows, depth), F32),
             jax.ShapeDtypeStruct((rows, depth), BF16),
         ],
         scratch_shapes=[
             pltpu.VMEM((rows, depth), F32),
-            pltpu.VMEM((2 * rows, piece), BF16),
+            pltpu.VMEM((2 * rows, PIECE), BF16),
         ],
         compiler_params=pltpu.CompilerParams(vmem_limit_bytes=56 * MIB),
         cost_estimate=pl.CostEstimate(
@@ -324,7 +370,7 @@
             transcendentals=0,
         ),
         name="feed_backward",
-    )(own_grad, other_grad, own_rows, other_rows, act, slope, expand, reduce)
+    )(own_grad, other_grad, own_rows, other_rows, act, slope, weights, weights)
 
 
 def normalize(values):
@@ -382,65 +428,44 @@
     def chosen(array, index, axis):
         return lax.dynamic_index_in_dim(array, index, axis, keepdims=False)
 
-    def trade(array, name):
-        return lax.ppermute(array, name, [(0, 1), (1, 0)])
-
-    def pair(own, other, axis, name):
+    def pair(own, other, axis, low):
         return jnp.where(
-            lax.axis_index(name) == 0,
-            jnp.stack([own, other], axis=axis),
-            jnp.stack([other, own], axis=axis),
+            low, jnp.stack([own, other], axis=axis), jnp.stack([other, own], axis=axis)
         )
 
     def by_core(own, other, axis):
-        return pair(own, other, axis, "c")
-
-    def halve(array, axis, name):
-        me = lax.axis_index(name)
+        return pair(own, other, axis, low_core)
+
+    def bit_of(name, step):
+        return (lax.axis_index(name) // step) % 2
+
+    def trade(array, name, step=1):
+        return lax.ppermute(array, name, [(i, i ^ step) for i in range(sizes[name])])
+
+    def widen(array, name, axis=0, step=1):
+        return pair(array, trade(array, name, step), axis, bit_of(name, step) == 0)
+
+    def halve(array, axis, name, step=1):
+        me = bit_of(name, step)
         return chosen(array, me, axis).astype(F32) + trade(
-            chosen(array, 1 - me, axis), name
+            chosen(array, 1 - me, axis), name, step
         ).astype(F32)
 
-    last = sizes["z"] - 1
-    up = [(i, i + 1) for i in range(last)]
-    down = [(i + 1, i) for i in range(last)]
-    height = lax.axis_index("z")
-
-    def chain_gather(block):
-        if last > 3:
-            return lax.all_gather(block, "z"), [[block]] * 3
-        below, above, steps = [], [], []
-        low_block, high_block = block, block
-        for _ in range(last):
-            low_block = lax.ppermute(low_block, "z", up)
-            high_block = lax.ppermute(high_block, "z", down)
-            below.append(low_block)
-            above.append(high_block)
-            steps.append([low_block, high_block])
-        line = jnp.stack(below[::-1] + [block] + above)
-        return lax.dynamic_slice_in_dim(line, last - height, last + 1, 0), steps
-
-    def chain_scatter(blocks, kind=BF16):
-        if last > 3:
-            return lax.psum_scatter(blocks, "z").astype(F32), [[blocks]] * 3
-        low_sum, high_sum, steps = None, None, []
-        for step in range(last):
-            low_send = chosen(blocks, jnp.minimum(last - step + height, last), 0)
-            high_send = chosen(blocks, jnp.maximum(height - last + step, 0), 0)
-            if step:
-                low_send = (low_send.astype(F32) + low_sum.astype(F32)).astype(kind)
-                high_send = (high_send.astype(F32) + high_sum.astype(F32)).astype(kind)
-            low_sum = lax.ppermute(low_send, "z", up)
-            high_sum = lax.ppermute(high_send, "z", down)
-            steps.append([low_sum, high_sum])
-        own = chosen(blocks, height, 0).astype(F32)
-        return own + low_sum.astype(F32) + high_sum.astype(F32), steps
-
-    pieces = [tokens[i * seq_count // CHUNKS : (i + 1) * seq_count // CHUNKS] for i in range(CHUNKS)]
-    gathered = []
-    for piece in pieces:
-        across = hop(piece, 2)
-        gathered.append((piece, swap(piece), across, swap(across)))
+    z_steps = [1 << i for i in range(sizes["z"].bit_length() - 1)]
+
+    def z_gather(array):
+        for index, step in enumerate(z_steps[::-1]):
+            array = widen(array, "z", index, step)
+        return array
+
+    def z_scatter(blocks, kind=BF16):
+        for step in z_steps:
+            blocks = blocks.reshape((blocks.shape[0] // 2, 2) + blocks.shape[1:])
+            blocks = halve(blocks.astype(kind), 1, "z", step)
+        return blocks[0]
+
+    across = hop(tokens, 2)
+    gathered = (tokens, swap(tokens), across, swap(across))
     seg_parts = segment_ids.reshape(seq_count, ctx_size, part)
     seg = jnp.concatenate([chosen(seg_parts, place ^ r, 1) for r in range(ctx_size)], axis=1)
     seg_key = seg[:, :, None]
@@ -460,18 +485,21 @@
     vector_count = 8 * share + expand_bias.shape[0]
     blocks = project_weight.reshape(share, 3, ctx_size, lanes)
     own_vectors = jnp.concatenate(vectors)
-    columns_of = [chosen(blocks, place ^ r, 2) for r in range(ctx_size)]
-    weights_from = [columns_of[0]] + [hop(columns_of[r], r) for r in (1, 2, 3)]
-    vectors_from = [own_vectors] + [hop(own_vectors, r) for r in (1, 2, 3)]
-    weights_from = jnp.stack(weights_from).reshape(ctx_size, share, 3 * lanes)
-    mine = jnp.concatenate([chosen(weights_from, place ^ r, 0) for r in range(ctx_size)], axis=0)
-    vectors_from = jnp.stack(vectors_from)
-    vectors_from = jnp.stack([chosen(vectors_from, place ^ r, 0) for r in range(ctx_size)])
     below = 16 * -(-ctx_size * vector_count // (48 * lanes))
+    held = jnp.concatenate(
+        [
+            jnp.moveaxis(blocks, 2, 0).reshape(ctx_size, -1),
+            jnp.broadcast_to(own_vectors, (ctx_size, vector_count)),
+        ],
+        axis=1,
+    )
+    held = lax.all_to_all(held, CTX, 0, 0, tiled=True)
+    mine = held[:, : share * 3 * lanes].reshape(ctx_size * share, 3 * lanes)
     vector_rows = jnp.pad(
-        vectors_from.reshape(-1), (0, below * 3 * lanes - ctx_size * vector_count)
+        held[:, share * 3 * lanes :].reshape(-1),
+        (0, below * 3 * lanes - ctx_size * vector_count),
     ).reshape(below, 3 * lanes)
-    whole_project = lax.all_gather(jnp.concatenate([mine, vector_rows]), SEQ, axis=0)
+    whole_project = z_gather(widen(jnp.concatenate([mine, vector_rows]), "y"))
     whole_project = whole_project.reshape(-1, ctx_size * share + below, 3 * lanes)
     full_project = whole_project[:, : ctx_size * share].reshape(width, 3 * lanes)
     packed = (
@@ -492,19 +520,34 @@
         ]
     )[None]
 
-    full_reduce = lax.all_gather(reduce_weight, CHIPS, axis=0, tiled=True)
     columns = expand_weight.reshape(share, chips, 2, own_hidden // chips)
     own_columns = chosen(columns, core, 2).reshape(share, own_hidden)
     far_columns = chosen(columns, 1 - core, 2).reshape(share, own_hidden)
-    both = by_core(own_columns, swap(far_columns), 0).reshape(2 * share, own_hidden)
-    both = pair(both, trade(both, "x"), 0, "x")
-    both = pair(both, trade(both, "y"), 0, "y")
-    full_expand, expand_steps = chain_gather(both)
-    full_expand = full_expand.reshape(width, own_hidden)
-
-    quarter = pair(output_weight, trade(output_weight, "x"), 0, "x")
-    quarter, output_steps = chain_gather(quarter)
-    out_half = pair(quarter, trade(quarter, "y"), 1, "y").reshape(chips, share, width)
+    both = by_core(own_columns, swap(far_columns), 0)
+
+    def in_pieces(array):
+        rows_of, wide = array.shape
+        return jnp.swapaxes(array.reshape(rows_of, wide // PIECE, PIECE), 0, 1).reshape(
+            -1, 2 * share, PIECE
+        )
+
+    weights = lax.all_gather(
+        jnp.concatenate(
+            [
+                in_pieces(both.reshape(2 * share, own_hidden)),
+                jnp.swapaxes(
+                    reduce_weight.reshape(2, 2 * share, width // PIECE, PIECE), 1, 2
+                ).reshape(-1, 2 * share, PIECE),
+                in_pieces(output_weight),
+            ]
+        ),
+        CHIPS,
+        axis=0,
+    ).reshape(chips, -1, 2 * share, PIECE)
+    feed_pieces = (own_hidden + 2 * width) // PIECE
+    out_half = jnp.swapaxes(
+        weights[:, feed_pieces:].reshape(chips, width // PIECE, share, PIECE), 1, 2
+    ).reshape(chips, share, width)
     full_output = by_core(out_half, swap(out_half), 1).reshape(ctx_size, lanes, width)
     full_output = jnp.concatenate(
         [chosen(full_output, place ^ r, 0) for r in range(ctx_size)], axis=0
@@ -516,12 +559,7 @@
     for index in range(CHUNKS):
         at = slice(index * seq_count // CHUNKS, (index + 1) * seq_count // CHUNKS)
         *mixed, all_rows, kept = attend(
-            gathered[index],
-            full_project,
-            bias_all,
-            seg_key[at],
-            seg_query[at],
-            (expand_steps[0], expand_steps[1], [out_half], expand_steps[2])[index],
+            gathered, full_project, bias_all, seg_key[at], seg_query[at], at.start, []
         )
         kept_rows.append(all_rows.reshape(-1, width))
         saved.append(kept)
@@ -536,7 +574,7 @@
     first = scaled_one * gain_one + shift_one
     first_low = first.astype(BF16)
     first_far = swap(first_low)
-    act, slope, own_sum, far_sum = feed(first_low, first_far, full_expand, exp_bias, full_reduce)
+    act, slope, own_sum, far_sum = feed(first_low, first_far, weights, exp_bias)
     reduced = own_sum + swap(far_sum).astype(F32) + red_bias
     scaled_two, inverse_two = normalize(first + reduced)
     layer_work = (scaled_two * gain_two + shift_two).astype(BF16).reshape(tokens.shape)
@@ -547,20 +585,10 @@
     )
     grad_reduced = grad_second.astype(BF16)
     reduce_bias_grad = jnp.sum(grad_reduced.astype(F32), axis=0)
-    expand_grad, reduce_grad, expand_bias_grad, own_back, far_back = feed_back(
-        grad_reduced,
-        swap(grad_reduced),
-        first_low,
-        first_far,
-        act,
-        slope,
-        full_expand,
-        full_reduce,
-    )
-    reduce_owned = lax.psum_scatter(reduce_grad, CHIPS, scatter_dimension=0, tiled=True)
-    expand_grad = expand_grad.reshape(sizes["z"], 2, sizes["x"], 2 * share, own_hidden)
-    expand_half = halve(expand_grad, 1, "y").astype(BF16)
-    expand_line, expand_steps = chain_scatter(expand_half)
+    weight_grad, expand_bias_grad, own_back, far_back = feed_back(
+        grad_reduced, swap(grad_reduced), first_low, first_far, act, slope, weights
+    )
+    weight_owned = lax.psum_scatter(weight_grad, CHIPS, scatter_dimension=0, tiled=True)[0]
     grad_first = grad_second + own_back + swap(far_back).astype(F32)
     grad_hidden, grad_gain_one, grad_shift_one = normalize_back(
         grad_first, scaled_one, inverse_one, gain_one
@@ -575,9 +603,10 @@
     output_grad = jnp.concatenate(
         [chosen(output_grad, place ^ r, 0) for r in range(ctx_size)], axis=0
     ).reshape(sizes["z"], 2, sizes["x"], 2, share, width)
-    output_half = halve(output_grad, 3, "c").astype(BF16)
-    output_half = halve(output_half, 1, "y").astype(BF16)
-    output_line, output_steps = chain_scatter(output_half)
+    output_grad = halve(output_grad, 3, "c").astype(BF16)
+    output_grad = halve(output_grad, 2, "x").astype(BF16)
+    output_grad = halve(output_grad, 1, "y")
+    output_owned = z_scatter(output_grad)
 
     project_parts = []
     work_parts = []
@@ -591,12 +620,7 @@
             full_project,
             seg_key[at],
             seg_query[at],
-            (
-                [],
-                [expand_half],
-                expand_steps[0] + output_steps[0] + work_parts[:1],
-                expand_steps[2] + output_steps[2] + work_parts[1:2] + [reduce_owned],
-            )[index],
+            [],
         )
         across = r2 + swap(r3).astype(F32)
         work_parts.append(
@@ -613,23 +637,26 @@
         for all_rows, grad_part in zip(kept_rows, project_parts)
     )
     grad_work = jnp.concatenate(work_parts, axis=0)
-    project_owned, _ = chain_scatter(
+    project_owned = z_scatter(
         halve(
             project_grad.astype(BF16).reshape(sizes["z"], 2, ctx_size * share, 3 * lanes), 1, "y"
-        ).astype(BF16)
+        )
     )
     project_owned = lax.all_to_all(
         project_owned.reshape(ctx_size, share, 3, lanes), CTX, 0, 2, tiled=False
     ).reshape(share, 3 * width)
-    expand_owned = halve(expand_line.astype(BF16), 0, "x")
-    output_owned = halve(output_line.astype(BF16), 0, "x")
-
-    far_rows = expand_owned.reshape(2, share, own_hidden)
+    expand_pieces = own_hidden // PIECE
+    far_rows = jnp.swapaxes(
+        weight_owned[:expand_pieces].reshape(expand_pieces, 2, share, PIECE), 0, 1
+    )
     expand_owned = by_core(
-        chosen(far_rows, core, 0).reshape(share, chips, -1),
-        swap(chosen(far_rows, 1 - core, 0)).reshape(share, chips, -1),
+        jnp.swapaxes(chosen(far_rows, core, 0), 0, 1).reshape(share, chips, -1),
+        jnp.swapaxes(swap(chosen(far_rows, 1 - core, 0)), 0, 1).reshape(share, chips, -1),
         2,
     ).reshape(share, hidden)
+    reduce_owned = jnp.swapaxes(
+        weight_owned[expand_pieces:].reshape(2, width // PIECE, 2 * share, PIECE), 1, 2
+    ).reshape(4 * share, width)
 
     column_sums = jnp.sum(jnp.concatenate(sum_parts, axis=0), axis=(0, 1))
     zeros = jnp.zeros((width,), F32)
@@ -657,7 +684,7 @@
     packed_grads = packed_grads.reshape(sizes["z"], 2, sizes["x"], 2, vector_count)
     for axis, name in ((3, "c"), (2, "x"), (1, "y")):
         packed_grads = halve(packed_grads, axis, name)
-    owned, _ = chain_scatter(packed_grads, F32)
+    owned = z_scatter(packed_grads, F32)
     small = [owned[i * share : (i + 1) * share] for i in range(8)]
     return (
         layer_work,

time: 769 us -> 660 us (0.86)
  starting transfers between devices: 149 us -> 41.1 us
  blocking collectives: 0 us -> 67.3 us
  local copies, waits for them, and re-layouts: 104 us -> 72 us
  other arithmetic: 63.8 us -> 50.6 us
  Pallas kernels: 178 us -> 169 us
  waiting for transfers between devices: 220 us -> 212 us
    ppermute x49 -> x16, starting transfers between devices: 113 us -> 20.2 us  [trade(): lax.ppermute(array, name, [(i, i ^ step) for i in range(sizes[name])])]
    all_to_all x0 -> x1, blocking collectives: none -> 67.3 us  [on_device(): held = lax.all_to_all(held, CTX, 0, 0, tiled=True)]
    ppermute x49 -> x16, waiting for transfers between devices: 178 us -> 148 us  [trade(): lax.ppermute(array, name, [(i, i ^ step) for i in range(sizes[name])])]
    unnamed x266 -> x116, local copies, waits for them, and re-layouts: 41.1 us -> 21.7 us
    all_to_all x1, waiting for transfers between devices: 3.02 us -> 21.2 us  [on_device(): lax.all_to_all(project_owned.reshape(ctx_size, share, 3, lanes), CTX, 0,...]
    ppermute x38 -> x15, starting transfers between devices: 27.8 us -> 12.6 us  [hop(): return lax.ppermute(array, CTX, [(i, i ^ step) for i in range(ctx_size)])]
    pallas_call x4 -> x2, Pallas kernels: 60.9 us -> 55.3 us  [attend_back(): pl.pallas_call(functools.partial(attend_back_kernel, len(after)), grid=(c...]
    dot_general x7 -> x5, matrix products: 27.7 us -> 26.4 us  [dot(): lax.dot_general(left, right, (((contract[0],), (contract[1],)), ((), ()))...]
  transfers between devices with their start and end apart: 114 -> 47, of which waited for: 41 -> 20; matrix products, arithmetic and copies ran while one was open for 20% -> 17% of each run, Pallas kernels for 12% -> 13%
where the time goes in v3:
time: 660 us; the launch traced here: 655 us
  waiting for transfers between devices  212 us (32%)
  Pallas kernels  169 us (26%)
  local copies, waits for them, and re-layouts  72 us (11%)
  blocking collectives  67.3 us (10%)
  other arithmetic  50.6 us (8%)
  starting transfers between devices  41.1 us (6%)
  matrix products  26.4 us (4%)
  between operations  16.1 us (2%)
    ppermute x16, waiting for transfers between devices, trade(): lax.ppermute(array, name, [(i, i ^ step) for i in range(sizes[name])])  148 us
    all_to_all x1, blocking collectives, on_device(): held = lax.all_to_all(held, CTX, 0, 0, tiled=True)  67.3 us
    pallas_call x2, Pallas kernels, attend_back(): pl.pallas_call(functools.partial(attend_back_kernel, len(after)), grid=(c...  55.3 us
    pallas_call x1, Pallas kernels, feed_back(): pl.pallas_call(functools.partial(feed_back_kernel, 512), grid=(hidden //...  51.9 us
    pallas_call x2, Pallas kernels, attend(): pl.pallas_call(functools.partial(attend_kernel, len(after)), grid=(count,...  32 us
    ppermute x15, waiting for transfers between devices, hop(): return lax.ppermute(array, CTX, [(i, i ^ step) for i in range(ctx_size)])  31.2 us
    pallas_call x1, Pallas kernels, feed(): pl.pallas_call(functools.partial(feed_kernel, 512), grid=(hidden // wide,...  30.2 us
    dot_general x5, matrix products, dot(): lax.dot_general(left, right, (((contract[0],), (contract[1],)), ((), ()))...  26.4 us
  transfers between devices with their start and end apart: 47, of which 20 were waited for; matrix products, arithmetic and copies ran while one was open for 17% of the time, Pallas kernels for 13%

profile of v3, /device:TPU:0, one launch (start us, length us, event | category | flops | bytes accessed | tf_op | source)
XLA Modules:
  0.0 654.9 jit_solution(11014991854121973114)
XLA Ops:
  19.2 67.3 %all_to_all.27 = bf16[4,2,12480]{2,1,0:T(2,128)(2,1)S(1)} all-to-all(bf16[4,2,12480]{2,1,0:T(2,128)(2,1)S(1)} %reshape.541), channel_id=1, replica_groups=mesh['z'=4,'y'=2,'x'=2,'c'=2] {'x','c'}, dimensions={0} | all-to-all | bytes 399360 | tf_op jit(solution)/shard_map/all_to_all | solution.py:496
  89.0 5.3 collective-permute-done.3
  97.9 45.4 %collective-permute-done.4 = bf16[2,144,768]{2,1,0:T(8,128)(2,1)S(1)} collective-permute-done((bf16[2,144,768]{2,1,0:T(8,128)(2,1)S(1)}, bf16[2,144,768]{2,1,0:T(8,128)(2,1)S(1)}, u32[]{:S(2)}, u32[]{:S(2)}) %collective-permute-start.4) | collective-permute-done | bytes 442400 | tf_op jit(solution)/shard_map/ppermute | solution.py:443
  146.4 40.1 %collective-permute-done.5 = bf16[2,2,144,768]{3,2,1,0:T(8,128)(2,1)} collective-permute-done((bf16[2,2,144,768]{3,2,1,0:T(8,128)(2,1)}, bf16[2,2,144,768]{3,2,1,0:T(8,128)(2,1)}, u32[]{:S(2)}, u32[]{:S(2)}) %collective-permute-start.5) | collective-permute-done | bytes 884768 | tf_op jit(solution)/shard_map/ppermute | solution.py:443
  190.9 16.2 %attend_forward.2 = (bf16[4,128,256]{2,1,0:T(8,128)(2,1)S(1)}, bf16[4,128,256]{2,1,0:T(8,128)(2,1)}, bf16[4,128,256]{2,1,0:T(8,128)(2,1)}, bf16[4,128,256]{2,1,0...) custom-call(bf16[8,128,1024]{2,1,0:T(8,128)(2,1)} %t0.3, ...), custom_call_target="tpu_custom_call" | custom-call | flops 7515144192 | bytes 10485760 | tf_op jit(solution)/shard_map/attend_forward/pallas_call | solution.py:80
  215.0 15.8 %attend_forward.3 = (bf16[4,128,256]{2,1,0:T(8,128)(2,1)S(1)}, bf16[4,128,256]{2,1,0:T(8,128)(2,1)}, bf16[4,128,256]{2,1,0:T(8,128)(2,1)}, bf16[4,128,256]{2,1,0...) custom-call(bf16[8,128,1024]{2,1,0:T(8,128)(2,1)} %t0.3, ...), custom_call_target="tpu_custom_call" | custom-call | flops 7515144192 | bytes 10485760 | tf_op jit(solution)/shard_map/attend_forward/pallas_call | solution.py:80
  234.7 5.7 collective-permute-done.10
  266.4 30.2 %feed_forward.1 = (bf16[2048,2048]{1,0:T(8,128)(2,1)}, bf16[2048,2048]{1,0:T(8,128)(2,1)}, f32[1024,1024]{1,0:T(8,128)}, bf16[1024,1024]{1,0:T(8,128)(2,1)}) custom-call(bf16[1024,1024]{1,0:T(8,128)(2,1)} %copy-done.19, bf16[1024,1024]{1,0:T(8,128)(2,1)} %copy-done.45, bf16[16,18,64,256]{3,2,1,0:T(8,128)(2,1)} %bitcast.301, f32[1,2048]{1,0:T(1,128)} %fusion.16.bias, ...), custom_call_target="tpu_custom_call" | custom-call | flops 17179869184 | bytes 29360128 | tf_op jit(solution)/shard_map/feed_forward/pallas_call | solution.py:257
  301.2 5.4 fusion.28
  318.8 51.9 %feed_backward.1 = (bf16[16,16,64,256]{3,2,1,0:T(8,128)(2,1)}, f32[1,2048]{1,0:T(1,128)}, f32[1024,1024]{1,0:T(8,128)}, bf16[1024,1024]{1,0:T(8,128)(2,1)}) custom-call(bf16[1024,1024]{1,0:T(8,128)(2,1)} %copy-done.20, bf16[1024,1024]{1,0:T(8,128)(2,1)} %copy-done.46, bf16[1024,1024]{1,0:T(8,128)(2,1)} %copy-done.19, bf16[1024,1024]{1,0:T(8,128)(2,1)} %copy-done.45, ...), custom_call_target="tpu_custom_call" | custom-call | flops 34359738368 | bytes 54525952 | tf_op jit(solution)/shard_map/feed_backward/pallas_call | solution.py:345
  375.3 10.1 %multiply_reduce_fusion = (f32[1024]{0:T(1024)}, f32[1024]{0:T(1024)S(1)}, f32[1024]{0:T(1024)S(1)}, f32[1024]{0:T(1024)S(1)}, f32[1024,1024]{1,0:T(8,128)S(1)}, /*index=5*/bf16[1024,1024]{1,0:T(8,128)(2,1)}) fusion(f32[1024,1024]{1,0:T(8,128)} %copy-done.10, f32[1024]{0:T(1024)S(1)} %add_rsqrt_fusion.1, f32[1024]{0:T(1024)S(1)} %broadcast_multiply_fusion.4, ...), kind=kLoop, calls=%fused_computation.14 | loop fusion | flops 24113152 | bytes 23121920 | tf_op jit(solution)/shard_map/reduce_sum | solution.py:387
  392.8 4.5 reshape.536
  397.3 8.2 %fusion.30 = (bf16[4,128,1,256]{3,2,1,0:T(2,128)(2,1)S(1)}, bf16[4,128,1,256]{3,2,1,0:T(2,128)(2,1)S(1)}, bf16[4,128,1,256]{3,2,1,0:T(2,128)(2,1)S(1)}, bf16[4,1...) fusion(bf16[8,128,4,256]{3,2,1,0:T(4,128)(2,1)} %reshape.536), kind=kLoop, calls=%fused_computation.161 | loop fusion | bytes 4194304 | tf_op jit(solution)/shard_map/slice | solution.py:616
  426.0 15.5 %collective-permute-done.20.g3 = bf16[4,128,256]{2,1,0:T(8,128)(2,1)} collective-permute-done((bf16[4,128,256]{2,1,0:T(8,128)(2,1)}, bf16[4,128,256]{2,1,0:T(8,128)(2,1)}, u32[]{:S(2)}, u32[]{:S(2)}) %collective-permute-start.20) | collective-permute-done | bytes 262176 | tf_op jit(solution)/shard_map/ppermute | solution.py:423
  441.5 27.7 %attend_backward.2 = (bf16[4,512,768]{2,1,0:T(8,128)(2,1)}, f32[4,128,1024]{2,1,0:T(8,128)}, bf16[4,128,1024]{2,1,0:T(8,128)(2,1)S(1)}, f32[4,128,1024]{2,1,0:T(...) custom-call(bf16[4,512,768]{2,1,0:T(8,128)(2,1)} %get-tuple-element.61.saved, ...), custom_call_target="tpu_custom_call" | custom-call | flops 13957595136 | bytes 22020096 | tf_op jit(solution)/shard_map/attend_backward/pallas_call | solution.py:155
  475.8 27.6 %attend_backward.3 = (bf16[4,512,768]{2,1,0:T(8,128)(2,1)}, f32[4,128,1024]{2,1,0:T(8,128)}, bf16[4,128,1024]{2,1,0:T(8,128)(2,1)S(1)}, f32[4,128,1024]{2,1,0:T(...) custom-call(bf16[4,512,768]{2,1,0:T(8,128)(2,1)} %get-tuple-element.66.saved, ...), custom_call_target="tpu_custom_call" | custom-call | flops 13957595136 | bytes 22020096 | tf_op jit(solution)/shard_map/attend_backward/pallas_call | solution.py:155
  513.1 5.8 collective-permute-start.35
  518.9 7.1 %fusion.34 = f32[1024,768,1]{1,0,2:T(8,128)} fusion(bf16[4,512,1024]{2,1,0:T(8,128)(2,1)S(1)} %copy-done.47, bf16[4,512,768]{2,1,0:T(8,128)(2,1)} %get-tuple-element.72), kind=kOutput, calls=%fused_computation.165 | convolution fusion | flops 3221225472 | bytes 10485760 | tf_op jit(solution)/shard_map/dot_general | solution.py:26
  526.2 7.8 %fusion.8 = bf16[1024,768]{1,0:T(8,128)(2,1)S(1)} fusion(f32[1024,768,1]{1,0,2:T(8,128)} %fusion.34, bf16[4,512,1024]{2,1,0:T(8,128)(2,1)} %get-tuple-element.73, bf16[4,512,768]{2,1,0:T(8,128)(2,1)} %get-tuple-element.74), kind=kOutput, calls=%fused_computation.29 | convolution fusion | flops 3222798336 | bytes 12058624 | tf_op jit(solution)/shard_map/dot_general | solution.py:26
  541.6 30.2 %collective-permute-done.30 = bf16[4,128,768]{2,1,0:T(8,128)(2,1)S(1)} collective-permute-done((bf16[4,128,768]{2,1,0:T(8,128)(2,1)S(1)}, bf16[4,128,768]{2,1,0:T(8,128)(2,1)S(1)}, u32[]{:S(2)}, u32[]{:S(2)}) %collective-permute-start.30) | collective-permute-done | bytes 786464 | tf_op jit(solution)/shard_map/ppermute | solution.py:443
  576.8 9.8 %collective-permute-done.39 = bf16[4,2,32,1024]{3,2,1,0:T(8,128)(2,1)S(1)} collective-permute-done((bf16[4,2,32,1024]{3,2,1,0:T(8,128)(2,1)S(1)}, bf16[4,2,32,1024]{3,2,1,0:T(8,128)(2,1)S(1)}, u32[]{:S(2)}, u32[]{:S(2)}) %collective-permute-start.39) | collective-permute-done | bytes 524320 | tf_op jit(solution)/shard_map/ppermute | solution.py:443
  587.1 6.2 collective-permute-done.40
  595.1 7.7 %collective-permute-done.32 = bf16[1,128,768]{2,1,0:T(8,128)(2,1)S(1)} collective-permute-done((bf16[1,128,768]{2,1,0:T(8,128)(2,1)S(1)}, bf16[1,128,768]{2,1,0:T(8,128)(2,1)S(1)}, u32[]{:S(2)}, u32[]{:S(2)}) %collective-permute-start.32) | collective-permute-done | bytes 196640 | tf_op jit(solution)/shard_map/ppermute | solution.py:443
  611.2 21.2 %all-to-all-done.1 = f32[4,32,3,1,256]{4,1,3,2,0:T(8,128)S(1)} async-done(((f32[4,32,3,1,256]{4,1,3,2,0:T(8,128)}), f32[4,32,3,1,256]{4,1,3,2,0:T(8,128)S(1)}, u32[]{:S(2)}, u32[]{:S(2)}) %all-to-all-start.1) | async-done | bytes 393248 | tf_op jit(solution)/shard_map/all_to_all | solution.py:645
  (363 shorter events, 166.4 us)
Async XLA Ops:
  7.2 201.7 %all-gather.3.cloned.1.call-start = ((), (), s32[]{:S(2)}) async-start(), calls=%async_computation.4 | async-start | bytes 10027008 | tf_op jit(solution)/shard_map/all_gather | solution.py:534
  14.1 629.1 %reduce-scatter.2.cloned.1.call-start = ((), (), s32[]{:S(2)}) async-start(), calls=%async_computation.3 | async-start | bytes 8912896 | tf_op jit(solution)/shard_map/reduce_scatter | solution.py:591
  14.2 83.2 %collective-permute-start.1 = (bf16[8,128,1024]{2,1,0:T(8,128)(2,1)}, bf16[8,128,1024]{2,1,0:T(8,128)(2,1)}, u32[]{:S(2)}, u32[]{:S(2)}) collective-permute-start(bf16[8,128,1024]{2,1,0:T(8,128)(2,1)} %t0.3), channel_id=1, source_target_pairs={{0,2},{1,3},{2,0},{3,1},{4,6},{5,7},{6,4},{7,5},{8,10},{9,11},{10,... | collective-permute-start | bytes 6291464 | tf_op jit(solution)/shard_map/ppermute | solution.py:423
  94.4 48.9 %collective-permute-start.4 = (bf16[2,144,768]{2,1,0:T(8,128)(2,1)S(1)}, bf16[2,144,768]{2,1,0:T(8,128)(2,1)S(1)}, u32[]{:S(2)}, u32[]{:S(2)}) collective-permute-start(bf16[2,144,768]{2,1,0:T(8,128)(2,1)S(1)} %maximum_select_fusion.5), channel_id=1, source_target_pairs={{0,16},{8,24},{16,0},{24,8},{1,17},{9,25},{17,1},{25,9},{2,18},{10... | collective-permute-start | bytes 1327112 | tf_op jit(solution)/shard_map/ppermute | solution.py:443
  97.3 92.3 %collective-permute-start = (bf16[8,128,1024]{2,1,0:T(8,128)(2,1)}, bf16[8,128,1024]{2,1,0:T(8,128)(2,1)}, u32[]{:S(2)}, u32[]{:S(2)}) collective-permute-start(bf16[8,128,1024]{2,1,0:T(8,128)(2,1)} %t0.3), channel_id=1, source_target_pairs={{0,1},{1,0},{2,3},{3,2},{4,5},{5,4},{6,7},{7,6},{8,9},{9,8},{10,11... | collective-permute-start | bytes 6291464 | tf_op jit(solution)/shard_map/ppermute | solution.py:426
  97.4 92.3 %collective-permute-start.2 = (bf16[8,128,1024]{2,1,0:T(8,128)(2,1)}, bf16[8,128,1024]{2,1,0:T(8,128)(2,1)}, u32[]{:S(2)}, u32[]{:S(2)}) collective-permute-start(bf16[8,128,1024]{2,1,0:T(8,128)(2,1)} %collective-permute-done.1.t2), channel_id=1, source_target_pairs={{0,1},{1,0},{2,3},{3,2},{4,5},{5,4},{6,7},{7,6},{8,9},{9,8},{10,11... | collective-permute-start | bytes 6291464 | tf_op jit(solution)/shard_map/ppermute | solution.py:426
  144.4 42.1 %collective-permute-start.5 = (bf16[2,2,144,768]{3,2,1,0:T(8,128)(2,1)}, bf16[2,2,144,768]{3,2,1,0:T(8,128)(2,1)}, u32[]{:S(2)}, u32[]{:S(2)}) collective-permute-start(bf16[2,2,144,768]{3,2,1,0:T(8,128)(2,1)} %maximum_select_fusion.3), channel_id=1, source_target_pairs={{0,8},{8,0},{16,24},{24,16},{1,9},{9,1},{17,25},{25,17},{2,10},{10... | collective-permute-start | bytes 2654216 | tf_op jit(solution)/shard_map/ppermute | solution.py:443
  207.1 25.3 %collective-permute-start.7 = (bf16[4,128,256]{2,1,0:T(8,128)(2,1)}, bf16[4,128,256]{2,1,0:T(8,128)(2,1)}, u32[]{:S(2)}, u32[]{:S(2)}) collective-permute-start(bf16[4,128,256]{2,1,0:T(8,128)(2,1)} %get-tuple-element.49), channel_id=1, source_target_pairs={{0,2},{1,3},{2,0},{3,1},{4,6},{5,7},{6,4},{7,5},{8,10},{9,11},{10,... | collective-permute-start | bytes 786440 | tf_op jit(solution)/shard_map/ppermute | solution.py:423
  207.7 27.0 %collective-permute-start.8 = (bf16[4,128,256]{2,1,0:T(8,128)(2,1)S(1)}, bf16[4,128,256]{2,1,0:T(8,128)(2,1)}, u32[]{:S(2)}, u32[]{:S(2)}) collective-permute-start(bf16[4,128,256]{2,1,0:T(8,128)(2,1)S(1)} %get-tuple-element.50), channel_id=1, source_target_pairs={{0,3},{1,2},{2,1},{3,0},{4,7},{5,6},{6,5},{7,4},{8,11},{9,10},{10,... | collective-permute-start | bytes 786440 | tf_op jit(solution)/shard_map/ppermute | solution.py:423
  214.6 35.2 %collective-permute-start.13 = (bf16[16,32,1024]{2,1,0:T(8,128)(2,1)}, bf16[16,32,1024]{2,1,0:T(8,128)(2,1)}, u32[]{:S(2)}, u32[]{:S(2)}) collective-permute-start(bf16[16,32,1024]{2,1,0:T(8,128)(2,1)} %reshape.508), channel_id=1, source_target_pairs={{0,1},{1,0},{2,3},{3,2},{4,5},{5,4},{6,7},{7,6},{8,9},{9,8},{10,11... | collective-permute-start | bytes 3145736 | tf_op jit(solution)/shard_map/ppermute | solution.py:426
  408.7 32.8 %collective-permute-start.20 = (bf16[4,128,256]{2,1,0:T(8,128)(2,1)}, bf16[4,128,256]{2,1,0:T(8,128)(2,1)}, u32[]{:S(2)}, u32[]{:S(2)}) collective-permute-start(bf16[4,128,256]{2,1,0:T(8,128)(2,1)} %bitcast.237), channel_id=1, source_target_pairs={{0,3},{1,2},{2,1},{3,0},{4,7},{5,6},{6,5},{7,4},{8,11},{9,10},{10,... | collective-permute-start | bytes 786440 | tf_op jit(solution)/shard_map/ppermute | solution.py:423
  416.3 54.9 %collective-permute-start.24 = (bf16[4,128,256]{2,1,0:T(8,128)(2,1)}, bf16[4,128,256]{2,1,0:T(8,128)(2,1)S(1)}, u32[]{:S(2)}, u32[]{:S(2)}) collective-permute-start(bf16[4,128,256]{2,1,0:T(8,128)(2,1)} %bitcast.235), channel_id=1, source_target_pairs={{0,1},{1,0},{2,3},{3,2},{4,5},{5,4},{6,7},{7,6},{8,9},{9,8},{10,11... | collective-permute-start | bytes 786440 | tf_op jit(solution)/shard_map/ppermute | solution.py:423
  417.7 53.5 %collective-permute-start.25 = (bf16[4,128,256]{2,1,0:T(8,128)(2,1)}, bf16[4,128,256]{2,1,0:T(8,128)(2,1)}, u32[]{:S(2)}, u32[]{:S(2)}) collective-permute-start(bf16[4,128,256]{2,1,0:T(8,128)(2,1)} %bitcast.234), channel_id=1, source_target_pairs={{0,2},{1,3},{2,0},{3,1},{4,6},{5,7},{6,4},{7,5},{8,10},{9,11},{10,... | collective-permute-start | bytes 786440 | tf_op jit(solution)/shard_map/ppermute | solution.py:423
  423.7 52.0 %collective-permute-start.26 = (bf16[4,128,256]{2,1,0:T(8,128)(2,1)}, bf16[4,128,256]{2,1,0:T(8,128)(2,1)}, u32[]{:S(2)}, u32[]{:S(2)}) collective-permute-start(bf16[4,128,256]{2,1,0:T(8,128)(2,1)} %bitcast.233), channel_id=1, source_target_pairs={{0,3},{1,2},{2,1},{3,0},{4,7},{5,6},{6,5},{7,4},{8,11},{9,10},{10,... | collective-permute-start | bytes 786440 | tf_op jit(solution)/shard_map/ppermute | solution.py:423
  512.0 27.3 %collective-permute-start.38 = (bf16[4,2,2,32,1024]{4,3,2,1,0:T(8,128)(2,1)}, bf16[4,2,2,32,1024]{4,3,2,1,0:T(8,128)(2,1)}, u32[]{:S(2)}, u32[]{:S(2)}) collective-permute-start(bf16[4,2,2,32,1024]{4,3,2,1,0:T(8,128)(2,1)} %dynamic-slice_bitcast_fusion), channel_id=1, source_target_pairs={{0,1},{1,0},{2,3},{3,2},{4,5},{5,4},{6,7},{7,6},{8,9},{9,8},{10,11... | collective-permute-start | bytes 3145736 | tf_op jit(solution)/shard_map/ppermute | solution.py:443
  535.9 35.9 %collective-permute-start.30 = (bf16[4,128,768]{2,1,0:T(8,128)(2,1)S(1)}, bf16[4,128,768]{2,1,0:T(8,128)(2,1)S(1)}, u32[]{:S(2)}, u32[]{:S(2)}) collective-permute-start(bf16[4,128,768]{2,1,0:T(8,128)(2,1)S(1)} %dynamic-slice_bitcast_fusion.1), channel_id=1, source_target_pairs={{0,4},{4,0},{1,5},{5,1},{2,6},{6,2},{3,7},{7,3},{8,12},{12,8},{9,1... | collective-permute-start | bytes 2359304 | tf_op jit(solution)/shard_map/ppermute | solution.py:443
  536.0 36.0 %collective-permute-start.22 = (bf16[4,128,1024]{2,1,0:T(8,128)(2,1)S(1)}, bf16[4,128,1024]{2,1,0:T(8,128)(2,1)S(1)}, u32[]{:S(2)}, u32[]{:S(2)}) collective-permute-start(bf16[4,128,1024]{2,1,0:T(8,128)(2,1)S(1)} %copy-done.7), channel_id=1, source_target_pairs={{0,1},{1,0},{2,3},{3,2},{4,5},{5,4},{6,7},{7,6},{8,9},{9,8},{10,11... | collective-permute-start | bytes 3145736 | tf_op jit(solution)/shard_map/ppermute | solution.py:426
  536.0 98.2 %collective-permute-start.21 = (bf16[4,128,1024]{2,1,0:T(8,128)(2,1)S(1)}, bf16[4,128,1024]{2,1,0:T(8,128)(2,1)}, u32[]{:S(2)}, u32[]{:S(2)}) collective-permute-start(bf16[4,128,1024]{2,1,0:T(8,128)(2,1)S(1)} %copy-done.3), channel_id=1, source_target_pairs={{0,1},{1,0},{2,3},{3,2},{4,5},{5,4},{6,7},{7,6},{8,9},{9,8},{10,11... | collective-permute-start | bytes 3145736 | tf_op jit(solution)/shard_map/ppermute | solution.py:426
  538.7 34.8 %collective-permute-start.28 = (bf16[4,128,1024]{2,1,0:T(8,128)(2,1)S(1)}, bf16[4,128,1024]{2,1,0:T(8,128)(2,1)S(1)}, u32[]{:S(2)}, u32[]{:S(2)}) collective-permute-start(bf16[4,128,1024]{2,1,0:T(8,128)(2,1)S(1)} %copy-done.9), channel_id=1, source_target_pairs={{0,1},{1,0},{2,3},{3,2},{4,5},{5,4},{6,7},{7,6},{8,9},{9,8},{10,11... | collective-permute-start | bytes 3145736 | tf_op jit(solution)/shard_map/ppermute | solution.py:426
  539.3 98.7 %collective-permute-start.27 = (bf16[4,128,1024]{2,1,0:T(8,128)(2,1)S(1)}, bf16[4,128,1024]{2,1,0:T(8,128)(2,1)}, u32[]{:S(2)}, u32[]{:S(2)}) collective-permute-start(bf16[4,128,1024]{2,1,0:T(8,128)(2,1)S(1)} %copy-done.5), channel_id=1, source_target_pairs={{0,1},{1,0},{2,3},{3,2},{4,5},{5,4},{6,7},{7,6},{8,9},{9,8},{10,11... | collective-permute-start | bytes 3145736 | tf_op jit(solution)/shard_map/ppermute | solution.py:426
  573.4 60.9 %collective-permute-start.23 = (bf16[4,128,1024]{2,1,0:T(8,128)(2,1)}, bf16[4,128,1024]{2,1,0:T(8,128)(2,1)}, u32[]{:S(2)}, u32[]{:S(2)}) collective-permute-start(bf16[4,128,1024]{2,1,0:T(8,128)(2,1)} %add_convert_fusion.2), channel_id=1, source_target_pairs={{0,2},{1,3},{2,0},{3,1},{4,6},{5,7},{6,4},{7,5},{8,10},{9,11},{10,... | collective-permute-start | bytes 3145736 | tf_op jit(solution)/shard_map/ppermute | solution.py:423
  586.6 51.4 %collective-permute-start.29 = (bf16[4,128,1024]{2,1,0:T(8,128)(2,1)}, bf16[4,128,1024]{2,1,0:T(8,128)(2,1)}, u32[]{:S(2)}, u32[]{:S(2)}) collective-permute-start(bf16[4,128,1024]{2,1,0:T(8,128)(2,1)} %add_convert_fusion.1), channel_id=1, source_target_pairs={{0,2},{1,3},{2,0},{3,1},{4,6},{5,7},{6,4},{7,5},{8,10},{9,11},{10,... | collective-permute-start | bytes 3145736 | tf_op jit(solution)/shard_map/ppermute | solution.py:423
  604.0 28.4 %all-to-all-start.1 = ((f32[4,32,3,1,256]{4,1,3,2,0:T(8,128)}), f32[4,32,3,1,256]{4,1,3,2,0:T(8,128)S(1)}, u32[]{:S(2)}, u32[]{:S(2)}) async-start(f32[4,32,3,1,256]{4,1,3,2,0:T(8,128)} %copy.231), calls=%async_computation.1 | async-start | bytes 786432 | tf_op jit(solution)/shard_map/all_to_all | solution.py:645
  607.9 25.7 %collective-permute-start.42 = (bf16[1,32,1024]{2,1,0:T(8,128)(2,1)S(1)}, bf16[1,32,1024]{2,1,0:T(8,128)(2,1)S(1)}, u32[]{:S(2)}, u32[]{:S(2)}) collective-permute-start(bf16[1,32,1024]{2,1,0:T(8,128)(2,1)S(1)} %constant_dynamic-slice_fusion), channel_id=1, source_target_pairs={{0,16},{8,24},{16,0},{24,8},{1,17},{9,25},{17,1},{25,9},{2,18},{10... | collective-permute-start | bytes 196616 | tf_op jit(solution)/shard_map/ppermute | solution.py:443
  (71 other events, 698.3 us)
Sparse Core Ops, SparseCore 0:
  14.2 165.2 all-gather.2
  371.3 201.0 reduce-scatter.1

commit v4 on v3

--- a/solution.py
+++ b/solution.py
@@ -203,9 +203,13 @@
     return flat(jnp.concatenate(halves, axis=1))
 
 
-def feed_kernel(block, own, other, expand, bias, reduce, act, slope, own_out, other_out, far_sum):
+def feed_kernel(*refs):
+    sources, (expand, bias, reduce, act, slope, own_out, other_out, far_sum) = (
+        refs[: 2 * CHUNKS],
+        refs[2 * CHUNKS :],
+    )
     step = pl.program_id(0)
-    rows = own.shape[0]
+    block = sources[0].shape[0]
 
     @pl.when(step == 0)
     def _():
@@ -214,16 +218,14 @@
 
     into = expand_piece(expand)
     back = reduce_piece(reduce)
-    work = [
-        (source, total, slice(i * block, (i + 1) * block), slice(start + i * block, start + (i + 1) * block))
-        for source, total, start in ((own, own_out, 0), (other, far_sum, rows))
-        for i in range(rows // block)
-    ]
-    ahead = dot(work[0][0][work[0][2]], into) + bias[...]
-    for index, (_, total, at, to) in enumerate(work):
+    ahead = dot(sources[0][...], into) + bias[...]
+    for index in range(2 * CHUNKS):
         inside = ahead
-        if index + 1 < len(work):
-            ahead = dot(work[index + 1][0][work[index + 1][2]], into) + bias[...]
+        if index + 1 < 2 * CHUNKS:
+            ahead = dot(sources[index + 1][...], into) + bias[...]
+        total = own_out if index < CHUNKS else far_sum
+        at = slice(index % CHUNKS * block, (index % CHUNKS + 1) * block)
+        to = slice(index * block, (index + 1) * block)
         square = inside * inside
         curve = jnp.tanh(inside * (0.7978845608028654 + 0.7978845608028654 * 0.044715 * square))
         half = 0.5 * curve + 0.5
@@ -249,15 +251,16 @@
 
 
 def feed(own, other, weights, bias):
-    rows, depth = own.shape
+    block, depth = own[0].shape
+    rows = CHUNKS * block
     hidden = bias.shape[1]
     pieces = 2
     wide = pieces * PIECE
     expand_spec, reduce_spec = feed_weights(weights, pieces, depth // PIECE)
     return pl.pallas_call(
-        functools.partial(feed_kernel, 512),
+        feed_kernel,
         grid=(hidden // wide,),
-        in_specs=[resident((rows, depth))] * 2
+        in_specs=[resident((block, depth))] * (2 * CHUNKS)
         + [expand_spec, column((1, wide)), reduce_spec],
         out_specs=[column((2 * rows, wide))] * 2 + [resident((rows, depth))] * 2,
         out_shape=[jax.ShapeDtypeStruct((2 * rows, hidden), BF16)] * 2
@@ -273,28 +276,16 @@
             transcendentals=2 * rows * hidden,
         ),
         name="feed_forward",
-    )(own, other, weights, bias, weights)
-
-
-def feed_back_kernel(
-    block,
-    own_grad,
-    other_grad,
-    own_rows,
-    other_rows,
-    act,
-    slope,
-    expand,
-    reduce,
-    weight_grad,
-    bias_grad,
-    own_out,
-    other_out,
-    far_sum,
-    inside,
-):
+    )(*own, *other, weights, bias, weights)
+
+
+def feed_back_kernel(*refs):
+    grads, sources = refs[: 2 * CHUNKS], refs[2 * CHUNKS : 4 * CHUNKS]
+    act, slope, expand, reduce, weight_grad, bias_grad, own_out, other_out, far_sum, inside = refs[
+        4 * CHUNKS :
+    ]
     step = pl.program_id(0)
-    rows = own_grad.shape[0]
+    block = grads[0].shape[0]
 
     @pl.when(step == 0)
     def _():
@@ -304,19 +295,21 @@
     into = expand_piece(expand)
     back = reduce_piece(reduce)
     bias_sum = jnp.zeros(bias_grad.shape, F32)
-    for source, total, start in ((own_grad, own_out, 0), (other_grad, far_sum, rows)):
-        for index in range(rows // block):
-            at = slice(index * block, (index + 1) * block)
-            to = slice(start + index * block, start + (index + 1) * block)
-            grad_act = dot(source[at], back, (1, 1))
-            part = (grad_act * slope[to].astype(F32)).astype(BF16)
-            inside[to] = part
-            bias_sum += jnp.sum(part.astype(F32), axis=0, keepdims=True)
-            total[at] += dot(part, into, (1, 1))
+    for index in range(2 * CHUNKS):
+        total = own_out if index < CHUNKS else far_sum
+        at = slice(index % CHUNKS * block, (index % CHUNKS + 1) * block)
+        to = slice(index * block, (index + 1) * block)
+        grad_act = dot(grads[index][...], back, (1, 1))
+        part = (grad_act * slope[to].astype(F32)).astype(BF16)
+        inside[to] = part
+        bias_sum += jnp.sum(part.astype(F32), axis=0, keepdims=True)
+        total[at] += dot(part, into, (1, 1))
     bias_grad[...] = bias_sum
     chips, pieces, height, _ = weight_grad.shape
     columns = pieces // 4
-    reduce_grad = dot(act[:rows], own_grad[...], (0, 0)) + dot(act[rows:], other_grad[...], (0, 0))
+    reduce_grad = sum(
+        dot(act[i * block : (i + 1) * block], grad[...], (0, 0)) for i, grad in enumerate(grads)
+    )
     count = PIECE // (2 * height)
     reduce_grad = reduce_grad.reshape(count, 2 * height, reduce_grad.shape[1]).astype(BF16)
     mine = pl.ds(step * count, count)
@@ -325,8 +318,9 @@
             weight_grad[mine, (2 + half) * columns + i] = reduce_grad[
                 :, half * height : (half + 1) * height, i * PIECE : (i + 1) * PIECE
             ]
-    flipped = dot(inside[:rows], own_rows[...], (0, 0)) + dot(
-        inside[rows:], other_rows[...], (0, 0)
+    flipped = sum(
+        dot(inside[i * block : (i + 1) * block], source[...], (0, 0))
+        for i, source in enumerate(sources)
     )
     expand_grad = jnp.transpose(flipped).reshape(chips, height, PIECE).astype(BF16)
     weight_grad[:, step] = expand_grad
@@ -336,16 +330,17 @@
         other_out[...] = far_sum[...].astype(BF16)
 
 
-def feed_back(own_grad, other_grad, own_rows, other_rows, act, slope, weights):
-    rows, depth = own_grad.shape
+def feed_back(grads, sources, act, slope, weights):
+    block, depth = grads[0].shape
+    rows = CHUNKS * block
     hidden = act.shape[1]
     chips, _, height, _ = weights.shape
     pieces = 2 * hidden // PIECE
     expand_spec, reduce_spec = feed_weights(weights, 1, depth // PIECE)
     return pl.pallas_call(
-        functools.partial(feed_back_kernel, 512),
+        feed_back_kernel,
         grid=(hidden // PIECE,),
-        in_specs=[resident((rows, depth))] * 4
+        in_specs=[resident((block, depth))] * (4 * CHUNKS)
         + [column((2 * rows, PIECE))] * 2
         + [expand_spec, reduce_spec],
         out_specs=[
@@ -370,7 +365,7 @@
             transcendentals=0,
         ),
         name="feed_backward",
-    )(own_grad, other_grad, own_rows, other_rows, act, slope, weights, weights)
+    )(*grads, *sources, act, slope, weights, weights)
 
 
 def normalize(values):
@@ -383,8 +378,181 @@
     grad_scaled = incoming * gain
     mean_one = jnp.mean(grad_scaled, axis=-1, keepdims=True)
     mean_two = jnp.mean(grad_scaled * scaled, axis=-1, keepdims=True)
-    outgoing = inverse * (grad_scaled - mean_one - scaled * mean_two)
-    return (outgoing, jnp.sum(incoming * scaled, axis=0), jnp.sum(incoming, axis=0))
+    return inverse * (grad_scaled - mean_one - scaled * mean_two)
+
+
+def add_sums(out, *rows):
+    rows = [jnp.sum(row, axis=0, keepdims=True) for row in rows]
+    rows.append(jnp.zeros((out.shape[0] - len(rows), out.shape[1]), F32))
+    rows = jnp.concatenate(rows, axis=0)
+
+    @pl.when(pl.program_id(0) == 0)
+    def _():
+        out[...] = rows
+
+    @pl.when(pl.program_id(0) > 0)
+    def _():
+        out[...] += rows
+
+
+OUT_BIAS, GAIN_ONE, SHIFT_ONE, RED_BIAS, GAIN_TWO, SHIFT_TWO = (slice(i, i + 1) for i in range(2, 8))
+SCALAR = pl.BlockSpec(memory_space=pltpu.SMEM)
+ROW_BLOCK = 256
+
+
+def row_call(kernel, name, ins, outs, arrays, rows, cost):
+    return pl.pallas_call(
+        kernel,
+        grid=(rows // ROW_BLOCK,),
+        in_specs=ins,
+        out_specs=[spec for spec, _ in outs],
+        out_shape=[shape for _, shape in outs],
+        compiler_params=pltpu.CompilerParams(vmem_limit_bytes=48 * MIB),
+        cost_estimate=pl.CostEstimate(flops=cost, bytes_accessed=rows << 14, transcendentals=rows),
+        name=name,
+    )(*arrays)
+
+
+def row_block(width, first=0):
+    return pl.BlockSpec((ROW_BLOCK, width), lambda i: (i + first, 0))
+
+
+def first_norm_kernel(place, m0, m1, m2, m3, tokens, weight, vectors, low, scaled, inverse, mixed):
+    total = tokens[...].astype(F32) + vectors[OUT_BIAS]
+    parts = [m[...].reshape(ROW_BLOCK, -1) for m in (m0, m1, m2, m3)]
+    mixed[...] = jnp.concatenate(parts, axis=1)
+    for step, part in enumerate(parts):
+        total += dot(part, weight[place[0] ^ step])
+    scaled_one, inverse_one = normalize(total)
+    scaled[...] = scaled_one
+    inverse[...] = inverse_one
+    low[...] = (scaled_one * vectors[GAIN_ONE] + vectors[SHIFT_ONE]).astype(BF16)
+
+
+def first_norm(place, mixed, rows, weight, vectors, chunk):
+    width = rows.shape[1]
+    count, part, lanes = mixed[0].shape
+    size = count * part
+    steps = size // ROW_BLOCK
+    return row_call(
+        first_norm_kernel,
+        "first_norm",
+        [SCALAR]
+        + [by_row((ROW_BLOCK // part, part, lanes))] * 4
+        + [row_block(width, chunk * steps), resident(weight.shape), resident(vectors.shape)],
+        [
+            (row_block(width), jax.ShapeDtypeStruct((size, width), BF16)),
+            (row_block(width), jax.ShapeDtypeStruct((size, width), F32)),
+            (row_block(1), jax.ShapeDtypeStruct((size, 1), F32)),
+            (row_block(width), jax.ShapeDtypeStruct((size, width), BF16)),
+        ],
+        (place, *mixed, rows, weight, vectors),
+        size,
+        2 * size * width * width,
+    )
+
+
+def second_norm_kernel(scaled, own, far, grad_out, vectors, layer, grad, low, sums):
+    first = scaled[...] * vectors[GAIN_ONE] + vectors[SHIFT_ONE]
+    reduced = own[...] + far[...].astype(F32) + vectors[RED_BIAS]
+    scaled_two, inverse_two = normalize(first + reduced)
+    layer[...] = (scaled_two * vectors[GAIN_TWO] + vectors[SHIFT_TWO]).astype(BF16)
+    incoming = grad_out[...].astype(F32)
+    grad_second = normalize_back(incoming, scaled_two, inverse_two, vectors[GAIN_TWO])
+    grad[...] = grad_second
+    low[...] = grad_second.astype(BF16)
+    add_sums(sums, incoming * scaled_two, incoming, grad_second.astype(BF16).astype(F32))
+
+
+def second_norm(scaled, own, far, grad_rows, vectors, chunk):
+    size, width = scaled.shape
+    steps = size // ROW_BLOCK
+    return row_call(
+        second_norm_kernel,
+        "second_norm",
+        [row_block(width)]
+        + [row_block(width, chunk * steps)] * 3
+        + [resident(vectors.shape)],
+        [
+            (row_block(width), jax.ShapeDtypeStruct((size, width), BF16)),
+            (row_block(width), jax.ShapeDtypeStruct((size, width), F32)),
+            (row_block(width), jax.ShapeDtypeStruct((size, width), BF16)),
+            (resident((8, width)), jax.ShapeDtypeStruct((8, width), F32)),
+        ],
+        (scaled, own, far, grad_rows, vectors),
+        size,
+        size * width * 40,
+    )
+
+
+def first_back_kernel(
+    place, grad, own, far, scaled, inverse, weight, vectors, hidden, low, m0, m1, m2, m3, sums
+):
+    incoming = grad[...] + own[...] + far[...].astype(F32)
+    grad_hidden = normalize_back(incoming, scaled[...], inverse[...], vectors[GAIN_ONE])
+    hidden[...] = grad_hidden
+    attended = grad_hidden.astype(BF16)
+    low[...] = attended
+    for step, out in enumerate((m0, m1, m2, m3)):
+        out[...] = dot(attended, weight[place[0] ^ step], (1, 1)).astype(BF16).reshape(out.shape)
+    add_sums(sums, incoming * scaled[...], incoming, attended.astype(F32))
+
+
+def first_back(place, grad, own, far, scaled, inverse, weight, vectors, chunk, part):
+    size, width = grad.shape
+    steps = size // ROW_BLOCK
+    lanes = weight.shape[1]
+    return row_call(
+        first_back_kernel,
+        "first_back",
+        [SCALAR, row_block(width)]
+        + [row_block(width, chunk * steps)] * 2
+        + [row_block(width), row_block(1), resident(weight.shape), resident(vectors.shape)],
+        [
+            (row_block(width), jax.ShapeDtypeStruct((size, width), F32)),
+            (row_block(width), jax.ShapeDtypeStruct((size, width), BF16)),
+        ]
+        + [
+            (
+                by_row((ROW_BLOCK // part, part, lanes)),
+                jax.ShapeDtypeStruct((size // part, part, lanes), BF16),
+            )
+        ]
+        * 4
+        + [(resident((8, width)), jax.ShapeDtypeStruct((8, width), F32))],
+        (place, grad, own, far, scaled, inverse, weight, vectors),
+        size,
+        2 * size * width * width,
+    )
+
+
+def output_grad_kernel(place, *refs):
+    mixed, grads, out = refs[:CHUNKS], refs[CHUNKS:-1], refs[-1]
+    lanes = out.shape[1]
+    for step in range(out.shape[0]):
+        at = slice(step * lanes, (step + 1) * lanes)
+        out[place[0] ^ step] = sum(
+            dot(m[:, at], g[...], (0, 0)) for m, g in zip(mixed, grads)
+        ).astype(BF16)
+
+
+def output_back(place, mixed, grads, ctx_size):
+    size, width = mixed[0].shape
+    shape = (ctx_size, width // ctx_size, width)
+    return pl.pallas_call(
+        output_grad_kernel,
+        grid=(1,),
+        in_specs=[SCALAR] + [resident((size, width))] * (2 * CHUNKS),
+        out_specs=resident(shape),
+        out_shape=jax.ShapeDtypeStruct(shape, BF16),
+        compiler_params=pltpu.CompilerParams(vmem_limit_bytes=48 * MIB),
+        cost_estimate=pl.CostEstimate(
+            flops=2 * CHUNKS * size * width * width,
+            bytes_accessed=4 * width * (width + CHUNKS * size),
+            transcendentals=0,
+        ),
+        name="output_backward",
+    )(place, *mixed, *grads)
 
 
 def on_device(
@@ -464,8 +632,6 @@
             blocks = halve(blocks.astype(kind), 1, "z", step)
         return blocks[0]
 
-    across = hop(tokens, 2)
-    gathered = (tokens, swap(tokens), across, swap(across))
     seg_parts = segment_ids.reshape(seq_count, ctx_size, part)
     seg = jnp.concatenate([chosen(seg_parts, place ^ r, 1) for r in range(ctx_size)], axis=1)
     seg_key = seg[:, :, None]
@@ -494,23 +660,39 @@
         axis=1,
     )
     held = lax.all_to_all(held, CTX, 0, 0, tiled=True)
+    sent, held = lax.optimization_barrier((tokens, held))
+    across = hop(sent, 2)
+    gathered = (tokens, swap(sent), across, swap(across))
     mine = held[:, : share * 3 * lanes].reshape(ctx_size * share, 3 * lanes)
     vector_rows = jnp.pad(
         held[:, share * 3 * lanes :].reshape(-1),
         (0, below * 3 * lanes - ctx_size * vector_count),
     ).reshape(below, 3 * lanes)
-    whole_project = z_gather(widen(jnp.concatenate([mine, vector_rows]), "y"))
-    whole_project = whole_project.reshape(-1, ctx_size * share + below, 3 * lanes)
+    out_rows = share * width // (3 * lanes)
+    out_pad = -out_rows % 16
+    out_flat = jnp.pad(output_weight.reshape(-1), (0, 3 * lanes * (out_rows + out_pad) - share * width))
+    both_out = widen(out_flat.reshape(-1, 3 * lanes), "x")
+    whole_project = lax.all_gather(
+        jnp.concatenate([mine, vector_rows, both_out.reshape(-1, 3 * lanes)]), SEQ, axis=0
+    )
+    first_rows = ctx_size * share + below
     full_project = whole_project[:, : ctx_size * share].reshape(width, 3 * lanes)
+    out_half = (
+        whole_project[:, first_rows:]
+        .reshape(chips, -1)[:, : share * width]
+        .reshape(chips, share, width)
+    )
+    full_output = by_core(out_half, swap(out_half), 1).reshape(ctx_size, lanes, width)
     packed = (
-        whole_project[:, ctx_size * share :]
+        whole_project[:, ctx_size * share : first_rows]
         .reshape(-1, below * 3 * lanes)[:, : ctx_size * vector_count]
         .reshape(everyone, vector_count)
         .astype(F32)
     )
-    full_query, full_value, out_bias, gain_one, shift_one, red_bias, gain_two, shift_two = [
-        packed[:, i * share : (i + 1) * share].reshape(width) for i in range(8)
-    ]
+    vectors = jnp.swapaxes(packed[:, : 8 * share].reshape(everyone, 8, share), 0, 1).reshape(
+        8, width
+    )
+    full_query, full_value = vectors[0], vectors[1]
     exp_bias = chosen(packed[:, 8 * share :].reshape(chips, 2, -1), core, 1).reshape(1, own_hidden)
     bias_all = jnp.concatenate(
         [
@@ -531,78 +713,84 @@
             -1, 2 * share, PIECE
         )
 
-    weights = lax.all_gather(
-        jnp.concatenate(
-            [
-                in_pieces(both.reshape(2 * share, own_hidden)),
-                jnp.swapaxes(
-                    reduce_weight.reshape(2, 2 * share, width // PIECE, PIECE), 1, 2
-                ).reshape(-1, 2 * share, PIECE),
-                in_pieces(output_weight),
-            ]
-        ),
-        CHIPS,
-        axis=0,
-    ).reshape(chips, -1, 2 * share, PIECE)
-    feed_pieces = (own_hidden + 2 * width) // PIECE
-    out_half = jnp.swapaxes(
-        weights[:, feed_pieces:].reshape(chips, width // PIECE, share, PIECE), 1, 2
-    ).reshape(chips, share, width)
-    full_output = by_core(out_half, swap(out_half), 1).reshape(ctx_size, lanes, width)
-    full_output = jnp.concatenate(
-        [chosen(full_output, place ^ r, 0) for r in range(ctx_size)], axis=0
-    )
-
-    saved = []
-    kept_rows = []
-    mixed_parts = []
+    own_pieces = jnp.concatenate(
+        [
+            in_pieces(both.reshape(2 * share, own_hidden)),
+            jnp.swapaxes(
+                reduce_weight.reshape(2, 2 * share, width // PIECE, PIECE), 1, 2
+            ).reshape(-1, 2 * share, PIECE),
+        ]
+    )
+    weights = lax.all_gather(widen(own_pieces, "x"), SEQ, axis=0).reshape(
+        chips, -1, 2 * share, PIECE
+    )
+
+    rows = tokens.reshape(rows_count, width)
+    where = place.reshape(1).astype(jnp.int32)
+    seqs = seq_count // CHUNKS
+    saved, kept_rows, mixed_low, first_low, scaled_one, inverse_one = [], [], [], [], [], []
     for index in range(CHUNKS):
-        at = slice(index * seq_count // CHUNKS, (index + 1) * seq_count // CHUNKS)
+        at = slice(index * seqs, (index + 1) * seqs)
         *mixed, all_rows, kept = attend(
             gathered, full_project, bias_all, seg_key[at], seg_query[at], at.start, []
         )
         kept_rows.append(all_rows.reshape(-1, width))
         saved.append(kept)
-        mixed_parts.append(
-            jnp.concatenate([mixed[0]] + [hop(mixed[r], r) for r in (1, 2, 3)], axis=2)
-        )
-    mixed_low = jnp.concatenate(mixed_parts, axis=0).reshape(rows_count, width)
-
-    rows = tokens.reshape(rows_count, width)
-    attended = dot(mixed_low, full_output) + out_bias
-    scaled_one, inverse_one = normalize(rows.astype(F32) + attended)
-    first = scaled_one * gain_one + shift_one
-    first_low = first.astype(BF16)
-    first_far = swap(first_low)
+        arrived = [mixed[0]] + [hop(mixed[r], r) for r in (1, 2, 3)]
+        low, scaled, inverse, joined = first_norm(
+            where, arrived, rows, full_output, vectors, index
+        )
+        mixed_low.append(joined)
+        first_low.append(low)
+        scaled_one.append(scaled)
+        inverse_one.append(inverse)
+    first_far = [swap(low) for low in first_low]
     act, slope, own_sum, far_sum = feed(first_low, first_far, weights, exp_bias)
-    reduced = own_sum + swap(far_sum).astype(F32) + red_bias
-    scaled_two, inverse_two = normalize(first + reduced)
-    layer_work = (scaled_two * gain_two + shift_two).astype(BF16).reshape(tokens.shape)
-
-    grad_rows = grad_out.reshape(rows_count, width).astype(F32)
-    grad_second, grad_gain_two, grad_shift_two = normalize_back(
-        grad_rows, scaled_two, inverse_two, gain_two
-    )
-    grad_reduced = grad_second.astype(BF16)
-    reduce_bias_grad = jnp.sum(grad_reduced.astype(F32), axis=0)
+    far_sum = swap(far_sum)
+
+    grad_rows = grad_out.reshape(rows_count, width)
+    layer_parts, grad_second, grad_reduced, second_sums = zip(
+        *(
+            second_norm(scaled_one[index], own_sum, far_sum, grad_rows, vectors, index)
+            for index in range(CHUNKS)
+        )
+    )
+    layer_work = jnp.concatenate(layer_parts, axis=0).reshape(tokens.shape)
     weight_grad, expand_bias_grad, own_back, far_back = feed_back(
-        grad_reduced, swap(grad_reduced), first_low, first_far, act, slope, weights
-    )
-    weight_owned = lax.psum_scatter(weight_grad, CHIPS, scatter_dimension=0, tiled=True)[0]
-    grad_first = grad_second + own_back + swap(far_back).astype(F32)
-    grad_hidden, grad_gain_one, grad_shift_one = normalize_back(
-        grad_first, scaled_one, inverse_one, gain_one
-    )
-    grad_attended = grad_hidden.astype(BF16)
-    output_bias_grad = jnp.sum(grad_attended.astype(F32), axis=0)
-    grad_mixed = dot(grad_attended, full_output, (1, 1)).astype(BF16)
-    grad_mixed = grad_mixed.reshape(seq_count, part, ctx_size, lanes)
-
-    output_grad = dot(mixed_low, grad_attended, (0, 0)).astype(BF16)
-    output_grad = output_grad.reshape(ctx_size, lanes, width)
-    output_grad = jnp.concatenate(
-        [chosen(output_grad, place ^ r, 0) for r in range(ctx_size)], axis=0
-    ).reshape(sizes["z"], 2, sizes["x"], 2, share, width)
+        grad_reduced + tuple(swap(grad) for grad in grad_reduced),
+        first_low + first_far,
+        act,
+        slope,
+        weights,
+    )
+    weight_owned = lax.psum_scatter(
+        weight_grad.reshape((-1, sizes["x"]) + weight_grad.shape[1:]),
+        SEQ,
+        scatter_dimension=0,
+        tiled=True,
+    )[0]
+    far_back = swap(far_back)
+    grad_hidden, grad_attended, grad_mixed, first_sums = [], [], [], []
+    for index in range(CHUNKS):
+        grad, low, *mixed, sums = first_back(
+            where,
+            grad_second[index],
+            own_back,
+            far_back,
+            scaled_one[index],
+            inverse_one[index],
+            full_output,
+            vectors,
+            index,
+            part,
+        )
+        grad_hidden.append(grad.reshape(seqs, part, width))
+        grad_attended.append(low)
+        grad_mixed.append([mixed[0]] + [hop(mixed[r], r) for r in (1, 2, 3)])
+        first_sums.append(sums)
+    output_grad = output_back(where, mixed_low, grad_attended, ctx_size).reshape(
+        sizes["z"], 2, sizes["x"], 2, share, width
+    )
     output_grad = halve(output_grad, 3, "c").astype(BF16)
     output_grad = halve(output_grad, 2, "x").astype(BF16)
     output_grad = halve(output_grad, 1, "y")
@@ -613,10 +801,9 @@
     sum_parts = []
     for index in range(CHUNKS):
         at = slice(index * seq_count // CHUNKS, (index + 1) * seq_count // CHUNKS)
-        grads = [grad_mixed[at, :, 0]] + [hop(grad_mixed[at, :, r], r) for r in (1, 2, 3)]
         grad_part, r0, r1, r2, r3, sums = attend_back(
             saved[index],
-            grads,
+            grad_mixed[index],
             full_project,
             seg_key[at],
             seg_query[at],
@@ -624,8 +811,7 @@
         )
         across = r2 + swap(r3).astype(F32)
         work_parts.append(
-            grad_hidden[index * rows_count // CHUNKS : (index + 1) * rows_count // CHUNKS]
-            .reshape(r0.shape)
+            grad_hidden[index]
             + r0
             + swap(r1).astype(F32)
             + hop(across.astype(BF16), 2).astype(F32)
@@ -645,6 +831,7 @@
     project_owned = lax.all_to_all(
         project_owned.reshape(ctx_size, share, 3, lanes), CTX, 0, 2, tiled=False
     ).reshape(share, 3 * width)
+    weight_owned = halve(weight_owned, 0, "x")
     expand_pieces = own_hidden // PIECE
     far_rows = jnp.swapaxes(
         weight_owned[:expand_pieces].reshape(expand_pieces, 2, share, PIECE), 0, 1
@@ -660,15 +847,16 @@
 
     column_sums = jnp.sum(jnp.concatenate(sum_parts, axis=0), axis=(0, 1))
     zeros = jnp.zeros((width,), F32)
+    first_sums, second_sums = sum(first_sums), sum(second_sums)
     grad_vectors = (
         lax.dynamic_update_slice_in_dim(zeros, column_sums[:lanes], place * lanes, 0),
         lax.dynamic_update_slice_in_dim(zeros, column_sums[2 * lanes :], place * lanes, 0),
-        output_bias_grad,
-        grad_gain_one,
-        grad_shift_one,
-        reduce_bias_grad,
-        grad_gain_two,
-        grad_shift_two,
+        first_sums[2],
+        first_sums[0],
+        first_sums[1],
+        second_sums[2],
+        second_sums[0],
+        second_sums[1],
     )
     hidden_sums = expand_bias_grad.reshape(chips, 1, own_hidden // chips)
     hidden_sums = jnp.where(

time: 660 us -> 573 us (0.87)
  blocking collectives: 67.3 us -> 0 us
  Pallas kernels: 169 us -> 203 us
  other arithmetic: 50.6 us -> 27 us
  matrix products: 26.4 us -> 10.3 us
  waiting for transfers between devices: 212 us -> 197 us
    ppermute x16, waiting for transfers between devices: 148 us -> 71.6 us  [trade(): lax.ppermute(array, name, [(i, i ^ step) for i in range(sizes[name])])]
    all_to_all x1 -> x0, blocking collectives: 67.3 us -> none  [on_device(): held = lax.all_to_all(held, CTX, 0, 0, tiled=True)]
    all_gather x1 -> x2, waiting for transfers between devices: 0.01 us -> 44.2 us  [the longest x1 44.2 us: on_device(): lax.all_gather(widen(own_pieces, 'x'), SEQ, axis=0)]
    pallas_call x2 -> x9, Pallas kernels: 82.2 us -> 117 us  [the longest x1 52.1 us: feed_back(): pl.pallas_call(feed_back_kernel, grid=(hidden // PIECE,), in_specs=[resid...]
    reduce_sum x8 -> x0, other arithmetic: 24.1 us -> none  [the longest x2 12 us: normalize_back(): jnp.sum(incoming * scaled, axis=0)]
    ppermute x15, waiting for transfers between devices: 31.2 us -> 48.6 us  [hop(): return lax.ppermute(array, CTX, [(i, i ^ step) for i in range(ctx_size)])]
    dot_general x5 -> x2, matrix products: 26.4 us -> 10.3 us  [dot(): lax.dot_general(left, right, (((contract[0],), (contract[1],)), ((), ()))...]
    unnamed x116 -> x137, local copies, waits for them, and re-layouts: 21.7 us -> 35.5 us
  transfers between devices with their start and end apart: 47 -> 51, of which waited for: 20 -> 19; matrix products, arithmetic and copies ran while one was open for 17% -> 14% of each run, Pallas kernels for 13% -> 20%
where the time goes in v4:
time: 573 us; the launch traced here: 568 us
  Pallas kernels  203 us (35%)
  waiting for transfers between devices  197 us (34%)
  local copies, waits for them, and re-layouts  76.5 us (13%)
  starting transfers between devices  38 us (7%)
  other arithmetic  27 us (5%)
  between operations  15.1 us (3%)
  matrix products  10.3 us (2%)
    ppermute x16, waiting for transfers between devices, trade(): lax.ppermute(array, name, [(i, i ^ step) for i in range(sizes[name])])  71.6 us
    pallas_call x2, Pallas kernels, attend_back(): pl.pallas_call(functools.partial(attend_back_kernel, len(after)), grid=(c...  55.5 us
    pallas_call x1, Pallas kernels, feed_back(): pl.pallas_call(feed_back_kernel, grid=(hidden // PIECE,), in_specs=[resid...  52.1 us
    ppermute x15, waiting for transfers between devices, hop(): return lax.ppermute(array, CTX, [(i, i ^ step) for i in range(ctx_size)])  48.6 us
    all_gather x1, waiting for transfers between devices, on_device(): lax.all_gather(widen(own_pieces, 'x'), SEQ, axis=0)  44.2 us
    unnamed x137, local copies, waits for them, and re-layouts  35.5 us
    pallas_call x1, Pallas kernels, feed(): pl.pallas_call(feed_kernel, grid=(hidden // wide,), in_specs=[resident((b...  30.7 us
    pallas_call x2, Pallas kernels, attend(): pl.pallas_call(functools.partial(attend_kernel, len(after)), grid=(count,...  30.7 us
  transfers between devices with their start and end apart: 51, of which 19 were waited for; matrix products, arithmetic and copies ran while one was open for 14% of the time, Pallas kernels for 20%

profile of v4, /device:TPU:0, one launch (start us, length us, event | category | flops | bytes accessed | tf_op | source)
XLA Modules:
  0.0 567.5 jit_solution(17224772718960967754)
XLA Ops:
  12.5 6.1 %concatenate.67 = bf16[384]{0:T(512)(128)(2,1)S(1)} concatenate(bf16[32]{0:T(256)(128)(2,1)} %param.19, bf16[32]{0:T(256)(128)(2,1)} %param.20, bf16[32]{0:T(256)(128)(2,1)} %param.22, bf16[32]{0:T(256)(128)(2,1)} %param.23, bf16[32]{0:T(256)(128)(2,1)} %param.24, bf16[32]{0:T(256)(128)(2,1)} %param.28, bf16[32]{0:T(256)(128)(2,1)} %param.29, bf16[32]{0:T(256)(128)(2,1)} %param.30, ...), dimensions={0} | concatenate | bytes 1536 | tf_op jit(solution)/shard_map/concatenate | solution.py:653
  24.8 5.1 all-to-all-done
  35.3 13.6 %collective-permute-done.14 = bf16[16,64,256]{2,0,1:T(8,128)(2,1)S(1)} collective-permute-done((bf16[16,64,256]{2,0,1:T(8,128)(2,1)S(1)}, bf16[16,64,256]{2,0,1:T(8,128)(2,1)S(1)}, u32[]{:S(2)}, u32[]{:S(2)}) %collective-permute-start.14) | collective-permute-done | bytes 524320 | tf_op jit(solution)/shard_map/ppermute | solution.py:611
  51.4 46.7 %collective-permute-done.1.t2 = bf16[8,128,1024]{2,1,0:T(8,128)(2,1)} collective-permute-done((bf16[8,128,1024]{2,1,0:T(8,128)(2,1)S(1)}, bf16[8,128,1024]{2,1,0:T(8,128)(2,1)}, u32[]{:S(2)}, u32[]{:S(2)}) %collective-permute-start.1) | collective-permute-done | bytes 2097184 | tf_op jit(solution)/shard_map/ppermute | solution.py:591
  112.8 15.7 %attend_forward.2 = (bf16[4,128,256]{2,1,0:T(8,128)(2,1)S(1)}, bf16[4,128,256]{2,1,0:T(8,128)(2,1)}, bf16[4,128,256]{2,1,0:T(8,128)(2,1)}, bf16[4,128,256]{2,1,0...) custom-call(bf16[8,128,1024]{2,1,0:T(8,128)(2,1)S(1)} %copy-done.2, ...), custom_call_target="tpu_custom_call" | custom-call | flops 7515144192 | bytes 10485760 | tf_op jit(solution)/shard_map/attend_forward/pallas_call | solution.py:80
  130.5 14.9 %attend_forward.3 = (bf16[4,128,256]{2,1,0:T(8,128)(2,1)S(1)}, bf16[4,128,256]{2,1,0:T(8,128)(2,1)S(1)}, bf16[4,128,256]{2,1,0:T(8,128)(2,1)S(1)}, bf16[4,128,25...) custom-call(bf16[8,128,1024]{2,1,0:T(8,128)(2,1)S(1)} %copy-done.2, ...), custom_call_target="tpu_custom_call" | custom-call | flops 7515144192 | bytes 10485760 | tf_op jit(solution)/shard_map/attend_forward/pallas_call | solution.py:80
  154.2 4.2 first_norm.2
  171.8 44.2 %all-gather.4.cloned.1.call-done = bf16[8,2,16,64,256]{4,3,2,1,0:T(8,128)(2,1)} async-done(((bf16[1,2,16,64,256]{4,3,2,1,0:T(8,128)(2,1)}), bf16[8,2,16,64,256]{4,3,2,1,0:T(8,128)(2,1)}) %all-gather.4.cloned.1.call-update) | async-done | bytes 8388624 | tf_op jit(solution)/shard_map/all_gather | solution.py:724
  216.0 30.7 %feed_forward.1 = (bf16[2048,2048]{1,0:T(8,128)(2,1)}, bf16[2048,2048]{1,0:T(8,128)(2,1)}, f32[1024,1024]{1,0:T(8,128)}, bf16[1024,1024]{1,0:T(8,128)(2,1)}) custom-call(bf16[512,1024]{1,0:T(8,128)(2,1)} %copy-done.24, bf16[512,1024]{1,0:T(8,128)(2,1)} %copy-done.27, bf16[512,1024]{1,0:T(8,128)(2,1)} %copy-done.58, ...), custom_call_target="tpu_custom_call" | custom-call | flops 17179869184 | bytes 29360128 | tf_op jit(solution)/shard_map/feed_forward/pallas_call | solution.py:260
  246.8 4.4 collective-permute-done.15.far
  259.0 4.4 second_norm.2
  269.3 52.1 %feed_backward.1 = (bf16[16,16,64,256]{3,2,1,0:T(8,128)(2,1)}, f32[1,2048]{1,0:T(1,128)}, f32[1024,1024]{1,0:T(8,128)}, bf16[1024,1024]{1,0:T(8,128)(2,1)}) custom-call(bf16[512,1024]{1,0:T(8,128)(2,1)} %copy-done.31, bf16[512,1024]{1,0:T(8,128)(2,1)} %copy-done.30, bf16[512,1024]{1,0:T(8,128)(2,1)} %copy-done.60, bf16[512,1024]{1,0:T(8,128)(2,1)} %copy-done.59, ...), custom_call_target="tpu_custom_call" | custom-call | flops 34359738368 | bytes 54525952 | tf_op jit(solution)/shard_map/feed_backward/pallas_call | solution.py:340
  326.0 7.4 %first_back.2 = (f32[512,1024]{1,0:T(8,128)S(1)}, bf16[512,1024]{1,0:T(8,128)(2,1)S(1)}, bf16[4,128,256]{2,1,0:T(8,128)(2,1)S(1)}, bf16[4,128,256]{2,1,0:T(8,128...) custom-call(s32[1]{0:T(128)} %bitcast.place, f32[512,1024]{1,0:T(8,128)} %copy-done.4, ...), custom_call_target="tpu_custom_call" | custom-call | flops 1073741824 | bytes 8388608 | tf_op jit(solution)/shard_map/first_back/pallas_call | solution.py:404
  337.0 6.4 %first_back.3 = (f32[512,1024]{1,0:T(8,128)S(1)}, bf16[512,1024]{1,0:T(8,128)(2,1)S(1)}, bf16[4,128,256]{2,1,0:T(8,128)(2,1)S(1)}, bf16[4,128,256]{2,1,0:T(8,128...) custom-call(s32[1]{0:T(128)} %bitcast.place, ...), custom_call_target="tpu_custom_call" | custom-call | flops 1073741824 | bytes 8388608 | tf_op jit(solution)/shard_map/first_back/pallas_call | solution.py:404
  357.9 27.8 %attend_backward.2 = (bf16[4,512,768]{2,1,0:T(8,128)(2,1)}, f32[4,128,1024]{2,1,0:T(8,128)}, bf16[4,128,1024]{2,1,0:T(8,128)(2,1)}, f32[4,128,1024]{2,1,0:T(8,12...) custom-call(bf16[4,512,768]{2,1,0:T(8,128)(2,1)} %get-tuple-element.106.saved, ...), custom_call_target="tpu_custom_call" | custom-call | flops 13957595136 | bytes 22020096 | tf_op jit(solution)/shard_map/attend_backward/pallas_call | solution.py:155
  388.2 27.7 %attend_backward.3 = (bf16[4,512,768]{2,1,0:T(8,128)(2,1)}, f32[4,128,1024]{2,1,0:T(8,128)}, bf16[4,128,1024]{2,1,0:T(8,128)(2,1)}, f32[4,128,1024]{2,1,0:T(8,12...) custom-call(bf16[4,512,768]{2,1,0:T(8,128)(2,1)} %get-tuple-element.118.saved, ...), custom_call_target="tpu_custom_call" | custom-call | flops 13957595136 | bytes 22020096 | tf_op jit(solution)/shard_map/attend_backward/pallas_call | solution.py:155
  424.4 5.7 %fusion.15 = f32[1024,768,1]{1,0,2:T(8,128)S(1)} fusion(bf16[4,512,1024]{2,1,0:T(8,128)(2,1)S(1)} %copy-done.61, bf16[4,512,768]{2,1,0:T(8,128)(2,1)} %get-tuple-element.128), kind=kOutput, calls=%fused_computation.107 | convolution fusion | flops 3221225472 | bytes 10485760 | tf_op jit(solution)/shard_map/dot_general | solution.py:26
  430.7 4.7 fusion
  445.3 15.5 %collective-permute-done.31 = bf16[4,128,768]{2,1,0:T(8,128)(2,1)S(1)} collective-permute-done((bf16[4,128,768]{2,1,0:T(8,128)(2,1)S(1)}, bf16[4,128,768]{2,1,0:T(8,128)(2,1)S(1)}, u32[]{:S(2)}, u32[]{:S(2)}) %collective-permute-start.31) | collective-permute-done | bytes 786464 | tf_op jit(solution)/shard_map/ppermute | solution.py:611
  466.4 8.5 %collective-permute-done.32 = bf16[2,128,768]{2,1,0:T(8,128)(2,1)S(1)} collective-permute-done((bf16[2,128,768]{2,1,0:T(8,128)(2,1)S(1)}, bf16[2,128,768]{2,1,0:T(8,128)(2,1)S(1)}, u32[]{:S(2)}, u32[]{:S(2)}) %collective-permute-start.32) | collective-permute-done | bytes 393248 | tf_op jit(solution)/shard_map/ppermute | solution.py:611
  483.1 5.1 collective-permute-done.33
  503.3 15.4 %all-to-all-done.1 = f32[4,32,3,1,256]{4,1,3,2,0:T(8,128)S(1)} async-done(((f32[4,32,3,1,256]{4,1,3,2,0:T(8,128)}), f32[4,32,3,1,256]{4,1,3,2,0:T(8,128)S(1)}, u32[]{:S(2)}, u32[]{:S(2)}) %all-to-all-start.1) | async-done | bytes 393248 | tf_op jit(solution)/shard_map/all_to_all | solution.py:831
  522.1 4.6 collective-permute-done.43
  532.2 18.8 %collective-permute-done.44 = bf16[16,64,256]{2,1,0:T(8,128)(2,1)S(1)} collective-permute-done((bf16[16,64,256]{2,1,0:T(8,128)(2,1)S(1)}, bf16[16,64,256]{2,1,0:T(8,128)(2,1)S(1)}, u32[]{:S(2)}, u32[]{:S(2)}) %collective-permute-start.44) | collective-permute-done | bytes 524320 | tf_op jit(solution)/shard_map/ppermute | solution.py:611
  (370 shorter events, 162.7 us)
Async XLA Ops:
  24.6 75.3 %all-gather.6.cloned.1.call-start = ((), (), s32[]{:S(2)}) async-start(), calls=%async_computation.5 | async-start | bytes 3317760 | tf_op jit(solution)/shard_map/all_gather | solution.py:675
  31.4 184.6 %all-gather.4.cloned.1.call-start = ((), (), s32[]{:S(2)}) async-start(), calls=%async_computation.3 | async-start | bytes 9437184 | tf_op jit(solution)/shard_map/all_gather | solution.py:724
  50.4 470.5 %reduce-scatter.2.cloned.1.call-start = ((), (), s32[]{:S(2)}) async-start(), calls=%async_computation.4 | async-start | bytes 9437184 | tf_op jit(solution)/shard_map/reduce_scatter | solution.py:766
  51.0 47.1 %collective-permute-start.1 = (bf16[8,128,1024]{2,1,0:T(8,128)(2,1)S(1)}, bf16[8,128,1024]{2,1,0:T(8,128)(2,1)}, u32[]{:S(2)}, u32[]{:S(2)}) collective-permute-start(bf16[8,128,1024]{2,1,0:T(8,128)(2,1)S(1)} %copy-done.2), channel_id=1, source_target_pairs={{0,2},{1,3},{2,0},{3,1},{4,6},{5,7},{6,4},{7,5},{8,10},{9,11},{10,... | collective-permute-start | bytes 6291464 | tf_op jit(solution)/shard_map/ppermute | solution.py:591
  51.4 61.4 %collective-permute-start = (bf16[8,128,1024]{2,1,0:T(8,128)(2,1)S(1)}, bf16[8,128,1024]{2,1,0:T(8,128)(2,1)}, u32[]{:S(2)}, u32[]{:S(2)}) collective-permute-start(bf16[8,128,1024]{2,1,0:T(8,128)(2,1)S(1)} %copy-done.2), channel_id=1, source_target_pairs={{0,1},{1,0},{2,3},{3,2},{4,5},{5,4},{6,7},{7,6},{8,9},{9,8},{10,11... | collective-permute-start | bytes 6291464 | tf_op jit(solution)/shard_map/ppermute | solution.py:594
  112.2 37.0 %collective-permute-start.7 = (bf16[16,32,1024]{2,1,0:T(8,128)(2,1)}, bf16[16,32,1024]{2,1,0:T(8,128)(2,1)}, u32[]{:S(2)}, u32[]{:S(2)}) collective-permute-start(bf16[16,32,1024]{2,1,0:T(8,128)(2,1)} %bitcast.102), channel_id=1, source_target_pairs={{0,1},{1,0},{2,3},{3,2},{4,5},{5,4},{6,7},{7,6},{8,9},{9,8},{10,11... | collective-permute-start | bytes 3145736 | tf_op jit(solution)/shard_map/ppermute | solution.py:594
  128.6 25.5 %collective-permute-start.5 = (bf16[4,128,256]{2,1,0:T(8,128)(2,1)}, bf16[4,128,256]{2,1,0:T(8,128)(2,1)}, u32[]{:S(2)}, u32[]{:S(2)}) collective-permute-start(bf16[4,128,256]{2,1,0:T(8,128)(2,1)} %get-tuple-element.83), channel_id=1, source_target_pairs={{0,2},{1,3},{2,0},{3,1},{4,6},{5,7},{6,4},{7,5},{8,10},{9,11},{10,... | collective-permute-start | bytes 786440 | tf_op jit(solution)/shard_map/ppermute | solution.py:591
  129.1 25.1 %collective-permute-start.6 = (bf16[4,128,256]{2,1,0:T(8,128)(2,1)}, bf16[4,128,256]{2,1,0:T(8,128)(2,1)}, u32[]{:S(2)}, u32[]{:S(2)}) collective-permute-start(bf16[4,128,256]{2,1,0:T(8,128)(2,1)} %get-tuple-element.84), channel_id=1, source_target_pairs={{0,3},{1,2},{2,1},{3,0},{4,7},{5,6},{6,5},{7,4},{8,11},{9,10},{10,... | collective-permute-start | bytes 786440 | tf_op jit(solution)/shard_map/ppermute | solution.py:591
  335.2 22.7 %collective-permute-start.19 = (bf16[4,128,256]{2,1,0:T(8,128)(2,1)}, bf16[4,128,256]{2,1,0:T(8,128)(2,1)}, u32[]{:S(2)}, u32[]{:S(2)}) collective-permute-start(bf16[4,128,256]{2,1,0:T(8,128)(2,1)} %get-tuple-element.108), channel_id=1, source_target_pairs={{0,1},{1,0},{2,3},{3,2},{4,5},{5,4},{6,7},{7,6},{8,9},{9,8},{10,11... | collective-permute-start | bytes 786440 | tf_op jit(solution)/shard_map/ppermute | solution.py:591
  335.4 22.5 %collective-permute-start.20 = (bf16[4,128,256]{2,1,0:T(8,128)(2,1)}, bf16[4,128,256]{2,1,0:T(8,128)(2,1)}, u32[]{:S(2)}, u32[]{:S(2)}) collective-permute-start(bf16[4,128,256]{2,1,0:T(8,128)(2,1)} %get-tuple-element.109), channel_id=1, source_target_pairs={{0,2},{1,3},{2,0},{3,1},{4,6},{5,7},{6,4},{7,5},{8,10},{9,11},{10,... | collective-permute-start | bytes 786440 | tf_op jit(solution)/shard_map/ppermute | solution.py:591
  347.1 39.6 %collective-permute-start.25 = (bf16[4,128,256]{2,1,0:T(8,128)(2,1)}, bf16[4,128,256]{2,1,0:T(8,128)(2,1)}, u32[]{:S(2)}, u32[]{:S(2)}) collective-permute-start(bf16[4,128,256]{2,1,0:T(8,128)(2,1)} %copy-done.37), channel_id=1, source_target_pairs={{0,1},{1,0},{2,3},{3,2},{4,5},{5,4},{6,7},{7,6},{8,9},{9,8},{10,11... | collective-permute-start | bytes 786440 | tf_op jit(solution)/shard_map/ppermute | solution.py:591
  347.7 39.0 %collective-permute-start.26 = (bf16[4,128,256]{2,1,0:T(8,128)(2,1)}, bf16[4,128,256]{2,1,0:T(8,128)(2,1)}, u32[]{:S(2)}, u32[]{:S(2)}) collective-permute-start(bf16[4,128,256]{2,1,0:T(8,128)(2,1)} %copy-done.36), channel_id=1, source_target_pairs={{0,2},{1,3},{2,0},{3,1},{4,6},{5,7},{6,4},{7,5},{8,10},{9,11},{10,... | collective-permute-start | bytes 786440 | tf_op jit(solution)/shard_map/ppermute | solution.py:591
  357.8 28.9 %collective-permute-start.27 = (bf16[4,128,256]{2,1,0:T(8,128)(2,1)}, bf16[4,128,256]{2,1,0:T(8,128)(2,1)}, u32[]{:S(2)}, u32[]{:S(2)}) collective-permute-start(bf16[4,128,256]{2,1,0:T(8,128)(2,1)} %get-tuple-element.122), channel_id=1, source_target_pairs={{0,3},{1,2},{2,1},{3,0},{4,7},{5,6},{6,5},{7,4},{8,11},{9,10},{10,... | collective-permute-start | bytes 786440 | tf_op jit(solution)/shard_map/ppermute | solution.py:591
  422.7 39.8 %collective-permute-start.39 = (bf16[4,2,2,32,1024]{4,3,0,1,2:T(8,128)(2,1)}, bf16[4,2,2,32,1024]{4,3,0,1,2:T(8,128)(2,1)}, u32[]{:S(2)}, u32[]{:S(2)}) collective-permute-start(bf16[4,2,2,32,1024]{4,3,0,1,2:T(8,128)(2,1)} %bitcast.175), channel_id=1, source_target_pairs={{0,1},{1,0},{2,3},{3,2},{4,5},{5,4},{6,7},{7,6},{8,9},{9,8},{10,11... | collective-permute-start | bytes 3145736 | tf_op jit(solution)/shard_map/ppermute | solution.py:611
  436.7 24.1 %collective-permute-start.31 = (bf16[4,128,768]{2,1,0:T(8,128)(2,1)S(1)}, bf16[4,128,768]{2,1,0:T(8,128)(2,1)S(1)}, u32[]{:S(2)}, u32[]{:S(2)}) collective-permute-start(bf16[4,128,768]{2,1,0:T(8,128)(2,1)S(1)} %dynamic-slice_bitcast_fusion), channel_id=1, source_target_pairs={{0,4},{4,0},{1,5},{5,1},{2,6},{6,2},{3,7},{7,3},{8,12},{12,8},{9,1... | collective-permute-start | bytes 2359304 | tf_op jit(solution)/shard_map/ppermute | solution.py:611
  443.2 85.4 %collective-permute-start.22 = (bf16[4,128,1024]{2,1,0:T(8,128)(2,1)}, bf16[4,128,1024]{2,1,0:T(8,128)(2,1)}, u32[]{:S(2)}, u32[]{:S(2)}) collective-permute-start(bf16[4,128,1024]{2,1,0:T(8,128)(2,1)} %get-tuple-element.112), channel_id=1, source_target_pairs={{0,1},{1,0},{2,3},{3,2},{4,5},{5,4},{6,7},{7,6},{8,9},{9,8},{10,11... | collective-permute-start | bytes 3145736 | tf_op jit(solution)/shard_map/ppermute | solution.py:594
  443.2 38.0 %collective-permute-start.23 = (bf16[4,128,1024]{2,1,0:T(8,128)(2,1)S(1)}, bf16[4,128,1024]{2,1,0:T(8,128)(2,1)S(1)}, u32[]{:S(2)}, u32[]{:S(2)}) collective-permute-start(bf16[4,128,1024]{2,1,0:T(8,128)(2,1)S(1)} %copy-done.23), channel_id=1, source_target_pairs={{0,1},{1,0},{2,3},{3,2},{4,5},{5,4},{6,7},{7,6},{8,9},{9,8},{10,11... | collective-permute-start | bytes 3145736 | tf_op jit(solution)/shard_map/ppermute | solution.py:594
  444.7 106.7 %collective-permute-start.28 = (bf16[4,128,1024]{2,1,0:T(8,128)(2,1)}, bf16[4,128,1024]{2,1,0:T(8,128)(2,1)}, u32[]{:S(2)}, u32[]{:S(2)}) collective-permute-start(bf16[4,128,1024]{2,1,0:T(8,128)(2,1)} %get-tuple-element.124), channel_id=1, source_target_pairs={{0,1},{1,0},{2,3},{3,2},{4,5},{5,4},{6,7},{7,6},{8,9},{9,8},{10,11... | collective-permute-start | bytes 3145736 | tf_op jit(solution)/shard_map/ppermute | solution.py:594
  474.9 23.2 %collective-permute-start.29 = (bf16[4,128,1024]{2,1,0:T(8,128)(2,1)S(1)}, bf16[4,128,1024]{2,1,0:T(8,128)(2,1)}, u32[]{:S(2)}, u32[]{:S(2)}) collective-permute-start(bf16[4,128,1024]{2,1,0:T(8,128)(2,1)S(1)} %copy-done.21), channel_id=1, source_target_pairs={{0,1},{1,0},{2,3},{3,2},{4,5},{5,4},{6,7},{7,6},{8,9},{9,8},{10,11... | collective-permute-start | bytes 3145736 | tf_op jit(solution)/shard_map/ppermute | solution.py:594
  488.2 40.4 %collective-permute-start.24 = (bf16[4,128,1024]{2,1,0:T(8,128)(2,1)}, bf16[4,128,1024]{2,1,0:T(8,128)(2,1)}, u32[]{:S(2)}, u32[]{:S(2)}) collective-permute-start(bf16[4,128,1024]{2,1,0:T(8,128)(2,1)} %add_convert_fusion.1), channel_id=1, source_target_pairs={{0,2},{1,3},{2,0},{3,1},{4,6},{5,7},{6,4},{7,5},{8,10},{9,11},{10,... | collective-permute-start | bytes 3145736 | tf_op jit(solution)/shard_map/ppermute | solution.py:591
  492.6 26.1 %all-to-all-start.1 = ((f32[4,32,3,1,256]{4,1,3,2,0:T(8,128)}), f32[4,32,3,1,256]{4,1,3,2,0:T(8,128)S(1)}, u32[]{:S(2)}, u32[]{:S(2)}) async-start(f32[4,32,3,1,256]{4,1,3,2,0:T(8,128)} %copy.175), calls=%async_computation.1 | async-start | bytes 786432 | tf_op jit(solution)/shard_map/all_to_all | solution.py:831
  498.1 21.8 %collective-permute-start.42 = (bf16[2,32,1024]{2,1,0:T(8,128)(2,1)}, bf16[2,32,1024]{2,1,0:T(8,128)(2,1)}, u32[]{:S(2)}, u32[]{:S(2)}) collective-permute-start(bf16[2,32,1024]{2,1,0:T(8,128)(2,1)} %dynamic-slice_bitcast_fusion.7), channel_id=1, source_target_pairs={{0,8},{8,0},{16,24},{24,16},{1,9},{9,1},{17,25},{25,17},{2,10},{10... | collective-permute-start | bytes 393224 | tf_op jit(solution)/shard_map/ppermute | solution.py:611
  501.3 50.1 %collective-permute-start.30 = (bf16[4,128,1024]{2,1,0:T(8,128)(2,1)}, bf16[4,128,1024]{2,1,0:T(8,128)(2,1)}, u32[]{:S(2)}, u32[]{:S(2)}) collective-permute-start(bf16[4,128,1024]{2,1,0:T(8,128)(2,1)} %add_convert_fusion), channel_id=1, source_target_pairs={{0,2},{1,3},{2,0},{3,1},{4,6},{5,7},{6,4},{7,5},{8,10},{9,11},{10,... | collective-permute-start | bytes 3145736 | tf_op jit(solution)/shard_map/ppermute | solution.py:591
  526.7 24.4 %collective-permute-start.44 = (bf16[16,64,256]{2,1,0:T(8,128)(2,1)S(1)}, bf16[16,64,256]{2,1,0:T(8,128)(2,1)S(1)}, u32[]{:S(2)}, u32[]{:S(2)}) collective-permute-start(bf16[16,64,256]{2,1,0:T(8,128)(2,1)S(1)} %dynamic-slice_bitcast_fusion.1), channel_id=1, source_target_pairs={{0,2},{2,0},{1,3},{3,1},{4,6},{6,4},{5,7},{7,5},{8,10},{10,8},{9,1... | collective-permute-start | bytes 1572872 | tf_op jit(solution)/shard_map/ppermute | solution.py:611
  (89 other events, 603.6 us)
Sparse Core Ops, SparseCore 0:
  31.5 58.6 all-gather.5
  92.4 123.5 all-gather.3
  321.6 147.0 reduce-scatter.1

commit v5 on v4

--- a/solution.py
+++ b/solution.py
@@ -36,6 +36,29 @@
     return pl.BlockSpec(shape, lambda i: (i,) + (0,) * (len(shape) - 1))
 
 
+def flat(block):
+    wide = block.shape[-1]
+    if block.shape[-2] % 16:
+        return block.astype(F32).reshape(-1, wide).astype(BF16)
+    return block.reshape(-1, wide)
+
+
+def hold_kernel(source, *refs):
+    refs[-1][...] = source[...]
+
+
+def hold(array, after):
+    return pl.pallas_call(
+        hold_kernel,
+        grid=(1,),
+        in_specs=[resident(array.shape)] + [ELSEWHERE] * len(after),
+        out_specs=resident(array.shape),
+        out_shape=jax.ShapeDtypeStruct(array.shape, array.dtype),
+        compiler_params=pltpu.CompilerParams(vmem_limit_bytes=16 * MIB),
+        name="hold",
+    )(array, *after)
+
+
 def softmax_down(scores, allowed):
     scores = jnp.where(allowed, scores, -1e30)
     top = jnp.max(scores, axis=0, keepdims=True)
@@ -49,17 +72,21 @@
     return (lane // HEAD_DIM == head).astype(F32)
 
 
-def attend_kernel(late, t0, t1, t2, t3, weight, bias, seg_key, seg_query, *refs):
+def attend_kernel(late, t0, t1, t2, t3, wq, wk, wv, bias, seg_key, seg_query, *refs):
     m0, m1, m2, m3, kept, saved = refs[late:]
     part = t0.shape[1]
     rows = jnp.concatenate([t[0] for t in (t0, t1, t2, t3)], axis=0)
     kept[0] = rows
-    project = dot(rows, weight[...]) + bias[...]
-    saved[0] = project.astype(BF16)
-    width = project.shape[1] // 3
-    queries = (project[:, :width].astype(BF16).astype(F32) * HEAD_DIM**-0.5).astype(BF16)
-    keys = project[:, width : 2 * width].astype(BF16).astype(F32)
-    values_t = jnp.transpose(project[:, 2 * width :]).astype(BF16)
+    width = wq.shape[2]
+    queries, keys, values = [
+        dot(rows, flat(w[...])) + bias[:, i * width : (i + 1) * width]
+        for i, w in enumerate((wq, wk, wv))
+    ]
+    for i, part_of in enumerate((queries, keys, values)):
+        saved[0, :, i * width : (i + 1) * width] = part_of.astype(BF16)
+    queries = (queries.astype(BF16).astype(F32) * HEAD_DIM**-0.5).astype(BF16)
+    keys = keys.astype(BF16).astype(F32)
+    values_t = jnp.transpose(values).astype(BF16)
     allowed = seg_key[0] == seg_query[0]
     mixed = []
     for head in range(width // HEAD_DIM):
@@ -72,17 +99,25 @@
         out[0] = mixed[index * part : (index + 1) * part]
 
 
+def project_specs(weight, depth):
+    shape = (weight.shape[0], depth // weight.shape[0], weight.shape[2])
+    return [
+        pl.BlockSpec(shape, lambda i, j=j: (0, j, 0), pipeline_mode=pl.Buffered(1))
+        for j in range(3)
+    ]
+
+
 def attend(tokens, weight, bias, seg_key, seg_query, first, after):
     count, part, depth = tokens[0].shape
     count = count // CHUNKS
-    wide = weight.shape[1]
+    wide = bias.shape[1]
     length = 4 * part
     return pl.pallas_call(
         functools.partial(attend_kernel, len(after)),
         grid=(count,),
         in_specs=[pl.BlockSpec((1, part, depth), lambda i: (i + first, 0, 0))] * 4
+        + project_specs(weight, depth)
         + [
-            resident((depth, wide)),
             resident((1, wide)),
             by_row((1, length, 1)),
             by_row((1, 1, length)),
@@ -102,10 +137,10 @@
             transcendentals=count * length * length * wide // (3 * HEAD_DIM),
         ),
         name="attend_forward",
-    )(*tokens, weight, bias, seg_key, seg_query, *after)
-
-
-def attend_back_kernel(late, saved, g0, g1, g2, g3, weight, seg_key, seg_query, *refs):
+    )(*tokens, weight, weight, weight, bias, seg_key, seg_query, *after)
+
+
+def attend_back_kernel(late, saved, g0, g1, g2, g3, wq, wk, wv, seg_key, seg_query, *refs):
     grad_project, r0, r1, r2, r3, sums = refs[late:]
     part = g0.shape[1]
     width = saved.shape[2] // 3
@@ -137,28 +172,28 @@
             grad_keys = jnp.where(here, keys_term, grad_keys)
             grad_values = jnp.where(here, values_term, grad_values)
     grad_queries = jnp.transpose(jnp.concatenate(grad_queries, axis=0))
-    whole = jnp.concatenate(
-        [grad_queries.astype(BF16), grad_keys.astype(BF16), grad_values.astype(BF16)], axis=1
-    )
-    grad_project[0] = whole
-    sums[0] = jnp.sum(whole.astype(F32), axis=0, keepdims=True)
+    terms = [grad_queries.astype(BF16), grad_keys.astype(BF16), grad_values.astype(BF16)]
+    for i, term in enumerate(terms):
+        grad_project[0, :, i * width : (i + 1) * width] = term
+        sums[0, :, i * width : (i + 1) * width] = jnp.sum(
+            term.astype(F32), axis=0, keepdims=True
+        )
+    rows = sum(dot(term, flat(w[...]), (1, 1)) for term, w in zip(terms, (wq, wk, wv)))
     for index, out in enumerate((r0, r1, r2, r3)):
-        out[0] = dot(whole[index * part : (index + 1) * part], weight[...], (1, 1)).astype(
-            out.dtype
-        )
+        out[0] = rows[index * part : (index + 1) * part].astype(out.dtype)
 
 
 def attend_back(saved, grads, weight, seg_key, seg_query, after):
     count, part, width = grads[0].shape
-    depth, wide = weight.shape
+    depth, wide = width * 4, width * 3
     length = 4 * part
     return pl.pallas_call(
         functools.partial(attend_back_kernel, len(after)),
         grid=(count,),
         in_specs=[by_row((1, length, wide))]
         + [by_row((1, part, width))] * 4
+        + project_specs(weight, depth)
         + [
-            resident((depth, wide)),
             by_row((1, length, 1)),
             by_row((1, 1, length)),
         ]
@@ -176,18 +211,11 @@
             transcendentals=count * length * length * wide // (3 * HEAD_DIM),
         ),
         name="attend_backward",
-    )(saved, *grads, weight, seg_key, seg_query, *after)
+    )(saved, *grads, weight, weight, weight, seg_key, seg_query, *after)
 
 
 def column(shape):
     return pl.BlockSpec(shape, lambda i: (0, i))
-
-
-def flat(block):
-    wide = block.shape[-1]
-    if block.shape[-2] % 16:
-        return block.astype(F32).reshape(-1, wide).astype(BF16)
-    return block.reshape(-1, wide)
 
 
 def expand_piece(ref):
@@ -651,41 +679,38 @@
     vector_count = 8 * share + expand_bias.shape[0]
     blocks = project_weight.reshape(share, 3, ctx_size, lanes)
     own_vectors = jnp.concatenate(vectors)
-    below = 16 * -(-ctx_size * vector_count // (48 * lanes))
+    vector_row = jnp.pad(own_vectors, (0, 3 * lanes - vector_count)).reshape(1, 3, 1, lanes)
     held = jnp.concatenate(
         [
-            jnp.moveaxis(blocks, 2, 0).reshape(ctx_size, -1),
-            jnp.broadcast_to(own_vectors, (ctx_size, vector_count)),
-        ],
-        axis=1,
-    )
-    held = lax.all_to_all(held, CTX, 0, 0, tiled=True)
+            blocks,
+            jnp.broadcast_to(vector_row, (1, 3, ctx_size, lanes)),
+            jnp.zeros((15, 3, ctx_size, lanes), BF16),
+        ]
+    )
+    held = lax.all_to_all(held, CTX, 2, 0, tiled=False)
     sent, held = lax.optimization_barrier((tokens, held))
     across = hop(sent, 2)
     gathered = (tokens, swap(sent), across, swap(across))
-    mine = held[:, : share * 3 * lanes].reshape(ctx_size * share, 3 * lanes)
-    vector_rows = jnp.pad(
-        held[:, share * 3 * lanes :].reshape(-1),
-        (0, below * 3 * lanes - ctx_size * vector_count),
-    ).reshape(below, 3 * lanes)
-    out_rows = share * width // (3 * lanes)
-    out_pad = -out_rows % 16
-    out_flat = jnp.pad(output_weight.reshape(-1), (0, 3 * lanes * (out_rows + out_pad) - share * width))
-    both_out = widen(out_flat.reshape(-1, 3 * lanes), "x")
+    mine = jnp.moveaxis(held[:, :share], 2, 0).reshape(-1, lanes)
+    vector_rows = held[:, share].reshape(ctx_size, 3 * lanes)[:, :vector_count].reshape(-1)
+    vector_rows = jnp.pad(vector_rows, (0, 16 * lanes - vector_rows.shape[0])).reshape(16, lanes)
+    out_pieces = jnp.swapaxes(output_weight.reshape(share, ctx_size, lanes), 0, 1)
     whole_project = lax.all_gather(
-        jnp.concatenate([mine, vector_rows, both_out.reshape(-1, 3 * lanes)]), SEQ, axis=0
-    )
-    first_rows = ctx_size * share + below
-    full_project = whole_project[:, : ctx_size * share].reshape(width, 3 * lanes)
-    out_half = (
-        whole_project[:, first_rows:]
-        .reshape(chips, -1)[:, : share * width]
-        .reshape(chips, share, width)
-    )
+        jnp.concatenate(
+            [mine, vector_rows, widen(out_pieces.reshape(-1, lanes), "x").reshape(-1, lanes)]
+        ),
+        SEQ,
+        axis=0,
+    )
+    first_rows = mine.shape[0]
+    full_project = whole_project
+    out_half = jnp.swapaxes(
+        whole_project[:, first_rows + 16 :].reshape(chips, ctx_size, share, lanes), 1, 2
+    ).reshape(chips, share, width)
     full_output = by_core(out_half, swap(out_half), 1).reshape(ctx_size, lanes, width)
     packed = (
-        whole_project[:, ctx_size * share : first_rows]
-        .reshape(-1, below * 3 * lanes)[:, : ctx_size * vector_count]
+        whole_project[:, first_rows : first_rows + 16]
+        .reshape(-1, 16 * lanes)[:, : ctx_size * vector_count]
         .reshape(everyone, vector_count)
         .astype(F32)
     )
@@ -721,6 +746,7 @@
             ).reshape(-1, 2 * share, PIECE),
         ]
     )
+    own_pieces = hold(own_pieces, [across])
     weights = lax.all_gather(widen(own_pieces, "x"), SEQ, axis=0).reshape(
         chips, -1, 2 * share, PIECE
     )
@@ -798,6 +824,8 @@
 
     project_parts = []
     work_parts = []
+    across_sums = []
+    work_hops = []
     sum_parts = []
     for index in range(CHUNKS):
         at = slice(index * seq_count // CHUNKS, (index + 1) * seq_count // CHUNKS)
@@ -807,14 +835,12 @@
             full_project,
             seg_key[at],
             seg_query[at],
-            [],
+            across_sums[:index],
         )
-        across = r2 + swap(r3).astype(F32)
+        across_sums.append((r2 + swap(r3).astype(F32)).astype(BF16))
+        work_hops.append(hop(across_sums[index], 2))
         work_parts.append(
-            grad_hidden[index]
-            + r0
-            + swap(r1).astype(F32)
-            + hop(across.astype(BF16), 2).astype(F32)
+            grad_hidden[index] + r0 + swap(r1).astype(F32) + work_hops[index].astype(F32)
         )
         project_parts.append(grad_part)
         sum_parts.append(sums)
@@ -823,11 +849,11 @@
         for all_rows, grad_part in zip(kept_rows, project_parts)
     )
     grad_work = jnp.concatenate(work_parts, axis=0)
-    project_owned = z_scatter(
-        halve(
-            project_grad.astype(BF16).reshape(sizes["z"], 2, ctx_size * share, 3 * lanes), 1, "y"
-        )
-    )
+    project_grad = hold(project_grad.astype(BF16), work_hops[:1])
+    project_half = halve(
+        project_grad.reshape(sizes["z"], 2, ctx_size * share, 3 * lanes), 1, "y"
+    )
+    project_owned = z_scatter(hold(project_half.astype(BF16), work_hops[1:]))
     project_owned = lax.all_to_all(
         project_owned.reshape(ctx_size, share, 3, lanes), CTX, 0, 2, tiled=False
     ).reshape(share, 3 * width)

time: 573 us -> 556 us (0.970)
  waiting for transfers between devices: 197 us -> 187 us
  Pallas kernels: 203 us -> 196 us
    ppermute x15, waiting for transfers between devices: 48.6 us -> 85.3 us  [hop(): return lax.ppermute(array, CTX, [(i, i ^ step) for i in range(ctx_size)])]
    ppermute x16, waiting for transfers between devices: 71.6 us -> 38.4 us  [trade(): lax.ppermute(array, name, [(i, i ^ step) for i in range(sizes[name])])]
    all_to_all x1, waiting for transfers between devices: 15.4 us -> 0.01 us  [on_device(): lax.all_to_all(project_owned.reshape(ctx_size, share, 3, lanes), CTX, 0,...]
    all_gather x1, waiting for transfers between devices: 44.2 us -> 50.9 us  [on_device(): lax.all_gather(widen(own_pieces, 'x'), SEQ, axis=0)]
    pallas_call x2, Pallas kernels: 55.5 us -> 49.3 us  [attend_back(): pl.pallas_call(functools.partial(attend_back_kernel, len(after)), grid=(c...]
    unnamed x137 -> x128, local copies, waits for them, and re-layouts: 35.5 us -> 32.3 us
  transfers between devices with their start and end apart: 51 -> 51, of which waited for: 19 -> 21; matrix products, arithmetic and copies ran while one was open for 14% -> 12% of each run, Pallas kernels for 20% -> 20%
where the time goes in v5:
time: 556 us; the launch traced here: 551 us
  Pallas kernels  196 us (35%)
  waiting for transfers between devices  187 us (34%)
  local copies, waits for them, and re-layouts  71.1 us (13%)
  starting transfers between devices  43.2 us (8%)
  other arithmetic  22.6 us (4%)
  between operations  15.1 us (3%)
  matrix products  14.9 us (3%)
    ppermute x15, waiting for transfers between devices, hop(): return lax.ppermute(array, CTX, [(i, i ^ step) for i in range(ctx_size)])  85.3 us
    pallas_call x1, Pallas kernels, feed_back(): pl.pallas_call(feed_back_kernel, grid=(hidden // PIECE,), in_specs=[resid...  52.1 us
    all_gather x1, waiting for transfers between devices, on_device(): lax.all_gather(widen(own_pieces, 'x'), SEQ, axis=0)  50.9 us
    pallas_call x2, Pallas kernels, attend_back(): pl.pallas_call(functools.partial(attend_back_kernel, len(after)), grid=(c...  49.3 us
    ppermute x16, waiting for transfers between devices, trade(): lax.ppermute(array, name, [(i, i ^ step) for i in range(sizes[name])])  38.4 us
    unnamed x128, local copies, waits for them, and re-layouts  32.3 us
    pallas_call x2, Pallas kernels, attend(): pl.pallas_call(functools.partial(attend_kernel, len(after)), grid=(count,...  31.6 us
    pallas_call x1, Pallas kernels, feed(): pl.pallas_call(feed_kernel, grid=(hidden // wide,), in_specs=[resident((b...  30.8 us
  transfers between devices with their start and end apart: 51, of which 21 were waited for; matrix products, arithmetic and copies ran while one was open for 12% of the time, Pallas kernels for 20%

profile of v5, /device:TPU:0, one launch (start us, length us, event | category | flops | bytes accessed | tf_op | source)
XLA Modules:
  0.0 550.8 jit_solution(17138363440965415052)
XLA Ops:
  7.2 6.1 %concatenate.67 = bf16[384]{0:T(512)(128)(2,1)S(1)} concatenate(bf16[32]{0:T(256)(128)(2,1)} %param.19, bf16[32]{0:T(256)(128)(2,1)} %param.20, bf16[32]{0:T(256)(128)(2,1)} %param.22, bf16[32]{0:T(256)(128)(2,1)} %param.23, bf16[32]{0:T(256)(128)(2,1)} %param.24, bf16[32]{0:T(256)(128)(2,1)} %param.28, bf16[32]{0:T(256)(128)(2,1)} %param.29, bf16[32]{0:T(256)(128)(2,1)} %param.30, ...), dimensions={0} | concatenate | bytes 1536 | tf_op jit(solution)/shard_map/concatenate | solution.py:681
  22.0 5.4 collective-permute-done.3
  32.3 43.4 %collective-permute-done.1.t2.refs_0_ = bf16[8,128,1024]{2,1,0:T(8,128)(2,1)} collective-permute-done((bf16[8,128,1024]{2,1,0:T(8,128)(2,1)S(1)}, bf16[8,128,1024]{2,1,0:T(8,128)(2,1)}, u32[]{:S(2)}, u32[]{:S(2)}) %collective-permute-start.1) | collective-permute-done | bytes 2097184 | tf_op jit(solution)/shard_map/ppermute | solution.py:619
  76.6 11.6 %collective-permute-done.14 = bf16[16,64,256]{2,1,0:T(8,128)(2,1)S(1)} collective-permute-done((bf16[16,64,256]{2,1,0:T(8,128)(2,1)S(1)}, bf16[16,64,256]{2,1,0:T(8,128)(2,1)S(1)}, u32[]{:S(2)}, u32[]{:S(2)}) %collective-permute-start.14) | collective-permute-done | bytes 524320 | tf_op jit(solution)/shard_map/ppermute | solution.py:639
  104.7 15.8 %attend_forward.2 = (bf16[4,128,256]{2,1,0:T(8,128)(2,1)S(1)}, bf16[4,128,256]{2,1,0:T(8,128)(2,1)}, bf16[4,128,256]{2,1,0:T(8,128)(2,1)}, bf16[4,128,256]{2,1,0...) custom-call(bf16[8,128,1024]{2,1,0:T(8,128)(2,1)S(1)} %copy-done.2, ...), custom_call_target="tpu_custom_call" | custom-call | flops 7515144192 | bytes 10485760 | tf_op jit(solution)/shard_map/attend_forward/pallas_call | solution.py:115
  122.4 15.8 %attend_forward.3 = (bf16[4,128,256]{2,1,0:T(8,128)(2,1)S(1)}, bf16[4,128,256]{2,1,0:T(8,128)(2,1)}, bf16[4,128,256]{2,1,0:T(8,128)(2,1)}, bf16[4,128,256]{2,1,0...) custom-call(bf16[8,128,1024]{2,1,0:T(8,128)(2,1)S(1)} %copy-done.2, ...), custom_call_target="tpu_custom_call" | custom-call | flops 7515144192 | bytes 10485760 | tf_op jit(solution)/shard_map/attend_forward/pallas_call | solution.py:115
  165.3 50.9 %all-gather.4.cloned.1.call-done = bf16[8,2,16,64,256]{4,3,2,1,0:T(8,128)(2,1)} async-done(((bf16[1,2,16,64,256]{4,3,2,1,0:T(8,128)(2,1)}), bf16[8,2,16,64,256]{4,3,2,1,0:T(8,128)(2,1)}) %all-gather.4.cloned.1.call-update) | async-done | bytes 8388624 | tf_op jit(solution)/shard_map/all_gather | solution.py:750
  216.1 30.8 %feed_forward.1 = (bf16[2048,2048]{1,0:T(8,128)(2,1)}, bf16[2048,2048]{1,0:T(8,128)(2,1)}, f32[1024,1024]{1,0:T(8,128)}, bf16[1024,1024]{1,0:T(8,128)(2,1)}) custom-call(bf16[512,1024]{1,0:T(8,128)(2,1)} %copy-done.28, bf16[512,1024]{1,0:T(8,128)(2,1)} %copy-done.29, bf16[512,1024]{1,0:T(8,128)(2,1)} %copy-done.55, bf16[512,1024]{1,0:T(8,128)(2,1)} %copy-done.56, ...), custom_call_target="tpu_custom_call" | custom-call | flops 17179869184 | bytes 29360128 | tf_op jit(solution)/shard_map/feed_forward/pallas_call | solution.py:288
  247.0 4.4 collective-permute-done.15.far
  258.3 4.4 second_norm.2
  267.7 52.1 %feed_backward.1 = (bf16[16,16,64,256]{3,2,1,0:T(8,128)(2,1)}, f32[1,2048]{1,0:T(1,128)}, f32[1024,1024]{1,0:T(8,128)}, bf16[1024,1024]{1,0:T(8,128)(2,1)}) custom-call(bf16[512,1024]{1,0:T(8,128)(2,1)} %copy-done.33, bf16[512,1024]{1,0:T(8,128)(2,1)} %copy-done.32, bf16[512,1024]{1,0:T(8,128)(2,1)} %copy-done.58, bf16[512,1024]{1,0:T(8,128)(2,1)} %copy-done.57, ...), custom_call_target="tpu_custom_call" | custom-call | flops 34359738368 | bytes 54525952 | tf_op jit(solution)/shard_map/feed_backward/pallas_call | solution.py:368
  326.6 6.1 %first_back.2 = (f32[512,1024]{1,0:T(8,128)S(1)}, bf16[512,1024]{1,0:T(8,128)(2,1)S(1)}, bf16[4,128,256]{2,1,0:T(8,128)(2,1)S(1)}, bf16[4,128,256]{2,1,0:T(8,128...) custom-call(s32[1]{0:T(128)} %bitcast.place, ...), custom_call_target="tpu_custom_call" | custom-call | flops 1073741824 | bytes 8388608 | tf_op jit(solution)/shard_map/first_back/pallas_call | solution.py:432
  336.9 7.4 %collective-permute-done.20.g2 = bf16[4,128,256]{2,1,0:T(8,128)(2,1)S(1)} collective-permute-done((bf16[4,128,256]{2,1,0:T(8,128)(2,1)S(1)}, bf16[4,128,256]{2,1,0:T(8,128)(2,1)S(1)}, u32[]{:S(2)}, u32[]{:S(2)}) %collective-permute-start.20) | collective-permute-done | bytes 262176 | tf_op jit(solution)/shard_map/ppermute | solution.py:619
  344.3 4.5 collective-permute-done.21.g3
  348.8 24.8 %attend_backward.2 = (bf16[4,512,768]{2,1,0:T(8,128)(2,1)}, f32[4,128,1024]{2,1,0:T(8,128)}, bf16[4,128,1024]{2,1,0:T(8,128)(2,1)S(1)}, f32[4,128,1024]{2,1,0:T(...) custom-call(bf16[4,512,768]{2,1,0:T(8,128)(2,1)} %get-tuple-element.106.saved, ...), custom_call_target="tpu_custom_call" | custom-call | flops 13957595136 | bytes 22020096 | tf_op jit(solution)/shard_map/attend_backward/pallas_call | solution.py:190
  376.9 5.9 %first_back.3 = (f32[512,1024]{1,0:T(8,128)S(1)}, bf16[512,1024]{1,0:T(8,128)(2,1)S(1)}, bf16[4,128,256]{2,1,0:T(8,128)(2,1)S(1)}, bf16[4,128,256]{2,1,0:T(8,128...) custom-call(s32[1]{0:T(128)} %bitcast.place, ...), custom_call_target="tpu_custom_call" | custom-call | flops 1073741824 | bytes 8388608 | tf_op jit(solution)/shard_map/first_back/pallas_call | solution.py:432
  403.6 24.5 %attend_backward.3 = (bf16[4,512,768]{2,1,0:T(8,128)(2,1)}, f32[4,128,1024]{2,1,0:T(8,128)}, bf16[4,128,1024]{2,1,0:T(8,128)(2,1)}, f32[4,128,1024]{2,1,0:T(8,12...) custom-call(bf16[4,512,768]{2,1,0:T(8,128)(2,1)} %get-tuple-element.118.saved, ...), custom_call_target="tpu_custom_call" | custom-call | flops 13957595136 | bytes 22020096 | tf_op jit(solution)/shard_map/attend_backward/pallas_call | solution.py:190
  435.6 7.2 %fusion.14 = f32[1024,768,1]{1,0,2:T(8,128)} fusion(bf16[4,512,1024]{2,1,0:T(8,128)(2,1)S(1)} %copy-done.59, bf16[4,512,768]{2,1,0:T(8,128)(2,1)} %get-tuple-element.128), kind=kOutput, calls=%fused_computation.106 | convolution fusion | flops 3221225472 | bytes 10485760 | tf_op jit(solution)/shard_map/dot_general | solution.py:26
  451.7 7.7 %fusion.source = bf16[1024,768]{1,0:T(8,128)(2,1)S(1)} fusion(f32[1024,768,1]{1,0,2:T(8,128)} %fusion.14, bf16[4,512,1024]{2,1,0:T(8,128)(2,1)} %get-tuple-element.129, bf16[4,512,768]{2,1,0:T(8,128)(2,1)} %get-tuple-element.130), kind=kOutput, calls=%fused_computation.2 | convolution fusion | flops 3222798336 | bytes 12058624 | tf_op jit(solution)/shard_map/dot_general | solution.py:26
  463.0 19.3 %collective-permute-done.24.refs_0_ = bf16[4,128,1024]{2,1,0:T(8,128)(2,1)S(1)} collective-permute-done((bf16[4,128,1024]{2,1,0:T(8,128)(2,1)S(1)}, bf16[4,128,1024]{2,1,0:T(8,128)(2,1)S(1)}, u32[]{:S(2)}, u32[]{:S(2)}) %collective-permute-start.24) | collective-permute-done | bytes 1048608 | tf_op jit(solution)/shard_map/ppermute | solution.py:619
  492.9 7.0 %collective-permute-done.31 = bf16[4,128,768]{2,1,0:T(8,128)(2,1)S(1)} collective-permute-done((bf16[4,128,768]{2,1,0:T(8,128)(2,1)S(1)}, bf16[4,128,768]{2,1,0:T(8,128)(2,1)S(1)}, u32[]{:S(2)}, u32[]{:S(2)}) %collective-permute-start.31) | collective-permute-done | bytes 786464 | tf_op jit(solution)/shard_map/ppermute | solution.py:639
  500.2 6.6 %collective-permute-done.30.refs_0_ = bf16[4,128,1024]{2,1,0:T(8,128)(2,1)S(1)} collective-permute-done((bf16[4,128,1024]{2,1,0:T(8,128)(2,1)S(1)}, bf16[4,128,1024]{2,1,0:T(8,128)(2,1)S(1)}, u32[]{:S(2)}, u32[]{:S(2)}) %collective-permute-start.30) | collective-permute-done | bytes 1048608 | tf_op jit(solution)/shard_map/ppermute | solution.py:619
  509.5 5.5 collective-permute-done.32
  521.5 4.7 convert_add_fusion.2
  (366 shorter events, 163.8 us)
Async XLA Ops:
  19.7 72.1 %all-gather.6.cloned.1.call-start = ((), (), s32[]{:S(2)}) async-start(), calls=%async_computation.5 | async-start | bytes 3022848 | tf_op jit(solution)/shard_map/all_gather | solution.py:698
  28.4 187.7 %all-gather.4.cloned.1.call-start = ((), (), s32[]{:S(2)}) async-start(), calls=%async_computation.3 | async-start | bytes 9437184 | tf_op jit(solution)/shard_map/all_gather | solution.py:750
  28.5 47.2 %collective-permute-start.1 = (bf16[8,128,1024]{2,1,0:T(8,128)(2,1)S(1)}, bf16[8,128,1024]{2,1,0:T(8,128)(2,1)}, u32[]{:S(2)}, u32[]{:S(2)}) collective-permute-start(bf16[8,128,1024]{2,1,0:T(8,128)(2,1)S(1)} %copy-done.2), channel_id=1, source_target_pairs={{0,2},{1,3},{2,0},{3,1},{4,6},{5,7},{6,4},{7,5},{8,10},{9,11},{10,... | collective-permute-start | bytes 6291464 | tf_op jit(solution)/shard_map/ppermute | solution.py:619
  75.7 12.5 %collective-permute-start.14 = (bf16[16,64,256]{2,1,0:T(8,128)(2,1)S(1)}, bf16[16,64,256]{2,1,0:T(8,128)(2,1)S(1)}, u32[]{:S(2)}, u32[]{:S(2)}) collective-permute-start(bf16[16,64,256]{2,1,0:T(8,128)(2,1)S(1)} %hold.3), channel_id=1, source_target_pairs={{0,2},{2,0},{1,3},{3,1},{4,6},{6,4},{5,7},{7,5},{8,10},{10,8},{9,1... | collective-permute-start | bytes 1572872 | tf_op jit(solution)/shard_map/ppermute | solution.py:639
  89.3 429.9 %reduce-scatter.2.cloned.1.call-start = ((), (), s32[]{:S(2)}) async-start(), calls=%async_computation.4 | async-start | bytes 9437184 | tf_op jit(solution)/shard_map/reduce_scatter | solution.py:792
  89.4 12.3 %collective-permute-start = (bf16[8,128,1024]{2,1,0:T(8,128)(2,1)S(1)}, bf16[8,128,1024]{2,1,0:T(8,128)(2,1)}, u32[]{:S(2)}, u32[]{:S(2)}) collective-permute-start(bf16[8,128,1024]{2,1,0:T(8,128)(2,1)S(1)} %copy-done.2), channel_id=1, source_target_pairs={{0,1},{1,0},{2,3},{3,2},{4,5},{5,4},{6,7},{7,6},{8,9},{9,8},{10,11... | collective-permute-start | bytes 6291464 | tf_op jit(solution)/shard_map/ppermute | solution.py:622
  89.5 12.2 %collective-permute-start.2 = (bf16[8,128,1024]{2,1,0:T(8,128)(2,1)}, bf16[8,128,1024]{2,1,0:T(8,128)(2,1)}, u32[]{:S(2)}, u32[]{:S(2)}) collective-permute-start(bf16[8,128,1024]{2,1,0:T(8,128)(2,1)} %collective-permute-done.1.t2.refs_0_), channel_id=1, source_target_pairs={{0,1},{1,0},{2,3},{3,2},{4,5},{5,4},{6,7},{7,6},{8,9},{9,8},{10,11... | collective-permute-start | bytes 6291464 | tf_op jit(solution)/shard_map/ppermute | solution.py:622
  101.6 42.1 %collective-permute-start.7 = (bf16[16,32,1024]{2,1,0:T(8,128)(2,1)}, bf16[16,32,1024]{2,1,0:T(8,128)(2,1)}, u32[]{:S(2)}, u32[]{:S(2)}) collective-permute-start(bf16[16,32,1024]{2,1,0:T(8,128)(2,1)} %reshape.324), channel_id=1, source_target_pairs={{0,1},{1,0},{2,3},{3,2},{4,5},{5,4},{6,7},{7,6},{8,9},{9,8},{10,11... | collective-permute-start | bytes 3145736 | tf_op jit(solution)/shard_map/ppermute | solution.py:622
  120.5 21.9 %collective-permute-start.4 = (bf16[4,128,256]{2,1,0:T(8,128)(2,1)}, bf16[4,128,256]{2,1,0:T(8,128)(2,1)}, u32[]{:S(2)}, u32[]{:S(2)}) collective-permute-start(bf16[4,128,256]{2,1,0:T(8,128)(2,1)} %get-tuple-element.82), channel_id=1, source_target_pairs={{0,1},{1,0},{2,3},{3,2},{4,5},{5,4},{6,7},{7,6},{8,9},{9,8},{10,11... | collective-permute-start | bytes 786440 | tf_op jit(solution)/shard_map/ppermute | solution.py:619
  120.9 27.2 %collective-permute-start.5 = (bf16[4,128,256]{2,1,0:T(8,128)(2,1)}, bf16[4,128,256]{2,1,0:T(8,128)(2,1)}, u32[]{:S(2)}, u32[]{:S(2)}) collective-permute-start(bf16[4,128,256]{2,1,0:T(8,128)(2,1)} %get-tuple-element.83), channel_id=1, source_target_pairs={{0,2},{1,3},{2,0},{3,1},{4,6},{5,7},{6,4},{7,5},{8,10},{9,11},{10,... | collective-permute-start | bytes 786440 | tf_op jit(solution)/shard_map/ppermute | solution.py:619
  122.2 25.9 %collective-permute-start.6 = (bf16[4,128,256]{2,1,0:T(8,128)(2,1)}, bf16[4,128,256]{2,1,0:T(8,128)(2,1)}, u32[]{:S(2)}, u32[]{:S(2)}) collective-permute-start(bf16[4,128,256]{2,1,0:T(8,128)(2,1)} %get-tuple-element.84), channel_id=1, source_target_pairs={{0,3},{1,2},{2,1},{3,0},{4,7},{5,6},{6,5},{7,4},{8,11},{9,10},{10,... | collective-permute-start | bytes 786440 | tf_op jit(solution)/shard_map/ppermute | solution.py:619
  141.6 13.8 %collective-permute-start.8 = (bf16[4,128,256]{2,1,0:T(8,128)(2,1)}, bf16[4,128,256]{2,1,0:T(8,128)(2,1)S(1)}, u32[]{:S(2)}, u32[]{:S(2)}) collective-permute-start(bf16[4,128,256]{2,1,0:T(8,128)(2,1)} %get-tuple-element.88), channel_id=1, source_target_pairs={{0,1},{1,0},{2,3},{3,2},{4,5},{5,4},{6,7},{7,6},{8,9},{9,8},{10,11... | collective-permute-start | bytes 786440 | tf_op jit(solution)/shard_map/ppermute | solution.py:619
  142.4 13.0 %collective-permute-start.9 = (bf16[4,128,256]{2,1,0:T(8,128)(2,1)}, bf16[4,128,256]{2,1,0:T(8,128)(2,1)S(1)}, u32[]{:S(2)}, u32[]{:S(2)}) collective-permute-start(bf16[4,128,256]{2,1,0:T(8,128)(2,1)} %get-tuple-element.89), channel_id=1, source_target_pairs={{0,2},{1,3},{2,0},{3,1},{4,6},{5,7},{6,4},{7,5},{8,10},{9,11},{10,... | collective-permute-start | bytes 786440 | tf_op jit(solution)/shard_map/ppermute | solution.py:619
  374.6 22.9 %collective-permute-start.23 = (bf16[4,128,1024]{2,1,0:T(8,128)(2,1)}, bf16[4,128,1024]{2,1,0:T(8,128)(2,1)}, u32[]{:S(2)}, u32[]{:S(2)}) collective-permute-start(bf16[4,128,1024]{2,1,0:T(8,128)(2,1)} %get-tuple-element.114), channel_id=1, source_target_pairs={{0,1},{1,0},{2,3},{3,2},{4,5},{5,4},{6,7},{7,6},{8,9},{9,8},{10,11... | collective-permute-start | bytes 3145736 | tf_op jit(solution)/shard_map/ppermute | solution.py:622
  390.8 12.8 %collective-permute-start.27 = (bf16[4,128,256]{2,1,0:T(8,128)(2,1)}, bf16[4,128,256]{2,1,0:T(8,128)(2,1)}, u32[]{:S(2)}, u32[]{:S(2)}) collective-permute-start(bf16[4,128,256]{2,1,0:T(8,128)(2,1)} %copy-done.36), channel_id=1, source_target_pairs={{0,3},{1,2},{2,1},{3,0},{4,7},{5,6},{6,5},{7,4},{8,11},{9,10},{10,... | collective-permute-start | bytes 786440 | tf_op jit(solution)/shard_map/ppermute | solution.py:619
  433.6 87.8 %collective-permute-start.22 = (bf16[4,128,1024]{2,1,0:T(8,128)(2,1)S(1)}, bf16[4,128,1024]{2,1,0:T(8,128)(2,1)}, u32[]{:S(2)}, u32[]{:S(2)}) collective-permute-start(bf16[4,128,1024]{2,1,0:T(8,128)(2,1)S(1)} %copy-done.20), channel_id=1, source_target_pairs={{0,1},{1,0},{2,3},{3,2},{4,5},{5,4},{6,7},{7,6},{8,9},{9,8},{10,11... | collective-permute-start | bytes 3145736 | tf_op jit(solution)/shard_map/ppermute | solution.py:622
  447.0 14.9 %collective-permute-start.40 = (bf16[4,2,32,1024]{3,2,0,1:T(8,128)(2,1)S(1)}, bf16[4,2,32,1024]{3,2,0,1:T(8,128)(2,1)S(1)}, u32[]{:S(2)}, u32[]{:S(2)}) collective-permute-start(bf16[4,2,32,1024]{3,2,0,1:T(8,128)(2,1)S(1)} %dynamic-slice_bitcast_fusion.2), channel_id=1, source_target_pairs={{0,2},{2,0},{1,3},{3,1},{4,6},{6,4},{5,7},{7,5},{8,10},{10,8},{9,1... | collective-permute-start | bytes 1572872 | tf_op jit(solution)/shard_map/ppermute | solution.py:639
  447.6 34.7 %collective-permute-start.24 = (bf16[4,128,1024]{2,1,0:T(8,128)(2,1)S(1)}, bf16[4,128,1024]{2,1,0:T(8,128)(2,1)S(1)}, u32[]{:S(2)}, u32[]{:S(2)}) collective-permute-start(bf16[4,128,1024]{2,1,0:T(8,128)(2,1)S(1)} %add_convert_fusion.1.refs_0_), channel_id=1, source_target_pairs={{0,2},{1,3},{2,0},{3,1},{4,6},{5,7},{6,4},{7,5},{8,10},{9,11},{10,... | collective-permute-start | bytes 3145736 | tf_op jit(solution)/shard_map/ppermute | solution.py:619
  449.1 34.3 %collective-permute-start.29 = (bf16[4,128,1024]{2,1,0:T(8,128)(2,1)}, bf16[4,128,1024]{2,1,0:T(8,128)(2,1)S(1)}, u32[]{:S(2)}, u32[]{:S(2)}) collective-permute-start(bf16[4,128,1024]{2,1,0:T(8,128)(2,1)} %copy-done.27), channel_id=1, source_target_pairs={{0,1},{1,0},{2,3},{3,2},{4,5},{5,4},{6,7},{7,6},{8,9},{9,8},{10,11... | collective-permute-start | bytes 3145736 | tf_op jit(solution)/shard_map/ppermute | solution.py:622
  459.4 74.5 %collective-permute-start.28 = (bf16[4,128,1024]{2,1,0:T(8,128)(2,1)}, bf16[4,128,1024]{2,1,0:T(8,128)(2,1)}, u32[]{:S(2)}, u32[]{:S(2)}) collective-permute-start(bf16[4,128,1024]{2,1,0:T(8,128)(2,1)} %get-tuple-element.124), channel_id=1, source_target_pairs={{0,1},{1,0},{2,3},{3,2},{4,5},{5,4},{6,7},{7,6},{8,9},{9,8},{10,11... | collective-permute-start | bytes 3145736 | tf_op jit(solution)/shard_map/ppermute | solution.py:622
  462.2 22.0 %collective-permute-start.41 = (bf16[4,32,1024]{2,1,0:T(8,128)(2,1)S(1)}, bf16[4,32,1024]{2,1,0:T(8,128)(2,1)S(1)}, u32[]{:S(2)}, u32[]{:S(2)}) collective-permute-start(bf16[4,32,1024]{2,1,0:T(8,128)(2,1)S(1)} %dynamic-slice_bitcast_fusion.6), channel_id=1, source_target_pairs={{0,4},{4,0},{1,5},{5,1},{2,6},{6,2},{3,7},{7,3},{8,12},{12,8},{9,1... | collective-permute-start | bytes 786440 | tf_op jit(solution)/shard_map/ppermute | solution.py:639
  482.5 17.5 %collective-permute-start.31 = (bf16[4,128,768]{2,1,0:T(8,128)(2,1)S(1)}, bf16[4,128,768]{2,1,0:T(8,128)(2,1)S(1)}, u32[]{:S(2)}, u32[]{:S(2)}) collective-permute-start(bf16[4,128,768]{2,1,0:T(8,128)(2,1)S(1)} %dynamic-slice_bitcast_fusion), channel_id=1, source_target_pairs={{0,4},{4,0},{1,5},{5,1},{2,6},{6,2},{3,7},{7,3},{8,12},{12,8},{9,1... | collective-permute-start | bytes 2359304 | tf_op jit(solution)/shard_map/ppermute | solution.py:639
  483.8 23.0 %collective-permute-start.30 = (bf16[4,128,1024]{2,1,0:T(8,128)(2,1)S(1)}, bf16[4,128,1024]{2,1,0:T(8,128)(2,1)S(1)}, u32[]{:S(2)}, u32[]{:S(2)}) collective-permute-start(bf16[4,128,1024]{2,1,0:T(8,128)(2,1)S(1)} %add_convert_fusion), channel_id=1, source_target_pairs={{0,2},{1,3},{2,0},{3,1},{4,6},{5,7},{6,4},{7,5},{8,10},{9,11},{10,... | collective-permute-start | bytes 3145736 | tf_op jit(solution)/shard_map/ppermute | solution.py:619
  489.4 19.4 %collective-permute-start.43 = (bf16[1,32,1024]{2,1,0:T(8,128)(2,1)S(1)}, bf16[1,32,1024]{2,1,0:T(8,128)(2,1)S(1)}, u32[]{:S(2)}, u32[]{:S(2)}) collective-permute-start(bf16[1,32,1024]{2,1,0:T(8,128)(2,1)S(1)} %constant_dynamic-slice_fusion), channel_id=1, source_target_pairs={{0,16},{8,24},{16,0},{24,8},{1,17},{9,25},{17,1},{25,9},{2,18},{10... | collective-permute-start | bytes 196616 | tf_op jit(solution)/shard_map/ppermute | solution.py:639
  (87 other events, 600.0 us)
Sparse Core Ops, SparseCore 0:
  28.5 56.3 all-gather.5
  89.5 126.6 all-gather.3
  319.9 146.9 reduce-scatter.1

commit v6 on v5

--- a/solution.py
+++ b/solution.py
@@ -57,6 +57,33 @@
         compiler_params=pltpu.CompilerParams(vmem_limit_bytes=16 * MIB),
         name="hold",
     )(array, *after)
+
+
+def unpack_kernel(pieces, *refs):
+    out = refs[-1]
+    height, lanes = out.shape[2], pieces.shape[2]
+    for half in range(2):
+        for i in range(out.shape[3] // lanes):
+            start = (half * (out.shape[3] // lanes) + i) * height
+            out[:, half, :, i * lanes : (i + 1) * lanes] = pieces[:, start : start + height]
+
+
+def unpack(gathered, share, width, after):
+    count, _, lanes = gathered.shape
+    columns = width // lanes
+    if share % 16:
+        pieces = gathered[:, : 2 * columns * share].reshape(count, 2, columns, share, lanes)
+        return jnp.swapaxes(pieces, 2, 3).reshape(2 * count, share, width)
+    return pl.pallas_call(
+        unpack_kernel,
+        grid=(1,),
+        in_specs=[pl.BlockSpec((count, 2 * columns * share, lanes), lambda i: (0, 0, 0))]
+        + [ELSEWHERE] * len(after),
+        out_specs=pl.BlockSpec((count, 2, share, width), lambda i: (0, 0, 0, 0)),
+        out_shape=jax.ShapeDtypeStruct((count, 2, share, width), BF16),
+        compiler_params=pltpu.CompilerParams(vmem_limit_bytes=16 * MIB),
+        name="unpack",
+    )(gathered, *after).reshape(2 * count, share, width)
 
 
 def softmax_down(scores, allowed):
@@ -102,7 +129,7 @@
 def project_specs(weight, depth):
     shape = (weight.shape[0], depth // weight.shape[0], weight.shape[2])
     return [
-        pl.BlockSpec(shape, lambda i, j=j: (0, j, 0), pipeline_mode=pl.Buffered(1))
+        pl.BlockSpec(shape, lambda i, j=j: (0, j + 2, 0), pipeline_mode=pl.Buffered(1))
         for j in range(3)
     ]
 
@@ -140,8 +167,15 @@
     )(*tokens, weight, weight, weight, bias, seg_key, seg_query, *after)
 
 
-def attend_back_kernel(late, saved, g0, g1, g2, g3, wq, wk, wv, seg_key, seg_query, *refs):
-    grad_project, r0, r1, r2, r3, sums = refs[late:]
+def attend_back_kernel(
+    late, earlier, saved, kept, g0, g1, g2, g3, wq, wk, wv, seg_key, seg_query, *refs
+):
+    grad_weight, r0, r1, r2, r3, sums, total = refs[late + earlier :]
+
+    @pl.when(pl.program_id(0) == 0)
+    def _():
+        total[...] = refs[0][...] if earlier else jnp.zeros_like(total)
+
     part = g0.shape[1]
     width = saved.shape[2] // 3
     factor = HEAD_DIM**-0.5
@@ -171,47 +205,63 @@
             here = lanes > 0.5
             grad_keys = jnp.where(here, keys_term, grad_keys)
             grad_values = jnp.where(here, values_term, grad_values)
-    grad_queries = jnp.transpose(jnp.concatenate(grad_queries, axis=0))
-    terms = [grad_queries.astype(BF16), grad_keys.astype(BF16), grad_values.astype(BF16)]
+    grad_queries = jnp.concatenate(grad_queries, axis=0)
+    terms = [
+        jnp.transpose(grad_queries).astype(BF16),
+        grad_keys.astype(BF16),
+        grad_values.astype(BF16),
+    ]
+    total[:width] += dot(grad_queries.astype(BF16), kept[0])
     for i, term in enumerate(terms):
-        grad_project[0, :, i * width : (i + 1) * width] = term
         sums[0, :, i * width : (i + 1) * width] = jnp.sum(
             term.astype(F32), axis=0, keepdims=True
         )
+        if i:
+            total[i * width : (i + 1) * width] += dot(term, kept[0], (0, 0))
     rows = sum(dot(term, flat(w[...]), (1, 1)) for term, w in zip(terms, (wq, wk, wv)))
     for index, out in enumerate((r0, r1, r2, r3)):
         out[0] = rows[index * part : (index + 1) * part].astype(out.dtype)
 
-
-def attend_back(saved, grads, weight, seg_key, seg_query, after):
+    @pl.when(pl.program_id(0) == pl.num_programs(0) - 1)
+    def _():
+        if grad_weight.dtype == BF16:
+            grad_weight[...] = jnp.transpose(total[...]).astype(BF16)
+        else:
+            grad_weight[...] = total[...]
+
+
+def attend_back(saved, kept, grads, weight, seg_key, seg_query, earlier, done, after):
     count, part, width = grads[0].shape
     depth, wide = width * 4, width * 3
     length = 4 * part
+    shape, kind = ((depth, wide), BF16) if done else ((wide, depth), F32)
     return pl.pallas_call(
-        functools.partial(attend_back_kernel, len(after)),
+        functools.partial(attend_back_kernel, len(after), len(earlier)),
         grid=(count,),
-        in_specs=[by_row((1, length, wide))]
+        in_specs=[by_row((1, length, wide)), by_row((1, length, depth))]
         + [by_row((1, part, width))] * 4
         + project_specs(weight, depth)
         + [
             by_row((1, length, 1)),
             by_row((1, 1, length)),
         ]
+        + [resident((wide, depth))] * len(earlier)
         + [ELSEWHERE] * len(after),
-        out_specs=[by_row((1, length, wide))]
+        out_specs=[resident(shape)]
         + [by_row((1, part, depth))] * 4
         + [by_row((1, 1, wide))],
-        out_shape=[jax.ShapeDtypeStruct((count, length, wide), BF16)]
+        out_shape=[jax.ShapeDtypeStruct(shape, kind)]
         + [jax.ShapeDtypeStruct((count, part, depth), t) for t in (F32, BF16, F32, BF16)]
         + [jax.ShapeDtypeStruct((count, 1, wide), F32)],
-        compiler_params=pltpu.CompilerParams(vmem_limit_bytes=48 * MIB),
+        scratch_shapes=[pltpu.VMEM((wide, depth), F32)],
+        compiler_params=pltpu.CompilerParams(vmem_limit_bytes=52 * MIB),
         cost_estimate=pl.CostEstimate(
-            flops=count * length * wide * (2 * depth + 40 * length // 3),
+            flops=count * length * wide * (4 * depth + 40 * length // 3),
             bytes_accessed=count * length * (3 * depth + 3 * wide) * 2,
             transcendentals=count * length * length * wide // (3 * HEAD_DIM),
         ),
         name="attend_backward",
-    )(saved, *grads, weight, weight, weight, seg_key, seg_query, *after)
+    )(saved, kept, *grads, weight, weight, weight, seg_key, seg_query, *earlier, *after)
 
 
 def column(shape):
@@ -237,7 +287,6 @@
         refs[2 * CHUNKS :],
     )
     step = pl.program_id(0)
-    block = sources[0].shape[0]
 
     @pl.when(step == 0)
     def _():
@@ -246,13 +295,21 @@
 
     into = expand_piece(expand)
     back = reduce_piece(reduce)
-    ahead = dot(sources[0][...], into) + bias[...]
-    for index in range(2 * CHUNKS):
+    block = 256
+    per = sources[0].shape[0] // block
+    half_count = CHUNKS * per
+
+    def inner(index):
+        start = index % per * block
+        return dot(sources[index // per][start : start + block], into) + bias[...]
+
+    ahead = inner(0)
+    for index in range(2 * half_count):
         inside = ahead
-        if index + 1 < 2 * CHUNKS:
-            ahead = dot(sources[index + 1][...], into) + bias[...]
-        total = own_out if index < CHUNKS else far_sum
-        at = slice(index % CHUNKS * block, (index % CHUNKS + 1) * block)
+        if index + 1 < 2 * half_count:
+            ahead = inner(index + 1)
+        total = own_out if index < half_count else far_sum
+        at = slice(index % half_count * block, (index % half_count + 1) * block)
         to = slice(index * block, (index + 1) * block)
         square = inside * inside
         curve = jnp.tanh(inside * (0.7978845608028654 + 0.7978845608028654 * 0.044715 * square))
@@ -677,39 +734,45 @@
         expand_bias,
     )
     vector_count = 8 * share + expand_bias.shape[0]
-    blocks = project_weight.reshape(share, 3, ctx_size, lanes)
     own_vectors = jnp.concatenate(vectors)
-    vector_row = jnp.pad(own_vectors, (0, 3 * lanes - vector_count)).reshape(1, 3, 1, lanes)
-    held = jnp.concatenate(
+    vector_row = jnp.pad(own_vectors, (0, 3 * lanes - vector_count))[None]
+    filler = jnp.concatenate([vector_row, jnp.zeros((15, 3 * lanes), BF16)])
+    held = jnp.stack(
         [
-            blocks,
-            jnp.broadcast_to(vector_row, (1, 3, ctx_size, lanes)),
-            jnp.zeros((15, 3, ctx_size, lanes), BF16),
+            jnp.concatenate(
+                [
+                    jnp.concatenate(
+                        [
+                            project_weight[:, (ctx_size * j + p) * lanes :][:, :lanes]
+                            for j in range(3)
+                        ],
+                        axis=1,
+                    ),
+                    filler,
+                ]
+            )
+            for p in range(ctx_size)
         ]
     )
-    held = lax.all_to_all(held, CTX, 2, 0, tiled=False)
+    held = lax.all_to_all(held, CTX, 0, 0, tiled=True)
     sent, held = lax.optimization_barrier((tokens, held))
     across = hop(sent, 2)
     gathered = (tokens, swap(sent), across, swap(across))
-    mine = jnp.moveaxis(held[:, :share], 2, 0).reshape(-1, lanes)
-    vector_rows = held[:, share].reshape(ctx_size, 3 * lanes)[:, :vector_count].reshape(-1)
+    mine = jnp.concatenate(
+        [held[:, :share, j * lanes : (j + 1) * lanes].reshape(-1, lanes) for j in range(3)]
+    )
+    vector_rows = held[:, share, :vector_count].reshape(-1)
     vector_rows = jnp.pad(vector_rows, (0, 16 * lanes - vector_rows.shape[0])).reshape(16, lanes)
-    out_pieces = jnp.swapaxes(output_weight.reshape(share, ctx_size, lanes), 0, 1)
-    whole_project = lax.all_gather(
-        jnp.concatenate(
-            [mine, vector_rows, widen(out_pieces.reshape(-1, lanes), "x").reshape(-1, lanes)]
-        ),
+    out_pieces = jnp.concatenate(
+        [output_weight[:, i * lanes : (i + 1) * lanes] for i in range(ctx_size)]
+    )
+    full_project = lax.all_gather(
+        jnp.concatenate([widen(out_pieces, "x").reshape(-1, lanes), mine, vector_rows]),
         SEQ,
         axis=0,
     )
-    first_rows = mine.shape[0]
-    full_project = whole_project
-    out_half = jnp.swapaxes(
-        whole_project[:, first_rows + 16 :].reshape(chips, ctx_size, share, lanes), 1, 2
-    ).reshape(chips, share, width)
-    full_output = by_core(out_half, swap(out_half), 1).reshape(ctx_size, lanes, width)
     packed = (
-        whole_project[:, first_rows : first_rows + 16]
+        full_project[:, -16:]
         .reshape(-1, 16 * lanes)[:, : ctx_size * vector_count]
         .reshape(everyone, vector_count)
         .astype(F32)
@@ -760,8 +823,11 @@
         *mixed, all_rows, kept = attend(
             gathered, full_project, bias_all, seg_key[at], seg_query[at], at.start, []
         )
-        kept_rows.append(all_rows.reshape(-1, width))
+        kept_rows.append(all_rows)
         saved.append(kept)
+        if index == 0:
+            out_half = unpack(full_project, share, width, mixed[:1])
+            full_output = by_core(out_half, swap(out_half), 1).reshape(ctx_size, lanes, width)
         arrived = [mixed[0]] + [hop(mixed[r], r) for r in (1, 2, 3)]
         low, scaled, inverse, joined = first_norm(
             where, arrived, rows, full_output, vectors, index
@@ -822,42 +888,55 @@
     output_grad = halve(output_grad, 1, "y")
     output_owned = z_scatter(output_grad)
 
-    project_parts = []
+    project_grad = []
     work_parts = []
     across_sums = []
     work_hops = []
     sum_parts = []
     for index in range(CHUNKS):
-        at = slice(index * seq_count // CHUNKS, (index + 1) * seq_count // CHUNKS)
-        grad_part, r0, r1, r2, r3, sums = attend_back(
+        at = slice(index * seqs, (index + 1) * seqs)
+        project_part, r0, r1, r2, r3, sums = attend_back(
             saved[index],
+            kept_rows[index],
             grad_mixed[index],
             full_project,
             seg_key[at],
             seg_query[at],
+            project_grad,
+            index == CHUNKS - 1,
             across_sums[:index],
         )
+        project_grad = [project_part]
         across_sums.append((r2 + swap(r3).astype(F32)).astype(BF16))
         work_hops.append(hop(across_sums[index], 2))
         work_parts.append(
             grad_hidden[index] + r0 + swap(r1).astype(F32) + work_hops[index].astype(F32)
         )
-        project_parts.append(grad_part)
         sum_parts.append(sums)
-    project_grad = sum(
-        dot(all_rows, grad_part.reshape(-1, 3 * lanes), (0, 0))
-        for all_rows, grad_part in zip(kept_rows, project_parts)
-    )
     grad_work = jnp.concatenate(work_parts, axis=0)
-    project_grad = hold(project_grad.astype(BF16), work_hops[:1])
-    project_half = halve(
-        project_grad.reshape(sizes["z"], 2, ctx_size * share, 3 * lanes), 1, "y"
-    )
-    project_owned = z_scatter(hold(project_half.astype(BF16), work_hops[1:]))
-    project_owned = lax.all_to_all(
-        project_owned.reshape(ctx_size, share, 3, lanes), CTX, 0, 2, tiled=False
-    ).reshape(share, 3 * width)
+    project_grad = hold(project_grad[0], work_hops[:1])
+    blocks = halve(project_grad.reshape(sizes["z"], 2, ctx_size * share, 3 * lanes), 1, "y")
+    for step in z_steps:
+        blocks = blocks.astype(BF16).reshape((blocks.shape[0] // 2, 2) + blocks.shape[1:])
+        blocks = halve(blocks, 1, "z", step)
+        if step == 1:
+            blocks = hold(blocks.astype(BF16), work_hops[1:])
     weight_owned = halve(weight_owned, 0, "x")
+    held = lax.all_to_all(
+        hold(blocks.astype(F32).reshape(ctx_size, share, 3 * lanes), [weight_owned]),
+        CTX,
+        0,
+        0,
+        tiled=True,
+    )
+    project_owned = jnp.concatenate(
+        [
+            held[p, :, j * lanes : (j + 1) * lanes]
+            for j in range(3)
+            for p in range(ctx_size)
+        ],
+        axis=1,
+    )
     expand_pieces = own_hidden // PIECE
     far_rows = jnp.swapaxes(
         weight_owned[:expand_pieces].reshape(expand_pieces, 2, share, PIECE), 0, 1

time: 556 us -> 549 us (0.987)
  matrix products: 14.9 us -> 0 us
  waiting for transfers between devices: 187 us -> 198 us
  Pallas kernels: 196 us -> 206 us
  local copies, waits for them, and re-layouts: 71.1 us -> 61.8 us
  starting transfers between devices: 43.2 us -> 36.2 us
    dot_general x2 -> x0, matrix products: 14.9 us -> none  [dot(): lax.dot_general(left, right, (((contract[0],), (contract[1],)), ((), ()))...]
    ppermute x16, waiting for transfers between devices: 38.4 us -> 52.4 us  [trade(): lax.ppermute(array, name, [(i, i ^ step) for i in range(sizes[name])])]
    pallas_call x2 -> x3, Pallas kernels: 49.3 us -> 60.6 us  [the longest x2 60.4 us: attend_back(): pl.pallas_call(functools.partial(attend_back_kernel, len(after), len(earl...]
    ppermute x15, waiting for transfers between devices: 85.3 us -> 76.8 us  [hop(): return lax.ppermute(array, CTX, [(i, i ^ step) for i in range(ctx_size)])]
    reshape x5 -> x0, local copies, waits for them, and re-layouts: 7.18 us -> none  [the longest x1 3.15 us: on_device(): whole_project[:, first_rows + 16:].reshape(chips, ctx_size, share, lanes)]
    all_gather x1, waiting for transfers between devices: 50.9 us -> 44.4 us  [on_device(): lax.all_gather(widen(own_pieces, 'x'), SEQ, axis=0)]
    ppermute x16, starting transfers between devices: 20.5 us -> 14.2 us  [trade(): lax.ppermute(array, name, [(i, i ^ step) for i in range(sizes[name])])]
    all_to_all x2, waiting for transfers between devices: 0.01 us -> 6.24 us  [the longest x1 6.24 us: on_device(): held = lax.all_to_all(held, CTX, 0, 0, tiled=True)]
  transfers between devices with their start and end apart: 51 -> 51, of which waited for: 21 -> 28; matrix products, arithmetic and copies ran while one was open for 12% -> 10% of each run, Pallas kernels for 20% -> 22%
where the time goes in v6:
time: 549 us; the launch traced here: 545 us
  Pallas kernels  206 us (38%)
  waiting for transfers between devices  198 us (36%)
  local copies, waits for them, and re-layouts  61.8 us (11%)
  starting transfers between devices  36.2 us (7%)
  other arithmetic  27.5 us (5%)
  between operations  15.3 us (3%)
    ppermute x15, waiting for transfers between devices, hop(): return lax.ppermute(array, CTX, [(i, i ^ step) for i in range(ctx_size)])  76.8 us
    pallas_call x2, Pallas kernels, attend_back(): pl.pallas_call(functools.partial(attend_back_kernel, len(after), len(earl...  60.4 us
    ppermute x16, waiting for transfers between devices, trade(): lax.ppermute(array, name, [(i, i ^ step) for i in range(sizes[name])])  52.4 us
    pallas_call x1, Pallas kernels, feed_back(): pl.pallas_call(feed_back_kernel, grid=(hidden // PIECE,), in_specs=[resid...  52.3 us
    all_gather x1, waiting for transfers between devices, on_device(): lax.all_gather(widen(own_pieces, 'x'), SEQ, axis=0)  44.4 us
    unnamed x139, local copies, waits for them, and re-layouts  36 us
    pallas_call x2, Pallas kernels, attend(): pl.pallas_call(functools.partial(attend_kernel, len(after)), grid=(count,...  30.8 us
    pallas_call x1, Pallas kernels, feed(): pl.pallas_call(feed_kernel, grid=(hidden // wide,), in_specs=[resident((b...  29.7 us
  transfers between devices with their start and end apart: 51, of which 28 were waited for; matrix products, arithmetic and copies ran while one was open for 10% of the time, Pallas kernels for 22%

profile of v6, /device:TPU:0, one launch (start us, length us, event | category | flops | bytes accessed | tf_op | source)
XLA Modules:
  0.0 544.6 jit_solution(8703678417292224146)
XLA Ops:
  11.1 6.1 %concatenate.100 = bf16[384]{0:T(512)(128)(2,1)S(1)} concatenate(bf16[32]{0:T(256)(128)(2,1)} %param.19, bf16[32]{0:T(256)(128)(2,1)} %param.20, bf16[32]{0:T(256)(128)(2,1)} %param.22, bf16[32]{0:T(256)(128)(2,1)} %param.23, bf16[32]{0:T(256)(128)(2,1)} %param.24, bf16[32]{0:T(256)(128)(2,1)} %param.28, bf16[32]{0:T(256)(128)(2,1)} %param.29, bf16[32]{0:T(256)(128)(2,1)} %param.30, ...), dimensions={0} | concatenate | bytes 1536 | tf_op jit(solution)/shard_map/concatenate | solution.py:737
  22.8 6.2 %all-to-all-done = bf16[4,48,768]{2,1,0:T(8,128)(2,1)S(1)} async-done(((bf16[4,48,768]{2,1,0:T(8,128)(2,1)}), bf16[4,48,768]{2,1,0:T(8,128)(2,1)S(1)}, u32[]{:S(2)}, u32[]{:S(2)}) %all-to-all-start) | async-done | bytes 294944 | tf_op jit(solution)/shard_map/all_to_all | solution.py:757
  33.8 43.5 %collective-permute-done.1.t2.refs_0_ = bf16[8,128,1024]{2,1,0:T(8,128)(2,1)} collective-permute-done((bf16[8,128,1024]{2,1,0:T(8,128)(2,1)S(1)}, bf16[8,128,1024]{2,1,0:T(8,128)(2,1)}, u32[]{:S(2)}, u32[]{:S(2)}) %collective-permute-start.1) | collective-permute-done | bytes 2097184 | tf_op jit(solution)/shard_map/ppermute | solution.py:676
  78.1 11.9 %collective-permute-done.14 = bf16[16,64,256]{2,1,0:T(8,128)(2,1)S(1)} collective-permute-done((bf16[16,64,256]{2,1,0:T(8,128)(2,1)S(1)}, bf16[16,64,256]{2,1,0:T(8,128)(2,1)S(1)}, u32[]{:S(2)}, u32[]{:S(2)}) %collective-permute-start.14) | collective-permute-done | bytes 524320 | tf_op jit(solution)/shard_map/ppermute | solution.py:696
  101.1 15.0 %attend_forward.2 = (bf16[4,128,256]{2,1,0:T(8,128)(2,1)S(1)}, bf16[4,128,256]{2,1,0:T(8,128)(2,1)S(1)}, bf16[4,128,256]{2,1,0:T(8,128)(2,1)S(1)}, bf16[4,128,25...) custom-call(bf16[8,128,1024]{2,1,0:T(8,128)(2,1)S(1)} %copy-done.2, ...), custom_call_target="tpu_custom_call" | custom-call | flops 7515144192 | bytes 10485760 | tf_op jit(solution)/shard_map/attend_forward/pallas_call | solution.py:142
  121.4 15.8 %attend_forward.3 = (bf16[4,128,256]{2,1,0:T(8,128)(2,1)S(1)}, bf16[4,128,256]{2,1,0:T(8,128)(2,1)}, bf16[4,128,256]{2,1,0:T(8,128)(2,1)}, bf16[4,128,256]{2,1,0...) custom-call(bf16[8,128,1024]{2,1,0:T(8,128)(2,1)S(1)} %copy-done.2, ...), custom_call_target="tpu_custom_call" | custom-call | flops 7515144192 | bytes 10485760 | tf_op jit(solution)/shard_map/attend_forward/pallas_call | solution.py:142
  147.3 4.7 collective-permute-done.10.m3
  172.6 44.4 %all-gather.4.cloned.1.call-done = bf16[8,2,16,64,256]{4,3,2,1,0:T(8,128)(2,1)} async-done(((bf16[1,2,16,64,256]{4,3,2,1,0:T(8,128)(2,1)}), bf16[8,2,16,64,256]{4,3,2,1,0:T(8,128)(2,1)}) %all-gather.4.cloned.1.call-update) | async-done | bytes 8388624 | tf_op jit(solution)/shard_map/all_gather | solution.py:813
  217.0 29.7 %feed_forward.1 = (bf16[2048,2048]{1,0:T(8,128)(2,1)}, bf16[2048,2048]{1,0:T(8,128)(2,1)}, f32[1024,1024]{1,0:T(8,128)}, bf16[1024,1024]{1,0:T(8,128)(2,1)}) custom-call(bf16[512,1024]{1,0:T(8,128)(2,1)} %copy-done.24, bf16[512,1024]{1,0:T(8,128)(2,1)} %copy-done.23, bf16[512,1024]{1,0:T(8,128)(2,1)} %collective-permute-done.11.refs_2_.refs_6_, ...), custom_call_target="tpu_custom_call" | custom-call | flops 17179869184 | bytes 29360128 | tf_op jit(solution)/shard_map/feed_forward/pallas_call | solution.py:345
  246.8 4.4 collective-permute-done.15.far
  252.5 4.1 second_norm.3
  259.1 4.4 second_norm.2
  269.5 52.3 %feed_backward.1 = (bf16[16,16,64,256]{3,2,1,0:T(8,128)(2,1)}, f32[1,2048]{1,0:T(1,128)}, f32[1024,1024]{1,0:T(8,128)}, bf16[1024,1024]{1,0:T(8,128)(2,1)}) custom-call(bf16[512,1024]{1,0:T(8,128)(2,1)} %copy-done.28, bf16[512,1024]{1,0:T(8,128)(2,1)} %copy-done.27, bf16[512,1024]{1,0:T(8,128)(2,1)} %copy-done.57, bf16[512,1024]{1,0:T(8,128)(2,1)} %copy-done.56, ...), custom_call_target="tpu_custom_call" | custom-call | flops 34359738368 | bytes 54525952 | tf_op jit(solution)/shard_map/feed_backward/pallas_call | solution.py:425
  329.0 6.0 %first_back.2 = (f32[512,1024]{1,0:T(8,128)S(1)}, bf16[512,1024]{1,0:T(8,128)(2,1)S(1)}, bf16[4,128,256]{2,1,0:T(8,128)(2,1)S(1)}, bf16[4,128,256]{2,1,0:T(8,128...) custom-call(s32[1]{0:T(128)} %bitcast.place, ...), custom_call_target="tpu_custom_call" | custom-call | flops 1073741824 | bytes 8388608 | tf_op jit(solution)/shard_map/first_back/pallas_call | solution.py:489
  337.9 7.4 %collective-permute-done.20.g2 = bf16[4,128,256]{2,1,0:T(8,128)(2,1)S(1)} collective-permute-done((bf16[4,128,256]{2,1,0:T(8,128)(2,1)S(1)}, bf16[4,128,256]{2,1,0:T(8,128)(2,1)S(1)}, u32[]{:S(2)}, u32[]{:S(2)}) %collective-permute-start.20) | collective-permute-done | bytes 262176 | tf_op jit(solution)/shard_map/ppermute | solution.py:676
  345.3 4.5 collective-permute-done.21.g3
  349.8 29.6 %attend_backward.2 = (f32[768,1024]{1,0:T(8,128)}, f32[4,128,1024]{2,1,0:T(8,128)}, bf16[4,128,1024]{2,1,0:T(8,128)(2,1)}, f32[4,128,1024]{2,1,0:T(8,128)}, bf16...) custom-call(bf16[4,512,768]{2,1,0:T(8,128)(2,1)} %get-tuple-element.106.saved, ...), custom_call_target="tpu_custom_call" | custom-call | flops 17178820608 | bytes 22020096 | tf_op jit(solution)/shard_map/attend_backward/pallas_call | solution.py:238
  380.2 5.8 %first_back.3 = (f32[512,1024]{1,0:T(8,128)S(1)}, bf16[512,1024]{1,0:T(8,128)(2,1)S(1)}, bf16[4,128,256]{2,1,0:T(8,128)(2,1)S(1)}, bf16[4,128,256]{2,1,0:T(8,128...) custom-call(s32[1]{0:T(128)} %bitcast.place, ...), custom_call_target="tpu_custom_call" | custom-call | flops 1073741824 | bytes 8388608 | tf_op jit(solution)/shard_map/first_back/pallas_call | solution.py:489
  407.9 30.8 %attend_backward.3 = (bf16[1024,768]{1,0:T(8,128)(2,1)}, f32[4,128,1024]{2,1,0:T(8,128)}, bf16[4,128,1024]{2,1,0:T(8,128)(2,1)}, f32[4,128,1024]{2,1,0:T(8,128)}...) custom-call(bf16[4,512,768]{2,1,0:T(8,128)(2,1)} %get-tuple-element.119.saved, ...), custom_call_target="tpu_custom_call" | custom-call | flops 17178820608 | bytes 22020096 | tf_op jit(solution)/shard_map/attend_backward/pallas_call | solution.py:238
  453.7 7.8 %collective-permute-done.41 = bf16[4,2,32,1024]{3,2,0,1:T(8,128)(2,1)} collective-permute-done((bf16[4,2,32,1024]{3,2,0,1:T(8,128)(2,1)}, bf16[4,2,32,1024]{3,2,0,1:T(8,128)(2,1)}, u32[]{:S(2)}, u32[]{:S(2)}) %collective-permute-start.41) | collective-permute-done | bytes 524320 | tf_op jit(solution)/shard_map/ppermute | solution.py:696
  469.5 4.3 collective-permute-done.42
  474.5 5.1 collective-permute-done.43
  489.2 12.4 %collective-permute-done.31 = bf16[4,128,768]{2,1,0:T(8,128)(2,1)S(1)} collective-permute-done((bf16[4,128,768]{2,1,0:T(8,128)(2,1)S(1)}, bf16[4,128,768]{2,1,0:T(8,128)(2,1)S(1)}, u32[]{:S(2)}, u32[]{:S(2)}) %collective-permute-start.31) | collective-permute-done | bytes 786464 | tf_op jit(solution)/shard_map/ppermute | solution.py:696
  504.6 7.5 %collective-permute-done.30.refs_0_ = bf16[4,128,1024]{2,1,0:T(8,128)(2,1)S(1)} collective-permute-done((bf16[4,128,1024]{2,1,0:T(8,128)(2,1)}, bf16[4,128,1024]{2,1,0:T(8,128)(2,1)S(1)}, u32[]{:S(2)}, u32[]{:S(2)}) %collective-permute-start.30) | collective-permute-done | bytes 1048608 | tf_op jit(solution)/shard_map/ppermute | solution.py:676
  (365 shorter events, 165.4 us)
Async XLA Ops:
  8.1 14.6 %collective-permute-start.3 = (bf16[128,256]{1,0:T(8,128)(2,1)S(1)}, bf16[128,256]{1,0:T(8,128)(2,1)S(1)}, u32[]{:S(2)}, u32[]{:S(2)}) collective-permute-start(bf16[128,256]{1,0:T(8,128)(2,1)S(1)} %get-tuple-element.175), channel_id=1, source_target_pairs={{0,2},{2,0},{1,3},{3,1},{4,6},{6,4},{5,7},{7,5},{8,10},{10,8},{9,1... | collective-permute-start | bytes 196616 | tf_op jit(solution)/shard_map/ppermute | solution.py:696
  22.7 69.8 %all-gather.6.cloned.1.call-start = ((), (), s32[]{:S(2)}) async-start(), calls=%async_computation.5 | async-start | bytes 3022848 | tf_op jit(solution)/shard_map/all_gather | solution.py:769
  29.9 187.1 %all-gather.4.cloned.1.call-start = ((), (), s32[]{:S(2)}) async-start(), calls=%async_computation.3 | async-start | bytes 9437184 | tf_op jit(solution)/shard_map/all_gather | solution.py:813
  30.0 47.3 %collective-permute-start.1 = (bf16[8,128,1024]{2,1,0:T(8,128)(2,1)S(1)}, bf16[8,128,1024]{2,1,0:T(8,128)(2,1)}, u32[]{:S(2)}, u32[]{:S(2)}) collective-permute-start(bf16[8,128,1024]{2,1,0:T(8,128)(2,1)S(1)} %copy-done.2), channel_id=1, source_target_pairs={{0,2},{1,3},{2,0},{3,1},{4,6},{5,7},{6,4},{7,5},{8,10},{9,11},{10,... | collective-permute-start | bytes 6291464 | tf_op jit(solution)/shard_map/ppermute | solution.py:676
  91.2 412.1 %reduce-scatter.2.cloned.1.call-start = ((), (), s32[]{:S(2)}) async-start(), calls=%async_computation.4 | async-start | bytes 9437184 | tf_op jit(solution)/shard_map/reduce_scatter | solution.py:858
  116.3 25.0 %collective-permute-start.7 = (bf16[16,32,1024]{2,1,0:T(8,128)(2,1)S(1)}, bf16[16,32,1024]{2,1,0:T(8,128)(2,1)}, u32[]{:S(2)}, u32[]{:S(2)}) collective-permute-start(bf16[16,32,1024]{2,1,0:T(8,128)(2,1)S(1)} %bitcast.226), channel_id=1, source_target_pairs={{0,1},{1,0},{2,3},{3,2},{4,5},{5,4},{6,7},{7,6},{8,9},{9,8},{10,11... | collective-permute-start | bytes 3145736 | tf_op jit(solution)/shard_map/ppermute | solution.py:679
  139.0 13.1 %collective-permute-start.10 = (bf16[4,128,256]{2,1,0:T(8,128)(2,1)}, bf16[4,128,256]{2,1,0:T(8,128)(2,1)S(1)}, u32[]{:S(2)}, u32[]{:S(2)}) collective-permute-start(bf16[4,128,256]{2,1,0:T(8,128)(2,1)} %get-tuple-element.90), channel_id=1, source_target_pairs={{0,3},{1,2},{2,1},{3,0},{4,7},{5,6},{6,5},{7,4},{8,11},{9,10},{10,... | collective-permute-start | bytes 786440 | tf_op jit(solution)/shard_map/ppermute | solution.py:676
  139.9 19.5 %collective-permute-start.4 = (bf16[4,128,256]{2,1,0:T(8,128)(2,1)}, bf16[4,128,256]{2,1,0:T(8,128)(2,1)S(1)}, u32[]{:S(2)}, u32[]{:S(2)}) collective-permute-start(bf16[4,128,256]{2,1,0:T(8,128)(2,1)} %copy-done.32), channel_id=1, source_target_pairs={{0,1},{1,0},{2,3},{3,2},{4,5},{5,4},{6,7},{7,6},{8,9},{9,8},{10,11... | collective-permute-start | bytes 786440 | tf_op jit(solution)/shard_map/ppermute | solution.py:676
  140.3 19.1 %collective-permute-start.5 = (bf16[4,128,256]{2,1,0:T(8,128)(2,1)}, bf16[4,128,256]{2,1,0:T(8,128)(2,1)S(1)}, u32[]{:S(2)}, u32[]{:S(2)}) collective-permute-start(bf16[4,128,256]{2,1,0:T(8,128)(2,1)} %copy-done.30), channel_id=1, source_target_pairs={{0,2},{1,3},{2,0},{3,1},{4,6},{5,7},{6,4},{7,5},{8,10},{9,11},{10,... | collective-permute-start | bytes 786440 | tf_op jit(solution)/shard_map/ppermute | solution.py:676
  141.3 22.0 %collective-permute-start.6 = (bf16[4,128,256]{2,1,0:T(8,128)(2,1)}, bf16[4,128,256]{2,1,0:T(8,128)(2,1)S(1)}, u32[]{:S(2)}, u32[]{:S(2)}) collective-permute-start(bf16[4,128,256]{2,1,0:T(8,128)(2,1)} %copy-done.29), channel_id=1, source_target_pairs={{0,3},{1,2},{2,1},{3,0},{4,7},{5,6},{6,5},{7,4},{8,11},{9,10},{10,... | collective-permute-start | bytes 786440 | tf_op jit(solution)/shard_map/ppermute | solution.py:676
  379.4 25.1 %collective-permute-start.23 = (bf16[4,128,1024]{2,1,0:T(8,128)(2,1)}, bf16[4,128,1024]{2,1,0:T(8,128)(2,1)}, u32[]{:S(2)}, u32[]{:S(2)}) collective-permute-start(bf16[4,128,1024]{2,1,0:T(8,128)(2,1)} %get-tuple-element.115), channel_id=1, source_target_pairs={{0,1},{1,0},{2,3},{3,2},{4,5},{5,4},{6,7},{7,6},{8,9},{9,8},{10,11... | collective-permute-start | bytes 3145736 | tf_op jit(solution)/shard_map/ppermute | solution.py:679
  389.7 18.1 %collective-permute-start.25 = (bf16[4,128,256]{2,1,0:T(8,128)(2,1)}, bf16[4,128,256]{2,1,0:T(8,128)(2,1)S(1)}, u32[]{:S(2)}, u32[]{:S(2)}) collective-permute-start(bf16[4,128,256]{2,1,0:T(8,128)(2,1)} %copy-done.31), channel_id=1, source_target_pairs={{0,1},{1,0},{2,3},{3,2},{4,5},{5,4},{6,7},{7,6},{8,9},{9,8},{10,11... | collective-permute-start | bytes 786440 | tf_op jit(solution)/shard_map/ppermute | solution.py:676
  389.9 18.0 %collective-permute-start.26 = (bf16[4,128,256]{2,1,0:T(8,128)(2,1)S(1)}, bf16[4,128,256]{2,1,0:T(8,128)(2,1)}, u32[]{:S(2)}, u32[]{:S(2)}) collective-permute-start(bf16[4,128,256]{2,1,0:T(8,128)(2,1)S(1)} %get-tuple-element.123), channel_id=1, source_target_pairs={{0,2},{1,3},{2,0},{3,1},{4,6},{5,7},{6,4},{7,5},{8,10},{9,11},{10,... | collective-permute-start | bytes 786440 | tf_op jit(solution)/shard_map/ppermute | solution.py:676
  391.4 16.5 %collective-permute-start.27 = (bf16[4,128,256]{2,1,0:T(8,128)(2,1)S(1)}, bf16[4,128,256]{2,1,0:T(8,128)(2,1)}, u32[]{:S(2)}, u32[]{:S(2)}) collective-permute-start(bf16[4,128,256]{2,1,0:T(8,128)(2,1)S(1)} %get-tuple-element.124), channel_id=1, source_target_pairs={{0,3},{1,2},{2,1},{3,0},{4,7},{5,6},{6,5},{7,4},{8,11},{9,10},{10,... | collective-permute-start | bytes 786440 | tf_op jit(solution)/shard_map/ppermute | solution.py:676
  404.1 38.4 %collective-permute-start.40 = (bf16[4,2,2,32,1024]{4,3,0,1,2:T(8,128)(2,1)}, bf16[4,2,2,32,1024]{4,3,0,1,2:T(8,128)(2,1)}, u32[]{:S(2)}, u32[]{:S(2)}) collective-permute-start(bf16[4,2,2,32,1024]{4,3,0,1,2:T(8,128)(2,1)} %bitcast.216), channel_id=1, source_target_pairs={{0,1},{1,0},{2,3},{3,2},{4,5},{5,4},{6,7},{7,6},{8,9},{9,8},{10,11... | collective-permute-start | bytes 3145736 | tf_op jit(solution)/shard_map/ppermute | solution.py:696
  446.4 15.1 %collective-permute-start.41 = (bf16[4,2,32,1024]{3,2,0,1:T(8,128)(2,1)}, bf16[4,2,32,1024]{3,2,0,1:T(8,128)(2,1)}, u32[]{:S(2)}, u32[]{:S(2)}) collective-permute-start(bf16[4,2,32,1024]{3,2,0,1:T(8,128)(2,1)} %dynamic-slice_bitcast_fusion.1), channel_id=1, source_target_pairs={{0,2},{2,0},{1,3},{3,1},{4,6},{6,4},{5,7},{7,5},{8,10},{10,8},{9,1... | collective-permute-start | bytes 1572872 | tf_op jit(solution)/shard_map/ppermute | solution.py:696
  451.6 35.6 %collective-permute-start.22 = (bf16[4,128,1024]{2,1,0:T(8,128)(2,1)S(1)}, bf16[4,128,1024]{2,1,0:T(8,128)(2,1)S(1)}, u32[]{:S(2)}, u32[]{:S(2)}) collective-permute-start(bf16[4,128,1024]{2,1,0:T(8,128)(2,1)S(1)} %copy-done.53), channel_id=1, source_target_pairs={{0,1},{1,0},{2,3},{3,2},{4,5},{5,4},{6,7},{7,6},{8,9},{9,8},{10,11... | collective-permute-start | bytes 3145736 | tf_op jit(solution)/shard_map/ppermute | solution.py:679
  451.6 31.2 %collective-permute-start.24 = (bf16[4,128,1024]{2,1,0:T(8,128)(2,1)S(1)}, bf16[4,128,1024]{2,1,0:T(8,128)(2,1)S(1)}, u32[]{:S(2)}, u32[]{:S(2)}) collective-permute-start(bf16[4,128,1024]{2,1,0:T(8,128)(2,1)S(1)} %copy-done.43), channel_id=1, source_target_pairs={{0,2},{1,3},{2,0},{3,1},{4,6},{5,7},{6,4},{7,5},{8,10},{9,11},{10,... | collective-permute-start | bytes 3145736 | tf_op jit(solution)/shard_map/ppermute | solution.py:676
  453.1 51.5 %collective-permute-start.28 = (bf16[4,128,1024]{2,1,0:T(8,128)(2,1)}, bf16[4,128,1024]{2,1,0:T(8,128)(2,1)}, u32[]{:S(2)}, u32[]{:S(2)}) collective-permute-start(bf16[4,128,1024]{2,1,0:T(8,128)(2,1)} %get-tuple-element.127), channel_id=1, source_target_pairs={{0,1},{1,0},{2,3},{3,2},{4,5},{5,4},{6,7},{7,6},{8,9},{9,8},{10,11... | collective-permute-start | bytes 3145736 | tf_op jit(solution)/shard_map/ppermute | solution.py:679
  453.3 30.6 %collective-permute-start.29 = (bf16[4,128,1024]{2,1,0:T(8,128)(2,1)S(1)}, bf16[4,128,1024]{2,1,0:T(8,128)(2,1)S(1)}, u32[]{:S(2)}, u32[]{:S(2)}) collective-permute-start(bf16[4,128,1024]{2,1,0:T(8,128)(2,1)S(1)} %copy-done.54), channel_id=1, source_target_pairs={{0,1},{1,0},{2,3},{3,2},{4,5},{5,4},{6,7},{7,6},{8,9},{9,8},{10,11... | collective-permute-start | bytes 3145736 | tf_op jit(solution)/shard_map/ppermute | solution.py:679
  483.0 18.5 %collective-permute-start.31 = (bf16[4,128,768]{2,1,0:T(8,128)(2,1)S(1)}, bf16[4,128,768]{2,1,0:T(8,128)(2,1)S(1)}, u32[]{:S(2)}, u32[]{:S(2)}) collective-permute-start(bf16[4,128,768]{2,1,0:T(8,128)(2,1)S(1)} %dynamic-slice_bitcast_fusion), channel_id=1, source_target_pairs={{0,4},{4,0},{1,5},{5,1},{2,6},{6,2},{3,7},{7,3},{8,12},{12,8},{9,1... | collective-permute-start | bytes 2359304 | tf_op jit(solution)/shard_map/ppermute | solution.py:696
  485.8 26.3 %collective-permute-start.30 = (bf16[4,128,1024]{2,1,0:T(8,128)(2,1)}, bf16[4,128,1024]{2,1,0:T(8,128)(2,1)S(1)}, u32[]{:S(2)}, u32[]{:S(2)}) collective-permute-start(bf16[4,128,1024]{2,1,0:T(8,128)(2,1)} %add_convert_fusion), channel_id=1, source_target_pairs={{0,2},{1,3},{2,0},{3,1},{4,6},{5,7},{6,4},{7,5},{8,10},{9,11},{10,... | collective-permute-start | bytes 3145736 | tf_op jit(solution)/shard_map/ppermute | solution.py:676
  503.4 12.6 %collective-permute-start.32 = (bf16[2,128,768]{2,1,0:T(8,128)(2,1)}, bf16[2,128,768]{2,1,0:T(8,128)(2,1)S(1)}, u32[]{:S(2)}, u32[]{:S(2)}) collective-permute-start(bf16[2,128,768]{2,1,0:T(8,128)(2,1)} %dynamic-slice_bitcast_fusion.3), channel_id=1, source_target_pairs={{0,8},{8,0},{16,24},{24,16},{1,9},{9,1},{17,25},{25,17},{2,10},{10... | collective-permute-start | bytes 1179656 | tf_op jit(solution)/shard_map/ppermute | solution.py:696
  504.4 16.8 %collective-permute-start.34 = (bf16[16,64,256]{2,1,0:T(8,128)(2,1)S(1)}, bf16[16,64,256]{2,1,0:T(8,128)(2,1)S(1)}, u32[]{:S(2)}, u32[]{:S(2)}) collective-permute-start(bf16[16,64,256]{2,1,0:T(8,128)(2,1)S(1)} %dynamic-slice_bitcast_fusion.2), channel_id=1, source_target_pairs={{0,2},{2,0},{1,3},{3,1},{4,6},{6,4},{5,7},{7,5},{8,10},{10,8},{9,1... | collective-permute-start | bytes 1572872 | tf_op jit(solution)/shard_map/ppermute | solution.py:696
  (85 other events, 500.8 us)
Sparse Core Ops, SparseCore 0:
  30.1 55.6 all-gather.5
  91.3 125.6 all-gather.3
  322.0 147.1 reduce-scatter.1

commit v7 on v6

--- a/solution.py
+++ b/solution.py
@@ -392,10 +392,11 @@
     bias_grad[...] = bias_sum
     chips, pieces, height, _ = weight_grad.shape
     columns = pieces // 4
+    wide = inside.shape[1]
     reduce_grad = sum(
         dot(act[i * block : (i + 1) * block], grad[...], (0, 0)) for i, grad in enumerate(grads)
     )
-    count = PIECE // (2 * height)
+    count = wide // (2 * height)
     reduce_grad = reduce_grad.reshape(count, 2 * height, reduce_grad.shape[1]).astype(BF16)
     mine = pl.ds(step * count, count)
     for half in range(2):
@@ -407,8 +408,11 @@
         dot(inside[i * block : (i + 1) * block], source[...], (0, 0))
         for i, source in enumerate(sources)
     )
-    expand_grad = jnp.transpose(flipped).reshape(chips, height, PIECE).astype(BF16)
-    weight_grad[:, step] = expand_grad
+    expand_grad = jnp.transpose(flipped).reshape(chips, height, wide).astype(BF16)
+    for i in range(wide // PIECE):
+        weight_grad[:, step * (wide // PIECE) + i] = expand_grad[
+            :, :, i * PIECE : (i + 1) * PIECE
+        ]
 
     @pl.when(step == pl.num_programs(0) - 1)
     def _():
@@ -421,16 +425,17 @@
     hidden = act.shape[1]
     chips, _, height, _ = weights.shape
     pieces = 2 * hidden // PIECE
-    expand_spec, reduce_spec = feed_weights(weights, 1, depth // PIECE)
+    expand_spec, reduce_spec = feed_weights(weights, 2, depth // PIECE)
+    wide = 2 * PIECE
     return pl.pallas_call(
         feed_back_kernel,
-        grid=(hidden // PIECE,),
+        grid=(hidden // wide,),
         in_specs=[resident((block, depth))] * (4 * CHUNKS)
-        + [column((2 * rows, PIECE))] * 2
+        + [column((2 * rows, wide))] * 2
         + [expand_spec, reduce_spec],
         out_specs=[
             resident((chips, pieces, height, PIECE)),
-            column((1, PIECE)),
+            column((1, wide)),
         ]
         + [resident((rows, depth))] * 2,
         out_shape=[
@@ -441,7 +446,7 @@
         ],
         scratch_shapes=[
             pltpu.VMEM((rows, depth), F32),
-            pltpu.VMEM((2 * rows, PIECE), BF16),
+            pltpu.VMEM((2 * rows, wide), BF16),
         ],
         compiler_params=pltpu.CompilerParams(vmem_limit_bytes=56 * MIB),
         cost_estimate=pl.CostEstimate(
@@ -734,9 +739,10 @@
         expand_bias,
     )
     vector_count = 8 * share + expand_bias.shape[0]
-    own_vectors = jnp.concatenate(vectors)
-    vector_row = jnp.pad(own_vectors, (0, 3 * lanes - vector_count))[None]
-    filler = jnp.concatenate([vector_row, jnp.zeros((15, 3 * lanes), BF16)])
+    filler = jnp.concatenate(
+        [jnp.pad(v[None], ((0, 0), (0, 3 * lanes - v.shape[0]))) for v in vectors]
+        + [jnp.zeros((16 - len(vectors), 3 * lanes), BF16)]
+    )
     held = jnp.stack(
         [
             jnp.concatenate(
@@ -761,8 +767,7 @@
     mine = jnp.concatenate(
         [held[:, :share, j * lanes : (j + 1) * lanes].reshape(-1, lanes) for j in range(3)]
     )
-    vector_rows = held[:, share, :vector_count].reshape(-1)
-    vector_rows = jnp.pad(vector_rows, (0, 16 * lanes - vector_rows.shape[0])).reshape(16, lanes)
+    vector_rows = held[:, share:, :lanes].reshape(-1, lanes)
     out_pieces = jnp.concatenate(
         [output_weight[:, i * lanes : (i + 1) * lanes] for i in range(ctx_size)]
     )
@@ -771,17 +776,12 @@
         SEQ,
         axis=0,
     )
-    packed = (
-        full_project[:, -16:]
-        .reshape(-1, 16 * lanes)[:, : ctx_size * vector_count]
-        .reshape(everyone, vector_count)
-        .astype(F32)
-    )
-    vectors = jnp.swapaxes(packed[:, : 8 * share].reshape(everyone, 8, share), 0, 1).reshape(
-        8, width
-    )
+    packed = full_project[:, -16 * ctx_size :].reshape(everyone, 16, lanes).astype(F32)
+    exp_bias = chosen(
+        packed[:, 8, : expand_bias.shape[0]].reshape(chips, 2, -1), core, 1
+    ).reshape(1, own_hidden)
+    vectors = jnp.swapaxes(packed[:, :8, :share], 0, 1).reshape(8, width)
     full_query, full_value = vectors[0], vectors[1]
-    exp_bias = chosen(packed[:, 8 * share :].reshape(chips, 2, -1), core, 1).reshape(1, own_hidden)
     bias_all = jnp.concatenate(
         [
             lax.dynamic_slice_in_dim(full_query, place * lanes, lanes),
@@ -884,9 +884,6 @@
         sizes["z"], 2, sizes["x"], 2, share, width
     )
     output_grad = halve(output_grad, 3, "c").astype(BF16)
-    output_grad = halve(output_grad, 2, "x").astype(BF16)
-    output_grad = halve(output_grad, 1, "y")
-    output_owned = z_scatter(output_grad)
 
     project_grad = []
     work_parts = []
@@ -904,7 +901,7 @@
             seg_query[at],
             project_grad,
             index == CHUNKS - 1,
-            across_sums[:index],
+            work_hops[:index],
         )
         project_grad = [project_part]
         across_sums.append((r2 + swap(r3).astype(F32)).astype(BF16))
@@ -914,13 +911,16 @@
         )
         sum_parts.append(sums)
     grad_work = jnp.concatenate(work_parts, axis=0)
-    project_grad = hold(project_grad[0], work_hops[:1])
-    blocks = halve(project_grad.reshape(sizes["z"], 2, ctx_size * share, 3 * lanes), 1, "y")
+    blocks = halve(
+        project_grad[0].reshape(sizes["z"], 2, ctx_size * share, 3 * lanes), 1, "y"
+    ).astype(BF16)
+    later = [blocks, work_hops[1]]
+    output_grad = halve(hold(output_grad, later), 2, "x").astype(BF16)
+    output_grad = halve(output_grad, 1, "y")
+    output_owned = z_scatter(output_grad)
     for step in z_steps:
         blocks = blocks.astype(BF16).reshape((blocks.shape[0] // 2, 2) + blocks.shape[1:])
         blocks = halve(blocks, 1, "z", step)
-        if step == 1:
-            blocks = hold(blocks.astype(BF16), work_hops[1:])
     weight_owned = halve(weight_owned, 0, "x")
     held = lax.all_to_all(
         hold(blocks.astype(F32).reshape(ctx_size, share, 3 * lanes), [weight_owned]),
@@ -974,7 +974,9 @@
         + [hidden_sums.reshape(everyone, -1)],
         axis=1,
     )
-    packed_grads = packed_grads.reshape(sizes["z"], 2, sizes["x"], 2, vector_count)
+    packed_grads = hold(packed_grads, later).reshape(
+        sizes["z"], 2, sizes["x"], 2, vector_count
+    )
     for axis, name in ((3, "c"), (2, "x"), (1, "y")):
         packed_grads = halve(packed_grads, axis, name)
     owned = z_scatter(packed_grads, F32)

time: 549 us -> 555 us (1.011)
  waiting for transfers between devices: 198 us -> 214 us
  local copies, waits for them, and re-layouts: 61.8 us -> 50 us
  starting transfers between devices: 36.2 us -> 42.3 us
    unnamed x139 -> x116, local copies, waits for them, and re-layouts: 36 us -> 25.6 us
    ppermute x15, waiting for transfers between devices: 76.8 us -> 83 us  [hop(): return lax.ppermute(array, CTX, [(i, i ^ step) for i in range(ctx_size)])]
    concatenate x1 -> x0, local copies, waits for them, and re-layouts: 6.09 us -> none  [on_device(): own_vectors = jnp.concatenate(vectors)]
    pad x2 -> x9, local copies, waits for them, and re-layouts: 0.02 us -> 5.95 us  [on_device(): jnp.pad(v[None], ((0, 0), (0, 3 * lanes - v.shape[0])))]
    ppermute x16, waiting for transfers between devices: 52.4 us -> 57.9 us  [trade(): lax.ppermute(array, name, [(i, i ^ step) for i in range(sizes[name])])]
where the time goes in v7:
time: 555 us; the launch traced here: 551 us
  waiting for transfers between devices  214 us (39%)
  Pallas kernels  201 us (36%)
  local copies, waits for them, and re-layouts  50 us (9%)
  starting transfers between devices  42.3 us (8%)
  other arithmetic  28.6 us (5%)
  between operations  15.2 us (3%)
    ppermute x15, waiting for transfers between devices, hop(): return lax.ppermute(array, CTX, [(i, i ^ step) for i in range(ctx_size)])  83 us
    pallas_call x2, Pallas kernels, attend_back(): pl.pallas_call(functools.partial(attend_back_kernel, len(after), len(earl...  59.9 us
    ppermute x16, waiting for transfers between devices, trade(): lax.ppermute(array, name, [(i, i ^ step) for i in range(sizes[name])])  57.9 us
    pallas_call x1, Pallas kernels, feed_back(): pl.pallas_call(feed_back_kernel, grid=(hidden // wide,), in_specs=[reside...  47.7 us
    all_gather x1, waiting for transfers between devices, on_device(): lax.all_gather(widen(own_pieces, 'x'), SEQ, axis=0)  44.2 us
    pallas_call x2, Pallas kernels, attend(): pl.pallas_call(functools.partial(attend_kernel, len(after)), grid=(count,...  30.8 us
    pallas_call x1, Pallas kernels, feed(): pl.pallas_call(feed_kernel, grid=(hidden // wide,), in_specs=[resident((b...  29.7 us
    pallas_call x6, Pallas kernels, row_call(): pl.pallas_call(kernel, grid=(rows // ROW_BLOCK,), in_specs=ins, out_specs...  28.3 us
  transfers between devices with their start and end apart: 51, of which 28 were waited for; matrix products, arithmetic and copies ran while one was open for 10% of the time, Pallas kernels for 22%

profile of v7, /device:TPU:0, one launch (start us, length us, event | category | flops | bytes accessed | tf_op | source)
XLA Modules:
  0.0 551.0 jit_solution(5481387367501823647)
XLA Ops:
  22.7 6.2 %all-to-all-done = bf16[4,48,768]{2,1,0:T(8,128)(2,1)S(1)} async-done(((bf16[4,48,768]{2,1,0:T(8,128)(2,1)}), bf16[4,48,768]{2,1,0:T(8,128)(2,1)S(1)}, u32[]{:S(2)}, u32[]{:S(2)}) %all-to-all-start) | async-done | bytes 294944 | tf_op jit(solution)/shard_map/all_to_all | solution.py:763
  33.6 43.5 %collective-permute-done.1.t2.refs_0_ = bf16[8,128,1024]{2,1,0:T(8,128)(2,1)} collective-permute-done((bf16[8,128,1024]{2,1,0:T(8,128)(2,1)S(1)}, bf16[8,128,1024]{2,1,0:T(8,128)(2,1)}, u32[]{:S(2)}, u32[]{:S(2)}) %collective-permute-start.1) | collective-permute-done | bytes 2097184 | tf_op jit(solution)/shard_map/ppermute | solution.py:681
  77.9 11.9 %collective-permute-done.14 = bf16[16,64,256]{2,1,0:T(8,128)(2,1)S(1)} collective-permute-done((bf16[16,64,256]{2,1,0:T(8,128)(2,1)S(1)}, bf16[16,64,256]{2,1,0:T(8,128)(2,1)S(1)}, u32[]{:S(2)}, u32[]{:S(2)}) %collective-permute-start.14) | collective-permute-done | bytes 524320 | tf_op jit(solution)/shard_map/ppermute | solution.py:701
  101.0 15.0 %attend_forward.2 = (bf16[4,128,256]{2,1,0:T(8,128)(2,1)S(1)}, bf16[4,128,256]{2,1,0:T(8,128)(2,1)S(1)}, bf16[4,128,256]{2,1,0:T(8,128)(2,1)S(1)}, bf16[4,128,25...) custom-call(bf16[8,128,1024]{2,1,0:T(8,128)(2,1)S(1)} %copy-done.2, ...), custom_call_target="tpu_custom_call" | custom-call | flops 7515144192 | bytes 10485760 | tf_op jit(solution)/shard_map/attend_forward/pallas_call | solution.py:142
  121.4 15.8 %attend_forward.3 = (bf16[4,128,256]{2,1,0:T(8,128)(2,1)S(1)}, bf16[4,128,256]{2,1,0:T(8,128)(2,1)}, bf16[4,128,256]{2,1,0:T(8,128)(2,1)}, bf16[4,128,256]{2,1,0...) custom-call(bf16[8,128,1024]{2,1,0:T(8,128)(2,1)S(1)} %copy-done.2, ...), custom_call_target="tpu_custom_call" | custom-call | flops 7515144192 | bytes 10485760 | tf_op jit(solution)/shard_map/attend_forward/pallas_call | solution.py:142
  172.6 44.2 %all-gather.4.cloned.1.call-done = bf16[8,2,16,64,256]{4,3,2,1,0:T(8,128)(2,1)} async-done(((bf16[1,2,16,64,256]{4,3,2,1,0:T(8,128)(2,1)}), bf16[8,2,16,64,256]{4,3,2,1,0:T(8,128)(2,1)}) %all-gather.4.cloned.1.call-update) | async-done | bytes 8388624 | tf_op jit(solution)/shard_map/all_gather | solution.py:813
  216.8 29.7 %feed_forward.1 = (bf16[2048,2048]{1,0:T(8,128)(2,1)}, bf16[2048,2048]{1,0:T(8,128)(2,1)}, f32[1024,1024]{1,0:T(8,128)}, bf16[1024,1024]{1,0:T(8,128)(2,1)}) custom-call(bf16[512,1024]{1,0:T(8,128)(2,1)} %copy-done.23, bf16[512,1024]{1,0:T(8,128)(2,1)} %copy-done.22, bf16[512,1024]{1,0:T(8,128)(2,1)} %copy-done.45, bf16[512,1024]{1,0:T(8,128)(2,1)} %copy-done.44, ...), custom_call_target="tpu_custom_call" | custom-call | flops 17179869184 | bytes 29360128 | tf_op jit(solution)/shard_map/feed_forward/pallas_call | solution.py:345
  246.6 4.4 collective-permute-done.15.far
  257.9 4.4 second_norm.2
  267.2 47.7 %feed_backward.1 = (bf16[16,16,64,256]{3,2,1,0:T(8,128)(2,1)}, f32[1,2048]{1,0:T(1,128)}, f32[1024,1024]{1,0:T(8,128)}, bf16[1024,1024]{1,0:T(8,128)(2,1)}) custom-call(bf16[512,1024]{1,0:T(8,128)(2,1)} %copy-done.25, bf16[512,1024]{1,0:T(8,128)(2,1)} %copy-done.24, bf16[512,1024]{1,0:T(8,128)(2,1)} %copy-done.47, bf16[512,1024]{1,0:T(8,128)(2,1)} %copy-done.46, ...), custom_call_target="tpu_custom_call" | custom-call | flops 34359738368 | bytes 54525952 | tf_op jit(solution)/shard_map/feed_backward/pallas_call | solution.py:430
  315.1 4.2 collective-permute-done.18.far
  320.7 6.1 %first_back.2 = (f32[512,1024]{1,0:T(8,128)S(1)}, bf16[512,1024]{1,0:T(8,128)(2,1)S(1)}, bf16[4,128,256]{2,1,0:T(8,128)(2,1)S(1)}, bf16[4,128,256]{2,1,0:T(8,128...) custom-call(s32[1]{0:T(128)} %bitcast.place, ...), custom_call_target="tpu_custom_call" | custom-call | flops 1073741824 | bytes 8388608 | tf_op jit(solution)/shard_map/first_back/pallas_call | solution.py:494
  331.0 7.4 %collective-permute-done.20.g2 = bf16[4,128,256]{2,1,0:T(8,128)(2,1)S(1)} collective-permute-done((bf16[4,128,256]{2,1,0:T(8,128)(2,1)S(1)}, bf16[4,128,256]{2,1,0:T(8,128)(2,1)S(1)}, u32[]{:S(2)}, u32[]{:S(2)}) %collective-permute-start.20) | collective-permute-done | bytes 262176 | tf_op jit(solution)/shard_map/ppermute | solution.py:681
  338.4 4.5 collective-permute-done.21.g3
  342.9 29.5 %attend_backward.2 = (f32[768,1024]{1,0:T(8,128)}, f32[4,128,1024]{2,1,0:T(8,128)}, bf16[4,128,1024]{2,1,0:T(8,128)(2,1)}, f32[4,128,1024]{2,1,0:T(8,128)}, bf16...) custom-call(bf16[4,512,768]{2,1,0:T(8,128)(2,1)} %get-tuple-element.106.saved, ...), custom_call_target="tpu_custom_call" | custom-call | flops 17178820608 | bytes 22020096 | tf_op jit(solution)/shard_map/attend_backward/pallas_call | solution.py:238
  382.0 5.9 %first_back.3 = (f32[512,1024]{1,0:T(8,128)S(1)}, bf16[512,1024]{1,0:T(8,128)(2,1)S(1)}, bf16[4,128,256]{2,1,0:T(8,128)(2,1)S(1)}, bf16[4,128,256]{2,1,0:T(8,128...) custom-call(s32[1]{0:T(128)} %bitcast.place, ...), custom_call_target="tpu_custom_call" | custom-call | flops 1073741824 | bytes 8388608 | tf_op jit(solution)/shard_map/first_back/pallas_call | solution.py:494
  396.7 13.8 %collective-permute-done.26.g2 = bf16[4,128,256]{2,1,0:T(8,128)(2,1)S(1)} collective-permute-done((bf16[4,128,256]{2,1,0:T(8,128)(2,1)S(1)}, bf16[4,128,256]{2,1,0:T(8,128)(2,1)S(1)}, u32[]{:S(2)}, u32[]{:S(2)}) %collective-permute-start.26) | collective-permute-done | bytes 262176 | tf_op jit(solution)/shard_map/ppermute | solution.py:681
  410.5 4.5 collective-permute-done.27.g3
  415.0 30.4 %attend_backward.3 = (bf16[1024,768]{1,0:T(8,128)(2,1)}, f32[4,128,1024]{2,1,0:T(8,128)}, bf16[4,128,1024]{2,1,0:T(8,128)(2,1)}, f32[4,128,1024]{2,1,0:T(8,128)}...) custom-call(bf16[4,512,768]{2,1,0:T(8,128)(2,1)} %get-tuple-element.119.saved, ...), custom_call_target="tpu_custom_call" | custom-call | flops 17178820608 | bytes 22020096 | tf_op jit(solution)/shard_map/attend_backward/pallas_call | solution.py:238
  456.3 12.1 %collective-permute-done.31 = bf16[4,128,768]{2,1,0:T(8,128)(2,1)} collective-permute-done((bf16[4,128,768]{2,1,0:T(8,128)(2,1)}, bf16[4,128,768]{2,1,0:T(8,128)(2,1)}, u32[]{:S(2)}, u32[]{:S(2)}) %collective-permute-start.31) | collective-permute-done | bytes 786464 | tf_op jit(solution)/shard_map/ppermute | solution.py:701
  473.5 7.0 %collective-permute-done.32 = bf16[2,128,768]{2,1,0:T(8,128)(2,1)S(1)} collective-permute-done((bf16[2,128,768]{2,1,0:T(8,128)(2,1)S(1)}, bf16[2,128,768]{2,1,0:T(8,128)(2,1)S(1)}, u32[]{:S(2)}, u32[]{:S(2)}) %collective-permute-start.32) | collective-permute-done | bytes 393248 | tf_op jit(solution)/shard_map/ppermute | solution.py:701
  484.4 8.7 %collective-permute-done.33 = bf16[1,128,768]{2,1,0:T(8,128)(2,1)S(1)} collective-permute-done((bf16[1,128,768]{2,1,0:T(8,128)(2,1)S(1)}, bf16[1,128,768]{2,1,0:T(8,128)(2,1)S(1)}, u32[]{:S(2)}, u32[]{:S(2)}) %collective-permute-start.33) | collective-permute-done | bytes 196640 | tf_op jit(solution)/shard_map/ppermute | solution.py:701
  504.3 4.8 collective-permute-done.41
  522.5 7.2 %collective-permute-done.34 = bf16[16,64,256]{2,1,0:T(8,128)(2,1)S(1)} collective-permute-done((bf16[16,64,256]{2,1,0:T(8,128)(2,1)S(1)}, bf16[16,64,256]{2,1,0:T(8,128)(2,1)S(1)}, u32[]{:S(2)}, u32[]{:S(2)}) %collective-permute-start.34) | collective-permute-done | bytes 524320 | tf_op jit(solution)/shard_map/ppermute | solution.py:701
  (342 shorter events, 166.8 us)
Async XLA Ops:
  8.0 14.6 %collective-permute-start.3 = (bf16[128,256]{1,0:T(8,128)(2,1)S(1)}, bf16[128,256]{1,0:T(8,128)(2,1)S(1)}, u32[]{:S(2)}, u32[]{:S(2)}) collective-permute-start(bf16[128,256]{1,0:T(8,128)(2,1)S(1)} %get-tuple-element.173), channel_id=1, source_target_pairs={{0,2},{2,0},{1,3},{3,1},{4,6},{6,4},{5,7},{7,5},{8,10},{10,8},{9,1... | collective-permute-start | bytes 196616 | tf_op jit(solution)/shard_map/ppermute | solution.py:701
  22.5 69.7 %all-gather.6.cloned.1.call-start = ((), (), s32[]{:S(2)}) async-start(), calls=%async_computation.5 | async-start | bytes 3244032 | tf_op jit(solution)/shard_map/all_gather | solution.py:774
  29.7 187.0 %all-gather.4.cloned.1.call-start = ((), (), s32[]{:S(2)}) async-start(), calls=%async_computation.3 | async-start | bytes 9437184 | tf_op jit(solution)/shard_map/all_gather | solution.py:813
  29.8 47.3 %collective-permute-start.1 = (bf16[8,128,1024]{2,1,0:T(8,128)(2,1)S(1)}, bf16[8,128,1024]{2,1,0:T(8,128)(2,1)}, u32[]{:S(2)}, u32[]{:S(2)}) collective-permute-start(bf16[8,128,1024]{2,1,0:T(8,128)(2,1)S(1)} %copy-done.2), channel_id=1, source_target_pairs={{0,2},{1,3},{2,0},{3,1},{4,6},{5,7},{6,4},{7,5},{8,10},{9,11},{10,... | collective-permute-start | bytes 6291464 | tf_op jit(solution)/shard_map/ppermute | solution.py:681
  77.2 12.6 %collective-permute-start.14 = (bf16[16,64,256]{2,1,0:T(8,128)(2,1)S(1)}, bf16[16,64,256]{2,1,0:T(8,128)(2,1)S(1)}, u32[]{:S(2)}, u32[]{:S(2)}) collective-permute-start(bf16[16,64,256]{2,1,0:T(8,128)(2,1)S(1)} %hold.4), channel_id=1, source_target_pairs={{0,2},{2,0},{1,3},{3,1},{4,6},{6,4},{5,7},{7,5},{8,10},{10,8},{9,1... | collective-permute-start | bytes 1572872 | tf_op jit(solution)/shard_map/ppermute | solution.py:701
  91.0 425.8 %reduce-scatter.2.cloned.1.call-start = ((), (), s32[]{:S(2)}) async-start(), calls=%async_computation.4 | async-start | bytes 9437184 | tf_op jit(solution)/shard_map/reduce_scatter | solution.py:858
  116.8 24.6 %collective-permute-start.7 = (bf16[16,32,1024]{2,1,0:T(8,128)(2,1)S(1)}, bf16[16,32,1024]{2,1,0:T(8,128)(2,1)}, u32[]{:S(2)}, u32[]{:S(2)}) collective-permute-start(bf16[16,32,1024]{2,1,0:T(8,128)(2,1)S(1)} %bitcast.237), channel_id=1, source_target_pairs={{0,1},{1,0},{2,3},{3,2},{4,5},{5,4},{6,7},{7,6},{8,9},{9,8},{10,11... | collective-permute-start | bytes 3145736 | tf_op jit(solution)/shard_map/ppermute | solution.py:684
  139.0 12.6 %collective-permute-start.10 = (bf16[4,128,256]{2,1,0:T(8,128)(2,1)}, bf16[4,128,256]{2,1,0:T(8,128)(2,1)S(1)}, u32[]{:S(2)}, u32[]{:S(2)}) collective-permute-start(bf16[4,128,256]{2,1,0:T(8,128)(2,1)} %get-tuple-element.90), channel_id=1, source_target_pairs={{0,3},{1,2},{2,1},{3,0},{4,7},{5,6},{6,5},{7,4},{8,11},{9,10},{10,... | collective-permute-start | bytes 786440 | tf_op jit(solution)/shard_map/ppermute | solution.py:681
  139.9 19.8 %collective-permute-start.4 = (bf16[4,128,256]{2,1,0:T(8,128)(2,1)}, bf16[4,128,256]{2,1,0:T(8,128)(2,1)S(1)}, u32[]{:S(2)}, u32[]{:S(2)}) collective-permute-start(bf16[4,128,256]{2,1,0:T(8,128)(2,1)} %copy-done.28), channel_id=1, source_target_pairs={{0,1},{1,0},{2,3},{3,2},{4,5},{5,4},{6,7},{7,6},{8,9},{9,8},{10,11... | collective-permute-start | bytes 786440 | tf_op jit(solution)/shard_map/ppermute | solution.py:681
  140.6 19.0 %collective-permute-start.5 = (bf16[4,128,256]{2,1,0:T(8,128)(2,1)}, bf16[4,128,256]{2,1,0:T(8,128)(2,1)S(1)}, u32[]{:S(2)}, u32[]{:S(2)}) collective-permute-start(bf16[4,128,256]{2,1,0:T(8,128)(2,1)} %copy-done.27), channel_id=1, source_target_pairs={{0,2},{1,3},{2,0},{3,1},{4,6},{5,7},{6,4},{7,5},{8,10},{9,11},{10,... | collective-permute-start | bytes 786440 | tf_op jit(solution)/shard_map/ppermute | solution.py:681
  141.4 21.4 %collective-permute-start.6 = (bf16[4,128,256]{2,1,0:T(8,128)(2,1)}, bf16[4,128,256]{2,1,0:T(8,128)(2,1)S(1)}, u32[]{:S(2)}, u32[]{:S(2)}) collective-permute-start(bf16[4,128,256]{2,1,0:T(8,128)(2,1)} %copy-done.26), channel_id=1, source_target_pairs={{0,3},{1,2},{2,1},{3,0},{4,7},{5,6},{6,5},{7,4},{8,11},{9,10},{10,... | collective-permute-start | bytes 786440 | tf_op jit(solution)/shard_map/ppermute | solution.py:681
  157.8 13.8 %collective-permute-start.12 = (bf16[512,1024]{1,0:T(8,128)(2,1)S(1)}, bf16[512,1024]{1,0:T(8,128)(2,1)S(1)}, u32[]{:S(2)}, u32[]{:S(2)}) collective-permute-start(bf16[512,1024]{1,0:T(8,128)(2,1)S(1)} %get-tuple-element.91.refs_1_.refs_5_), channel_id=1, source_target_pairs={{0,1},{1,0},{2,3},{3,2},{4,5},{5,4},{6,7},{7,6},{8,9},{9,8},{10,11... | collective-permute-start | bytes 3145736 | tf_op jit(solution)/shard_map/ppermute | solution.py:684
  330.8 12.1 %collective-permute-start.21 = (bf16[4,128,256]{2,1,0:T(8,128)(2,1)S(1)}, bf16[4,128,256]{2,1,0:T(8,128)(2,1)S(1)}, u32[]{:S(2)}, u32[]{:S(2)}) collective-permute-start(bf16[4,128,256]{2,1,0:T(8,128)(2,1)S(1)} %get-tuple-element.111), channel_id=1, source_target_pairs={{0,3},{1,2},{2,1},{3,0},{4,7},{5,6},{6,5},{7,4},{8,11},{9,10},{10,... | collective-permute-start | bytes 786440 | tf_op jit(solution)/shard_map/ppermute | solution.py:681
  378.7 36.3 %collective-permute-start.24 = (bf16[4,128,1024]{2,1,0:T(8,128)(2,1)}, bf16[4,128,1024]{2,1,0:T(8,128)(2,1)}, u32[]{:S(2)}, u32[]{:S(2)}) collective-permute-start(bf16[4,128,1024]{2,1,0:T(8,128)(2,1)} %add_convert_fusion.1), channel_id=1, source_target_pairs={{0,2},{1,3},{2,0},{3,1},{4,6},{5,7},{6,4},{7,5},{8,10},{9,11},{10,... | collective-permute-start | bytes 3145736 | tf_op jit(solution)/shard_map/ppermute | solution.py:681
  389.4 21.1 %collective-permute-start.26 = (bf16[4,128,256]{2,1,0:T(8,128)(2,1)S(1)}, bf16[4,128,256]{2,1,0:T(8,128)(2,1)S(1)}, u32[]{:S(2)}, u32[]{:S(2)}) collective-permute-start(bf16[4,128,256]{2,1,0:T(8,128)(2,1)S(1)} %get-tuple-element.123), channel_id=1, source_target_pairs={{0,2},{1,3},{2,0},{3,1},{4,6},{5,7},{6,4},{7,5},{8,10},{9,11},{10,... | collective-permute-start | bytes 786440 | tf_op jit(solution)/shard_map/ppermute | solution.py:681
  389.8 25.2 %collective-permute-start.27 = (bf16[4,128,256]{2,1,0:T(8,128)(2,1)S(1)}, bf16[4,128,256]{2,1,0:T(8,128)(2,1)S(1)}, u32[]{:S(2)}, u32[]{:S(2)}) collective-permute-start(bf16[4,128,256]{2,1,0:T(8,128)(2,1)S(1)} %get-tuple-element.124), channel_id=1, source_target_pairs={{0,3},{1,2},{2,1},{3,0},{4,7},{5,6},{6,5},{7,4},{8,11},{9,10},{10,... | collective-permute-start | bytes 786440 | tf_op jit(solution)/shard_map/ppermute | solution.py:681
  396.2 53.3 %collective-permute-start.40 = (bf16[4,2,2,32,1024]{4,3,2,1,0:T(8,128)(2,1)S(1)}, bf16[4,2,2,32,1024]{4,3,2,1,0:T(8,128)(2,1)}, u32[]{:S(2)}, u32[]{:S(2)}) collective-permute-start(bf16[4,2,2,32,1024]{4,3,2,1,0:T(8,128)(2,1)S(1)} %dynamic-slice_bitcast_fusion), channel_id=1, source_target_pairs={{0,1},{1,0},{2,3},{3,2},{4,5},{5,4},{6,7},{7,6},{8,9},{9,8},{10,11... | collective-permute-start | bytes 3145736 | tf_op jit(solution)/shard_map/ppermute | solution.py:701
  446.1 23.8 %collective-permute-start.22 = (bf16[4,128,1024]{2,1,0:T(8,128)(2,1)}, bf16[4,128,1024]{2,1,0:T(8,128)(2,1)}, u32[]{:S(2)}, u32[]{:S(2)}) collective-permute-start(bf16[4,128,1024]{2,1,0:T(8,128)(2,1)} %get-tuple-element.113), channel_id=1, source_target_pairs={{0,1},{1,0},{2,3},{3,2},{4,5},{5,4},{6,7},{7,6},{8,9},{9,8},{10,11... | collective-permute-start | bytes 3145736 | tf_op jit(solution)/shard_map/ppermute | solution.py:684
  448.3 20.1 %collective-permute-start.31 = (bf16[4,128,768]{2,1,0:T(8,128)(2,1)}, bf16[4,128,768]{2,1,0:T(8,128)(2,1)}, u32[]{:S(2)}, u32[]{:S(2)}) collective-permute-start(bf16[4,128,768]{2,1,0:T(8,128)(2,1)} %dynamic-slice_bitcast_fusion.1), channel_id=1, source_target_pairs={{0,4},{4,0},{1,5},{5,1},{2,6},{6,2},{3,7},{7,3},{8,12},{12,8},{9,1... | collective-permute-start | bytes 2359304 | tf_op jit(solution)/shard_map/ppermute | solution.py:701
  452.2 45.8 %collective-permute-start.28 = (bf16[4,128,1024]{2,1,0:T(8,128)(2,1)}, bf16[4,128,1024]{2,1,0:T(8,128)(2,1)}, u32[]{:S(2)}, u32[]{:S(2)}) collective-permute-start(bf16[4,128,1024]{2,1,0:T(8,128)(2,1)} %get-tuple-element.127), channel_id=1, source_target_pairs={{0,1},{1,0},{2,3},{3,2},{4,5},{5,4},{6,7},{7,6},{8,9},{9,8},{10,11... | collective-permute-start | bytes 3145736 | tf_op jit(solution)/shard_map/ppermute | solution.py:684
  454.8 25.8 %collective-permute-start.30 = (bf16[4,128,1024]{2,1,0:T(8,128)(2,1)S(1)}, bf16[4,128,1024]{2,1,0:T(8,128)(2,1)S(1)}, u32[]{:S(2)}, u32[]{:S(2)}) collective-permute-start(bf16[4,128,1024]{2,1,0:T(8,128)(2,1)S(1)} %add_convert_fusion), channel_id=1, source_target_pairs={{0,2},{1,3},{2,0},{3,1},{4,6},{5,7},{6,4},{7,5},{8,10},{9,11},{10,... | collective-permute-start | bytes 3145736 | tf_op jit(solution)/shard_map/ppermute | solution.py:681
  480.8 12.2 %collective-permute-start.33 = (bf16[1,128,768]{2,1,0:T(8,128)(2,1)S(1)}, bf16[1,128,768]{2,1,0:T(8,128)(2,1)S(1)}, u32[]{:S(2)}, u32[]{:S(2)}) collective-permute-start(bf16[1,128,768]{2,1,0:T(8,128)(2,1)S(1)} %constant_dynamic-slice_fusion.11), channel_id=1, source_target_pairs={{0,16},{8,24},{16,0},{24,8},{1,17},{9,25},{17,1},{25,9},{2,18},{10... | collective-permute-start | bytes 589832 | tf_op jit(solution)/shard_map/ppermute | solution.py:701
  495.4 13.7 %collective-permute-start.41 = (bf16[4,2,32,1024]{3,2,1,0:T(8,128)(2,1)S(1)}, bf16[4,2,32,1024]{3,2,1,0:T(8,128)(2,1)S(1)}, u32[]{:S(2)}, u32[]{:S(2)}) collective-permute-start(bf16[4,2,32,1024]{3,2,1,0:T(8,128)(2,1)S(1)} %dynamic-slice_bitcast_fusion.2), channel_id=1, source_target_pairs={{0,2},{2,0},{1,3},{3,1},{4,6},{6,4},{5,7},{7,5},{8,10},{10,8},{9,1... | collective-permute-start | bytes 1572872 | tf_op jit(solution)/shard_map/ppermute | solution.py:701
  521.8 14.2 %collective-permute-start.44 = (bf16[1,32,1024]{2,1,0:T(8,128)(2,1)S(1)}, bf16[1,32,1024]{2,1,0:T(8,128)(2,1)S(1)}, u32[]{:S(2)}, u32[]{:S(2)}) collective-permute-start(bf16[1,32,1024]{2,1,0:T(8,128)(2,1)S(1)} %constant_dynamic-slice_fusion), channel_id=1, source_target_pairs={{0,16},{8,24},{16,0},{24,8},{1,17},{9,25},{17,1},{25,9},{2,18},{10... | collective-permute-start | bytes 196616 | tf_op jit(solution)/shard_map/ppermute | solution.py:701
  (75 other events, 504.5 us)
Sparse Core Ops, SparseCore 0:
  29.9 57.9 all-gather.5
  91.1 125.6 all-gather.3
  315.1 147.1 reduce-scatter.1

commit v8 on v7

--- a/solution.py
+++ b/solution.py
@@ -251,7 +251,7 @@
         + [by_row((1, part, depth))] * 4
         + [by_row((1, 1, wide))],
         out_shape=[jax.ShapeDtypeStruct(shape, kind)]
-        + [jax.ShapeDtypeStruct((count, part, depth), t) for t in (F32, BF16, F32, BF16)]
+        + [jax.ShapeDtypeStruct((count, part, depth), t) for t in (F32, BF16, BF16, BF16)]
         + [jax.ShapeDtypeStruct((count, 1, wide), F32)],
         scratch_shapes=[pltpu.VMEM((wide, depth), F32)],
         compiler_params=pltpu.CompilerParams(vmem_limit_bytes=52 * MIB),
@@ -739,9 +739,8 @@
         expand_bias,
     )
     vector_count = 8 * share + expand_bias.shape[0]
-    filler = jnp.concatenate(
-        [jnp.pad(v[None], ((0, 0), (0, 3 * lanes - v.shape[0]))) for v in vectors]
-        + [jnp.zeros((16 - len(vectors), 3 * lanes), BF16)]
+    filler = jnp.pad(jnp.stack(vectors[:8]), ((0, 8), (0, 3 * lanes - share))) + jnp.pad(
+        expand_bias[None], ((8, 7), (0, 3 * lanes - expand_bias.shape[0]))
     )
     held = jnp.stack(
         [
@@ -883,8 +882,6 @@
     output_grad = output_back(where, mixed_low, grad_attended, ctx_size).reshape(
         sizes["z"], 2, sizes["x"], 2, share, width
     )
-    output_grad = halve(output_grad, 3, "c").astype(BF16)
-
     project_grad = []
     work_parts = []
     across_sums = []
@@ -901,29 +898,29 @@
             seg_query[at],
             project_grad,
             index == CHUNKS - 1,
-            work_hops[:index],
+            across_sums[:1] if index else grad_attended[1:],
         )
         project_grad = [project_part]
-        across_sums.append((r2 + swap(r3).astype(F32)).astype(BF16))
+        across_sums.append((r2.astype(F32) + swap(r3).astype(F32)).astype(BF16))
         work_hops.append(hop(across_sums[index], 2))
         work_parts.append(
             grad_hidden[index] + r0 + swap(r1).astype(F32) + work_hops[index].astype(F32)
         )
         sum_parts.append(sums)
     grad_work = jnp.concatenate(work_parts, axis=0)
+    project_grad = [hold(project_grad[0], work_hops[:1])]
     blocks = halve(
         project_grad[0].reshape(sizes["z"], 2, ctx_size * share, 3 * lanes), 1, "y"
     ).astype(BF16)
     later = [blocks, work_hops[1]]
-    output_grad = halve(hold(output_grad, later), 2, "x").astype(BF16)
-    output_grad = halve(output_grad, 1, "y")
-    output_owned = z_scatter(output_grad)
     for step in z_steps:
         blocks = blocks.astype(BF16).reshape((blocks.shape[0] // 2, 2) + blocks.shape[1:])
         blocks = halve(blocks, 1, "z", step)
-    weight_owned = halve(weight_owned, 0, "x")
+        if step == 1:
+            weight_owned = halve(weight_owned, 0, "x")
+            blocks = hold(blocks.astype(BF16), [weight_owned])
     held = lax.all_to_all(
-        hold(blocks.astype(F32).reshape(ctx_size, share, 3 * lanes), [weight_owned]),
+        blocks.astype(F32).reshape(ctx_size, share, 3 * lanes),
         CTX,
         0,
         0,
@@ -974,12 +971,19 @@
         + [hidden_sums.reshape(everyone, -1)],
         axis=1,
     )
-    packed_grads = hold(packed_grads, later).reshape(
-        sizes["z"], 2, sizes["x"], 2, vector_count
-    )
+    packed_grads = jnp.pad(packed_grads, ((0, 0), (0, width - vector_count))).astype(BF16)
+    shared = jnp.concatenate(
+        [
+            output_grad.reshape(everyone, share, width),
+            hold(packed_grads, later)[:, None],
+        ],
+        axis=1,
+    ).reshape(sizes["z"], 2, sizes["x"], 2, share + 1, width)
     for axis, name in ((3, "c"), (2, "x"), (1, "y")):
-        packed_grads = halve(packed_grads, axis, name)
-    owned = z_scatter(packed_grads, F32)
+        shared = halve(shared, axis, name).astype(BF16)
+    shared = z_scatter(shared)
+    output_owned = shared[:share]
+    owned = shared[share, :vector_count]
     small = [owned[i * share : (i + 1) * share] for i in range(8)]
     return (
         layer_work,

time: 555 us -> 553 us (level)
  local copies, waits for them, and re-layouts: 50 us -> 64.4 us
  waiting for transfers between devices: 214 us -> 204 us
  starting transfers between devices: 42.3 us -> 34.8 us
    unnamed x116 -> x152, local copies, waits for them, and re-layouts: 25.6 us -> 44.9 us
    ppermute x15, waiting for transfers between devices: 83 us -> 74.6 us  [hop(): return lax.ppermute(array, CTX, [(i, i ^ step) for i in range(ctx_size)])]
    ppermute x16 -> x11, starting transfers between devices: 18.2 us -> 11.8 us  [trade(): lax.ppermute(array, name, [(i, i ^ step) for i in range(sizes[name])])]
    pad x9 -> x1, local copies, waits for them, and re-layouts: 5.95 us -> 0.01 us  [on_device(): jnp.pad(packed_grads, ((0, 0), (0, width - vector_count))).astype(BF16)]
    ppermute x16 -> x11, waiting for transfers between devices: 57.9 us -> 57.7 us  [trade(): lax.ppermute(array, name, [(i, i ^ step) for i in range(sizes[name])])]
  transfers between devices with their start and end apart: 51 -> 46, of which waited for: 28 -> 25; matrix products, arithmetic and copies ran while one was open for 10% -> 10% of each run, Pallas kernels for 22% -> 22%
where the time goes in v8:
time: 553 us; the launch traced here: 549 us
  waiting for transfers between devices  204 us (37%)
  Pallas kernels  200 us (36%)
  local copies, waits for them, and re-layouts  64.4 us (12%)
  starting transfers between devices  34.8 us (6%)
  other arithmetic  30.4 us (5%)
  between operations  15.1 us (3%)
    ppermute x15, waiting for transfers between devices, hop(): return lax.ppermute(array, CTX, [(i, i ^ step) for i in range(ctx_size)])  74.6 us
    pallas_call x2, Pallas kernels, attend_back(): pl.pallas_call(functools.partial(attend_back_kernel, len(after), len(earl...  60.1 us
    ppermute x11, waiting for transfers between devices, trade(): lax.ppermute(array, name, [(i, i ^ step) for i in range(sizes[name])])  57.7 us
    pallas_call x1, Pallas kernels, feed_back(): pl.pallas_call(feed_back_kernel, grid=(hidden // wide,), in_specs=[reside...  47.6 us
    unnamed x152, local copies, waits for them, and re-layouts  44.9 us
    all_gather x1, waiting for transfers between devices, on_device(): lax.all_gather(widen(own_pieces, 'x'), SEQ, axis=0)  44.3 us
    pallas_call x2, Pallas kernels, attend(): pl.pallas_call(functools.partial(attend_kernel, len(after)), grid=(count,...  30.8 us
    pallas_call x1, Pallas kernels, feed(): pl.pallas_call(feed_kernel, grid=(hidden // wide,), in_specs=[resident((b...  29.6 us
  transfers between devices with their start and end apart: 46, of which 25 were waited for; matrix products, arithmetic and copies ran while one was open for 10% of the time, Pallas kernels for 22%

profile of v8, /device:TPU:0, one launch (start us, length us, event | category | flops | bytes accessed | tf_op | source)
XLA Modules:
  0.0 548.5 jit_solution(11539399887602889529)
XLA Ops:
  17.8 6.2 %all-to-all-done = bf16[4,48,768]{2,1,0:T(8,128)(2,1)S(1)} async-done(((bf16[4,48,768]{2,1,0:T(8,128)(2,1)}), bf16[4,48,768]{2,1,0:T(8,128)(2,1)S(1)}, u32[]{:S(2)}, u32[]{:S(2)}) %all-to-all-start) | async-done | bytes 294944 | tf_op jit(solution)/shard_map/all_to_all | solution.py:762
  28.8 43.5 %collective-permute-done.1.t2.refs_0_ = bf16[8,128,1024]{2,1,0:T(8,128)(2,1)} collective-permute-done((bf16[8,128,1024]{2,1,0:T(8,128)(2,1)S(1)}, bf16[8,128,1024]{2,1,0:T(8,128)(2,1)}, u32[]{:S(2)}, u32[]{:S(2)}) %collective-permute-start.1) | collective-permute-done | bytes 2097184 | tf_op jit(solution)/shard_map/ppermute | solution.py:681
  73.1 11.9 %collective-permute-done.14 = bf16[16,64,256]{2,1,0:T(8,128)(2,1)S(1)} collective-permute-done((bf16[16,64,256]{2,1,0:T(8,128)(2,1)S(1)}, bf16[16,64,256]{2,1,0:T(8,128)(2,1)S(1)}, u32[]{:S(2)}, u32[]{:S(2)}) %collective-permute-start.14) | collective-permute-done | bytes 524320 | tf_op jit(solution)/shard_map/ppermute | solution.py:701
  96.1 15.0 %attend_forward.2 = (bf16[4,128,256]{2,1,0:T(8,128)(2,1)S(1)}, bf16[4,128,256]{2,1,0:T(8,128)(2,1)S(1)}, bf16[4,128,256]{2,1,0:T(8,128)(2,1)S(1)}, bf16[4,128,25...) custom-call(bf16[8,128,1024]{2,1,0:T(8,128)(2,1)S(1)} %copy-done.2, ...), custom_call_target="tpu_custom_call" | custom-call | flops 7515144192 | bytes 10485760 | tf_op jit(solution)/shard_map/attend_forward/pallas_call | solution.py:142
  116.5 15.8 %attend_forward.3 = (bf16[4,128,256]{2,1,0:T(8,128)(2,1)S(1)}, bf16[4,128,256]{2,1,0:T(8,128)(2,1)}, bf16[4,128,256]{2,1,0:T(8,128)(2,1)}, bf16[4,128,256]{2,1,0...) custom-call(bf16[8,128,1024]{2,1,0:T(8,128)(2,1)S(1)} %copy-done.2, ...), custom_call_target="tpu_custom_call" | custom-call | flops 7515144192 | bytes 10485760 | tf_op jit(solution)/shard_map/attend_forward/pallas_call | solution.py:142
  167.6 44.3 %all-gather.4.cloned.1.call-done = bf16[8,2,16,64,256]{4,3,2,1,0:T(8,128)(2,1)} async-done(((bf16[1,2,16,64,256]{4,3,2,1,0:T(8,128)(2,1)}), bf16[8,2,16,64,256]{4,3,2,1,0:T(8,128)(2,1)}) %all-gather.4.cloned.1.call-update) | async-done | bytes 8388624 | tf_op jit(solution)/shard_map/all_gather | solution.py:812
  211.9 29.6 %feed_forward.1 = (bf16[2048,2048]{1,0:T(8,128)(2,1)}, bf16[2048,2048]{1,0:T(8,128)(2,1)}, f32[1024,1024]{1,0:T(8,128)}, bf16[1024,1024]{1,0:T(8,128)(2,1)}) custom-call(bf16[512,1024]{1,0:T(8,128)(2,1)} %copy-done.37, bf16[512,1024]{1,0:T(8,128)(2,1)} %copy-done.36, bf16[512,1024]{1,0:T(8,128)(2,1)} %copy-done.62, bf16[512,1024]{1,0:T(8,128)(2,1)} %copy-done.61, ...), custom_call_target="tpu_custom_call" | custom-call | flops 17179869184 | bytes 29360128 | tf_op jit(solution)/shard_map/feed_forward/pallas_call | solution.py:345
  241.7 4.4 collective-permute-done.15.far
  247.3 4.1 second_norm.3
  254.0 4.4 second_norm.2
  264.4 47.6 %feed_backward.1 = (bf16[16,16,64,256]{3,2,1,0:T(8,128)(2,1)}, f32[1,2048]{1,0:T(1,128)}, f32[1024,1024]{1,0:T(8,128)}, bf16[1024,1024]{1,0:T(8,128)(2,1)}) custom-call(bf16[512,1024]{1,0:T(8,128)(2,1)} %copy-done.39, bf16[512,1024]{1,0:T(8,128)(2,1)} %copy-done.38, bf16[512,1024]{1,0:T(8,128)(2,1)} %copy-done.64, bf16[512,1024]{1,0:T(8,128)(2,1)} %copy-done.63, ...), custom_call_target="tpu_custom_call" | custom-call | flops 34359738368 | bytes 54525952 | tf_op jit(solution)/shard_map/feed_backward/pallas_call | solution.py:430
  313.8 4.0 collective-permute-done.18.far
  319.1 6.0 %first_back.2 = (f32[512,1024]{1,0:T(8,128)S(1)}, bf16[512,1024]{1,0:T(8,128)(2,1)S(1)}, bf16[4,128,256]{2,1,0:T(8,128)(2,1)S(1)}, bf16[4,128,256]{2,1,0:T(8,128...) custom-call(s32[1]{0:T(128)} %bitcast.place, ...), custom_call_target="tpu_custom_call" | custom-call | flops 1073741824 | bytes 8388608 | tf_op jit(solution)/shard_map/first_back/pallas_call | solution.py:494
  329.3 5.8 %first_back.3 = (f32[512,1024]{1,0:T(8,128)S(1)}, bf16[512,1024]{1,0:T(8,128)(2,1)S(1)}, bf16[4,128,256]{2,1,0:T(8,128)(2,1)S(1)}, bf16[4,128,256]{2,1,0:T(8,128...) custom-call(s32[1]{0:T(128)} %bitcast.place, ...), custom_call_target="tpu_custom_call" | custom-call | flops 1073741824 | bytes 8388608 | tf_op jit(solution)/shard_map/first_back/pallas_call | solution.py:494
  341.3 29.6 %attend_backward.2 = (f32[768,1024]{1,0:T(8,128)}, f32[4,128,1024]{2,1,0:T(8,128)}, bf16[4,128,1024]{2,1,0:T(8,128)(2,1)}, bf16[4,128,1024]{2,1,0:T(8,128)(2,1)}...) custom-call(bf16[4,512,768]{2,1,0:T(8,128)(2,1)} %get-tuple-element.106.saved, ...), custom_call_target="tpu_custom_call" | custom-call | flops 17178820608 | bytes 22020096 | tf_op jit(solution)/shard_map/attend_backward/pallas_call | solution.py:238
  380.8 4.7 collective-permute-done.27.g3
  385.5 30.5 %attend_backward.3 = (bf16[1024,768]{1,0:T(8,128)(2,1)}, f32[4,128,1024]{2,1,0:T(8,128)}, bf16[4,128,1024]{2,1,0:T(8,128)(2,1)}, bf16[4,128,1024]{2,1,0:T(8,128)...) custom-call(bf16[4,512,768]{2,1,0:T(8,128)(2,1)} %get-tuple-element.120.saved, ...), custom_call_target="tpu_custom_call" | custom-call | flops 17178820608 | bytes 22020096 | tf_op jit(solution)/shard_map/attend_backward/pallas_call | solution.py:238
  429.4 13.4 %collective-permute-done.24.refs_0_ = bf16[4,128,1024]{2,1,0:T(8,128)(2,1)S(1)} collective-permute-done((bf16[4,128,1024]{2,1,0:T(8,128)(2,1)}, bf16[4,128,1024]{2,1,0:T(8,128)(2,1)S(1)}, u32[]{:S(2)}, u32[]{:S(2)}) %collective-permute-start.24) | collective-permute-done | bytes 1048608 | tf_op jit(solution)/shard_map/ppermute | solution.py:681
  450.5 13.0 %collective-permute-done.31 = bf16[4,128,768]{2,1,0:T(8,128)(2,1)} collective-permute-done((bf16[4,128,768]{2,1,0:T(8,128)(2,1)S(1)}, bf16[4,128,768]{2,1,0:T(8,128)(2,1)}, u32[]{:S(2)}, u32[]{:S(2)}) %collective-permute-start.31) | collective-permute-done | bytes 786464 | tf_op jit(solution)/shard_map/ppermute | solution.py:701
  478.9 9.7 %collective-permute-done.36 = bf16[4,2,33,1024]{3,0,2,1:T(4,128)(2,1)S(1)} collective-permute-done((bf16[4,2,33,1024]{3,0,2,1:T(4,128)(2,1)S(1)}, bf16[4,2,33,1024]{3,0,2,1:T(4,128)(2,1)S(1)}, u32[]{:S(2)}, u32[]{:S(2)}) %collective-permute-start.36) | collective-permute-done | bytes 540704 | tf_op jit(solution)/shard_map/ppermute | solution.py:701
  491.8 5.5 collective-permute-done.37
  498.3 4.8 pad_maximum_fusion
  513.3 6.2 %collective-permute-done.33 = bf16[16,64,256]{2,1,0:T(8,128)(2,1)S(1)} collective-permute-done((bf16[16,64,256]{2,1,0:T(8,128)(2,1)S(1)}, bf16[16,64,256]{2,1,0:T(8,128)(2,1)S(1)}, u32[]{:S(2)}, u32[]{:S(2)}) %collective-permute-start.33) | collective-permute-done | bytes 524320 | tf_op jit(solution)/shard_map/ppermute | solution.py:701
  520.7 8.5 %collective-permute-done.34 = bf16[1,128,768]{2,1,0:T(8,128)(2,1)S(1)} collective-permute-done((bf16[1,128,768]{2,1,0:T(8,128)(2,1)S(1)}, bf16[1,128,768]{2,1,0:T(8,128)(2,1)S(1)}, u32[]{:S(2)}, u32[]{:S(2)}) %collective-permute-start.34) | collective-permute-done | bytes 196640 | tf_op jit(solution)/shard_map/ppermute | solution.py:701
  (349 shorter events, 164.8 us)
Async XLA Ops:
  17.7 69.7 %all-gather.6.cloned.1.call-start = ((), (), s32[]{:S(2)}) async-start(), calls=%async_computation.5 | async-start | bytes 3244032 | tf_op jit(solution)/shard_map/all_gather | solution.py:773
  24.9 187.0 %all-gather.4.cloned.1.call-start = ((), (), s32[]{:S(2)}) async-start(), calls=%async_computation.3 | async-start | bytes 9437184 | tf_op jit(solution)/shard_map/all_gather | solution.py:812
  25.0 47.3 %collective-permute-start.1 = (bf16[8,128,1024]{2,1,0:T(8,128)(2,1)S(1)}, bf16[8,128,1024]{2,1,0:T(8,128)(2,1)}, u32[]{:S(2)}, u32[]{:S(2)}) collective-permute-start(bf16[8,128,1024]{2,1,0:T(8,128)(2,1)S(1)} %copy-done.2), channel_id=1, source_target_pairs={{0,2},{1,3},{2,0},{3,1},{4,6},{5,7},{6,4},{7,5},{8,10},{9,11},{10,... | collective-permute-start | bytes 6291464 | tf_op jit(solution)/shard_map/ppermute | solution.py:681
  72.4 12.6 %collective-permute-start.14 = (bf16[16,64,256]{2,1,0:T(8,128)(2,1)S(1)}, bf16[16,64,256]{2,1,0:T(8,128)(2,1)S(1)}, u32[]{:S(2)}, u32[]{:S(2)}) collective-permute-start(bf16[16,64,256]{2,1,0:T(8,128)(2,1)S(1)} %hold.4), channel_id=1, source_target_pairs={{0,2},{2,0},{1,3},{3,1},{4,6},{6,4},{5,7},{7,5},{8,10},{10,8},{9,1... | collective-permute-start | bytes 1572872 | tf_op jit(solution)/shard_map/ppermute | solution.py:701
  86.1 419.9 %reduce-scatter.2.cloned.1.call-start = ((), (), s32[]{:S(2)}) async-start(), calls=%async_computation.4 | async-start | bytes 9437184 | tf_op jit(solution)/shard_map/reduce_scatter | solution.py:857
  111.9 24.7 %collective-permute-start.7 = (bf16[16,32,1024]{2,1,0:T(8,128)(2,1)S(1)}, bf16[16,32,1024]{2,1,0:T(8,128)(2,1)}, u32[]{:S(2)}, u32[]{:S(2)}) collective-permute-start(bf16[16,32,1024]{2,1,0:T(8,128)(2,1)S(1)} %bitcast.227), channel_id=1, source_target_pairs={{0,1},{1,0},{2,3},{3,2},{4,5},{5,4},{6,7},{7,6},{8,9},{9,8},{10,11... | collective-permute-start | bytes 3145736 | tf_op jit(solution)/shard_map/ppermute | solution.py:684
  134.2 12.6 %collective-permute-start.10 = (bf16[4,128,256]{2,1,0:T(8,128)(2,1)}, bf16[4,128,256]{2,1,0:T(8,128)(2,1)S(1)}, u32[]{:S(2)}, u32[]{:S(2)}) collective-permute-start(bf16[4,128,256]{2,1,0:T(8,128)(2,1)} %get-tuple-element.90), channel_id=1, source_target_pairs={{0,3},{1,2},{2,1},{3,0},{4,7},{5,6},{6,5},{7,4},{8,11},{9,10},{10,... | collective-permute-start | bytes 786440 | tf_op jit(solution)/shard_map/ppermute | solution.py:681
  135.0 23.4 %collective-permute-start.4 = (bf16[4,128,256]{2,1,0:T(8,128)(2,1)}, bf16[4,128,256]{2,1,0:T(8,128)(2,1)S(1)}, u32[]{:S(2)}, u32[]{:S(2)}) collective-permute-start(bf16[4,128,256]{2,1,0:T(8,128)(2,1)} %copy-done.42), channel_id=1, source_target_pairs={{0,1},{1,0},{2,3},{3,2},{4,5},{5,4},{6,7},{7,6},{8,9},{9,8},{10,11... | collective-permute-start | bytes 786440 | tf_op jit(solution)/shard_map/ppermute | solution.py:681
  135.7 22.7 %collective-permute-start.5 = (bf16[4,128,256]{2,1,0:T(8,128)(2,1)}, bf16[4,128,256]{2,1,0:T(8,128)(2,1)S(1)}, u32[]{:S(2)}, u32[]{:S(2)}) collective-permute-start(bf16[4,128,256]{2,1,0:T(8,128)(2,1)} %copy-done.41), channel_id=1, source_target_pairs={{0,2},{1,3},{2,0},{3,1},{4,6},{5,7},{6,4},{7,5},{8,10},{9,11},{10,... | collective-permute-start | bytes 786440 | tf_op jit(solution)/shard_map/ppermute | solution.py:681
  136.5 21.9 %collective-permute-start.6 = (bf16[4,128,256]{2,1,0:T(8,128)(2,1)}, bf16[4,128,256]{2,1,0:T(8,128)(2,1)S(1)}, u32[]{:S(2)}, u32[]{:S(2)}) collective-permute-start(bf16[4,128,256]{2,1,0:T(8,128)(2,1)} %copy-done.40), channel_id=1, source_target_pairs={{0,3},{1,2},{2,1},{3,0},{4,7},{5,6},{6,5},{7,4},{8,11},{9,10},{10,... | collective-permute-start | bytes 786440 | tf_op jit(solution)/shard_map/ppermute | solution.py:681
  156.6 10.1 %collective-permute-start.12 = (bf16[512,1024]{1,0:T(8,128)(2,1)S(1)}, bf16[512,1024]{1,0:T(8,128)(2,1)S(1)}, u32[]{:S(2)}, u32[]{:S(2)}) collective-permute-start(bf16[512,1024]{1,0:T(8,128)(2,1)S(1)} %get-tuple-element.91.refs_1_.refs_5_), channel_id=1, source_target_pairs={{0,1},{1,0},{2,3},{3,2},{4,5},{5,4},{6,7},{7,6},{8,9},{9,8},{10,11... | collective-permute-start | bytes 3145736 | tf_op jit(solution)/shard_map/ppermute | solution.py:684
  327.5 10.0 %collective-permute-start.19 = (bf16[4,128,256]{2,1,0:T(8,128)(2,1)S(1)}, bf16[4,128,256]{2,1,0:T(8,128)(2,1)S(1)}, u32[]{:S(2)}, u32[]{:S(2)}) collective-permute-start(bf16[4,128,256]{2,1,0:T(8,128)(2,1)S(1)} %get-tuple-element.109), channel_id=1, source_target_pairs={{0,1},{1,0},{2,3},{3,2},{4,5},{5,4},{6,7},{7,6},{8,9},{9,8},{10,11... | collective-permute-start | bytes 786440 | tf_op jit(solution)/shard_map/ppermute | solution.py:681
  329.1 12.2 %collective-permute-start.21 = (bf16[4,128,256]{2,1,0:T(8,128)(2,1)S(1)}, bf16[4,128,256]{2,1,0:T(8,128)(2,1)S(1)}, u32[]{:S(2)}, u32[]{:S(2)}) collective-permute-start(bf16[4,128,256]{2,1,0:T(8,128)(2,1)S(1)} %get-tuple-element.111), channel_id=1, source_target_pairs={{0,3},{1,2},{2,1},{3,0},{4,7},{5,6},{6,5},{7,4},{8,11},{9,10},{10,... | collective-permute-start | bytes 786440 | tf_op jit(solution)/shard_map/ppermute | solution.py:681
  373.2 12.3 %collective-permute-start.27 = (bf16[4,128,256]{2,1,0:T(8,128)(2,1)S(1)}, bf16[4,128,256]{2,1,0:T(8,128)(2,1)S(1)}, u32[]{:S(2)}, u32[]{:S(2)}) collective-permute-start(bf16[4,128,256]{2,1,0:T(8,128)(2,1)S(1)} %get-tuple-element.125), channel_id=1, source_target_pairs={{0,3},{1,2},{2,1},{3,0},{4,7},{5,6},{6,5},{7,4},{8,11},{9,10},{10,... | collective-permute-start | bytes 786440 | tf_op jit(solution)/shard_map/ppermute | solution.py:681
  416.0 10.3 %collective-permute-start.29 = (bf16[4,128,1024]{2,1,0:T(8,128)(2,1)}, bf16[4,128,1024]{2,1,0:T(8,128)(2,1)}, u32[]{:S(2)}, u32[]{:S(2)}) collective-permute-start(bf16[4,128,1024]{2,1,0:T(8,128)(2,1)} %get-tuple-element.130), channel_id=1, source_target_pairs={{0,1},{1,0},{2,3},{3,2},{4,5},{5,4},{6,7},{7,6},{8,9},{9,8},{10,11... | collective-permute-start | bytes 3145736 | tf_op jit(solution)/shard_map/ppermute | solution.py:684
  416.7 26.2 %collective-permute-start.24 = (bf16[4,128,1024]{2,1,0:T(8,128)(2,1)}, bf16[4,128,1024]{2,1,0:T(8,128)(2,1)S(1)}, u32[]{:S(2)}, u32[]{:S(2)}) collective-permute-start(bf16[4,128,1024]{2,1,0:T(8,128)(2,1)} %add_convert_fusion.1.refs_1_), channel_id=1, source_target_pairs={{0,2},{1,3},{2,0},{3,1},{4,6},{5,7},{6,4},{7,5},{8,10},{9,11},{10,... | collective-permute-start | bytes 3145736 | tf_op jit(solution)/shard_map/ppermute | solution.py:681
  429.0 35.8 %collective-permute-start.30 = (bf16[4,128,1024]{2,1,0:T(8,128)(2,1)}, bf16[4,128,1024]{2,1,0:T(8,128)(2,1)S(1)}, u32[]{:S(2)}, u32[]{:S(2)}) collective-permute-start(bf16[4,128,1024]{2,1,0:T(8,128)(2,1)} %add_convert_fusion), channel_id=1, source_target_pairs={{0,2},{1,3},{2,0},{3,1},{4,6},{5,7},{6,4},{7,5},{8,10},{9,11},{10,... | collective-permute-start | bytes 3145736 | tf_op jit(solution)/shard_map/ppermute | solution.py:681
  445.3 18.2 %collective-permute-start.31 = (bf16[4,128,768]{2,1,0:T(8,128)(2,1)S(1)}, bf16[4,128,768]{2,1,0:T(8,128)(2,1)}, u32[]{:S(2)}, u32[]{:S(2)}) collective-permute-start(bf16[4,128,768]{2,1,0:T(8,128)(2,1)S(1)} %dynamic-slice_bitcast_fusion.1), channel_id=1, source_target_pairs={{0,4},{4,0},{1,5},{5,1},{2,6},{6,2},{3,7},{7,3},{8,12},{12,8},{9,1... | collective-permute-start | bytes 2359304 | tf_op jit(solution)/shard_map/ppermute | solution.py:701
  471.6 18.2 %collective-permute-start.28 = (bf16[4,128,1024]{2,1,0:T(8,128)(2,1)}, bf16[4,128,1024]{2,1,0:T(8,128)(2,1)S(1)}, u32[]{:S(2)}, u32[]{:S(2)}) collective-permute-start(bf16[4,128,1024]{2,1,0:T(8,128)(2,1)} %get-tuple-element.128), channel_id=1, source_target_pairs={{0,1},{1,0},{2,3},{3,2},{4,5},{5,4},{6,7},{7,6},{8,9},{9,8},{10,11... | collective-permute-start | bytes 3145736 | tf_op jit(solution)/shard_map/ppermute | solution.py:684
  473.8 14.8 %collective-permute-start.36 = (bf16[4,2,33,1024]{3,0,2,1:T(4,128)(2,1)S(1)}, bf16[4,2,33,1024]{3,0,2,1:T(4,128)(2,1)S(1)}, u32[]{:S(2)}, u32[]{:S(2)}) collective-permute-start(bf16[4,2,33,1024]{3,0,2,1:T(4,128)(2,1)S(1)} %dynamic-slice_bitcast_fusion.2), channel_id=1, source_target_pairs={{0,2},{2,0},{1,3},{3,1},{4,6},{6,4},{5,7},{7,5},{8,10},{10,8},{9,1... | collective-permute-start | bytes 1622024 | tf_op jit(solution)/shard_map/ppermute | solution.py:701
  478.7 30.2 %collective-permute-start.32 = (bf16[2,128,768]{2,1,0:T(8,128)(2,1)S(1)}, bf16[2,128,768]{2,1,0:T(8,128)(2,1)S(1)}, u32[]{:S(2)}, u32[]{:S(2)}) collective-permute-start(bf16[2,128,768]{2,1,0:T(8,128)(2,1)S(1)} %dynamic-slice_bitcast_fusion.4), channel_id=1, source_target_pairs={{0,8},{8,0},{16,24},{24,16},{1,9},{9,1},{17,25},{25,17},{2,10},{10... | collective-permute-start | bytes 1179656 | tf_op jit(solution)/shard_map/ppermute | solution.py:701
  507.3 12.3 %collective-permute-start.33 = (bf16[16,64,256]{2,1,0:T(8,128)(2,1)S(1)}, bf16[16,64,256]{2,1,0:T(8,128)(2,1)S(1)}, u32[]{:S(2)}, u32[]{:S(2)}) collective-permute-start(bf16[16,64,256]{2,1,0:T(8,128)(2,1)S(1)} %dynamic-slice_bitcast_fusion.3), channel_id=1, source_target_pairs={{0,2},{2,0},{1,3},{3,1},{4,6},{6,4},{5,7},{7,5},{8,10},{10,8},{9,1... | collective-permute-start | bytes 1572872 | tf_op jit(solution)/shard_map/ppermute | solution.py:701
  520.6 14.8 %collective-permute-start.40 = (f32[8,32,256]{2,1,0:T(8,128)S(1)}, f32[8,32,256]{2,1,0:T(8,128)S(1)}, u32[]{:S(2)}, u32[]{:S(2)}) collective-permute-start(f32[8,32,256]{2,1,0:T(8,128)S(1)} %get-tuple-element.156), channel_id=1, source_target_pairs={{0,1},{1,0},{2,3},{3,2},{4,5},{5,4},{6,7},{7,6},{8,9},{9,8},{10,11... | collective-permute-start | bytes 786440 | tf_op jit(solution)/shard_map/ppermute | solution.py:684
  530.0 10.9 %all-to-all-start.1 = ((f32[4,32,768]{2,1,0:T(8,128)}), f32[4,32,768]{2,1,0:T(8,128)S(1)}, u32[]{:S(2)}, u32[]{:S(2)}) async-start(f32[4,32,768]{2,1,0:T(8,128)} %bitcast.62), calls=%async_computation.2 | async-start | bytes 786432 | tf_op jit(solution)/shard_map/all_to_all | solution.py:922
  (87 other events, 559.1 us)
Sparse Core Ops, SparseCore 0:
  25.0 57.9 all-gather.5
  86.3 125.6 all-gather.3
  312.2 147.1 reduce-scatter.1

commit v9 on v7

--- a/solution.py
+++ b/solution.py
@@ -57,6 +57,42 @@
         compiler_params=pltpu.CompilerParams(vmem_limit_bytes=16 * MIB),
         name="hold",
     )(array, *after)
+
+
+def add_kernel(left, right, *refs):
+    refs[-1][...] = (left[...].astype(F32) + right[...].astype(F32)).astype(BF16)
+
+
+def add_low(left, right, after):
+    block = (1,) + left.shape[1:]
+    return pl.pallas_call(
+        add_kernel,
+        grid=(left.shape[0],),
+        in_specs=[by_row(block)] * 2 + [ELSEWHERE] * len(after),
+        out_specs=by_row(block),
+        out_shape=jax.ShapeDtypeStruct(left.shape, BF16),
+        compiler_params=pltpu.CompilerParams(vmem_limit_bytes=16 * MIB),
+        name="add_low",
+    )(left, right, *after)
+
+
+def join_kernel(top, below, *refs):
+    out = refs[-1]
+    out[:, : top.shape[1]] = top[...]
+    out[:, top.shape[1] :] = below[...]
+
+
+def join(top, below, after):
+    shape = (top.shape[0], top.shape[1] + below.shape[1], top.shape[2])
+    return pl.pallas_call(
+        join_kernel,
+        grid=(1,),
+        in_specs=[resident(top.shape), resident(below.shape)] + [ELSEWHERE] * len(after),
+        out_specs=resident(shape),
+        out_shape=jax.ShapeDtypeStruct(shape, BF16),
+        compiler_params=pltpu.CompilerParams(vmem_limit_bytes=32 * MIB),
+        name="join",
+    )(top, below, *after)
 
 
 def unpack_kernel(pieces, *refs):
@@ -251,7 +287,7 @@
         + [by_row((1, part, depth))] * 4
         + [by_row((1, 1, wide))],
         out_shape=[jax.ShapeDtypeStruct(shape, kind)]
-        + [jax.ShapeDtypeStruct((count, part, depth), t) for t in (F32, BF16, F32, BF16)]
+        + [jax.ShapeDtypeStruct((count, part, depth), t) for t in (F32, BF16, BF16, BF16)]
         + [jax.ShapeDtypeStruct((count, 1, wide), F32)],
         scratch_shapes=[pltpu.VMEM((wide, depth), F32)],
         compiler_params=pltpu.CompilerParams(vmem_limit_bytes=52 * MIB),
@@ -576,8 +612,9 @@
 
 
 def first_back_kernel(
-    place, grad, own, far, scaled, inverse, weight, vectors, hidden, low, m0, m1, m2, m3, sums
+    late, place, grad, own, far, scaled, inverse, weight, vectors, *refs
 ):
+    hidden, low, m0, m1, m2, m3, sums = refs[late:]
     incoming = grad[...] + own[...] + far[...].astype(F32)
     grad_hidden = normalize_back(incoming, scaled[...], inverse[...], vectors[GAIN_ONE])
     hidden[...] = grad_hidden
@@ -588,16 +625,17 @@
     add_sums(sums, incoming * scaled[...], incoming, attended.astype(F32))
 
 
-def first_back(place, grad, own, far, scaled, inverse, weight, vectors, chunk, part):
+def first_back(place, grad, own, far, scaled, inverse, weight, vectors, chunk, part, after):
     size, width = grad.shape
     steps = size // ROW_BLOCK
     lanes = weight.shape[1]
     return row_call(
-        first_back_kernel,
+        functools.partial(first_back_kernel, len(after)),
         "first_back",
         [SCALAR, row_block(width)]
         + [row_block(width, chunk * steps)] * 2
-        + [row_block(width), row_block(1), resident(weight.shape), resident(vectors.shape)],
+        + [row_block(width), row_block(1), resident(weight.shape), resident(vectors.shape)]
+        + [ELSEWHERE] * len(after),
         [
             (row_block(width), jax.ShapeDtypeStruct((size, width), F32)),
             (row_block(width), jax.ShapeDtypeStruct((size, width), BF16)),
@@ -610,14 +648,14 @@
         ]
         * 4
         + [(resident((8, width)), jax.ShapeDtypeStruct((8, width), F32))],
-        (place, grad, own, far, scaled, inverse, weight, vectors),
+        (place, grad, own, far, scaled, inverse, weight, vectors, *after),
         size,
         2 * size * width * width,
     )
 
 
 def output_grad_kernel(place, *refs):
-    mixed, grads, out = refs[:CHUNKS], refs[CHUNKS:-1], refs[-1]
+    mixed, grads, out = refs[:CHUNKS], refs[CHUNKS : 2 * CHUNKS], refs[-1]
     lanes = out.shape[1]
     for step in range(out.shape[0]):
         at = slice(step * lanes, (step + 1) * lanes)
@@ -626,13 +664,15 @@
         ).astype(BF16)
 
 
-def output_back(place, mixed, grads, ctx_size):
+def output_back(place, mixed, grads, ctx_size, after):
     size, width = mixed[0].shape
     shape = (ctx_size, width // ctx_size, width)
     return pl.pallas_call(
         output_grad_kernel,
         grid=(1,),
-        in_specs=[SCALAR] + [resident((size, width))] * (2 * CHUNKS),
+        in_specs=[SCALAR]
+        + [resident((size, width))] * (2 * CHUNKS)
+        + [ELSEWHERE] * len(after),
         out_specs=resident(shape),
         out_shape=jax.ShapeDtypeStruct(shape, BF16),
         compiler_params=pltpu.CompilerParams(vmem_limit_bytes=48 * MIB),
@@ -642,7 +682,7 @@
             transcendentals=0,
         ),
         name="output_backward",
-    )(place, *mixed, *grads)
+    )(place, *mixed, *grads, *after)
 
 
 def on_device(
@@ -739,9 +779,8 @@
         expand_bias,
     )
     vector_count = 8 * share + expand_bias.shape[0]
-    filler = jnp.concatenate(
-        [jnp.pad(v[None], ((0, 0), (0, 3 * lanes - v.shape[0]))) for v in vectors]
-        + [jnp.zeros((16 - len(vectors), 3 * lanes), BF16)]
+    filler = jnp.pad(jnp.stack(vectors[:8]), ((0, 8), (0, 3 * lanes - share))) + jnp.pad(
+        expand_bias[None], ((8, 7), (0, 3 * lanes - expand_bias.shape[0]))
     )
     held = jnp.stack(
         [
@@ -875,15 +914,44 @@
             vectors,
             index,
             part,
+            grad_mixed[0][1:2] if index else [],
         )
         grad_hidden.append(grad.reshape(seqs, part, width))
         grad_attended.append(low)
         grad_mixed.append([mixed[0]] + [hop(mixed[r], r) for r in (1, 2, 3)])
         first_sums.append(sums)
-    output_grad = output_back(where, mixed_low, grad_attended, ctx_size).reshape(
-        sizes["z"], 2, sizes["x"], 2, share, width
-    )
-    output_grad = halve(output_grad, 3, "c").astype(BF16)
+    def shared_sums(after):
+        output_grad = output_back(where, mixed_low, grad_attended, ctx_size, after)
+        zeros = jnp.zeros((width,), F32)
+        first_total, second_total = sum(first_sums), sum(second_sums)
+        grad_vectors = (
+            zeros,
+            zeros,
+            first_total[2],
+            first_total[0],
+            first_total[1],
+            second_total[2],
+            second_total[0],
+            second_total[1],
+        )
+        hidden_sums = expand_bias_grad.reshape(chips, 1, own_hidden // chips)
+        hidden_sums = jnp.where(
+            low_core,
+            jnp.concatenate([hidden_sums, jnp.zeros_like(hidden_sums)], axis=1),
+            jnp.concatenate([jnp.zeros_like(hidden_sums), hidden_sums], axis=1),
+        )
+        packed_grads = jnp.concatenate(
+            [vector.reshape(everyone, share) for vector in grad_vectors]
+            + [hidden_sums.reshape(everyone, -1)],
+            axis=1,
+        )
+        packed_grads = jnp.pad(packed_grads, ((0, 0), (0, width - vector_count))).astype(BF16)
+        shared = jnp.concatenate(
+            [output_grad.reshape(everyone, share, width), packed_grads[:, None]], axis=1
+        ).reshape(sizes["z"], 2, sizes["x"], 2, share + 1, width)
+        shared_chip = halve(shared, 3, "c").astype(BF16)
+        shared = halve(shared_chip, 2, "x").astype(BF16)
+        return shared_chip, shared
 
     project_grad = []
     work_parts = []
@@ -892,6 +960,8 @@
     sum_parts = []
     for index in range(CHUNKS):
         at = slice(index * seqs, (index + 1) * seqs)
+        if index == 1:
+            shared_chip, shared = shared_sums(grad_mixed[1][1:] + sum_parts)
         project_part, r0, r1, r2, r3, sums = attend_back(
             saved[index],
             kept_rows[index],
@@ -901,37 +971,59 @@
             seg_query[at],
             project_grad,
             index == CHUNKS - 1,
-            work_hops[:index],
+            across_sums[:1] + [shared_chip] if index else grad_attended[1:],
         )
         project_grad = [project_part]
-        across_sums.append((r2 + swap(r3).astype(F32)).astype(BF16))
+        across_sums.append(add_low(r2, swap(r3), work_hops[:1] if index else grad_mixed[1][1:]))
         work_hops.append(hop(across_sums[index], 2))
         work_parts.append(
             grad_hidden[index] + r0 + swap(r1).astype(F32) + work_hops[index].astype(F32)
         )
         sum_parts.append(sums)
     grad_work = jnp.concatenate(work_parts, axis=0)
-    blocks = halve(
-        project_grad[0].reshape(sizes["z"], 2, ctx_size * share, 3 * lanes), 1, "y"
+    column_sums = jnp.sum(jnp.concatenate(sum_parts, axis=0), axis=(0, 1))
+    holders = sizes["z"] * 2
+    owners = holders // ctx_size
+    bias_grads = jnp.concatenate(
+        [
+            column_sums[at : at + lanes].reshape(owners, ctx_size, share)
+            for at in (0, 2 * lanes)
+        ],
+        axis=2,
+    )
+    bias_grads = jnp.pad(
+        bias_grads, ((0, 0), (0, 16 - ctx_size), (0, 3 * lanes - 2 * share))
     ).astype(BF16)
-    later = [blocks, work_hops[1]]
-    output_grad = halve(hold(output_grad, later), 2, "x").astype(BF16)
-    output_grad = halve(output_grad, 1, "y")
-    output_owned = z_scatter(output_grad)
-    for step in z_steps:
-        blocks = blocks.astype(BF16).reshape((blocks.shape[0] // 2, 2) + blocks.shape[1:])
-        blocks = halve(blocks, 1, "z", step)
+    bias_grads = lax.dynamic_update_slice_in_dim(
+        jnp.zeros((holders, 16, 3 * lanes), BF16), bias_grads, place * owners, 0
+    )
+    blocks = join(
+        project_grad[0].reshape(holders, ctx_size * share, 3 * lanes),
+        bias_grads,
+        work_hops[:1],
+    )
+    blocks = halve(blocks.reshape((sizes["z"], 2) + blocks.shape[1:]), 1, "y").astype(BF16)
+    blocks = hold(blocks, work_hops[1:])
+    shared = halve(hold(shared, [blocks]), 1, "y")
+    shared = z_scatter(shared)
+    output_owned = shared[:share]
+    owned = shared[share, :vector_count]
+    blocks = z_scatter(blocks)
     weight_owned = halve(weight_owned, 0, "x")
-    held = lax.all_to_all(
-        hold(blocks.astype(F32).reshape(ctx_size, share, 3 * lanes), [weight_owned]),
-        CTX,
-        0,
-        0,
-        tiled=True,
-    )
+    blocks = jnp.concatenate(
+        [
+            blocks[: ctx_size * share].reshape(ctx_size, share, 3 * lanes),
+            jnp.pad(
+                blocks[ctx_size * share :][:ctx_size, None], ((0, 0), (0, 7), (0, 0))
+            ),
+        ],
+        axis=1,
+    )
+    held = lax.all_to_all(hold(blocks, [weight_owned]), CTX, 0, 0, tiled=True)
+    bias_owned = jnp.sum(held[:, share, : 2 * share], axis=0)
     project_owned = jnp.concatenate(
         [
-            held[p, :, j * lanes : (j + 1) * lanes]
+            held[p, :share, j * lanes : (j + 1) * lanes]
             for j in range(3)
             for p in range(ctx_size)
         ],
@@ -950,43 +1042,13 @@
         weight_owned[expand_pieces:].reshape(2, width // PIECE, 2 * share, PIECE), 1, 2
     ).reshape(4 * share, width)
 
-    column_sums = jnp.sum(jnp.concatenate(sum_parts, axis=0), axis=(0, 1))
-    zeros = jnp.zeros((width,), F32)
-    first_sums, second_sums = sum(first_sums), sum(second_sums)
-    grad_vectors = (
-        lax.dynamic_update_slice_in_dim(zeros, column_sums[:lanes], place * lanes, 0),
-        lax.dynamic_update_slice_in_dim(zeros, column_sums[2 * lanes :], place * lanes, 0),
-        first_sums[2],
-        first_sums[0],
-        first_sums[1],
-        second_sums[2],
-        second_sums[0],
-        second_sums[1],
-    )
-    hidden_sums = expand_bias_grad.reshape(chips, 1, own_hidden // chips)
-    hidden_sums = jnp.where(
-        low_core,
-        jnp.concatenate([hidden_sums, jnp.zeros_like(hidden_sums)], axis=1),
-        jnp.concatenate([jnp.zeros_like(hidden_sums), hidden_sums], axis=1),
-    )
-    packed_grads = jnp.concatenate(
-        [vector.reshape(everyone, share) for vector in grad_vectors]
-        + [hidden_sums.reshape(everyone, -1)],
-        axis=1,
-    )
-    packed_grads = hold(packed_grads, later).reshape(
-        sizes["z"], 2, sizes["x"], 2, vector_count
-    )
-    for axis, name in ((3, "c"), (2, "x"), (1, "y")):
-        packed_grads = halve(packed_grads, axis, name)
-    owned = z_scatter(packed_grads, F32)
     small = [owned[i * share : (i + 1) * share] for i in range(8)]
     return (
         layer_work,
         grad_work,
         project_owned.astype(F32),
-        small[0],
-        small[1],
+        bias_owned[:share],
+        bias_owned[share:],
         output_owned.astype(F32),
         small[2],
         small[3],

time: 555 us -> 532 us (0.959)
  waiting for transfers between devices: 214 us -> 189 us
  local copies, waits for them, and re-layouts: 50 us -> 63.1 us
  other arithmetic: 28.6 us -> 19 us
  starting transfers between devices: 42.3 us -> 35.7 us
    ppermute x15, waiting for transfers between devices: 83 us -> 54.8 us  [hop(): return lax.ppermute(array, CTX, [(i, i ^ step) for i in range(ctx_size)])]
    unnamed x116 -> x158, local copies, waits for them, and re-layouts: 25.6 us -> 40 us
    all_gather x1, waiting for transfers between devices: 44.2 us -> 52.1 us  [on_device(): lax.all_gather(widen(own_pieces, 'x'), SEQ, axis=0)]
    ppermute x16 -> x11, waiting for transfers between devices: 57.9 us -> 51.6 us  [trade(): lax.ppermute(array, name, [(i, i ^ step) for i in range(sizes[name])])]
    pad x9 -> x1, local copies, waits for them, and re-layouts: 5.95 us -> 0.01 us  [shared_sums(): jnp.pad(packed_grads, ((0, 0), (0, width - vector_count))).astype(BF16)]
    ppermute x16 -> x11, starting transfers between devices: 18.2 us -> 13.7 us  [trade(): lax.ppermute(array, name, [(i, i ^ step) for i in range(sizes[name])])]
  transfers between devices with their start and end apart: 51 -> 46, of which waited for: 28 -> 22; matrix products, arithmetic and copies ran while one was open for 10% -> 8% of each run, Pallas kernels for 22% -> 23%
where the time goes in v9:
time: 532 us; the launch traced here: 528 us
  Pallas kernels  206 us (39%)
  waiting for transfers between devices  189 us (36%)
  local copies, waits for them, and re-layouts  63.1 us (12%)
  starting transfers between devices  35.7 us (7%)
  other arithmetic  19 us (4%)
  between operations  15.2 us (3%)
    pallas_call x2, Pallas kernels, attend_back(): pl.pallas_call(functools.partial(attend_back_kernel, len(after), len(earl...  60 us
    ppermute x15, waiting for transfers between devices, hop(): return lax.ppermute(array, CTX, [(i, i ^ step) for i in range(ctx_size)])  54.8 us
    all_gather x1, waiting for transfers between devices, on_device(): lax.all_gather(widen(own_pieces, 'x'), SEQ, axis=0)  52.1 us
    ppermute x11, waiting for transfers between devices, trade(): lax.ppermute(array, name, [(i, i ^ step) for i in range(sizes[name])])  51.6 us
    pallas_call x1, Pallas kernels, feed_back(): pl.pallas_call(feed_back_kernel, grid=(hidden // wide,), in_specs=[reside...  47.7 us
    unnamed x158, local copies, waits for them, and re-layouts  40 us
    pallas_call x6, Pallas kernels, row_call(): pl.pallas_call(kernel, grid=(rows // ROW_BLOCK,), in_specs=ins, out_specs...  30.6 us
    pallas_call x2, Pallas kernels, attend(): pl.pallas_call(functools.partial(attend_kernel, len(after)), grid=(count,...  30.5 us
  transfers between devices with their start and end apart: 46, of which 22 were waited for; matrix products, arithmetic and copies ran while one was open for 8% of the time, Pallas kernels for 23%

profile of v9, /device:TPU:0, one launch (start us, length us, event | category | flops | bytes accessed | tf_op | source)
XLA Modules:
  0.0 528.0 jit_solution(15497683297205432022)
XLA Ops:
  17.8 6.2 %all-to-all-done = bf16[4,48,768]{2,1,0:T(8,128)(2,1)S(1)} async-done(((bf16[4,48,768]{2,1,0:T(8,128)(2,1)}), bf16[4,48,768]{2,1,0:T(8,128)(2,1)S(1)}, u32[]{:S(2)}, u32[]{:S(2)}) %all-to-all-start) | async-done | bytes 294944 | tf_op jit(solution)/shard_map/all_to_all | solution.py:802
  28.8 43.5 %collective-permute-done.1.t2.refs_0_ = bf16[8,128,1024]{2,1,0:T(8,128)(2,1)} collective-permute-done((bf16[8,128,1024]{2,1,0:T(8,128)(2,1)S(1)}, bf16[8,128,1024]{2,1,0:T(8,128)(2,1)}, u32[]{:S(2)}, u32[]{:S(2)}) %collective-permute-start.1) | collective-permute-done | bytes 2097184 | tf_op jit(solution)/shard_map/ppermute | solution.py:721
  73.1 11.9 %collective-permute-done.14 = bf16[16,64,256]{2,1,0:T(8,128)(2,1)S(1)} collective-permute-done((bf16[16,64,256]{2,1,0:T(8,128)(2,1)S(1)}, bf16[16,64,256]{2,1,0:T(8,128)(2,1)S(1)}, u32[]{:S(2)}, u32[]{:S(2)}) %collective-permute-start.14) | collective-permute-done | bytes 524320 | tf_op jit(solution)/shard_map/ppermute | solution.py:741
  96.1 15.0 %attend_forward.2 = (bf16[4,128,256]{2,1,0:T(8,128)(2,1)S(1)}, bf16[4,128,256]{2,1,0:T(8,128)(2,1)S(1)}, bf16[4,128,256]{2,1,0:T(8,128)(2,1)S(1)}, bf16[4,128,25...) custom-call(bf16[8,128,1024]{2,1,0:T(8,128)(2,1)S(1)} %copy-done.2, ...), custom_call_target="tpu_custom_call" | custom-call | flops 7515144192 | bytes 10485760 | tf_op jit(solution)/shard_map/attend_forward/pallas_call | solution.py:178
  118.4 15.5 %attend_forward.3 = (bf16[4,128,256]{2,1,0:T(8,128)(2,1)S(1)}, bf16[4,128,256]{2,1,0:T(8,128)(2,1)}, bf16[4,128,256]{2,1,0:T(8,128)(2,1)S(1)}, bf16[4,128,256]{2...) custom-call(bf16[8,128,1024]{2,1,0:T(8,128)(2,1)S(1)} %copy-done.2, ...), custom_call_target="tpu_custom_call" | custom-call | flops 7515144192 | bytes 10485760 | tf_op jit(solution)/shard_map/attend_forward/pallas_call | solution.py:178
  141.8 4.2 first_norm.2
  159.9 52.1 %all-gather.4.cloned.1.call-done = bf16[8,2,16,64,256]{4,3,2,1,0:T(8,128)(2,1)} async-done(((bf16[1,2,16,64,256]{4,3,2,1,0:T(8,128)(2,1)}), bf16[8,2,16,64,256]{4,3,2,1,0:T(8,128)(2,1)}) %all-gather.4.cloned.1.call-update) | async-done | bytes 8388624 | tf_op jit(solution)/shard_map/all_gather | solution.py:852
  211.9 29.7 %feed_forward.1 = (bf16[2048,2048]{1,0:T(8,128)(2,1)}, bf16[2048,2048]{1,0:T(8,128)(2,1)}, f32[1024,1024]{1,0:T(8,128)}, bf16[1024,1024]{1,0:T(8,128)(2,1)}) custom-call(bf16[512,1024]{1,0:T(8,128)(2,1)} %copy-done.33, bf16[512,1024]{1,0:T(8,128)(2,1)} %copy-done.36, bf16[512,1024]{1,0:T(8,128)(2,1)} %copy-done.66, ...), custom_call_target="tpu_custom_call" | custom-call | flops 17179869184 | bytes 29360128 | tf_op jit(solution)/shard_map/feed_forward/pallas_call | solution.py:381
  241.7 4.4 collective-permute-done.15.far
  247.4 4.1 second_norm.2
  254.0 4.4 second_norm.3
  264.5 47.7 %feed_backward.1 = (bf16[16,16,64,256]{3,2,1,0:T(8,128)(2,1)}, f32[1,2048]{1,0:T(1,128)}, f32[1024,1024]{1,0:T(8,128)}, bf16[1024,1024]{1,0:T(8,128)(2,1)}) custom-call(bf16[512,1024]{1,0:T(8,128)(2,1)} %copy-done.37, bf16[512,1024]{1,0:T(8,128)(2,1)} %copy-done.38, bf16[512,1024]{1,0:T(8,128)(2,1)} %copy-done.67, bf16[512,1024]{1,0:T(8,128)(2,1)} %copy-done.68, ...), custom_call_target="tpu_custom_call" | custom-call | flops 34359738368 | bytes 54525952 | tf_op jit(solution)/shard_map/feed_backward/pallas_call | solution.py:466
  312.4 4.4 collective-permute-done.18.far
  316.7 7.4 %first_back.2 = (f32[512,1024]{1,0:T(8,128)S(1)}, bf16[512,1024]{1,0:T(8,128)(2,1)S(1)}, bf16[4,128,256]{2,1,0:T(8,128)(2,1)S(1)}, bf16[4,128,256]{2,1,0:T(8,128...) custom-call(s32[1]{0:T(128)} %bitcast.place, f32[512,1024]{1,0:T(8,128)} %copy-done.6, ...), custom_call_target="tpu_custom_call" | custom-call | flops 1073741824 | bytes 8388608 | tf_op jit(solution)/shard_map/first_back/pallas_call | solution.py:530
  328.4 6.5 %first_back.3 = (f32[512,1024]{1,0:T(8,128)S(1)}, bf16[512,1024]{1,0:T(8,128)(2,1)S(1)}, bf16[4,128,256]{2,1,0:T(8,128)(2,1)S(1)}, bf16[4,128,256]{2,1,0:T(8,128...) custom-call(s32[1]{0:T(128)} %bitcast.place, f32[512,1024]{1,0:T(8,128)} %copy-done.5, ...), custom_call_target="tpu_custom_call" | custom-call | flops 1073741824 | bytes 8388608 | tf_op jit(solution)/shard_map/first_back/pallas_call | solution.py:530
  340.3 29.6 %attend_backward.2 = (f32[768,1024]{1,0:T(8,128)}, f32[4,128,1024]{2,1,0:T(8,128)}, bf16[4,128,1024]{2,1,0:T(8,128)(2,1)}, bf16[4,128,1024]{2,1,0:T(8,128)(2,1)}...) custom-call(bf16[4,512,768]{2,1,0:T(8,128)(2,1)} %get-tuple-element.106.saved, ...), custom_call_target="tpu_custom_call" | custom-call | flops 17178820608 | bytes 22020096 | tf_op jit(solution)/shard_map/attend_backward/pallas_call | solution.py:274
  382.6 4.0 collective-permute-done.23.right
  394.1 30.4 %attend_backward.3 = (bf16[1024,768]{1,0:T(8,128)(2,1)}, f32[4,128,1024]{2,1,0:T(8,128)}, bf16[4,128,1024]{2,1,0:T(8,128)(2,1)}, bf16[4,128,1024]{2,1,0:T(8,128)...) custom-call(bf16[4,512,768]{2,1,0:T(8,128)(2,1)} %get-tuple-element.123.saved, ...), custom_call_target="tpu_custom_call" | custom-call | flops 17178820608 | bytes 22020096 | tf_op jit(solution)/shard_map/attend_backward/pallas_call | solution.py:274
  437.7 4.4 collective-permute-done.36
  445.5 8.2 %collective-permute-done.32 = bf16[4,144,768]{2,1,0:T(8,128)(2,1)} collective-permute-done((bf16[4,144,768]{2,1,0:T(8,128)(2,1)}, bf16[4,144,768]{2,1,0:T(8,128)(2,1)}, u32[]{:S(2)}, u32[]{:S(2)}) %collective-permute-start.32) | collective-permute-done | bytes 884768 | tf_op jit(solution)/shard_map/ppermute | solution.py:741
  455.0 8.9 %collective-permute-done.31.refs_0_ = bf16[4,128,1024]{2,1,0:T(8,128)(2,1)S(1)} collective-permute-done((bf16[4,128,1024]{2,1,0:T(8,128)(2,1)S(1)}, bf16[4,128,1024]{2,1,0:T(8,128)(2,1)S(1)}, u32[]{:S(2)}, u32[]{:S(2)}) %collective-permute-start.31) | collective-permute-done | bytes 1048608 | tf_op jit(solution)/shard_map/ppermute | solution.py:721
  467.1 6.9 %collective-permute-done.37 = bf16[4,33,1024]{2,1,0:T(8,128)(2,1)S(1)} collective-permute-done((bf16[4,33,1024]{2,1,0:T(8,128)(2,1)S(1)}, bf16[4,33,1024]{2,1,0:T(8,128)(2,1)S(1)}, u32[]{:S(2)}, u32[]{:S(2)}) %collective-permute-start.37) | collective-permute-done | bytes 270368 | tf_op jit(solution)/shard_map/ppermute | solution.py:741
  483.8 11.9 %collective-permute-done.39 = bf16[1,33,1024]{2,1,0:T(8,128)(2,1)S(1)} collective-permute-done((bf16[1,33,1024]{2,1,0:T(8,128)(2,1)S(1)}, bf16[1,33,1024]{2,1,0:T(8,128)(2,1)S(1)}, u32[]{:S(2)}, u32[]{:S(2)}) %collective-permute-start.39) | collective-permute-done | bytes 67616 | tf_op jit(solution)/shard_map/ppermute | solution.py:741
  499.0 5.2 collective-permute-done.34
  (362 shorter events, 146.2 us)
Async XLA Ops:
  17.7 69.7 %all-gather.6.cloned.1.call-start = ((), (), s32[]{:S(2)}) async-start(), calls=%async_computation.5 | async-start | bytes 3244032 | tf_op jit(solution)/shard_map/all_gather | solution.py:813
  24.9 187.0 %all-gather.4.cloned.1.call-start = ((), (), s32[]{:S(2)}) async-start(), calls=%async_computation.3 | async-start | bytes 9437184 | tf_op jit(solution)/shard_map/all_gather | solution.py:852
  25.0 47.3 %collective-permute-start.1 = (bf16[8,128,1024]{2,1,0:T(8,128)(2,1)S(1)}, bf16[8,128,1024]{2,1,0:T(8,128)(2,1)}, u32[]{:S(2)}, u32[]{:S(2)}) collective-permute-start(bf16[8,128,1024]{2,1,0:T(8,128)(2,1)S(1)} %copy-done.2), channel_id=1, source_target_pairs={{0,2},{1,3},{2,0},{3,1},{4,6},{5,7},{6,4},{7,5},{8,10},{9,11},{10,... | collective-permute-start | bytes 6291464 | tf_op jit(solution)/shard_map/ppermute | solution.py:721
  72.4 12.6 %collective-permute-start.14 = (bf16[16,64,256]{2,1,0:T(8,128)(2,1)S(1)}, bf16[16,64,256]{2,1,0:T(8,128)(2,1)S(1)}, u32[]{:S(2)}, u32[]{:S(2)}) collective-permute-start(bf16[16,64,256]{2,1,0:T(8,128)(2,1)S(1)} %hold.4), channel_id=1, source_target_pairs={{0,2},{2,0},{1,3},{3,1},{4,6},{6,4},{5,7},{7,5},{8,10},{10,8},{9,1... | collective-permute-start | bytes 1572872 | tf_op jit(solution)/shard_map/ppermute | solution.py:741
  86.2 410.1 %reduce-scatter.2.cloned.1.call-start = ((), (), s32[]{:S(2)}) async-start(), calls=%async_computation.4 | async-start | bytes 9437184 | tf_op jit(solution)/shard_map/reduce_scatter | solution.py:897
  112.0 25.7 %collective-permute-start.7 = (bf16[16,32,1024]{2,1,0:T(8,128)(2,1)S(1)}, bf16[16,32,1024]{2,1,0:T(8,128)(2,1)}, u32[]{:S(2)}, u32[]{:S(2)}) collective-permute-start(bf16[16,32,1024]{2,1,0:T(8,128)(2,1)S(1)} %bitcast.222), channel_id=1, source_target_pairs={{0,1},{1,0},{2,3},{3,2},{4,5},{5,4},{6,7},{7,6},{8,9},{9,8},{10,11... | collective-permute-start | bytes 3145736 | tf_op jit(solution)/shard_map/ppermute | solution.py:724
  113.4 23.3 %collective-permute-start.4 = (bf16[4,128,256]{2,1,0:T(8,128)(2,1)}, bf16[4,128,256]{2,1,0:T(8,128)(2,1)}, u32[]{:S(2)}, u32[]{:S(2)}) collective-permute-start(bf16[4,128,256]{2,1,0:T(8,128)(2,1)} %copy-done.47), channel_id=1, source_target_pairs={{0,1},{1,0},{2,3},{3,2},{4,5},{5,4},{6,7},{7,6},{8,9},{9,8},{10,11... | collective-permute-start | bytes 786440 | tf_op jit(solution)/shard_map/ppermute | solution.py:721
  113.9 27.9 %collective-permute-start.5 = (bf16[4,128,256]{2,1,0:T(8,128)(2,1)}, bf16[4,128,256]{2,1,0:T(8,128)(2,1)}, u32[]{:S(2)}, u32[]{:S(2)}) collective-permute-start(bf16[4,128,256]{2,1,0:T(8,128)(2,1)} %copy-done.44), channel_id=1, source_target_pairs={{0,2},{1,3},{2,0},{3,1},{4,6},{5,7},{6,4},{7,5},{8,10},{9,11},{10,... | collective-permute-start | bytes 786440 | tf_op jit(solution)/shard_map/ppermute | solution.py:721
  114.7 27.0 %collective-permute-start.6 = (bf16[4,128,256]{2,1,0:T(8,128)(2,1)}, bf16[4,128,256]{2,1,0:T(8,128)(2,1)}, u32[]{:S(2)}, u32[]{:S(2)}) collective-permute-start(bf16[4,128,256]{2,1,0:T(8,128)(2,1)} %copy-done.43), channel_id=1, source_target_pairs={{0,3},{1,2},{2,1},{3,0},{4,7},{5,6},{6,5},{7,4},{8,11},{9,10},{10,... | collective-permute-start | bytes 786440 | tf_op jit(solution)/shard_map/ppermute | solution.py:721
  137.7 12.2 %collective-permute-start.10 = (bf16[4,128,256]{2,1,0:T(8,128)(2,1)}, bf16[4,128,256]{2,1,0:T(8,128)(2,1)S(1)}, u32[]{:S(2)}, u32[]{:S(2)}) collective-permute-start(bf16[4,128,256]{2,1,0:T(8,128)(2,1)} %copy-done.45), channel_id=1, source_target_pairs={{0,3},{1,2},{2,1},{3,0},{4,7},{5,6},{6,5},{7,4},{8,11},{9,10},{10,... | collective-permute-start | bytes 786440 | tf_op jit(solution)/shard_map/ppermute | solution.py:721
  326.4 13.6 %collective-permute-start.20 = (bf16[4,128,256]{2,1,0:T(8,128)(2,1)}, bf16[4,128,256]{2,1,0:T(8,128)(2,1)}, u32[]{:S(2)}, u32[]{:S(2)}) collective-permute-start(bf16[4,128,256]{2,1,0:T(8,128)(2,1)} %get-tuple-element.110), channel_id=1, source_target_pairs={{0,2},{1,3},{2,0},{3,1},{4,6},{5,7},{6,4},{7,5},{8,10},{9,11},{10,... | collective-permute-start | bytes 786440 | tf_op jit(solution)/shard_map/ppermute | solution.py:721
  327.9 12.4 %collective-permute-start.21 = (bf16[4,128,256]{2,1,0:T(8,128)(2,1)}, bf16[4,128,256]{2,1,0:T(8,128)(2,1)}, u32[]{:S(2)}, u32[]{:S(2)}) collective-permute-start(bf16[4,128,256]{2,1,0:T(8,128)(2,1)} %get-tuple-element.111), channel_id=1, source_target_pairs={{0,3},{1,2},{2,1},{3,0},{4,7},{5,6},{6,5},{7,4},{8,11},{9,10},{10,... | collective-permute-start | bytes 786440 | tf_op jit(solution)/shard_map/ppermute | solution.py:721
  338.0 32.4 %collective-permute-start.24 = (bf16[4,128,256]{2,1,0:T(8,128)(2,1)}, bf16[4,128,256]{2,1,0:T(8,128)(2,1)S(1)}, u32[]{:S(2)}, u32[]{:S(2)}) collective-permute-start(bf16[4,128,256]{2,1,0:T(8,128)(2,1)} %get-tuple-element.119), channel_id=1, source_target_pairs={{0,1},{1,0},{2,3},{3,2},{4,5},{5,4},{6,7},{7,6},{8,9},{9,8},{10,11... | collective-permute-start | bytes 786440 | tf_op jit(solution)/shard_map/ppermute | solution.py:721
  338.4 31.9 %collective-permute-start.25 = (bf16[4,128,256]{2,1,0:T(8,128)(2,1)}, bf16[4,128,256]{2,1,0:T(8,128)(2,1)S(1)}, u32[]{:S(2)}, u32[]{:S(2)}) collective-permute-start(bf16[4,128,256]{2,1,0:T(8,128)(2,1)} %get-tuple-element.120), channel_id=1, source_target_pairs={{0,2},{1,3},{2,0},{3,1},{4,6},{5,7},{6,4},{7,5},{8,10},{9,11},{10,... | collective-permute-start | bytes 786440 | tf_op jit(solution)/shard_map/ppermute | solution.py:721
  340.0 30.5 %collective-permute-start.26 = (bf16[4,128,256]{2,1,0:T(8,128)(2,1)}, bf16[4,128,256]{2,1,0:T(8,128)(2,1)S(1)}, u32[]{:S(2)}, u32[]{:S(2)}) collective-permute-start(bf16[4,128,256]{2,1,0:T(8,128)(2,1)} %get-tuple-element.121), channel_id=1, source_target_pairs={{0,3},{1,2},{2,1},{3,0},{4,7},{5,6},{6,5},{7,4},{8,11},{9,10},{10,... | collective-permute-start | bytes 786440 | tf_op jit(solution)/shard_map/ppermute | solution.py:721
  388.8 39.9 %collective-permute-start.27 = (bf16[4,128,1024]{2,1,0:T(8,128)(2,1)S(1)}, bf16[4,128,1024]{2,1,0:T(8,128)(2,1)S(1)}, u32[]{:S(2)}, u32[]{:S(2)}) collective-permute-start(bf16[4,128,1024]{2,1,0:T(8,128)(2,1)S(1)} %add_low.2.refs_1_), channel_id=1, source_target_pairs={{0,2},{1,3},{2,0},{3,1},{4,6},{5,7},{6,4},{7,5},{8,10},{9,11},{10,... | collective-permute-start | bytes 3145736 | tf_op jit(solution)/shard_map/ppermute | solution.py:721
  425.0 18.3 %collective-permute-start.22 = (bf16[4,128,1024]{2,1,0:T(8,128)(2,1)}, bf16[4,128,1024]{2,1,0:T(8,128)(2,1)}, u32[]{:S(2)}, u32[]{:S(2)}) collective-permute-start(bf16[4,128,1024]{2,1,0:T(8,128)(2,1)} %get-tuple-element.116), channel_id=1, source_target_pairs={{0,1},{1,0},{2,3},{3,2},{4,5},{5,4},{6,7},{7,6},{8,9},{9,8},{10,11... | collective-permute-start | bytes 3145736 | tf_op jit(solution)/shard_map/ppermute | solution.py:724
  426.8 15.3 %collective-permute-start.36 = (bf16[4,2,33,1024]{3,0,2,1:T(4,128)(2,1)S(1)}, bf16[4,2,33,1024]{3,0,2,1:T(4,128)(2,1)}, u32[]{:S(2)}, u32[]{:S(2)}) collective-permute-start(bf16[4,2,33,1024]{3,0,2,1:T(4,128)(2,1)S(1)} %copy.185), channel_id=1, source_target_pairs={{0,2},{2,0},{1,3},{3,1},{4,6},{6,4},{5,7},{7,5},{8,10},{10,8},{9,1... | collective-permute-start | bytes 1622024 | tf_op jit(solution)/shard_map/ppermute | solution.py:741
  431.2 22.4 %collective-permute-start.32 = (bf16[4,144,768]{2,1,0:T(8,128)(2,1)}, bf16[4,144,768]{2,1,0:T(8,128)(2,1)}, u32[]{:S(2)}, u32[]{:S(2)}) collective-permute-start(bf16[4,144,768]{2,1,0:T(8,128)(2,1)} %dynamic-slice_bitcast_fusion.1), channel_id=1, source_target_pairs={{0,4},{4,0},{1,5},{5,1},{2,6},{6,2},{3,7},{7,3},{8,12},{12,8},{9,1... | collective-permute-start | bytes 2654216 | tf_op jit(solution)/shard_map/ppermute | solution.py:741
  435.6 28.4 %collective-permute-start.31 = (bf16[4,128,1024]{2,1,0:T(8,128)(2,1)S(1)}, bf16[4,128,1024]{2,1,0:T(8,128)(2,1)S(1)}, u32[]{:S(2)}, u32[]{:S(2)}) collective-permute-start(bf16[4,128,1024]{2,1,0:T(8,128)(2,1)S(1)} %add_low.3), channel_id=1, source_target_pairs={{0,2},{1,3},{2,0},{3,1},{4,6},{5,7},{6,4},{7,5},{8,10},{9,11},{10,... | collective-permute-start | bytes 3145736 | tf_op jit(solution)/shard_map/ppermute | solution.py:721
  437.7 27.7 %collective-permute-start.29 = (bf16[4,128,1024]{2,1,0:T(8,128)(2,1)S(1)}, bf16[4,128,1024]{2,1,0:T(8,128)(2,1)S(1)}, u32[]{:S(2)}, u32[]{:S(2)}) collective-permute-start(bf16[4,128,1024]{2,1,0:T(8,128)(2,1)S(1)} %copy-done.65), channel_id=1, source_target_pairs={{0,1},{1,0},{2,3},{3,2},{4,5},{5,4},{6,7},{7,6},{8,9},{9,8},{10,11... | collective-permute-start | bytes 3145736 | tf_op jit(solution)/shard_map/ppermute | solution.py:724
  464.5 16.8 %collective-permute-start.33 = (bf16[2,144,768]{2,0,1:T(2,128)(2,1)S(1)}, bf16[2,144,768]{2,0,1:T(2,128)(2,1)S(1)}, u32[]{:S(2)}, u32[]{:S(2)}) collective-permute-start(bf16[2,144,768]{2,0,1:T(2,128)(2,1)S(1)} %bitcast.269), channel_id=1, source_target_pairs={{0,8},{8,0},{16,24},{24,16},{1,9},{9,1},{17,25},{25,17},{2,10},{10... | collective-permute-start | bytes 1327112 | tf_op jit(solution)/shard_map/ppermute | solution.py:741
  479.8 15.8 %collective-permute-start.39 = (bf16[1,33,1024]{2,1,0:T(8,128)(2,1)S(1)}, bf16[1,33,1024]{2,1,0:T(8,128)(2,1)S(1)}, u32[]{:S(2)}, u32[]{:S(2)}) collective-permute-start(bf16[1,33,1024]{2,1,0:T(8,128)(2,1)S(1)} %constant_dynamic-slice_fusion), channel_id=1, source_target_pairs={{0,16},{8,24},{16,0},{24,8},{1,17},{9,25},{17,1},{25,9},{2,18},{10... | collective-permute-start | bytes 202760 | tf_op jit(solution)/shard_map/ppermute | solution.py:741
  482.2 22.1 %collective-permute-start.34 = (bf16[1,144,768]{2,0,1:T(2,128)(2,1)S(1)}, bf16[1,144,768]{2,0,1:T(2,128)(2,1)S(1)}, u32[]{:S(2)}, u32[]{:S(2)}) collective-permute-start(bf16[1,144,768]{2,0,1:T(2,128)(2,1)S(1)} %constant_dynamic-slice_fusion.1), channel_id=1, source_target_pairs={{0,16},{8,24},{16,0},{24,8},{1,17},{9,25},{17,1},{25,9},{2,18},{10... | collective-permute-start | bytes 663560 | tf_op jit(solution)/shard_map/ppermute | solution.py:741
  (91 other events, 521.9 us)
Sparse Core Ops, SparseCore 0:
  25.0 57.9 all-gather.5
  86.3 125.6 all-gather.3
  312.3 147.1 reduce-scatter.1

commit v10 on v9

--- a/solution.py
+++ b/solution.py
@@ -1004,12 +1004,12 @@
     )
     blocks = halve(blocks.reshape((sizes["z"], 2) + blocks.shape[1:]), 1, "y").astype(BF16)
     blocks = hold(blocks, work_hops[1:])
-    shared = halve(hold(shared, [blocks]), 1, "y")
+    weight_owned = halve(weight_owned, 0, "x")
+    shared = halve(hold(shared, [blocks, weight_owned]), 1, "y")
     shared = z_scatter(shared)
     output_owned = shared[:share]
     owned = shared[share, :vector_count]
     blocks = z_scatter(blocks)
-    weight_owned = halve(weight_owned, 0, "x")
     blocks = jnp.concatenate(
         [
             blocks[: ctx_size * share].reshape(ctx_size, share, 3 * lanes),
@@ -1019,7 +1019,7 @@
         ],
         axis=1,
     )
-    held = lax.all_to_all(hold(blocks, [weight_owned]), CTX, 0, 0, tiled=True)
+    held = lax.all_to_all(blocks, CTX, 0, 0, tiled=True)
     bias_owned = jnp.sum(held[:, share, : 2 * share], axis=0)
     project_owned = jnp.concatenate(
         [

time: 532 us -> 557 us (1.047)
  waiting for transfers between devices: 189 us -> 207 us
  other arithmetic: 19 us -> 27.4 us
    ppermute x11, waiting for transfers between devices: 51.6 us -> 75.9 us  [trade(): lax.ppermute(array, name, [(i, i ^ step) for i in range(sizes[name])])]
  transfers between devices with their start and end apart: 46 -> 46, of which waited for: 22 -> 22; matrix products, arithmetic and copies ran while one was open for 8% -> 9% of each run, Pallas kernels for 23% -> 22%
where the time goes in v10:
time: 557 us; the launch traced here: 553 us
  waiting for transfers between devices  207 us (37%)
  Pallas kernels  206 us (37%)
  local copies, waits for them, and re-layouts  65.5 us (12%)
  starting transfers between devices  32 us (6%)
  other arithmetic  27.4 us (5%)
  between operations  15.2 us (3%)
    ppermute x11, waiting for transfers between devices, trade(): lax.ppermute(array, name, [(i, i ^ step) for i in range(sizes[name])])  75.9 us
    pallas_call x2, Pallas kernels, attend_back(): pl.pallas_call(functools.partial(attend_back_kernel, len(after), len(earl...  60 us
    all_gather x1, waiting for transfers between devices, on_device(): lax.all_gather(widen(own_pieces, 'x'), SEQ, axis=0)  52.1 us
    ppermute x15, waiting for transfers between devices, hop(): return lax.ppermute(array, CTX, [(i, i ^ step) for i in range(ctx_size)])  49.9 us
    pallas_call x1, Pallas kernels, feed_back(): pl.pallas_call(feed_back_kernel, grid=(hidden // wide,), in_specs=[reside...  47.7 us
    unnamed x158, local copies, waits for them, and re-layouts  40.8 us
    pallas_call x2, Pallas kernels, attend(): pl.pallas_call(functools.partial(attend_kernel, len(after)), grid=(count,...  30.5 us
    pallas_call x6, Pallas kernels, row_call(): pl.pallas_call(kernel, grid=(rows // ROW_BLOCK,), in_specs=ins, out_specs...  29.9 us
  transfers between devices with their start and end apart: 46, of which 22 were waited for; matrix products, arithmetic and copies ran while one was open for 9% of the time, Pallas kernels for 22%

profile of v10, /device:TPU:0, one launch (start us, length us, event | category | flops | bytes accessed | tf_op | source)
XLA Modules:
  0.0 552.5 jit_solution(1872434944089617384)
XLA Ops:
  17.8 6.2 %all-to-all-done = bf16[4,48,768]{2,1,0:T(8,128)(2,1)S(1)} async-done(((bf16[4,48,768]{2,1,0:T(8,128)(2,1)}), bf16[4,48,768]{2,1,0:T(8,128)(2,1)S(1)}, u32[]{:S(2)}, u32[]{:S(2)}) %all-to-all-start) | async-done | bytes 294944 | tf_op jit(solution)/shard_map/all_to_all | solution.py:802
  28.8 43.5 %collective-permute-done.1.t2.refs_0_ = bf16[8,128,1024]{2,1,0:T(8,128)(2,1)} collective-permute-done((bf16[8,128,1024]{2,1,0:T(8,128)(2,1)S(1)}, bf16[8,128,1024]{2,1,0:T(8,128)(2,1)}, u32[]{:S(2)}, u32[]{:S(2)}) %collective-permute-start.1) | collective-permute-done | bytes 2097184 | tf_op jit(solution)/shard_map/ppermute | solution.py:721
  73.1 11.9 %collective-permute-done.14 = bf16[16,64,256]{2,1,0:T(8,128)(2,1)S(1)} collective-permute-done((bf16[16,64,256]{2,1,0:T(8,128)(2,1)S(1)}, bf16[16,64,256]{2,1,0:T(8,128)(2,1)S(1)}, u32[]{:S(2)}, u32[]{:S(2)}) %collective-permute-start.14) | collective-permute-done | bytes 524320 | tf_op jit(solution)/shard_map/ppermute | solution.py:741
  96.1 15.0 %attend_forward.2 = (bf16[4,128,256]{2,1,0:T(8,128)(2,1)S(1)}, bf16[4,128,256]{2,1,0:T(8,128)(2,1)S(1)}, bf16[4,128,256]{2,1,0:T(8,128)(2,1)S(1)}, bf16[4,128,25...) custom-call(bf16[8,128,1024]{2,1,0:T(8,128)(2,1)S(1)} %copy-done.2, ...), custom_call_target="tpu_custom_call" | custom-call | flops 7515144192 | bytes 10485760 | tf_op jit(solution)/shard_map/attend_forward/pallas_call | solution.py:178
  118.4 15.5 %attend_forward.3 = (bf16[4,128,256]{2,1,0:T(8,128)(2,1)S(1)}, bf16[4,128,256]{2,1,0:T(8,128)(2,1)}, bf16[4,128,256]{2,1,0:T(8,128)(2,1)S(1)}, bf16[4,128,256]{2...) custom-call(bf16[8,128,1024]{2,1,0:T(8,128)(2,1)S(1)} %copy-done.2, ...), custom_call_target="tpu_custom_call" | custom-call | flops 7515144192 | bytes 10485760 | tf_op jit(solution)/shard_map/attend_forward/pallas_call | solution.py:178
  141.8 4.2 first_norm.2
  159.9 52.1 %all-gather.4.cloned.1.call-done = bf16[8,2,16,64,256]{4,3,2,1,0:T(8,128)(2,1)} async-done(((bf16[1,2,16,64,256]{4,3,2,1,0:T(8,128)(2,1)}), bf16[8,2,16,64,256]{4,3,2,1,0:T(8,128)(2,1)}) %all-gather.4.cloned.1.call-update) | async-done | bytes 8388624 | tf_op jit(solution)/shard_map/all_gather | solution.py:852
  211.9 29.7 %feed_forward.1 = (bf16[2048,2048]{1,0:T(8,128)(2,1)}, bf16[2048,2048]{1,0:T(8,128)(2,1)}, f32[1024,1024]{1,0:T(8,128)}, bf16[1024,1024]{1,0:T(8,128)(2,1)}) custom-call(bf16[512,1024]{1,0:T(8,128)(2,1)} %copy-done.33, bf16[512,1024]{1,0:T(8,128)(2,1)} %copy-done.36, bf16[512,1024]{1,0:T(8,128)(2,1)} %copy-done.66, ...), custom_call_target="tpu_custom_call" | custom-call | flops 17179869184 | bytes 29360128 | tf_op jit(solution)/shard_map/feed_forward/pallas_call | solution.py:381
  241.7 4.4 collective-permute-done.15.far
  247.4 4.1 second_norm.2
  254.0 4.4 second_norm.3
  264.4 47.7 %feed_backward.1 = (bf16[16,16,64,256]{3,2,1,0:T(8,128)(2,1)}, f32[1,2048]{1,0:T(1,128)}, f32[1024,1024]{1,0:T(8,128)}, bf16[1024,1024]{1,0:T(8,128)(2,1)}) custom-call(bf16[512,1024]{1,0:T(8,128)(2,1)} %copy-done.37, bf16[512,1024]{1,0:T(8,128)(2,1)} %copy-done.38, bf16[512,1024]{1,0:T(8,128)(2,1)} %copy-done.67, bf16[512,1024]{1,0:T(8,128)(2,1)} %copy-done.68, ...), custom_call_target="tpu_custom_call" | custom-call | flops 34359738368 | bytes 54525952 | tf_op jit(solution)/shard_map/feed_backward/pallas_call | solution.py:466
  312.3 4.4 collective-permute-done.18.far
  316.6 6.7 %first_back.2 = (f32[512,1024]{1,0:T(8,128)S(1)}, bf16[512,1024]{1,0:T(8,128)(2,1)S(1)}, bf16[4,128,256]{2,1,0:T(8,128)(2,1)S(1)}, bf16[4,128,256]{2,1,0:T(8,128...) custom-call(s32[1]{0:T(128)} %bitcast.place, ...), custom_call_target="tpu_custom_call" | custom-call | flops 1073741824 | bytes 8388608 | tf_op jit(solution)/shard_map/first_back/pallas_call | solution.py:530
  327.8 6.4 %first_back.3 = (f32[512,1024]{1,0:T(8,128)S(1)}, bf16[512,1024]{1,0:T(8,128)(2,1)S(1)}, bf16[4,128,256]{2,1,0:T(8,128)(2,1)S(1)}, bf16[4,128,256]{2,1,0:T(8,128...) custom-call(s32[1]{0:T(128)} %bitcast.place, ...), custom_call_target="tpu_custom_call" | custom-call | flops 1073741824 | bytes 8388608 | tf_op jit(solution)/shard_map/first_back/pallas_call | solution.py:530
  342.0 29.6 %attend_backward.2 = (f32[768,1024]{1,0:T(8,128)}, f32[4,128,1024]{2,1,0:T(8,128)}, bf16[4,128,1024]{2,1,0:T(8,128)(2,1)}, bf16[4,128,1024]{2,1,0:T(8,128)(2,1)}...) custom-call(bf16[4,512,768]{2,1,0:T(8,128)(2,1)} %get-tuple-element.106.saved, ...), custom_call_target="tpu_custom_call" | custom-call | flops 17178820608 | bytes 22020096 | tf_op jit(solution)/shard_map/attend_backward/pallas_call | solution.py:274
  384.6 4.0 collective-permute-done.23.right
  396.1 30.5 %attend_backward.3 = (bf16[1024,768]{1,0:T(8,128)(2,1)}, f32[4,128,1024]{2,1,0:T(8,128)}, bf16[4,128,1024]{2,1,0:T(8,128)(2,1)}, bf16[4,128,1024]{2,1,0:T(8,128)...) custom-call(bf16[4,512,768]{2,1,0:T(8,128)(2,1)} %get-tuple-element.123.saved, ...), custom_call_target="tpu_custom_call" | custom-call | flops 17178820608 | bytes 22020096 | tf_op jit(solution)/shard_map/attend_backward/pallas_call | solution.py:274
  438.3 15.2 %collective-permute-done.32 = bf16[4,144,768]{2,1,0:T(8,128)(2,1)} collective-permute-done((bf16[4,144,768]{2,1,0:T(8,128)(2,1)}, bf16[4,144,768]{2,1,0:T(8,128)(2,1)}, u32[]{:S(2)}, u32[]{:S(2)}) %collective-permute-start.32) | collective-permute-done | bytes 884768 | tf_op jit(solution)/shard_map/ppermute | solution.py:741
  455.0 5.3 collective-permute-done.31.refs_0_
  464.4 6.4 %collective-permute-done.35 = bf16[4,2,33,1024]{3,0,2,1:T(4,128)(2,1)} collective-permute-done((bf16[4,2,33,1024]{3,0,2,1:T(4,128)(2,1)}, bf16[4,2,33,1024]{3,0,2,1:T(4,128)(2,1)}, u32[]{:S(2)}, u32[]{:S(2)}) %collective-permute-start.35) | collective-permute-done | bytes 540704 | tf_op jit(solution)/shard_map/ppermute | solution.py:741
  478.9 15.5 %collective-permute-done.34 = bf16[1,144,768]{2,0,1:T(2,128)(2,1)S(1)} collective-permute-done((bf16[1,144,768]{2,0,1:T(2,128)(2,1)S(1)}, bf16[1,144,768]{2,0,1:T(2,128)(2,1)S(1)}, u32[]{:S(2)}, u32[]{:S(2)}) %collective-permute-start.34) | collective-permute-done | bytes 221216 | tf_op jit(solution)/shard_map/ppermute | solution.py:741
  509.9 13.0 %collective-permute-done.36 = bf16[16,64,256]{2,1,0:T(8,128)(2,1)S(1)} collective-permute-done((bf16[16,64,256]{2,1,0:T(8,128)(2,1)S(1)}, bf16[16,64,256]{2,1,0:T(8,128)(2,1)S(1)}, u32[]{:S(2)}, u32[]{:S(2)}) %collective-permute-start.36) | collective-permute-done | bytes 524320 | tf_op jit(solution)/shard_map/ppermute | solution.py:741
  525.5 7.1 %collective-permute-done.37 = bf16[4,33,1024]{2,1,0:T(8,128)(2,1)S(1)} collective-permute-done((bf16[4,33,1024]{2,1,0:T(8,128)(2,1)S(1)}, bf16[4,33,1024]{2,1,0:T(8,128)(2,1)S(1)}, u32[]{:S(2)}, u32[]{:S(2)}) %collective-permute-start.37) | collective-permute-done | bytes 270368 | tf_op jit(solution)/shard_map/ppermute | solution.py:741
  (361 shorter events, 154.4 us)
Async XLA Ops:
  17.7 69.7 %all-gather.6.cloned.1.call-start = ((), (), s32[]{:S(2)}) async-start(), calls=%async_computation.5 | async-start | bytes 3244032 | tf_op jit(solution)/shard_map/all_gather | solution.py:813
  24.9 187.0 %all-gather.4.cloned.1.call-start = ((), (), s32[]{:S(2)}) async-start(), calls=%async_computation.3 | async-start | bytes 9437184 | tf_op jit(solution)/shard_map/all_gather | solution.py:852
  25.0 47.3 %collective-permute-start.1 = (bf16[8,128,1024]{2,1,0:T(8,128)(2,1)S(1)}, bf16[8,128,1024]{2,1,0:T(8,128)(2,1)}, u32[]{:S(2)}, u32[]{:S(2)}) collective-permute-start(bf16[8,128,1024]{2,1,0:T(8,128)(2,1)S(1)} %copy-done.2), channel_id=1, source_target_pairs={{0,2},{1,3},{2,0},{3,1},{4,6},{5,7},{6,4},{7,5},{8,10},{9,11},{10,... | collective-permute-start | bytes 6291464 | tf_op jit(solution)/shard_map/ppermute | solution.py:721
  72.4 12.6 %collective-permute-start.14 = (bf16[16,64,256]{2,1,0:T(8,128)(2,1)S(1)}, bf16[16,64,256]{2,1,0:T(8,128)(2,1)S(1)}, u32[]{:S(2)}, u32[]{:S(2)}) collective-permute-start(bf16[16,64,256]{2,1,0:T(8,128)(2,1)S(1)} %hold.3), channel_id=1, source_target_pairs={{0,2},{2,0},{1,3},{3,1},{4,6},{6,4},{5,7},{7,5},{8,10},{10,8},{9,1... | collective-permute-start | bytes 1572872 | tf_op jit(solution)/shard_map/ppermute | solution.py:741
  86.2 422.2 %reduce-scatter.2.cloned.1.call-start = ((), (), s32[]{:S(2)}) async-start(), calls=%async_computation.4 | async-start | bytes 9437184 | tf_op jit(solution)/shard_map/reduce_scatter | solution.py:897
  112.1 25.7 %collective-permute-start.7 = (bf16[16,32,1024]{2,1,0:T(8,128)(2,1)S(1)}, bf16[16,32,1024]{2,1,0:T(8,128)(2,1)}, u32[]{:S(2)}, u32[]{:S(2)}) collective-permute-start(bf16[16,32,1024]{2,1,0:T(8,128)(2,1)S(1)} %bitcast.222), channel_id=1, source_target_pairs={{0,1},{1,0},{2,3},{3,2},{4,5},{5,4},{6,7},{7,6},{8,9},{9,8},{10,11... | collective-permute-start | bytes 3145736 | tf_op jit(solution)/shard_map/ppermute | solution.py:724
  113.5 23.4 %collective-permute-start.4 = (bf16[4,128,256]{2,1,0:T(8,128)(2,1)}, bf16[4,128,256]{2,1,0:T(8,128)(2,1)}, u32[]{:S(2)}, u32[]{:S(2)}) collective-permute-start(bf16[4,128,256]{2,1,0:T(8,128)(2,1)} %copy-done.49), channel_id=1, source_target_pairs={{0,1},{1,0},{2,3},{3,2},{4,5},{5,4},{6,7},{7,6},{8,9},{9,8},{10,11... | collective-permute-start | bytes 786440 | tf_op jit(solution)/shard_map/ppermute | solution.py:721
  114.0 27.8 %collective-permute-start.5 = (bf16[4,128,256]{2,1,0:T(8,128)(2,1)}, bf16[4,128,256]{2,1,0:T(8,128)(2,1)}, u32[]{:S(2)}, u32[]{:S(2)}) collective-permute-start(bf16[4,128,256]{2,1,0:T(8,128)(2,1)} %copy-done.46), channel_id=1, source_target_pairs={{0,2},{1,3},{2,0},{3,1},{4,6},{5,7},{6,4},{7,5},{8,10},{9,11},{10,... | collective-permute-start | bytes 786440 | tf_op jit(solution)/shard_map/ppermute | solution.py:721
  114.8 27.0 %collective-permute-start.6 = (bf16[4,128,256]{2,1,0:T(8,128)(2,1)}, bf16[4,128,256]{2,1,0:T(8,128)(2,1)}, u32[]{:S(2)}, u32[]{:S(2)}) collective-permute-start(bf16[4,128,256]{2,1,0:T(8,128)(2,1)} %copy-done.45), channel_id=1, source_target_pairs={{0,3},{1,2},{2,1},{3,0},{4,7},{5,6},{6,5},{7,4},{8,11},{9,10},{10,... | collective-permute-start | bytes 786440 | tf_op jit(solution)/shard_map/ppermute | solution.py:721
  136.0 13.0 %collective-permute-start.8 = (bf16[4,128,256]{2,1,0:T(8,128)(2,1)}, bf16[4,128,256]{2,1,0:T(8,128)(2,1)}, u32[]{:S(2)}, u32[]{:S(2)}) collective-permute-start(bf16[4,128,256]{2,1,0:T(8,128)(2,1)} %get-tuple-element.88), channel_id=1, source_target_pairs={{0,1},{1,0},{2,3},{3,2},{4,5},{5,4},{6,7},{7,6},{8,9},{9,8},{10,11... | collective-permute-start | bytes 786440 | tf_op jit(solution)/shard_map/ppermute | solution.py:721
  136.8 12.2 %collective-permute-start.9 = (bf16[4,128,256]{2,1,0:T(8,128)(2,1)}, bf16[4,128,256]{2,1,0:T(8,128)(2,1)S(1)}, u32[]{:S(2)}, u32[]{:S(2)}) collective-permute-start(bf16[4,128,256]{2,1,0:T(8,128)(2,1)} %copy-done.48), channel_id=1, source_target_pairs={{0,2},{1,3},{2,0},{3,1},{4,6},{5,7},{6,4},{7,5},{8,10},{9,11},{10,... | collective-permute-start | bytes 786440 | tf_op jit(solution)/shard_map/ppermute | solution.py:721
  137.8 12.2 %collective-permute-start.10 = (bf16[4,128,256]{2,1,0:T(8,128)(2,1)}, bf16[4,128,256]{2,1,0:T(8,128)(2,1)S(1)}, u32[]{:S(2)}, u32[]{:S(2)}) collective-permute-start(bf16[4,128,256]{2,1,0:T(8,128)(2,1)} %copy-done.47), channel_id=1, source_target_pairs={{0,3},{1,2},{2,1},{3,0},{4,7},{5,6},{6,5},{7,4},{8,11},{9,10},{10,... | collective-permute-start | bytes 786440 | tf_op jit(solution)/shard_map/ppermute | solution.py:721
  325.8 12.8 %collective-permute-start.20 = (bf16[4,128,256]{2,1,0:T(8,128)(2,1)S(1)}, bf16[4,128,256]{2,1,0:T(8,128)(2,1)S(1)}, u32[]{:S(2)}, u32[]{:S(2)}) collective-permute-start(bf16[4,128,256]{2,1,0:T(8,128)(2,1)S(1)} %get-tuple-element.110), channel_id=1, source_target_pairs={{0,2},{1,3},{2,0},{3,1},{4,6},{5,7},{6,4},{7,5},{8,10},{9,11},{10,... | collective-permute-start | bytes 786440 | tf_op jit(solution)/shard_map/ppermute | solution.py:721
  336.6 35.5 %collective-permute-start.24 = (bf16[4,128,256]{2,1,0:T(8,128)(2,1)}, bf16[4,128,256]{2,1,0:T(8,128)(2,1)S(1)}, u32[]{:S(2)}, u32[]{:S(2)}) collective-permute-start(bf16[4,128,256]{2,1,0:T(8,128)(2,1)} %get-tuple-element.119), channel_id=1, source_target_pairs={{0,1},{1,0},{2,3},{3,2},{4,5},{5,4},{6,7},{7,6},{8,9},{9,8},{10,11... | collective-permute-start | bytes 786440 | tf_op jit(solution)/shard_map/ppermute | solution.py:721
  337.1 35.0 %collective-permute-start.25 = (bf16[4,128,256]{2,1,0:T(8,128)(2,1)}, bf16[4,128,256]{2,1,0:T(8,128)(2,1)S(1)}, u32[]{:S(2)}, u32[]{:S(2)}) collective-permute-start(bf16[4,128,256]{2,1,0:T(8,128)(2,1)} %get-tuple-element.120), channel_id=1, source_target_pairs={{0,2},{1,3},{2,0},{3,1},{4,6},{5,7},{6,4},{7,5},{8,10},{9,11},{10,... | collective-permute-start | bytes 786440 | tf_op jit(solution)/shard_map/ppermute | solution.py:721
  338.6 33.5 %collective-permute-start.26 = (bf16[4,128,256]{2,1,0:T(8,128)(2,1)S(1)}, bf16[4,128,256]{2,1,0:T(8,128)(2,1)S(1)}, u32[]{:S(2)}, u32[]{:S(2)}) collective-permute-start(bf16[4,128,256]{2,1,0:T(8,128)(2,1)S(1)} %get-tuple-element.121), channel_id=1, source_target_pairs={{0,3},{1,2},{2,1},{3,0},{4,7},{5,6},{6,5},{7,4},{8,11},{9,10},{10,... | collective-permute-start | bytes 786440 | tf_op jit(solution)/shard_map/ppermute | solution.py:721
  390.8 36.6 %collective-permute-start.27 = (bf16[4,128,1024]{2,1,0:T(8,128)(2,1)S(1)}, bf16[4,128,1024]{2,1,0:T(8,128)(2,1)S(1)}, u32[]{:S(2)}, u32[]{:S(2)}) collective-permute-start(bf16[4,128,1024]{2,1,0:T(8,128)(2,1)S(1)} %add_low.2.refs_1_), channel_id=1, source_target_pairs={{0,2},{1,3},{2,0},{3,1},{4,6},{5,7},{6,4},{7,5},{8,10},{9,11},{10,... | collective-permute-start | bytes 3145736 | tf_op jit(solution)/shard_map/ppermute | solution.py:721
  430.0 23.6 %collective-permute-start.32 = (bf16[4,144,768]{2,1,0:T(8,128)(2,1)}, bf16[4,144,768]{2,1,0:T(8,128)(2,1)}, u32[]{:S(2)}, u32[]{:S(2)}) collective-permute-start(bf16[4,144,768]{2,1,0:T(8,128)(2,1)} %dynamic-slice_bitcast_fusion.1), channel_id=1, source_target_pairs={{0,4},{4,0},{1,5},{5,1},{2,6},{6,2},{3,7},{7,3},{8,12},{12,8},{9,1... | collective-permute-start | bytes 2654216 | tf_op jit(solution)/shard_map/ppermute | solution.py:741
  433.9 26.3 %collective-permute-start.31 = (bf16[4,128,1024]{2,1,0:T(8,128)(2,1)}, bf16[4,128,1024]{2,1,0:T(8,128)(2,1)}, u32[]{:S(2)}, u32[]{:S(2)}) collective-permute-start(bf16[4,128,1024]{2,1,0:T(8,128)(2,1)} %add_low.3), channel_id=1, source_target_pairs={{0,2},{1,3},{2,0},{3,1},{4,6},{5,7},{6,4},{7,5},{8,10},{9,11},{10,... | collective-permute-start | bytes 3145736 | tf_op jit(solution)/shard_map/ppermute | solution.py:721
  435.4 40.3 %collective-permute-start.22 = (bf16[4,128,1024]{2,1,0:T(8,128)(2,1)}, bf16[4,128,1024]{2,1,0:T(8,128)(2,1)}, u32[]{:S(2)}, u32[]{:S(2)}) collective-permute-start(bf16[4,128,1024]{2,1,0:T(8,128)(2,1)} %get-tuple-element.116), channel_id=1, source_target_pairs={{0,1},{1,0},{2,3},{3,2},{4,5},{5,4},{6,7},{7,6},{8,9},{9,8},{10,11... | collective-permute-start | bytes 3145736 | tf_op jit(solution)/shard_map/ppermute | solution.py:724
  437.7 33.1 %collective-permute-start.35 = (bf16[4,2,33,1024]{3,0,2,1:T(4,128)(2,1)}, bf16[4,2,33,1024]{3,0,2,1:T(4,128)(2,1)}, u32[]{:S(2)}, u32[]{:S(2)}) collective-permute-start(bf16[4,2,33,1024]{3,0,2,1:T(4,128)(2,1)} %copy.187), channel_id=1, source_target_pairs={{0,2},{2,0},{1,3},{3,1},{4,6},{6,4},{5,7},{7,5},{8,10},{10,8},{9,1... | collective-permute-start | bytes 1622024 | tf_op jit(solution)/shard_map/ppermute | solution.py:741
  464.4 35.3 %collective-permute-start.29 = (bf16[4,128,1024]{2,1,0:T(8,128)(2,1)}, bf16[4,128,1024]{2,1,0:T(8,128)(2,1)}, u32[]{:S(2)}, u32[]{:S(2)}) collective-permute-start(bf16[4,128,1024]{2,1,0:T(8,128)(2,1)} %get-tuple-element.137), channel_id=1, source_target_pairs={{0,1},{1,0},{2,3},{3,2},{4,5},{5,4},{6,7},{7,6},{8,9},{9,8},{10,11... | collective-permute-start | bytes 3145736 | tf_op jit(solution)/shard_map/ppermute | solution.py:724
  474.1 20.3 %collective-permute-start.34 = (bf16[1,144,768]{2,0,1:T(2,128)(2,1)S(1)}, bf16[1,144,768]{2,0,1:T(2,128)(2,1)S(1)}, u32[]{:S(2)}, u32[]{:S(2)}) collective-permute-start(bf16[1,144,768]{2,0,1:T(2,128)(2,1)S(1)} %constant_dynamic-slice_fusion.1), channel_id=1, source_target_pairs={{0,16},{8,24},{16,0},{24,8},{1,17},{9,25},{17,1},{25,9},{2,18},{10... | collective-permute-start | bytes 663560 | tf_op jit(solution)/shard_map/ppermute | solution.py:741
  509.4 13.5 %collective-permute-start.36 = (bf16[16,64,256]{2,1,0:T(8,128)(2,1)S(1)}, bf16[16,64,256]{2,1,0:T(8,128)(2,1)S(1)}, u32[]{:S(2)}, u32[]{:S(2)}) collective-permute-start(bf16[16,64,256]{2,1,0:T(8,128)(2,1)S(1)} %dynamic-slice_bitcast_fusion.3), channel_id=1, source_target_pairs={{0,2},{2,0},{1,3},{3,1},{4,6},{6,4},{5,7},{7,5},{8,10},{10,8},{9,1... | collective-permute-start | bytes 1572872 | tf_op jit(solution)/shard_map/ppermute | solution.py:741
  (91 other events, 580.9 us)
Sparse Core Ops, SparseCore 0:
  25.0 57.9 all-gather.5
  86.3 125.6 all-gather.3
  312.2 147.1 reduce-scatter.1
